TPU v7x, 32 devices: a whole 2x2x4 slice. The times are simulated.
32 devices in a mesh: ctx: 16 (over z, y, x), wsh: 2 (over core).
Axes of the slice: x: 2, y: 2, z: 4, core: 2. Of those that a mesh axis runs over, the one named last changes fastest.
Arguments:
- tokens: bfloat16 [2, 2, 8192, 768], P(None, 'wsh', 'ctx'), may hold values from -6 to 6
- cotangent: bfloat16 [2, 2, 8192, 768], P(None, 'wsh', 'ctx'), may hold values from -6 to 6
- light_qkv: bfloat16 [768, 1536], P('wsh'), may hold values from -0.21875 to 0.21875
- light_out: bfloat16 [512, 768], P('wsh'), may hold values from -4 to 4
- heavy_qkv: bfloat16 [768, 2304], P('wsh'), may hold values from -0.21875 to 0.21875
- heavy_out: bfloat16 [768, 768], P('wsh'), may hold values from -4 to 4
- light_gu: bfloat16 [768, 2048], P('wsh'), may hold values from -0.21875 to 0.21875
- light_down: bfloat16 [1024, 768], P('wsh'), may hold values from -0.1875 to 0.1875
- heavy_gu: bfloat16 [768, 8192], P('wsh'), may hold values from -0.21875 to 0.21875
- heavy_down: bfloat16 [4096, 768], P('wsh'), may hold values from -0.09375 to 0.09375
- routers: bfloat16 [3, 768], P(None, 'wsh'), may hold values from -0.21875 to 0.21875
- gains: bfloat16 [2, 768], P(None, 'wsh'), may hold values from 0.5 to 1.5
- doc_starts: int32 [2, 2, 5], P(None, 'wsh'), may hold values from 0 to 8191, as said below
- q_index: int32 [2, 2, 1024], P(None, 'wsh', 'ctx'), may hold values from 0 to 8191, as said below
- kv_index: int32 [2, 2, 1024], P(None, 'wsh', 'ctx'), may hold values from 0 to 8191, as said below
- ff_index: int32 [2, 2, 1024], P(None, 'wsh', 'ctx'), may hold values from 0 to 8191, as said below
Outputs:
- out_tokens: bfloat16 [2, 2, 8192, 768], P(None, 'wsh', 'ctx')
- grad_tokens: bfloat16 [2, 2, 8192, 768], P(None, 'wsh', 'ctx')
- grad_light_qkv: float32 [768, 1536], P('wsh')
- grad_light_out: float32 [512, 768], P('wsh')
- grad_heavy_qkv: float32 [768, 2304], P('wsh')
- grad_heavy_out: float32 [768, 768], P('wsh')
- grad_light_gu: float32 [768, 2048], P('wsh')
- grad_light_down: float32 [1024, 768], P('wsh')
- grad_heavy_gu: float32 [768, 8192], P('wsh')
- grad_heavy_down: float32 [4096, 768], P('wsh')
- grad_routers: float32 [3, 768], P(None, 'wsh')
- grad_gains: float32 [2, 768], P(None, 'wsh')
Inputs may be any that keep to these rules, and one draw needn't show every extreme that they name: `doc_starts`: per micro-batch and stream the 5 starts rise strictly; the first is 0, the second lies in the first 512 - 128 positions, the third in the last 128 positions of the first 512, the fourth in the first 128 positions of the last 512, the fifth later in the last 512 (512, 8192 as on the slice in use). `q_index`: the entries of the block of 64 that lies on one index of ctx are distinct positions of that index's own 512 positions, rising. `kv_index`: the entries of the block of 64 that lies on one index of ctx are distinct positions of that index's own 512 positions, rising; every document start is among them. `ff_index`: the entries of the block of 64 that lies on one index of ctx are distinct positions of that index's own 512 positions, rising.
All inputs are finite; a program needn't handle non-finite values.
Results may differ from a plain program's by a relative error of at most 0.023.
Values may be sent and summed in bfloat16 or wider, within the bound.
No kernel may reach another device: no remote copies, remote signals or barrier semaphores. Data moves between devices by JAX's collectives and lax.ppermute only.
A program may use at most 320 MiB of HBM per device.

v0:
```python
import jax
import jax.numpy as jnp
from jax import lax
from jax.sharding import PartitionSpec as P

HD = 64
WIN = 128


EPS = 1e-06


def padded(shard, sides, width):
    for axis, dim in sides:
        size, length = (lax.axis_size(axis), shard.shape[dim])
        up = [(i, (i + 1) % size) for i in range(size - 1)]
        down = [(j, i) for i, j in up]
        last = lax.slice_in_dim(shard, length - width, length, axis=dim)
        leading = lax.slice_in_dim(shard, 0, width, axis=dim)
        before = lax.ppermute(last, axis, up)
        after = lax.ppermute(leading, axis, down)
        shard = jnp.concatenate([before, shard, after], axis=dim)
    return shard


def shortened(shard):

    def short(part):
        return part.astype(jnp.bfloat16) if part.dtype == jnp.float32 else part

    return jax.tree.map(short, shard)


def matmul(left, right):
    return jnp.dot(left, right, preferred_element_type=jnp.float32)


def matmul_right(left, right):
    return lax.dot_general(
        left, right, (((1,), (1,)), ((), ())), preferred_element_type=jnp.float32
    )


def matmul_left(left, right):
    return lax.dot_general(
        left, right, (((0,), (0,)), ((), ())), preferred_element_type=jnp.float32
    )


def norm_rows(values, gain):
    return values * lax.rsqrt(jnp.mean(values * values, axis=-1, keepdims=True) + EPS) * gain


def gated(gate_up):
    half = gate_up.shape[-1] // 2
    return jax.nn.gelu(gate_up[:, :half], approximate=True) * gate_up[:, half:]


def gated_back(gate_up, grad):
    unused, pull = jax.vjp(gated, gate_up)
    return pull(grad)[0]


def segment_of(positions, starts):
    return jnp.sum((positions[:, None] >= starts[None, :]).astype(jnp.int32), axis=1) - 1


def split_heads(values, count):
    return values.reshape(values.shape[0], count, -1).transpose(1, 0, 2)


def join_heads(values):
    return values.transpose(1, 0, 2).reshape(values.shape[1], -1)


def attend_forward(query, key, value, allowed, factor):
    scores = jnp.einsum("hqd,hkd->hqk", query, key, preferred_element_type=jnp.float32) * factor
    scores = jnp.where(allowed[None], scores, -1e30)
    probs = jax.nn.softmax(scores, axis=-1)
    weights = probs.astype(jnp.bfloat16)
    mixed = jnp.einsum("hqk,hkd->hqd", weights, value, preferred_element_type=jnp.float32)
    return (probs, weights, mixed)


def attend_backward(key, value, probs, grad_out, factor):
    grad_probs = jnp.einsum("hqd,hkd->hqk", grad_out, value, preferred_element_type=jnp.float32)
    grad_scores = probs * (grad_probs - jnp.sum(probs * grad_probs, axis=-1, keepdims=True))
    grad_low = grad_scores.astype(jnp.bfloat16)
    grad_query = (
        jnp.einsum("hqk,hkd->hqd", grad_low, key, preferred_element_type=jnp.float32) * factor
    )
    return (grad_low, grad_query)


def per_device(
    tokens,
    cotangent,
    light_qkv,
    light_out,
    heavy_qkv,
    heavy_out,
    light_gu,
    light_down,
    heavy_gu,
    heavy_down,
    routers,
    gains,
    doc_starts,
    q_index,
    kv_index,
    ff_index,
):
    shards = (
        light_qkv,
        light_out,
        heavy_qkv,
        heavy_out,
        light_gu,
        light_down,
        heavy_gu,
        heavy_down,
        routers,
        gains,
    )
    tok = tokens.shape[2]
    width = tokens.shape[3]
    seq_len = tok * lax.axis_size("ctx")
    base = lax.axis_index("ctx") * tok
    window = WIN
    factor = HD ** (-0.5)
    inner = light_qkv.shape[1] // 3
    light_count = inner // HD
    heavy_count = width // HD
    results = []
    grad_inputs = []
    totals = None
    for micro in range(tokens.shape[0]):
        gathered = (
            lax.all_gather(shards[0], "wsh", axis=0, tiled=True),
            lax.all_gather(shards[1], "wsh", axis=0, tiled=True),
            lax.all_gather(shards[2], "wsh", axis=0, tiled=True),
            lax.all_gather(shards[3], "wsh", axis=0, tiled=True),
            lax.all_gather(shards[4], "wsh", axis=0, tiled=True),
            lax.all_gather(shards[5], "wsh", axis=0, tiled=True),
            lax.all_gather(shards[6], "wsh", axis=0, tiled=True),
            lax.all_gather(shards[7], "wsh", axis=0, tiled=True),
            lax.all_gather(shards[8], "wsh", axis=1, tiled=True),
            lax.all_gather(shards[9], "wsh", axis=1, tiled=True),
        )
        w_lqkv, w_lout, w_hqkv, w_hout, w_lgu, w_ldown, w_hgu, w_hdown, w_route, w_gain = gathered
        route_full = w_route.astype(jnp.float32)
        gain_one = w_gain[0].astype(jnp.float32)
        gain_two = w_gain[1].astype(jnp.float32)
        stream = tokens[micro, 0].astype(jnp.float32)
        upstream = cotangent[micro, 0]
        starts = doc_starts[micro, 0]
        normed_one = norm_rows(stream, gain_one)
        normed_low = normed_one.astype(jnp.bfloat16)
        light_proj = matmul(normed_low, w_lqkv).astype(jnp.bfloat16)
        padded_pair = padded(light_proj[:, inner:], (("ctx", 0),), window)
        positions = base + jnp.arange(tok, dtype=jnp.int32)
        segments = segment_of(positions, starts)
        near_positions = base - window + jnp.arange(tok + 2 * window, dtype=jnp.int32)
        inside = (near_positions >= 0) & (near_positions < seq_len)
        near_segments = jnp.where(inside, segment_of(near_positions, starts), -1)
        offsets = (
            jnp.arange(tok, dtype=jnp.int32)[:, None]
            + window
            - jnp.arange(tok + 2 * window, dtype=jnp.int32)[None, :]
        )
        window_mask = (jnp.abs(offsets) < window) & (segments[:, None] == near_segments[None, :])
        light_q_heads = split_heads(light_proj[:, :inner], light_count)
        light_k_heads = split_heads(padded_pair[:, :inner], light_count)
        light_v_heads = split_heads(padded_pair[:, inner:], light_count)
        light_probs, light_weights, light_mixed = attend_forward(
            light_q_heads, light_k_heads, light_v_heads, window_mask, factor
        )
        light_context = join_heads(light_mixed).astype(jnp.bfloat16)
        light_branch = matmul(light_context, w_lout)
        query_local = q_index[micro, 0] - base
        key_local = kv_index[micro, 0] - base
        ffn_local = ff_index[micro, 0] - base
        query_rows = normed_low[query_local]
        key_rows = normed_low[key_local]
        query_gate = jax.nn.sigmoid(matmul(query_rows, w_route[0]))
        key_gate = jax.nn.sigmoid(matmul(key_rows, w_route[1]))
        heavy_query = matmul(query_rows, w_hqkv[:, :width]).astype(jnp.bfloat16)
        key_source = normed_one[key_local]
        key_input = (key_source * key_gate[:, None]).astype(jnp.bfloat16)
        heavy_pair = matmul(key_input, w_hqkv[:, width:]).astype(jnp.bfloat16)
        every_pair, every_segment = (
            lax.all_gather(heavy_pair, "ctx", axis=0, tiled=True),
            lax.all_gather(segments[key_local], "ctx", axis=0, tiled=True),
        )
        heavy_mask = segments[query_local][:, None] == every_segment[None, :]
        heavy_q_heads = split_heads(heavy_query, heavy_count)
        heavy_k_heads = split_heads(every_pair[:, :width], heavy_count)
        heavy_v_heads = split_heads(every_pair[:, width:], heavy_count)
        heavy_probs, heavy_weights, heavy_mixed = attend_forward(
            heavy_q_heads, heavy_k_heads, heavy_v_heads, heavy_mask, factor
        )
        heavy_context = join_heads(heavy_mixed).astype(jnp.bfloat16)
        heavy_branch = matmul(heavy_context, w_hout)
        middle = (
            stream
            + light_branch
            + jnp.zeros_like(stream).at[query_local].add(heavy_branch * query_gate[:, None])
        )
        normed_two = norm_rows(middle, gain_two)
        second_low = normed_two.astype(jnp.bfloat16)
        light_gate_up = matmul(second_low, w_lgu)
        light_hidden = gated(light_gate_up).astype(jnp.bfloat16)
        light_ffn = matmul(light_hidden, w_ldown)
        ffn_rows = second_low[ffn_local]
        ffn_gate = jax.nn.sigmoid(matmul(ffn_rows, w_route[2]))
        heavy_gate_up = matmul(ffn_rows, w_hgu)
        heavy_hidden = gated(heavy_gate_up).astype(jnp.bfloat16)
        heavy_ffn = matmul(heavy_hidden, w_hdown)
        combined = (
            middle
            + light_ffn
            + jnp.zeros_like(stream).at[ffn_local].add(heavy_ffn * ffn_gate[:, None])
        )
        results.append(combined.astype(jnp.bfloat16))
        gathered = (
            lax.all_gather(shards[0], "wsh", axis=0, tiled=True),
            lax.all_gather(shards[1], "wsh", axis=0, tiled=True),
            lax.all_gather(shards[2], "wsh", axis=0, tiled=True),
            lax.all_gather(shards[3], "wsh", axis=0, tiled=True),
            lax.all_gather(shards[4], "wsh", axis=0, tiled=True),
            lax.all_gather(shards[5], "wsh", axis=0, tiled=True),
            lax.all_gather(shards[6], "wsh", axis=0, tiled=True),
            lax.all_gather(shards[7], "wsh", axis=0, tiled=True),
            lax.all_gather(shards[8], "wsh", axis=1, tiled=True),
            lax.all_gather(shards[9], "wsh", axis=1, tiled=True),
        )
        w_lqkv, w_lout, w_hqkv, w_hout, w_lgu, w_ldown, w_hgu, w_hdown, w_route, w_gain = gathered
        route_full = w_route.astype(jnp.float32)
        grad_top = upstream.astype(jnp.float32)
        grad_rows_f = grad_top[ffn_local]
        grad_heavy_ffn = (grad_rows_f * ffn_gate[:, None]).astype(jnp.bfloat16)
        grad_ffn_score = jnp.sum(grad_rows_f * heavy_ffn, axis=-1) * ffn_gate * (1.0 - ffn_gate)
        grad_heavy_gu = gated_back(heavy_gate_up, matmul_right(grad_heavy_ffn, w_hdown)).astype(
            jnp.bfloat16
        )
        grad_light_gu = gated_back(light_gate_up, matmul_right(upstream, w_ldown)).astype(
            jnp.bfloat16
        )
        grad_second = matmul_right(grad_light_gu, w_lgu)
        grad_ffn_rows = matmul_right(grad_heavy_gu, w_hgu) + grad_ffn_score[:, None] * route_full[2]
        grad_second = grad_second.at[ffn_local].add(grad_ffn_rows)
        unused, pull_two = jax.vjp(norm_rows, middle, gain_two)
        grad_middle, grad_gain_two = pull_two(grad_second)
        grad_middle = grad_middle + grad_top
        grad_light_branch = grad_middle.astype(jnp.bfloat16)
        grad_rows_q = grad_middle[query_local]
        grad_heavy_branch = (grad_rows_q * query_gate[:, None]).astype(jnp.bfloat16)
        grad_query_score = (
            jnp.sum(grad_rows_q * heavy_branch, axis=-1) * query_gate * (1.0 - query_gate)
        )
        grad_heavy_context = matmul_right(grad_heavy_branch, w_hout).astype(jnp.bfloat16)
        grad_light_context = matmul_right(grad_light_branch, w_lout).astype(jnp.bfloat16)
        grad_heavy_heads = split_heads(grad_heavy_context, heavy_count)
        heavy_grad_low, grad_heavy_q = attend_backward(
            heavy_k_heads, heavy_v_heads, heavy_probs, grad_heavy_heads, factor
        )
        grad_key = (
            jnp.einsum(
                "hqk,hqd->hkd", heavy_grad_low, heavy_q_heads, preferred_element_type=jnp.float32
            )
            * factor
        )
        grad_value = jnp.einsum(
            "hqk,hqd->hkd", heavy_weights, grad_heavy_heads, preferred_element_type=jnp.float32
        )
        grad_heavy_pair = lax.psum_scatter(
            jnp.concatenate([join_heads(grad_key), join_heads(grad_value)], axis=1).astype(
                jnp.bfloat16
            ),
            "ctx",
            scatter_dimension=0,
            tiled=True,
        )
        grad_heavy_query = join_heads(grad_heavy_q).astype(jnp.bfloat16)
        grad_key_input = matmul_right(grad_heavy_pair, w_hqkv[:, width:])
        grad_key_score = jnp.sum(grad_key_input * key_source, axis=-1) * key_gate * (1.0 - key_gate)
        grad_query_rows = (
            matmul_right(grad_heavy_query, w_hqkv[:, :width])
            + grad_query_score[:, None] * route_full[0]
        )
        grad_key_rows = grad_key_input * key_gate[:, None] + grad_key_score[:, None] * route_full[1]
        grad_light_heads = split_heads(grad_light_context, light_count)
        light_grad_low, grad_light_q = attend_backward(
            light_k_heads, light_v_heads, light_probs, grad_light_heads, factor
        )
        grad_light_k = (
            jnp.einsum(
                "hqk,hqd->hkd", light_grad_low, light_q_heads, preferred_element_type=jnp.float32
            )
            * factor
        )
        grad_light_v = jnp.einsum(
            "hqk,hqd->hkd", light_weights, grad_light_heads, preferred_element_type=jnp.float32
        )
        grad_padded = jnp.concatenate([join_heads(grad_light_k), join_heads(grad_light_v)], axis=1)
        rim_grads = jnp.concatenate([grad_padded[:window], grad_padded[tok + window :]], axis=0)
        returned = padded(rim_grads.astype(jnp.bfloat16), (("ctx", 0),), window).astype(
            rim_grads.dtype
        )
        grad_own = grad_padded[window : tok + window]
        grad_own = (
            grad_own.at[:window]
            .add(returned[:window])
            .at[tok - window :]
            .add(returned[3 * window :])
        )
        grad_light_proj = jnp.concatenate([join_heads(grad_light_q), grad_own], axis=1).astype(
            jnp.bfloat16
        )
        grad_first = matmul_right(grad_light_proj, w_lqkv)
        grad_first = (
            grad_first.at[query_local].add(grad_query_rows).at[key_local].add(grad_key_rows)
        )
        unused, pull_one = jax.vjp(norm_rows, stream, gain_one)
        grad_stream, grad_gain_one = pull_one(grad_first)
        grad_inputs.append((grad_stream + grad_middle).astype(jnp.bfloat16))
        grad_route = jnp.stack(
            [
                matmul(grad_query_score, query_rows.astype(jnp.float32)),
                matmul(grad_key_score, key_rows.astype(jnp.float32)),
                matmul(grad_ffn_score, ffn_rows.astype(jnp.float32)),
            ]
        )
        grad_heavy_proj = jnp.concatenate(
            [matmul_left(query_rows, grad_heavy_query), matmul_left(key_input, grad_heavy_pair)],
            axis=1,
        )
        weight_grads = (
            matmul_left(normed_low, grad_light_proj),
            matmul_left(light_context, grad_light_branch),
            grad_heavy_proj,
            matmul_left(heavy_context, grad_heavy_branch),
            matmul_left(second_low, grad_light_gu),
            matmul_left(light_hidden, upstream),
            matmul_left(ffn_rows, grad_heavy_gu),
            matmul_left(heavy_hidden, grad_heavy_ffn),
            grad_route,
            jnp.stack([grad_gain_one, grad_gain_two]),
        )
        owned = (
            lax.psum_scatter(
                weight_grads[0].astype(jnp.bfloat16), "wsh", scatter_dimension=0, tiled=True
            ).astype(jnp.float32),
            lax.psum_scatter(
                weight_grads[1].astype(jnp.bfloat16), "wsh", scatter_dimension=0, tiled=True
            ).astype(jnp.float32),
            lax.psum_scatter(
                weight_grads[2].astype(jnp.bfloat16), "wsh", scatter_dimension=0, tiled=True
            ).astype(jnp.float32),
            lax.psum_scatter(
                weight_grads[3].astype(jnp.bfloat16), "wsh", scatter_dimension=0, tiled=True
            ).astype(jnp.float32),
            lax.psum_scatter(
                weight_grads[4].astype(jnp.bfloat16), "wsh", scatter_dimension=0, tiled=True
            ).astype(jnp.float32),
            lax.psum_scatter(
                weight_grads[5].astype(jnp.bfloat16), "wsh", scatter_dimension=0, tiled=True
            ).astype(jnp.float32),
            lax.psum_scatter(
                weight_grads[6].astype(jnp.bfloat16), "wsh", scatter_dimension=0, tiled=True
            ).astype(jnp.float32),
            lax.psum_scatter(
                weight_grads[7].astype(jnp.bfloat16), "wsh", scatter_dimension=0, tiled=True
            ).astype(jnp.float32),
            lax.psum_scatter(
                weight_grads[8].astype(jnp.bfloat16), "wsh", scatter_dimension=1, tiled=True
            ).astype(jnp.float32),
            lax.psum_scatter(
                weight_grads[9].astype(jnp.bfloat16), "wsh", scatter_dimension=1, tiled=True
            ).astype(jnp.float32),
        )
        totals = owned if totals is None else tuple((a + b for a, b in zip(totals, owned)))
    summed = jax.tree.map(lambda part: part.astype(jnp.float32), lax.psum(shortened(totals), "ctx"))
    out_tokens = jnp.stack(results)[:, None]
    grad_tokens = jnp.stack(grad_inputs)[:, None]
    return (
        out_tokens,
        grad_tokens,
        summed[0],
        summed[1],
        summed[2],
        summed[3],
        summed[4],
        summed[5],
        summed[6],
        summed[7],
        summed[8],
        summed[9],
    )


def solution(mesh):
    return jax.shard_map(
        per_device,
        mesh=mesh,
        in_specs=(
            P(None, "wsh", "ctx", None),
            P(None, "wsh", "ctx", None),
            P("wsh", None),
            P("wsh", None),
            P("wsh", None),
            P("wsh", None),
            P("wsh", None),
            P("wsh", None),
            P("wsh", None),
            P("wsh", None),
            P(None, "wsh"),
            P(None, "wsh"),
            P(None, "wsh", None),
            P(None, "wsh", "ctx"),
            P(None, "wsh", "ctx"),
            P(None, "wsh", "ctx"),
        ),
        out_specs=(
            P(None, "wsh", "ctx", None),
            P(None, "wsh", "ctx", None),
            P("wsh", None),
            P("wsh", None),
            P("wsh", None),
            P("wsh", None),
            P("wsh", None),
            P("wsh", None),
            P("wsh", None),
            P("wsh", None),
            P(None, "wsh"),
            P(None, "wsh"),
        ),
        check_vma=False,
    )
```

profile of v0, /device:TPU:0, one launch (start us, length us, event | category | flops | bytes accessed | tf_op | source)
XLA Modules:
  0.0 1406.2 jit_solution(16120011620535073589)
XLA Ops:
  54.8 15.1 %all-reduce.10 = (s32[1024]{0:T(1024)S(1)}, s32[1024]{0:T(1024)S(1)}) all-reduce(s32[1024]{0:T(1024)S(1)} %dynamic-update-slice.13, s32[1024]{0:T(1024)S(1)} %dynamic-update-slice.12), channel_id=3, replica_groups=mesh['ctx'=16,'wsh'=2] {'ctx'}, use_global_device_ids=true, to_apply=%add.9 | all-reduce | flops 2048 | bytes 16384
  125.2 10.5 fusion.246
  143.4 10.6 fusion.248
  173.6 23.2 %all-gather.16.cloned.1.call-done = bf16[1024,1536]{1,0:T(8,128)(2,1)} async-done(((bf16[64,1536]{1,0:T(8,128)(2,1)}), bf16[1024,1536]{1,0:T(8,128)(2,1)}) %all-gather.16.cloned.1.call-update) | async-done | bytes 3145744 | tf_op jit(solution)/shard_map/all_gather | solution.py:192
  260.9 8.2 fusion.264
  269.1 11.3 all-gather.26.cloned.1.call-done
  404.1 11.7 multiply_reduce_fusion
  444.7 8.9 multiply_reduce_fusion.1
  462.1 9.4 multiply_convert_fusion.1
  487.2 9.3 collective-permute-done.5
  536.4 102.8 %reduce-scatter.69.cloned.1.call-done = bf16[64,1536]{1,0:T(8,128)(2,1)} async-done(((bf16[1024,1536]{1,0:T(8,128)(2,1)}), bf16[64,1536]{1,0:T(8,128)(2,1)}) %reduce-scatter.69.cloned.1.call-update) | async-done | bytes 196624
  687.4 10.2 reduce-scatter.55.cloned.1.call-done
  697.5 12.5 reduce-scatter.57.cloned.1.call-done
  712.5 11.4 reduce-scatter.37.cloned.1.call-done
  723.8 13.4 reduce-scatter.35.cloned.1.call-done
  770.2 14.9 %reduce-scatter.65.cloned.1.call-done = bf16[2048,768]{1,0:T(8,128)(2,1)} async-done(((bf16[4096,768]{1,0:T(8,128)(2,1)}), bf16[2048,768]{1,0:T(8,128)(2,1)}) %reduce-scatter.65.cloned.1.call-update) | async-done | bytes 3145744 | tf_op jit(solution)/shard_map/reduce_scatter | solution.py:372
  785.1 18.1 %reduce-scatter.63.cloned.1.call-done = bf16[2048,768]{1,0:T(8,128)(2,1)} async-done(((bf16[4096,768]{1,0:T(8,128)(2,1)}), bf16[2048,768]{1,0:T(8,128)(2,1)}) %reduce-scatter.63.cloned.1.call-update) | async-done | bytes 3145744 | tf_op jit(solution)/shard_map/reduce_scatter | solution.py:372
  808.5 9.4 reduce-scatter.43.cloned.1.call-done
  817.8 15.5 %reduce-scatter.45.cloned.1.call-done = bf16[384,2304]{1,0:T(8,128)(2,1)} async-done(((bf16[768,2304]{1,0:T(8,128)(2,1)}), bf16[384,2304]{1,0:T(8,128)(2,1)}) %reduce-scatter.45.cloned.1.call-update) | async-done | bytes 1769488 | tf_op jit(solution)/shard_map/reduce_scatter | solution.py:357
  836.9 21.8 %reduce-scatter.61.cloned.1.call-done = bf16[384,8192]{1,0:T(8,128)(2,1)} async-done(((bf16[768,8192]{1,0:T(8,128)(2,1)}), bf16[384,8192]{1,0:T(8,128)(2,1)}) %reduce-scatter.61.cloned.1.call-update) | async-done | bytes 6291472 | tf_op jit(solution)/shard_map/reduce_scatter | solution.py:369
  858.7 24.8 %reduce-scatter.59.cloned.1.call-done = bf16[384,8192]{1,0:T(8,128)(2,1)} async-done(((bf16[768,8192]{1,0:T(8,128)(2,1)}), bf16[384,8192]{1,0:T(8,128)(2,1)}) %reduce-scatter.59.cloned.1.call-update) | async-done | bytes 6291472 | tf_op jit(solution)/shard_map/reduce_scatter | solution.py:369
  883.6 9.9 add_convert_fusion
  928.4 44.1 %all-reduce.11 = (bf16[3,384]{1,0:T(4,128)(2,1)S(1)}, bf16[2,384]{1,0:T(2,128)(2,1)S(1)}) all-reduce(bf16[3,384]{1,0:T(4,128)(2,1)S(1)} %add_convert_fusion.20, bf16[2,384]{1,0:T(2,128)(2,1)S(1)} %add_convert_fusion.21), channel_id=1, replica_groups=mesh['ctx'=16,'wsh'=2] {'ctx'}, use_global_device_ids=true, to_apply=%region_68.69 | all-reduce | flops 1920 | bytes 7680 | tf_op jit(solution)/shard_map/psum | solution.py:383
  973.6 403.7 %all-reduce.15.cloned.1.call-done = (bf16[384,1536]{1,0:T(8,128)(2,1)}, bf16[256,768]{1,0:T(8,128)(2,1)}, bf16[384,2304]{1,0:T(8,128)(2,1)}, bf16[384,768]{1,0:T...) async-done(((bf16[384,1536]{1,0:T(8,128)(2,1)}, bf16[256,768]{1,0:T(8,128)(2,1)}, ...) | async-done | bytes 15728656 | tf_op jit(solution)/shard_map/psum | solution.py:383
  (819 shorter events, 557.7 us)
Async XLA Ops:
  35.5 200.1 %all-gather.20.cloned.1.call-start = ((), (), s32[]{:S(2)}) async-start(), calls=%async_computation.26 | async-start | bytes 4718592 | tf_op jit(solution)/shard_map/all_gather | solution.py:143
  36.1 205.7 %all-gather.22.cloned.1.call-start = ((), (), s32[]{:S(2)}) async-start(), calls=%async_computation.27 | async-start | bytes 2359296 | tf_op jit(solution)/shard_map/all_gather | solution.py:144
  36.9 224.0 %all-gather.24.cloned.1.call-start = ((), (), s32[]{:S(2)}) async-start(), calls=%async_computation.28 | async-start | bytes 18874368 | tf_op jit(solution)/shard_map/all_gather | solution.py:145
  37.7 242.8 %all-gather.26.cloned.1.call-start = ((), (), s32[]{:S(2)}) async-start(), calls=%async_computation.29 | async-start | bytes 9437184 | tf_op jit(solution)/shard_map/all_gather | solution.py:146
  38.4 490.9 %reduce-scatter.67.cloned.1.call-start = ((), (), s32[]{:S(2)}) async-start(), calls=%async_computation.47 | async-start | bytes 3342336
  367.0 272.2 %reduce-scatter.69.cloned.1.call-start = ((), (), s32[]{:S(2)}) async-start(), calls=%async_computation.48 | async-start | bytes 3342336
  388.2 290.9 %reduce-scatter.39.cloned.1.call-start = ((), (), s32[]{:S(2)}) async-start(), calls=%async_computation.33 | async-start | bytes 1179648 | tf_op jit(solution)/shard_map/reduce_scatter | solution.py:354
  390.7 288.3 %reduce-scatter.41.cloned.1.call-start = ((), (), s32[]{:S(2)}) async-start(), calls=%async_computation.34 | async-start | bytes 1179648 | tf_op jit(solution)/shard_map/reduce_scatter | solution.py:354
  393.4 287.6 %reduce-scatter.49.cloned.1.call-start = ((), (), s32[]{:S(2)}) async-start(), calls=%async_computation.38 | async-start | bytes 1769472 | tf_op jit(solution)/shard_map/reduce_scatter | solution.py:360
  395.9 289.3 %reduce-scatter.47.cloned.1.call-start = ((), (), s32[]{:S(2)}) async-start(), calls=%async_computation.37 | async-start | bytes 1769472 | tf_op jit(solution)/shard_map/reduce_scatter | solution.py:360
  398.4 299.1 %reduce-scatter.55.cloned.1.call-start = ((), (), s32[]{:S(2)}) async-start(), calls=%async_computation.41 | async-start | bytes 2359296 | tf_op jit(solution)/shard_map/reduce_scatter | solution.py:366
  402.1 307.9 %reduce-scatter.57.cloned.1.call-start = ((), (), s32[]{:S(2)}) async-start(), calls=%async_computation.42 | async-start | bytes 2359296 | tf_op jit(solution)/shard_map/reduce_scatter | solution.py:366
  438.8 285.0 %reduce-scatter.37.cloned.1.call-start = ((), (), s32[]{:S(2)}) async-start(), calls=%async_computation.32 | async-start | bytes 3538944 | tf_op jit(solution)/shard_map/reduce_scatter | solution.py:351
  462.0 275.2 %reduce-scatter.35.cloned.1.call-start = ((), (), s32[]{:S(2)}) async-start(), calls=%async_computation.31 | async-start | bytes 3538944 | tf_op jit(solution)/shard_map/reduce_scatter | solution.py:351
  500.9 259.1 %reduce-scatter.51.cloned.1.call-start = ((), (), s32[]{:S(2)}) async-start(), calls=%async_computation.39 | async-start | bytes 4718592 | tf_op jit(solution)/shard_map/reduce_scatter | solution.py:363
  507.2 259.3 %reduce-scatter.53.cloned.1.call-start = ((), (), s32[]{:S(2)}) async-start(), calls=%async_computation.40 | async-start | bytes 4718592 | tf_op jit(solution)/shard_map/reduce_scatter | solution.py:363
  514.1 270.9 %reduce-scatter.65.cloned.1.call-start = ((), (), s32[]{:S(2)}) async-start(), calls=%async_computation.46 | async-start | bytes 9437184 | tf_op jit(solution)/shard_map/reduce_scatter | solution.py:372
  519.8 283.4 %reduce-scatter.63.cloned.1.call-start = ((), (), s32[]{:S(2)}) async-start(), calls=%async_computation.45 | async-start | bytes 9437184 | tf_op jit(solution)/shard_map/reduce_scatter | solution.py:372
  525.3 292.5 %reduce-scatter.43.cloned.1.call-start = ((), (), s32[]{:S(2)}) async-start(), calls=%async_computation.35 | async-start | bytes 5308416 | tf_op jit(solution)/shard_map/reduce_scatter | solution.py:357
  533.2 300.1 %reduce-scatter.45.cloned.1.call-start = ((), (), s32[]{:S(2)}) async-start(), calls=%async_computation.36 | async-start | bytes 5308416 | tf_op jit(solution)/shard_map/reduce_scatter | solution.py:357
  643.0 215.7 %reduce-scatter.61.cloned.1.call-start = ((), (), s32[]{:S(2)}) async-start(), calls=%async_computation.44 | async-start | bytes 18874368 | tf_op jit(solution)/shard_map/reduce_scatter | solution.py:369
  651.2 232.4 %reduce-scatter.59.cloned.1.call-start = ((), (), s32[]{:S(2)}) async-start(), calls=%async_computation.43 | async-start | bytes 18874368 | tf_op jit(solution)/shard_map/reduce_scatter | solution.py:369
  659.3 258.1 %reduce-scatter.75.cloned.1.call-start = ((), (), s32[]{:S(2)}) async-start(), calls=%async_computation.51 | async-start | bytes 294912
  759.8 617.6 %all-reduce.15.cloned.1.call-start = ((), (), s32[]{:S(2)}) async-start(), calls=%async_computation.53 | async-start | bytes 31457280 | tf_op jit(solution)/shard_map/psum | solution.py:383
  (238 other events, 3254.7 us)
Sparse Core Ops, SparseCore 0:
  9.6 15.3 all-gather.13
  26.6 12.1 all-gather.11
  41.6 78.9 all-gather.27
  123.2 73.5 all-gather.15
  207.3 13.2 all-gather.19
  222.2 10.9 all-gather.21
  234.8 26.0 all-gather.23
  262.4 17.9 all-gather.25
  367.1 136.8 reduce-scatter.66
  509.6 129.5 reduce-scatter.68
  675.3 9.8 reduce-scatter.46
  687.3 10.2 reduce-scatter.54
  699.7 10.2 reduce-scatter.56
  712.7 11.1 reduce-scatter.36
  726.2 11.0 reduce-scatter.34
  739.4 12.0 reduce-scatter.50
  754.4 12.0 reduce-scatter.52
  769.4 15.6 reduce-scatter.64
  787.5 15.6 reduce-scatter.62
  805.3 12.5 reduce-scatter.42
  820.7 12.5 reduce-scatter.44
  836.0 22.6 reduce-scatter.60
  860.9 22.6 reduce-scatter.58
  935.0 442.3 all-reduce.14
  (8 shorter events, 68.9 us)
where the time goes:
time: 1420 us; the launch traced here: 1410 us
  waiting for transfers between devices  751 us (53%)
  matrix products  283 us (20%)
  other arithmetic  144 us (10%)
  local copies, waits for them, and re-layouts  118 us (8%)
  blocking collectives  67 us (5%)
  starting transfers between devices  25.2 us (2%)
  between operations  17.9 us (1%)
    psum x1, waiting for transfers between devices, per_device(): lax.psum(shortened(totals), 'ctx')  404 us
    unnamed x38, waiting for transfers between devices  115 us
    dot_general x30, matrix products, matmul(): return jnp.dot(left, right, preferred_element_type=jnp.float32)  62.8 us
    dot_general x18, matrix products, matmul_right(): lax.dot_general(left, right, (((1,), (1,)), ((), ())), preferred_element_...  62.1 us
    dot_general x18, matrix products, matmul_left(): lax.dot_general(left, right, (((0,), (0,)), ((), ())), preferred_element_...  58.4 us
    unnamed x457, local copies, waits for them, and re-layouts  47.7 us
    reduce_scatter x2, waiting for transfers between devices, per_device(): lax.psum_scatter(weight_grads[6].astype(jnp.bfloat16), 'wsh', scatter_dim...  46.6 us
    psum x1, blocking collectives, per_device(): lax.psum(shortened(totals), 'ctx')  44.1 us
  transfers between devices with their start and end apart: 40, of which 25 were waited for; matrix products, arithmetic and copies ran while one was open for 29% of the time, Pallas kernels for 0%

commit v1 on v0

v1 whole, which is shorter than its diff:
```python
import functools

import jax
import jax.numpy as jnp
from jax import lax
from jax.experimental import pallas as pl
from jax.experimental.pallas import tpu as pltpu
from jax.sharding import PartitionSpec as P

HD = 64
WIN = 128
LANES = 128
COLS = 256
FAR = -1e30
EPS = 1e-06
BF = jnp.bfloat16
F32 = jnp.float32


def mm(left, right):
    return lax.dot_general(left, right, (((1,), (0,)), ((), ())), preferred_element_type=F32)


def mm_t(left, right):
    return lax.dot_general(left, right, (((1,), (1,)), ((), ())), preferred_element_type=F32)


def t_mm(left, right):
    return lax.dot_general(left, right, (((0,), (0,)), ((), ())), preferred_element_type=F32)


def pick(onehot, values):
    high = values.astype(BF)
    low = (values - high.astype(F32)).astype(BF)
    return mm(onehot, high) + mm(onehot, low)


def iota(shape, dim):
    return lax.broadcasted_iota(jnp.int32, shape, dim)


def onehot_cols(positions, base, length):
    return (iota((positions.shape[0], length), 1) == positions - base).astype(F32).astype(BF)


def onehot_rows(positions, base, length):
    return (iota((length, positions.shape[1]), 0) == positions - base).astype(F32).astype(BF)


def segment(info, micro, positions):
    total = jnp.full(positions.shape, -1, jnp.int32)
    for start in range(5):
        total += (positions >= info[4 + micro * 5 + start]).astype(jnp.int32)
    return total


def inverse_rms(values):
    return lax.rsqrt(jnp.mean(values * values, axis=-1, keepdims=True) + EPS)


def halves(info, values):
    half = values.shape[1] // 2
    first, second = (values[:, :half], values[:, half:])
    lower = info[0] == 0
    return (jnp.where(lower, first, second), jnp.where(lower, second, first))


def unhalved(info, own, other):
    lower = info[0] == 0
    return jnp.concatenate([jnp.where(lower, own, other), jnp.where(lower, other, own)], axis=1)


def call(body, outs, grid, in_specs, out_specs, args, scratch=(), flops=0, moved=0, limit=48):
    return pl.pallas_call(
        body,
        out_shape=outs,
        grid_spec=pltpu.PrefetchScalarGridSpec(
            num_scalar_prefetch=1,
            grid=grid,
            in_specs=in_specs,
            out_specs=out_specs,
            scratch_shapes=list(scratch),
        ),
        compiler_params=pltpu.CompilerParams(vmem_limit_bytes=limit * 1024 * 1024),
        cost_estimate=pl.CostEstimate(flops=flops, bytes_accessed=moved, transcendentals=0),
    )(*args)


def whole(shape):
    rank = len(shape)
    return pl.BlockSpec(tuple(shape), lambda *unused: (0,) * rank)


def one_of(shape):
    rank = len(shape)
    return pl.BlockSpec((1,) + tuple(shape[1:]), lambda i, *unused: (i,) + (0,) * (rank - 1))


def sds(shape, dtype):
    return jax.ShapeDtypeStruct(tuple(shape), dtype)


def routed_body(info, x, cols, small, w_own, w_got, q_out, kv_out, hq_out, kin_out, h1k_out, gate_out):
    micros, tok, width = x.shape
    rows = cols.shape[2]
    base = info[1]
    gain = small[3:4].astype(F32)
    taken_q, taken_k = ([], [])
    for m in range(micros):
        both = jnp.concatenate([cols[0, m], cols[1, m]], axis=0)
        got = mm(onehot_cols(both, base, tok), x[m])
        taken_q.append(got[:rows])
        taken_k.append(got[rows:])
    xq, xk = (jnp.concatenate(taken_q, axis=0), jnp.concatenate(taken_k, axis=0))
    low_q = (xq * inverse_rms(xq) * gain).astype(BF)
    h1k = xk * inverse_rms(xk) * gain
    low_k = h1k.astype(BF)
    gate_q = jax.nn.sigmoid(
        jnp.sum(low_q.astype(F32) * small[0:1].astype(F32), axis=-1, keepdims=True)
    )
    gate_k = jax.nn.sigmoid(
        jnp.sum(low_k.astype(F32) * small[1:2].astype(F32), axis=-1, keepdims=True)
    )
    kin = (h1k * gate_k).astype(BF)
    own_q, other_q = halves(info, low_q)
    own_k, other_k = halves(info, kin)
    query = mm(own_q, w_own[:, :width]) + mm(other_q, w_got[:, :width])
    pair = mm(own_k, w_own[:, width:]) + mm(other_k, w_got[:, width:])
    lane = iota((rows, LANES), 1)
    for m in range(micros):
        part = slice(m * rows, (m + 1) * rows)
        q_out[m, :, :width] = query[part].astype(BF)
        kv_out[m, :, : 2 * width] = pair[part].astype(BF)
        seg_q = segment(info, m, cols[0, m])
        seg_k = segment(info, m, cols[1, m])
        q_out[m, :, width:] = (lane == seg_q).astype(F32).astype(BF)
        kv_out[m, :, 2 * width :] = jnp.where((lane < 8) & (lane != seg_k), FAR, 0.0).astype(BF)
        hq_out[m] = low_q[part]
        kin_out[m] = kin[part]
        h1k_out[m] = h1k[part]
        gate_out[m] = jnp.where(lane == 0, gate_q[part], gate_k[part])


def routed_in(info, x, cols, small, w_own, w_got):
    micros, unused, width = x.shape
    rows = cols.shape[2]
    shapes = [
        sds((micros, rows, width + LANES), BF),
        sds((micros, rows, 2 * width + LANES), BF),
        sds((micros, rows, width), BF),
        sds((micros, rows, width), BF),
        sds((micros, rows, width), F32),
        sds((micros, rows, LANES), F32),
    ]
    args = (info, x, cols, small, w_own, w_got)
    return call(
        routed_body,
        shapes,
        (1,),
        [whole(a.shape) for a in args[1:]],
        [whole(s.shape) for s in shapes],
        args,
        flops=2 * micros * rows * width * 3 * width,
        moved=9_000_000,
    )


def light_in_body(info, x, small, w_own, w_got, out):
    values = x[0].astype(F32)
    low = (values * inverse_rms(values) * small[3:4].astype(F32)).astype(BF)
    own, other = halves(info, low)
    out[0] = (mm(own, w_own[...]) + mm(other, w_got[...])).astype(BF)


def light_in(info, x, small, w_own, w_got):
    micros, tok, width = x.shape
    columns = w_own.shape[1]
    split = 2
    rows = tok // split
    spec = lambda n: pl.BlockSpec((1, rows, n), lambda i, *u: (i // split, i % split, 0))
    return call(
        light_in_body,
        sds((micros, tok, columns), BF),
        (micros * split,),
        [spec(width), whole(small.shape), whole(w_own.shape), whole(w_got.shape)],
        spec(columns),
        (info, x, small, w_own, w_got),
        flops=2 * micros * tok * width * columns,
        moved=8_000_000,
    )


def fill_near(near, qkv, before, after):
    tok = qkv.shape[1]
    inner = near.shape[1] // 2
    near[:WIN] = before[0]
    near[WIN : WIN + tok] = qkv[0, :, inner:]
    near[WIN + tok :] = after[0]


def light_bias(info, micro, block):
    start = info[1] + block * WIN
    rows, columns = (WIN, 3 * WIN)
    row_pos = start + iota((rows, 1), 0)
    col_pos = start - WIN + iota((1, columns), 1)
    seg_row = segment(info, micro, row_pos)
    seg_col = jnp.where((col_pos >= 0) & (col_pos < info[2]), segment(info, micro, col_pos), -1)
    shift = iota((rows, columns), 0) + WIN - iota((rows, columns), 1)
    allowed = (jnp.abs(shift) < WIN) & (seg_row == seg_col)
    bias = jnp.where(allowed, 0.0, FAR)
    return jnp.concatenate([bias, bias], axis=0)


def stacked(pair, low_lane):
    zero = jnp.zeros_like(pair)
    return jnp.concatenate(
        [jnp.where(low_lane, pair, zero), jnp.where(low_lane, zero, pair)], axis=0
    )


def merged(values, low_lane):
    rows = values.shape[0] // 2
    return jnp.where(low_lane, values[:rows], values[rows:])


def light_fwd_body(info, qkv, before, after, out, lse_out, near):
    micro = pl.program_id(0)
    tok = qkv.shape[1]
    inner = out.shape[2]
    fill_near(near, qkv, before, after)
    low_lane = iota((WIN, LANES), 1) < HD
    lane = iota((WIN, LANES), 1)

    def block_step(block, carry):
        at = pl.ds(pl.multiple_of(block * WIN, WIN), WIN)
        around = pl.ds(pl.multiple_of(block * WIN, WIN), 3 * WIN)
        bias = light_bias(info, micro, block)
        stats = jnp.zeros((WIN, LANES), F32)
        for pair in range(inner // LANES):
            cut = slice(pair * LANES, (pair + 1) * LANES)
            query = stacked(qkv[0, at, cut] * BF(HD**-0.5), low_lane)
            scores = mm_t(query, near[around, cut]) + bias
            top = jnp.max(scores, axis=-1, keepdims=True)
            weights = jnp.exp(scores - top)
            total = jnp.sum(weights, axis=-1, keepdims=True)
            value = near[around, inner + pair * LANES : inner + (pair + 1) * LANES]
            mixed = mm((weights * (1.0 / total)).astype(BF), value)
            out[0, at, cut] = merged(mixed, low_lane).astype(BF)
            lse = top + jnp.log(total)
            stats = jnp.where(lane == 2 * pair, lse[:WIN], stats)
            stats = jnp.where(lane == 2 * pair + 1, lse[WIN:], stats)
        lse_out[0, at, :] = stats
        return carry

    lax.fori_loop(0, tok // WIN, block_step, 0)


def light_fwd(info, qkv, before, after):
    micros, tok, columns = qkv.shape
    inner = columns // 3
    shapes = [sds((micros, tok, inner), BF), sds((micros, tok, LANES), F32)]
    args = (info, qkv, before, after)
    return call(
        light_fwd_body,
        shapes,
        (micros,),
        [one_of(a.shape) for a in args[1:]],
        [one_of(s.shape) for s in shapes],
        args,
        scratch=[pltpu.VMEM((tok + 2 * WIN, 2 * inner), BF)],
        flops=4_000_000_000,
        moved=6_000_000,
    )


def light_bwd_body(info, qkv, before, after, lse, grad, dq_out, own_out, low_out, high_out, near, dk, dv):
    micro = pl.program_id(0)
    tok = qkv.shape[1]
    inner = grad.shape[2]
    fill_near(near, qkv, before, after)
    dk[...] = jnp.zeros_like(dk)
    dv[...] = jnp.zeros_like(dv)
    low_lane = iota((WIN, LANES), 1) < HD

    def block_step(block, carry):
        at = pl.ds(pl.multiple_of(block * WIN, WIN), WIN)
        around = pl.ds(pl.multiple_of(block * WIN, WIN), 3 * WIN)
        bias = light_bias(info, micro, block)
        stats = lse[0, at, :]
        for pair in range(inner // LANES):
            cut = slice(pair * LANES, (pair + 1) * LANES)
            query = stacked(qkv[0, at, cut] * BF(HD**-0.5), low_lane)
            key = near[around, cut]
            value = near[around, inner + pair * LANES : inner + (pair + 1) * LANES]
            shift = jnp.concatenate(
                [stats[:, 2 * pair : 2 * pair + 1], stats[:, 2 * pair + 1 : 2 * pair + 2]], axis=0
            )
            probs = jnp.exp(mm_t(query, key) + bias - shift)
            upper = stacked(grad[0, at, cut], low_lane)
            grad_probs = mm_t(upper, value)
            center = jnp.sum(probs * grad_probs, axis=-1, keepdims=True)
            slope = (probs * (grad_probs - center)).astype(BF)
            dq_out[0, at, cut] = (merged(mm(slope, key), low_lane) * HD**-0.5).astype(BF)
            dk[around, cut] += t_mm(slope, query)
            dv[around, cut] += t_mm(probs.astype(BF), upper)
        return carry

    lax.fori_loop(0, tok // WIN, block_step, 0)
    own_out[0, :, :inner] = dk[WIN : WIN + tok]
    own_out[0, :, inner:] = dv[WIN : WIN + tok]
    low_out[0, :, :inner] = dk[:WIN].astype(BF)
    low_out[0, :, inner:] = dv[:WIN].astype(BF)
    high_out[0, :, :inner] = dk[WIN + tok :].astype(BF)
    high_out[0, :, inner:] = dv[WIN + tok :].astype(BF)


def light_bwd(info, qkv, before, after, lse, grad):
    micros, tok, columns = qkv.shape
    inner = columns // 3
    shapes = [
        sds((micros, tok, inner), BF),
        sds((micros, tok, 2 * inner), F32),
        sds((micros, WIN, 2 * inner), BF),
        sds((micros, WIN, 2 * inner), BF),
    ]
    args = (info, qkv, before, after, lse, grad)
    return call(
        light_bwd_body,
        shapes,
        (micros,),
        [one_of(a.shape) for a in args[1:]],
        [one_of(s.shape) for s in shapes],
        args,
        scratch=[
            pltpu.VMEM((tok + 2 * WIN, 2 * inner), BF),
            pltpu.VMEM((tok + 2 * WIN, inner), F32),
            pltpu.VMEM((tok + 2 * WIN, inner), F32),
        ],
        flops=10_000_000_000,
        moved=14_000_000,
    )


def heavy_scores(query, parts, bias, cut):
    return [mm_t(query, part[:, cut]) + b for part, b in zip(parts, bias)]


def heavy_fwd_body(info, q, kv_a, kv_b, out, lse_out):
    rows, width = out.shape
    parts = (kv_a, kv_b)
    low_lane = iota((rows, LANES), 1) < HD
    lane = iota((rows, LANES), 1)
    feature = jnp.concatenate([q[:, width:]] * 2, axis=0)
    bias = [mm_t(feature, part[:, 2 * width :]) for part in parts]
    stats = jnp.zeros((rows, LANES), F32)
    for pair in range(width // LANES):
        cut = slice(pair * LANES, (pair + 1) * LANES)
        query = stacked(q[:, cut] * BF(HD**-0.5), low_lane)
        scores = heavy_scores(query, parts, bias, cut)
        top = functools.reduce(
            jnp.maximum, [jnp.max(s, axis=-1, keepdims=True) for s in scores]
        )
        weights = [jnp.exp(s - top) for s in scores]
        total = sum(jnp.sum(w, axis=-1, keepdims=True) for w in weights)
        scale = 1.0 / total
        mixed = sum(
            mm((w * scale).astype(BF), part[:, width + pair * LANES : width + (pair + 1) * LANES])
            for w, part in zip(weights, parts)
        )
        out[:, cut] = merged(mixed, low_lane).astype(BF)
        lse = top + jnp.log(total)
        stats = jnp.where(lane == 2 * pair, lse[:rows], stats)
        stats = jnp.where(lane == 2 * pair + 1, lse[rows:], stats)
    lse_out[...] = stats


def heavy_fwd(info, q, kv_a, kv_b):
    rows = q.shape[0]
    width = q.shape[1] - LANES
    shapes = [sds((rows, width), BF), sds((rows, LANES), F32)]
    args = (info, q, kv_a, kv_b)
    return call(
        heavy_fwd_body,
        shapes,
        (1,),
        [whole(a.shape) for a in args[1:]],
        [whole(s.shape) for s in shapes],
        args,
        flops=1_500_000_000,
        moved=4_000_000,
    )


def heavy_bwd_body(info, q, kv_a, kv_b, lse, grad, dq_out, da_out, db_out):
    rows, width = grad.shape
    parts = (kv_a, kv_b)
    low_lane = iota((rows, LANES), 1) < HD
    feature = jnp.concatenate([q[:, width:]] * 2, axis=0)
    bias = [mm_t(feature, part[:, 2 * width :]) for part in parts]
    for pair in range(width // LANES):
        cut = slice(pair * LANES, (pair + 1) * LANES)
        upcut = slice(width + pair * LANES, width + (pair + 1) * LANES)
        query = stacked(q[:, cut] * BF(HD**-0.5), low_lane)
        shift = jnp.concatenate(
            [lse[:, 2 * pair : 2 * pair + 1], lse[:, 2 * pair + 1 : 2 * pair + 2]], axis=0
        )
        probs = [jnp.exp(s - shift) for s in heavy_scores(query, parts, bias, cut)]
        upper = stacked(grad[:, cut], low_lane)
        grads = [mm_t(upper, part[:, upcut]) for part in parts]
        center = sum(jnp.sum(p * g, axis=-1, keepdims=True) for p, g in zip(probs, grads))
        slopes = [(p * (g - center)).astype(BF) for p, g in zip(probs, grads)]
        dq = sum(mm(s, part[:, cut]) for s, part in zip(slopes, parts))
        dq_out[:, cut] = (merged(dq, low_lane) * HD**-0.5).astype(BF)
        for target, slope, prob in zip((da_out, db_out), slopes, probs):
            target[:, cut] = t_mm(slope, query).astype(BF)
            target[:, upcut] = t_mm(prob.astype(BF), upper).astype(BF)


def heavy_bwd(info, q, kv_a, kv_b, lse, grad):
    rows = q.shape[0]
    width = q.shape[1] - LANES
    shapes = [sds((rows, width), BF)] + [sds((kv.shape[0], 2 * width), BF) for kv in (kv_a, kv_b)]
    args = (info, q, kv_a, kv_b, lse, grad)
    return call(
        heavy_bwd_body,
        shapes,
        (1,),
        [whole(a.shape) for a in args[1:]],
        [whole(s.shape) for s in shapes],
        args,
        flops=4_000_000_000,
        moved=8_000_000,
    )


def middle_body(info, x, up, cols, rows, small, gate, lo, lout, ho, hout, y_out, low_out, ffr_out, dzh_out, hy_out, gf_out):
    tok = x.shape[1]
    base = info[1]
    hy = mm(ho[0], hout[...])
    hy_out[0] = hy
    spread = onehot_rows(rows[0, 0], base, tok)
    y = x[0].astype(F32) + mm(lo[0], lout[...]) + pick(spread, hy * gate[0, :, 0:1])
    y_out[0] = y
    low = (y * inverse_rms(y) * small[4:5].astype(F32)).astype(BF)
    low_out[0] = low
    take = onehot_cols(cols[2, 0], base, tok)
    taken = mm(take, low)
    ffr_out[0] = taken.astype(BF)
    gf = jax.nn.sigmoid(jnp.sum(taken * small[2:3].astype(F32), axis=-1, keepdims=True))
    dzh_out[0] = (mm(take, up[0]) * gf).astype(BF)
    gf_out[0] = jnp.broadcast_to(gf, gf_out.shape[1:])


def second_of(shape):
    rank = len(shape)
    return pl.BlockSpec(
        (shape[0], 1) + tuple(shape[2:]), lambda i, *unused: (0, i) + (0,) * (rank - 2)
    )


def middle(info, x, up, cols, rows, small, gate, lo, lout, ho, hout):
    micros, tok, width = x.shape
    count = cols.shape[2]
    shapes = [
        sds((micros, tok, width), F32),
        sds((micros, tok, width), BF),
        sds((micros, count, width), BF),
        sds((micros, count, width), BF),
        sds((micros, count, width), F32),
        sds((micros, count, LANES), F32),
    ]
    args = (info, x, up, cols, rows, small, gate, lo, lout, ho, hout)
    return call(
        middle_body,
        shapes,
        (micros,),
        [
            one_of(x.shape),
            one_of(up.shape),
            second_of(cols.shape),
            second_of(rows.shape),
            whole(small.shape),
            one_of(gate.shape),
            one_of(lo.shape),
            whole(lout.shape),
            one_of(ho.shape),
            whole(hout.shape),
        ],
        [one_of(s.shape) for s in shapes],
        args,
        flops=2_000_000_000,
        moved=12_000_000,
    )


def pack_rows(target, values):
    step = values.shape[0] // 16
    cuts = values.shape[1] // COLS
    for slot in range(16):
        for cut in range(cuts):
            at = slot * step * cuts + cut * step
            target[0, at : at + step] = values[
                slot * step : (slot + 1) * step, cut * COLS : (cut + 1) * COLS
            ].astype(BF)


def ffn_body(info, a, ct, wg, wu, wd, z_out, dh_out, own_gu, other_gu, own_dn, other_dn):
    step = pl.program_id(0)
    half = pl.num_programs(0) // 2
    width = a.shape[1] // 2
    low, upstream = (a[...], ct[...])
    g, u = (mm(low, wg[...]), mm(low, wu[...]))
    back = mm_t(upstream, wd[...])
    root = (2.0 / 3.141592653589793) ** 0.5
    square = g * g
    tanh = jnp.tanh(root * g * (1.0 + 0.044715 * square))
    bell = 0.5 * (1.0 + tanh)
    gelu = g * bell
    hidden = (gelu * u).astype(BF)
    slope = bell + 0.5 * g * (1.0 - tanh * tanh) * (root * (1.0 + 3 * 0.044715 * square))
    dg = (back * u * slope).astype(BF)
    du = (back * gelu).astype(BF)
    z = mm(hidden, wd[...])
    dh = mm_t(dg, wg[...]) + mm_t(du, wu[...])

    @pl.when(step == 0)
    def first():
        z_out[...] = z
        dh_out[...] = dh

    @pl.when(step > 0)
    def later():
        z_out[...] += z
        dh_out[...] += dh

    down = t_mm(hidden, upstream)

    @pl.when(step < half)
    def send():
        pack_rows(other_dn, down)

    @pl.when(step >= half)
    def keep():
        pack_rows(own_dn, down)

    own = a[:, pl.ds(pl.multiple_of(info[0] * width, width), width)]
    other = a[:, pl.ds(pl.multiple_of((1 - info[0]) * width, width), width)]
    own_gu[0, :width] = t_mm(own, dg).astype(BF)
    own_gu[0, width:] = t_mm(own, du).astype(BF)
    other_gu[0, :width] = t_mm(other, dg).astype(BF)
    other_gu[0, width:] = t_mm(other, du).astype(BF)


def ffn(info, a, ct, w_gu, w_down):
    rows, width = a.shape
    hidden = w_down.shape[0]
    block = COLS
    steps = hidden // block
    half = steps // 2

    def natural(i, info):
        return jnp.where(i < half, (1 - info[0]) * half + i, info[0] * half + i - half)

    unit = (1, width, COLS)
    shapes = [
        sds((rows, width), F32),
        sds((rows, width), F32),
        sds((steps,) + unit[1:], BF),
        sds((steps,) + unit[1:], BF),
        sds((half,) + unit[1:], BF),
        sds((half,) + unit[1:], BF),
    ]
    return call(
        ffn_body,
        shapes,
        (steps,),
        [
            whole(a.shape),
            whole(ct.shape),
            pl.BlockSpec((width, block), lambda i, info: (0, natural(i, info))),
            pl.BlockSpec((width, block), lambda i, info: (0, steps + natural(i, info))),
            pl.BlockSpec((block, width), lambda i, info: (natural(i, info), 0)),
        ],
        [
            whole((rows, width)),
            whole((rows, width)),
            pl.BlockSpec(unit, lambda i, info: (natural(i, info), 0, 0)),
            pl.BlockSpec(unit, lambda i, info: (natural(i, info), 0, 0)),
            pl.BlockSpec(unit, lambda i, info: (jnp.maximum(i - half, 0), 0, 0)),
            pl.BlockSpec(unit, lambda i, info: (jnp.minimum(i, half - 1), 0, 0)),
        ],
        (info, a, ct, w_gu, w_gu, w_down),
        flops=2 * 9 * rows * hidden * width,
        moved=2 * 2 * 3 * hidden * width + rows * width * 12,
    )


def mid_back_body(
    info, y, up, z, dh2, zh, dff, ffr, gf, cols, rows, small, gate, lout, hout, hy, hq,
    out, dy_out, dlo_out, dho_out, dhy_out, dsq_out, part_out,
):
    tok = y.shape[1]
    base = info[1]
    micro = pl.program_id(0)
    spread = onehot_rows(rows[2, 0], base, tok)
    take = onehot_cols(cols[2, 0], base, tok)
    values, top = (y[0], up[0].astype(F32))
    open_f = gf[0, :, 0:1]
    zhv = zh[0]
    out[0] = (values + z[0] + pick(spread, zhv * open_f)).astype(BF)
    taken = mm(take, up[0])
    dsf = jnp.sum(taken * zhv, axis=-1, keepdims=True) * open_f * (1.0 - open_f)
    back = dh2[0] + pick(spread, dff[0] + dsf * small[2:3].astype(F32))
    inv = inverse_rms(values)
    scaled = back * small[4:5].astype(F32)
    mean = jnp.mean(values * scaled, axis=-1, keepdims=True)
    dy = top + inv * scaled - values * (inv * inv * inv * mean)
    dy_out[0] = dy
    dgain = jnp.sum(back * values * inv, axis=0, keepdims=True)
    drf = jnp.sum(dsf * ffr[0].astype(F32), axis=0, keepdims=True)
    dlo_out[0] = mm_t(dy.astype(BF), lout[...]).astype(BF)
    dyq = pick(onehot_cols(cols[0, 0], base, tok), dy)
    open_q = gate[0, :, 0:1]
    dhy = (dyq * open_q).astype(BF)
    dhy_out[0] = dhy
    dsq = jnp.sum(dyq * hy[0], axis=-1, keepdims=True) * open_q * (1.0 - open_q)
    dsq_out[0] = jnp.broadcast_to(dsq, dsq_out.shape[1:])
    drq = jnp.sum(dsq * hq[0].astype(F32), axis=0, keepdims=True)
    dho_out[0] = mm_t(dhy, hout[...]).astype(BF)
    row = iota(part_out.shape, 0)
    part = jnp.where(row == 0, drq, jnp.where(row == 2, drf, jnp.where(row == 4, dgain, 0.0)))

    @pl.when(micro == 0)
    def first():
        part_out[...] = part

    @pl.when(micro > 0)
    def later():
        part_out[...] += part


def mid_back(info, y, up, z, dh2, zh, dff, ffr, gf, cols, rows, small, gate, lout, hout, hy, hq):
    micros, tok, width = y.shape
    count = cols.shape[2]
    shapes = [
        sds((micros, tok, width), BF),
        sds((micros, tok, width), F32),
        sds((micros, tok, lout.shape[0]), BF),
        sds((micros, count, width), BF),
        sds((micros, count, width), BF),
        sds((micros, count, LANES), F32),
        sds((8, width), F32),
    ]
    return call(
        mid_back_body,
        shapes,
        (micros,),
        [
            one_of(y.shape),
            one_of(up.shape),
            one_of(z.shape),
            one_of(dh2.shape),
            one_of(zh.shape),
            one_of(dff.shape),
            one_of(ffr.shape),
            one_of(gf.shape),
            second_of(cols.shape),
            second_of(rows.shape),
            whole(small.shape),
            one_of(gate.shape),
            whole(lout.shape),
            whole(hout.shape),
            one_of(hy.shape),
            one_of(hq.shape),
        ],
        [one_of(s.shape) for s in shapes[:-1]] + [whole(shapes[-1].shape)],
        (info, y, up, z, dh2, zh, dff, ffr, gf, cols, rows, small, gate, lout, hout, hy, hq),
        flops=3_000_000_000,
        moved=22_000_000,
    )


def in_back_body(
    info, x, dy, dq, own, got_low, got_high, dhq, dhkv, dsq, rows, small, gate, hq, kin, h1k, l_own, l_got, h_own, h_got,
    grad_out, dl_out, part_out,
):
    tok, width = x.shape[1:]
    micro = pl.program_id(0)
    base = info[1]
    inner = dq.shape[2]
    dl_out[0, :, :inner] = dq[0]
    dl_out[0, WIN : tok - WIN, inner:] = own[0, WIN : tok - WIN].astype(BF)
    dl_out[0, :WIN, inner:] = (own[0, :WIN] + got_low[0].astype(F32)).astype(BF)
    dl_out[0, tok - WIN :, inner:] = (own[0, tok - WIN :] + got_high[0].astype(F32)).astype(BF)
    light = dl_out[0]
    back = unhalved(info, mm_t(light, l_own[...]), mm_t(light, l_got[...]))
    dkin = unhalved(
        info, mm_t(dhkv[0], h_own[:, width:]), mm_t(dhkv[0], h_got[:, width:])
    )
    open_k = gate[0, :, 1:2]
    source = h1k[0]
    dskv = jnp.sum(dkin * source, axis=-1, keepdims=True) * open_k * (1.0 - open_k)
    to_q = unhalved(info, mm_t(dhq[0], h_own[:, :width]), mm_t(dhq[0], h_got[:, :width]))
    to_q += dsq[0, :, 0:1] * small[0:1].astype(F32)
    to_k = dkin * open_k + dskv * small[1:2].astype(F32)
    back += pick(onehot_rows(rows[0, 0], base, tok), to_q)
    back += pick(onehot_rows(rows[1, 0], base, tok), to_k)
    values = x[0].astype(F32)
    inv = inverse_rms(values)
    scaled = back * small[3:4].astype(F32)
    mean = jnp.mean(values * scaled, axis=-1, keepdims=True)
    grad_out[0] = (dy[0] + inv * scaled - values * (inv * inv * inv * mean)).astype(BF)
    dgain = jnp.sum(back * values * inv, axis=0, keepdims=True)
    drk = jnp.sum(dskv * source.astype(BF).astype(F32), axis=0, keepdims=True)
    row = iota(part_out.shape, 0)
    part = jnp.where(row == 1, drk, jnp.where(row == 3, dgain, 0.0))

    @pl.when(micro == 0)
    def first():
        part_out[...] = part

    @pl.when(micro > 0)
    def later():
        part_out[...] += part


def in_back(info, x, dy, dq, own, got_low, got_high, dhq, dhkv, dsq, rows, small, gate, hq, kin, h1k, l_own, l_got, h_own, h_got):
    micros, tok, width = x.shape
    shapes = [
        sds((micros, tok, width), BF),
        sds((micros, tok, l_own.shape[1]), BF),
        sds((8, width), F32),
    ]
    firsts = (x, dy, dq, own, got_low, got_high, dhq, dhkv, dsq)
    return call(
        in_back_body,
        shapes,
        (micros,),
        [one_of(a.shape) for a in firsts]
        + [second_of(rows.shape), whole(small.shape)]
        + [one_of(a.shape) for a in (gate, hq, kin, h1k)]
        + [whole(a.shape) for a in (l_own, l_got, h_own, h_got)],
        [one_of(s.shape) for s in shapes[:-1]] + [whole(shapes[-1].shape)],
        (info,) + firsts + (rows, small, gate, hq, kin, h1k, l_own, l_got, h_own, h_got),
        flops=4_000_000_000,
        moved=22_000_000,
    )


def grads_body(info, x, small, dl, hq, dhq, kin, dhkv, lo, dy, ho, dhy, own_out, other_out, low):
    micros, tok, width = x.shape
    half = width // 2
    for m in range(micros):
        values = x[m].astype(F32)
        low[m] = (values * inverse_rms(values) * small[3:4].astype(F32)).astype(BF)
    inner = lo.shape[2]
    for target, side in ((other_out, 1 - info[0]), (own_out, info[0])):
        cut = pl.ds(pl.multiple_of(side * half, half), half)

        def put(unit, left, right):
            for block in range(right[0].shape[1] // COLS):
                at = unit + block
                total = sum(
                    t_mm(a, b[:, block * COLS : (block + 1) * COLS]) for a, b in zip(left, right)
                )
                target[at // 2, (at % 2) * half : (at % 2 + 1) * half] = total.astype(BF)
            return unit + right[0].shape[1] // COLS

        every = range(micros)
        unit = put(0, [low[m, :, cut] for m in every], [dl[m] for m in every])
        unit = put(unit, [hq[m, :, cut] for m in every], [dhq[m] for m in every])
        unit = put(unit, [kin[m, :, cut] for m in every], [dhkv[m] for m in every])
        unit = put(unit, [ho[m, :, cut] for m in every], [dhy[m] for m in every])
        part = inner // 2
        small_cut = pl.ds(pl.multiple_of(side * part, part), part)
        total = sum(t_mm(lo[m, :, small_cut], dy[m].astype(BF)) for m in every)
        pack_rows(target.at[pl.ds(unit // 2, 1)], total)


def attention_grads(info, x, small, dl, hq, dhq, kin, dhkv, lo, dy, ho, dhy):
    micros, tok, width = x.shape
    units = (dl.shape[2] + dhq.shape[2] + dhkv.shape[2] + dhy.shape[2]) // COLS
    shapes = [sds((units // 2 + 1, width, COLS), BF)] * 2
    args = (info, x, small, dl, hq, dhq, kin, dhkv, lo, dy, ho, dhy)
    return call(
        grads_body,
        shapes,
        (1,),
        [whole(a.shape) for a in args[1:]],
        [whole(s.shape) for s in shapes],
        args,
        scratch=[pltpu.VMEM(x.shape, BF)],
        flops=2 * micros * tok * width * 2100,
        moved=20_000_000,
    )


def mask_of(slot, order):
    bits = len(order)
    return sum(order[b] for b in range(bits) if (slot >> (bits - 1 - b)) & 1)


def fold_body(order, counts, info, *refs):
    sources = refs[: 2 * len(counts)]
    keep, send = refs[2 * len(counts) :]
    slots = 1 << len(order)
    size = keep.shape[2]
    step = pl.program_id(0)
    start = 0
    for which, count in enumerate(counts):
        own, got = sources[2 * which : 2 * which + 2]

        @pl.when((step >= start) & (step < start + count))
        def part():
            for slot in range(slots):
                owner = jnp.bitwise_xor(info[3], mask_of(slot, order))
                at = pl.ds(pl.multiple_of(owner * size, size), size)
                total = (own[0, at, :].astype(F32) + got[0, at, :].astype(F32)).astype(BF)
                if slot < slots // 2:
                    keep[slot, 0] = total
                else:
                    send[slot - slots // 2, 0] = total

        start += count


def fold(info, order, parts):
    slots = 1 << len(order)
    width = parts[0][0].shape[1]
    counts = [part[3] for part in parts]
    total = sum(counts)
    shape = sds((slots // 2, total, width // slots, COLS), BF)
    args, specs = ([], [])
    start = 0
    for own, got, first, count in parts:
        index = functools.partial(
            lambda first, start, count, i, *u: (
                first + jnp.minimum(jnp.maximum(i - start, 0), count - 1),
                0,
                0,
            ),
            first,
            start,
            count,
        )
        args += [own, got]
        specs += [pl.BlockSpec((1, width, COLS), index)] * 2
        start += count
    spec = pl.BlockSpec((slots // 2, 1, width // slots, COLS), lambda i, *u: (0, i, 0, 0))
    return call(
        functools.partial(fold_body, order, counts),
        [shape, shape],
        (total,),
        specs,
        [spec, spec],
        (info, *args),
        moved=total * width * COLS * 6,
    )


def flipped(value, bit):
    size = lax.axis_size("ctx")
    return lax.ppermute(value, "ctx", [(i, i ^ bit) for i in range(size)])


def scatter_sum(keep, send, order):
    for bit in order:
        got = flipped(send, bit)
        half = keep.shape[0] // 2
        if half == 0:
            return (keep.astype(F32) + got.astype(F32)).astype(BF)
        send = (keep[half:].astype(F32) + got[half:].astype(F32)).astype(BF)
        keep = (keep[:half].astype(F32) + got[:half].astype(F32)).astype(BF)


def gather_pair(value, order):
    for bit in order[:-1]:
        value = jnp.concatenate([value, flipped(value, bit)], axis=0)
    return (value, flipped(value, order[-1]))


def reduced(info, order, parts):
    keep, send = fold(info, order, parts)
    own = scatter_sum(keep, send, order)
    return gather_pair(own, tuple(reversed(order)))


def place(info, order, near, far, block, part, half, write):
    slots = 1 << len(order)
    back = tuple(reversed(order))
    for slot in range(slots):
        mask = sum(back[b] for b in range(len(order)) if (slot >> b) & 1)
        owner = jnp.bitwise_xor(info[3], mask)
        source = near if slot < slots // 2 else far
        value = source[slot % (slots // 2), block].astype(F32)
        write(owner, value)


def unpack_gu_body(order, starts, info, near, far, out):
    side = pl.program_id(1)
    size = near.shape[2]

    def write(owner, value):
        per = out.shape[0] // size

        @pl.when(owner // per == side)
        def hit():
            out[pl.ds(pl.multiple_of((owner % per) * size, size), size), :] = value

    place(info, order, near, far, 0, None, None, write)


def unpack_dn_body(order, info, near, far, out):
    size = near.shape[2]
    cuts = out.shape[1] // COLS
    rows = size // cuts

    def write(owner, value):
        for cut in range(cuts):
            out[
                pl.ds(pl.multiple_of(owner * rows, rows), rows), cut * COLS : (cut + 1) * COLS
            ] = value[cut * rows : (cut + 1) * rows]

    place(info, order, near, far, 0, None, None, write)


def unpack_gu(info, order, pair, first, count, total, base, previous):
    near, far = pair
    slots, unused, size, unused_too = near.shape
    rows = size * slots
    spec = pl.BlockSpec((slots, 1, size, COLS), lambda i, s, *u: (0, first + i, 0, 0))
    out = sds((rows, 2 * total * COLS), F32)
    body = functools.partial(unpack_gu_body, order, None)
    args, specs = ([info, near, far], [spec, spec])
    aliases = {}
    if previous is not None:
        args.append(previous)
        specs.append(pl.BlockSpec(memory_space=pl.ANY))
        aliases = {3: 0}
        inner = body
        body = lambda info, near, far, unused, out: inner(info, near, far, out)
    return pl.pallas_call(
        body,
        out_shape=out,
        grid_spec=pltpu.PrefetchScalarGridSpec(
            num_scalar_prefetch=1,
            grid=(count, 2),
            in_specs=specs,
            out_specs=pl.BlockSpec((rows, COLS), lambda i, s, *u: (0, s * total + base + i)),
        ),
        input_output_aliases=aliases,
        cost_estimate=pl.CostEstimate(flops=0, bytes_accessed=count * rows * COLS * 12, transcendentals=0),
    )(*args)


def unpack_dn(info, order, pair, first, count, total, base, previous):
    near, far = pair
    slots, unused, size, unused_too = near.shape
    width = 2 * slots * size
    cuts = width // COLS
    rows = width * COLS // width
    spec = pl.BlockSpec((slots, 1, size, COLS), lambda i, *u: (0, first + i, 0, 0))
    out = sds((total * rows, width), F32)
    body = functools.partial(unpack_dn_body, order)
    args, specs = ([info, near, far], [spec, spec])
    aliases = {}
    if previous is not None:
        args.append(previous)
        specs.append(pl.BlockSpec(memory_space=pl.ANY))
        aliases = {3: 0}
        inner = body
        body = lambda info, near, far, unused, out: inner(info, near, far, out)
    return pl.pallas_call(
        body,
        out_shape=out,
        grid_spec=pltpu.PrefetchScalarGridSpec(
            num_scalar_prefetch=1,
            grid=(count,),
            in_specs=specs,
            out_specs=pl.BlockSpec((rows, width), lambda i, *u: (base + i, 0)),
        ),
        input_output_aliases=aliases,
        cost_estimate=pl.CostEstimate(flops=0, bytes_accessed=count * rows * width * 6, transcendentals=0),
    )(*args)


def unpack_attention_body(orders, widths, info, *refs):
    pairs, outs = (refs[: 2 * len(orders)], refs[2 * len(orders) :])
    unit = 0
    homes = []
    for which, columns in enumerate(widths):
        for block in range(columns // COLS):
            homes.append((which, block))
    start = 0
    for which, order in enumerate(orders):
        near, far = pairs[2 * which : 2 * which + 2]
        size = near.shape[2]
        for block in range(near.shape[1]):
            at = start + block

            def write(owner, value, at=at):
                if 2 * at >= len(homes):
                    out = outs[len(widths)]
                    cuts = out.shape[1] // COLS
                    rows = size // cuts
                    for cut in range(cuts):
                        out[
                            pl.ds(pl.multiple_of(owner * rows, rows), rows),
                            cut * COLS : (cut + 1) * COLS,
                        ] = value[cut * rows : (cut + 1) * rows]
                    return
                per = outs[0].shape[0] // size
                for side in range(2):
                    which_out, column = homes[2 * at + side]
                    out = outs[which_out]

                    @pl.when(owner // per == side)
                    def hit(out=out, column=column):
                        out[
                            pl.ds(pl.multiple_of((owner % per) * size, size), size),
                            column * COLS : (column + 1) * COLS,
                        ] = value

            place(info, order, near, far, block, None, None, write)
        start += near.shape[1]


def unpack_attention(info, orders, pairs, widths, inner):
    slots, unused, size, unused_too = pairs[0][0].shape
    half = slots * size
    shapes = [sds((half, w), F32) for w in widths] + [sds((inner // 2, 2 * half), F32)]
    args = [info] + [part for pair in pairs for part in pair]
    return call(
        functools.partial(unpack_attention_body, orders, widths),
        shapes,
        (1,),
        [whole(a.shape) for a in args[1:]],
        [whole(s.shape) for s in shapes],
        args,
        moved=14_000_000,
    )


def plain_gu(own, other):
    blocks, width, cols = own.shape

    def rows(part):
        return part.reshape(blocks, 2, width // 2, cols).transpose(2, 1, 0, 3).reshape(width // 2, -1)

    return jnp.concatenate([rows(own), rows(other)], axis=0)


def plain_dn(own, other):
    blocks, width, cols = own.shape
    cuts = width // cols

    def rows(part):
        return (
            part.reshape(blocks, 16, cuts, width // (16 * cuts), cols)
            .transpose(0, 1, 3, 2, 4)
            .reshape(-1, width)
        )

    return jnp.concatenate([rows(own), rows(other)], axis=0)


def plain_units(own, other, widths):
    def unit(part, at):
        half = part.shape[1] // 2
        return part[at // 2, (at % 2) * half : (at % 2 + 1) * half]

    result, at = ([], 0)
    for columns in widths:
        count = columns // COLS
        result.append(
            jnp.concatenate(
                [
                    jnp.concatenate([unit(part, at + i) for i in range(count)], axis=1)
                    for part in (own, other)
                ],
                axis=0,
            )
        )
        at += count
    return result


def plain_sum(grads):
    parts = [lax.psum_scatter(g.astype(BF), "wsh", scatter_dimension=0, tiled=True) for g in grads]
    return tuple(g.astype(F32) for g in lax.psum(parts, "ctx"))


def per_device(
    tokens, cotangent, light_qkv, light_out, heavy_qkv, heavy_out, light_gu, light_down, heavy_gu, heavy_down,
    routers, gains, doc_starts, q_index, kv_index, ff_index,
):
    micros, unused, tok, width = tokens.shape
    count, groups = (lax.axis_size("ctx"), lax.axis_size("wsh"))
    direct = groups == 2 and count == 16
    place_ctx = lax.axis_index("ctx")
    side = lax.axis_index("wsh") if direct else 0
    base = place_ctx * tok
    info = jnp.concatenate(
        [
            jnp.stack([jnp.int32(side), base, jnp.int32(tok * count), place_ctx]).astype(jnp.int32),
            doc_starts[:, 0].reshape(-1),
        ]
    )
    swap = [(0, 1), (1, 0)]

    def pair_of(shard):
        if direct:
            return (shard, lax.ppermute(shard, "wsh", swap))
        full = lax.all_gather(shard, "wsh", axis=0, tiled=True)
        return (full[: full.shape[0] // 2], full[full.shape[0] // 2 :])

    def full_of(shard, axis=0):
        return lax.all_gather(shard, "wsh", axis=axis, tiled=True)

    vectors = jnp.concatenate([routers, gains, jnp.zeros((3, routers.shape[1]), BF)], axis=0)
    if direct:
        got = lax.ppermute(vectors, "wsh", swap)
        small = jnp.concatenate(
            [jnp.where(side == 0, vectors, got), jnp.where(side == 0, got, vectors)], axis=1
        )
    else:
        small = full_of(vectors, 1)
    h_own, h_got = pair_of(heavy_qkv)
    l_own, l_got = pair_of(light_qkv)
    w_lout, w_hout = (full_of(light_out), full_of(heavy_out))
    w_hgu, w_hdown = (full_of(heavy_gu), full_of(heavy_down))
    w_lgu, w_ldown = (full_of(light_gu), full_of(light_down))

    x, up = (tokens[:, 0], cotangent[:, 0])
    index = jnp.stack([q_index[:, 0], kv_index[:, 0], ff_index[:, 0]])
    cols, rows = (index[..., None], index[:, :, None, :])

    q_pay, kv_pay, hq_in, kin, h1k, gate = routed_in(info, x, cols, small, h_own, h_got)
    kv_orders = ((8, 4, 2, 1), (8, 4, 1, 2))
    pairs = []
    for m in range(micros):
        if direct:
            pairs.append(gather_pair(kv_pay[m], kv_orders[m % 2]))
        else:
            every = lax.all_gather(kv_pay[m], "ctx", axis=0, tiled=True)
            pairs.append((every[: every.shape[0] // 2], every[every.shape[0] // 2 :]))
    qkv = light_in(info, x, small, l_own, l_got)
    inner = qkv.shape[2] // 3
    upward = [(i, i + 1) for i in range(count - 1)]
    downward = [(i + 1, i) for i in range(count - 1)]
    before = lax.ppermute(qkv[:, tok - WIN :, inner:], "ctx", upward)
    after = lax.ppermute(qkv[:, :WIN, inner:], "ctx", downward)
    lo, light_lse = light_fwd(info, qkv, before, after)
    heavy = [heavy_fwd(info, q_pay[m], *pairs[m]) for m in range(micros)]
    ho = jnp.stack([h[0] for h in heavy])
    y, low2, ffr, dzh, hy, gf = middle(info, x, up, cols, rows, small, gate, lo, w_lout, ho, w_hout)
    routed = ffr.shape[1]

    def flat(value):
        return value.reshape(-1, value.shape[-1])

    zh, dff, hgu_own, hgu_send, hdn_own, hdn_send = ffn(info, flat(ffr), flat(dzh), w_hgu, w_hdown)
    z, dh2, lgu_own, lgu_send, ldn_own, ldn_send = ffn(info, flat(low2), flat(up), w_lgu, w_ldown)
    if direct:
        hgu_got, hdn_got, lgu_got, ldn_got = (
            lax.ppermute(part, "wsh", swap) for part in (hgu_send, hdn_send, lgu_send, ldn_send)
        )
        orders = ((1, 2, 4, 8), (2, 1, 4, 8), (4, 1, 2, 8))
        chunks = (
            reduced(info, orders[0], [(hgu_own, hgu_got, 0, 8), (lgu_own, lgu_got, 0, 2)]),
            reduced(info, orders[1], [(hgu_own, hgu_got, 8, 8), (lgu_own, lgu_got, 2, 2)]),
            reduced(info, orders[2], [(hdn_own, hdn_got, 0, 8), (ldn_own, ldn_got, 0, 2)]),
        )

    def by_micro(value):
        return value.reshape(micros, -1, value.shape[-1])

    out_tokens, dy, dlo, dho, dhy, dsq, part_two = mid_back(
        info, y, up, by_micro(z), by_micro(dh2), by_micro(zh), by_micro(dff), ffr, gf, cols, rows, small, gate, w_lout,
        w_hout, hy, hq_in,
    )
    dhq, dhkv = ([], [])
    for m in range(micros):
        dq, near, far = heavy_bwd(info, q_pay[m], *pairs[m], heavy[m][1], dho[m])
        dhq.append(dq)
        if direct:
            order = tuple(reversed(kv_orders[m % 2]))
            shape = (count // 2, routed, 2 * width)
            dhkv.append(scatter_sum(near.reshape(shape), far.reshape(shape), order)[0])
        else:
            every = jnp.concatenate([near, far], axis=0)
            dhkv.append(lax.psum_scatter(every, "ctx", scatter_dimension=0, tiled=True))
    dhq, dhkv = (jnp.stack(dhq), jnp.stack(dhkv))
    dlq, dl_own, rim_low, rim_high = light_bwd(info, qkv, before, after, light_lse, dlo)
    got_low = lax.ppermute(rim_high, "ctx", upward)
    got_high = lax.ppermute(rim_low, "ctx", downward)
    grad_tokens, dl, part_one = in_back(
        info, x, dy, dlq, dl_own, got_low, got_high, dhq, dhkv, dsq, rows, small, gate, hq_in, kin, h1k, l_own, l_got,
        h_own, h_got,
    )
    att_own, att_send = attention_grads(info, x, small, dl, hq_in, dhq, kin, dhkv, lo, dy, ho, dhy)
    widths = (light_qkv.shape[1], heavy_qkv.shape[1], heavy_out.shape[1])
    vector = part_one + part_two
    if direct:
        att_got = lax.ppermute(att_send, "wsh", swap)
        pieces = ((0, 4), (4, 3), (7, 3))
        sums = [
            reduced(info, order, [(att_own, att_got, first, size)])
            for order, (first, size) in zip(orders, pieces)
        ]
        half = width // 2
        mine = lax.dynamic_slice_in_dim(vector, side * half, half, 1)
        given = lax.dynamic_slice_in_dim(vector, (1 - side) * half, half, 1)
        mine = mine + lax.ppermute(given, "wsh", swap)
        vector = jnp.sum(lax.all_gather(mine, "ctx", axis=0), axis=0)
        g_lqkv, g_hqkv, g_hout, g_lout = unpack_attention(info, orders, sums, widths, inner)
        first = unpack_gu(info, orders[0], chunks[0], 0, 8, 16, 0, None)
        g_hgu = unpack_gu(info, orders[1], chunks[1], 0, 8, 16, 8, first)
        first = unpack_gu(info, orders[0], chunks[0], 8, 2, 4, 0, None)
        g_lgu = unpack_gu(info, orders[1], chunks[1], 8, 2, 4, 2, first)
        g_hdown = unpack_dn(info, orders[2], chunks[2], 0, 8, 8, 0, None)
        g_ldown = unpack_dn(info, orders[2], chunks[2], 8, 2, 2, 0, None)
    else:
        g_lqkv, g_hqkv, g_hout = plain_units(att_own, att_send, widths)
        last = slice(att_own.shape[0] - 1, att_own.shape[0])
        g_lqkv, g_lout, g_hqkv, g_hout, g_lgu, g_ldown, g_hgu, g_hdown = plain_sum(
            [
                g_lqkv,
                plain_dn(att_own[last], att_send[last]),
                g_hqkv,
                g_hout,
                plain_gu(lgu_own, lgu_send),
                plain_dn(ldn_own, ldn_send),
                plain_gu(hgu_own, hgu_send),
                plain_dn(hdn_own, hdn_send),
            ]
        )
        vector = lax.psum(vector, ("ctx", "wsh"))
        part = width // groups
        vector = lax.dynamic_slice_in_dim(vector, lax.axis_index("wsh") * part, part, 1)
    return (
        out_tokens[:, None],
        grad_tokens[:, None],
        g_lqkv,
        g_lout,
        g_hqkv,
        g_hout,
        g_lgu,
        g_ldown,
        g_hgu,
        g_hdown,
        vector[:3],
        vector[3:5],
    )


def solution(mesh):
    return jax.shard_map(
        per_device,
        mesh=mesh,
        in_specs=(
            P(None, "wsh", "ctx", None),
            P(None, "wsh", "ctx", None),
            P("wsh", None),
            P("wsh", None),
            P("wsh", None),
            P("wsh", None),
            P("wsh", None),
            P("wsh", None),
            P("wsh", None),
            P("wsh", None),
            P(None, "wsh"),
            P(None, "wsh"),
            P(None, "wsh", None),
            P(None, "wsh", "ctx"),
            P(None, "wsh", "ctx"),
            P(None, "wsh", "ctx"),
        ),
        out_specs=(
            P(None, "wsh", "ctx", None),
            P(None, "wsh", "ctx", None),
            P("wsh", None),
            P("wsh", None),
            P("wsh", None),
            P("wsh", None),
            P("wsh", None),
            P("wsh", None),
            P("wsh", None),
            P("wsh", None),
            P(None, "wsh"),
            P(None, "wsh"),
        ),
        check_vma=False,
    )
```

time: 1420 us -> 847 us (0.60)
  waiting for transfers between devices: 751 us -> 392 us
  matrix products: 283 us -> 0 us
  Pallas kernels: 0 us -> 254 us
  other arithmetic: 144 us -> 21.8 us
  local copies, waits for them, and re-layouts: 118 us -> 18.4 us
  starting transfers between devices: 25.2 us -> 91 us
  blocking collectives: 67 us -> 43.7 us
    psum x1 -> x0, waiting for transfers between devices: 404 us -> none  [per_device(): lax.psum(shortened(totals), 'ctx')]
    ppermute x8 -> x77, waiting for transfers between devices: 21.6 us -> 389 us  [the longest x64 347 us: flipped(): return lax.ppermute(value, 'ctx', [(i, i ^ bit) for i in range(size)])]
    dot_general x86 -> x0, matrix products: 254 us -> none  [the longest x30 62.8 us: matmul(): return jnp.dot(left, right, preferred_element_type=jnp.float32)]
    pallas_call x0 -> x27, Pallas kernels: none -> 254 us  [the longest x21 208 us: call(): pl.pallas_call(body, out_shape=outs, grid_spec=pltpu.PrefetchScalarGridSp...]
    reduce_scatter x16 -> x0, waiting for transfers between devices: 163 us -> none  [the longest x2 46.6 us: per_device(): lax.psum_scatter(weight_grads[6].astype(jnp.bfloat16), 'wsh', scatter_dim...]
    unnamed x38 -> x5, waiting for transfers between devices: 115 us -> 3.11 us
    ppermute x8 -> x77, starting transfers between devices: 22.7 us -> 90.8 us  [the longest x64 80 us: flipped(): return lax.ppermute(value, 'ctx', [(i, i ^ bit) for i in range(size)])]
    convert_element_type x27 -> x32, other arithmetic: 77.4 us -> 13.2 us  [the longest x16 12.3 us: scatter_sum(): keep = (keep[:half].astype(F32) + got[:half].astype(F32)).astype(BF)]
  transfers between devices with their start and end apart: 40 -> 82, of which waited for: 25 -> 41; matrix products, arithmetic and copies ran while one was open for 29% -> 3% of each run, Pallas kernels for 0% -> 23%
where the time goes in v1:
time: 847 us; the launch traced here: 836 us
  waiting for transfers between devices  392 us (46%)
  Pallas kernels  254 us (30%)
  starting transfers between devices  91 us (11%)
  blocking collectives  43.7 us (5%)
  other arithmetic  21.8 us (3%)
  local copies, waits for them, and re-layouts  18.4 us (2%)
  between operations  15.7 us (2%)
    ppermute x64, waiting for transfers between devices, flipped(): return lax.ppermute(value, 'ctx', [(i, i ^ bit) for i in range(size)])  347 us
    pallas_call x21, Pallas kernels, call(): pl.pallas_call(body, out_shape=outs, grid_spec=pltpu.PrefetchScalarGridSp...  208 us
    ppermute x64, starting transfers between devices, flipped(): return lax.ppermute(value, 'ctx', [(i, i ^ bit) for i in range(size)])  80 us
    all_gather x1, blocking collectives, per_device(): vector = jnp.sum(lax.all_gather(mine, 'ctx', axis=0), axis=0)  41.3 us
    ppermute x1, waiting for transfers between devices, per_device(): before = lax.ppermute(qkv[:, tok - WIN:, inner:], 'ctx', upward)  40.9 us
    pallas_call x4, Pallas kernels, unpack_gu(): pl.pallas_call(body, out_shape=out, grid_spec=pltpu.PrefetchScalarGridSpe...  35.3 us
  transfers between devices with their start and end apart: 82, of which 41 were waited for; matrix products, arithmetic and copies ran while one was open for 3% of the time, Pallas kernels for 23%

profile of v1, /device:TPU:0, one launch (start us, length us, event | category | flops | bytes accessed | tf_op | source)
XLA Modules:
  0.0 836.3 jit_solution(10289749085132319348)
XLA Ops:
  25.4 15.1 %collective-permute-done.5 = bf16[64,1664]{1,0:T(8,128)(2,1)S(1)} collective-permute-done((bf16[64,1664]{1,0:T(8,128)(2,1)S(1)}, bf16[64,1664]{1,0:T(8,128)(2,1)S(1)}, u32[]{:S(2)}, u32[]{:S(2)}) %collective-permute-start.5) | collective-permute-done | bytes 213024 | tf_op jit(solution)/shard_map/ppermute | solution.py:863
  64.5 10.2 %collective-permute-done.7 = bf16[256,1664]{1,0:T(8,128)(2,1)S(1)} collective-permute-done((bf16[256,1664]{1,0:T(8,128)(2,1)S(1)}, bf16[256,1664]{1,0:T(8,128)(2,1)S(1)}, u32[]{:S(2)}, u32[]{:S(2)}) %collective-permute-start.7) | collective-permute-done | bytes 852000 | tf_op jit(solution)/shard_map/ppermute | solution.py:863
  101.0 40.9 %collective-permute-done.3.before = bf16[2,128,1024]{2,1,0:T(8,128)(2,1)S(1)} collective-permute-done((bf16[2,128,1024]{2,1,0:T(8,128)(2,1)S(1)}, bf16[2,128,1024]{2,1,0:T(8,128)(2,1)S(1)}, u32[]{:S(2)}, u32[]{:S(2)}) %collective-permute-start.3) | collective-permute-done | bytes 524320 | tf_op jit(solution)/shard_map/ppermute | solution.py:1151
  142.9 15.1 %shard_map.249 = (bf16[2,512,512]{2,1,0:T(8,128)(2,1)S(1)}, f32[2,512,128]{2,1,0:T(8,128)S(1)}) custom-call(s32[14]{0:T(128)S(1)} %concatenate.97.info, bf16[2,512,1536]{2,1,0:T(8,128)(2,1)S(1)} %copy-done.23, bf16[2,128,1024]{2,1,0:T(8,128)(2,1)S(1)} %collective-permute-done.3.before, bf16[2,128,1024]{2,1,0:T(8,128)(2,1)S(1)} %collective-permute-done.4.after), custom_call_target="tpu_custom_call" | custom-call | flops 4000000000 | bytes 6000000 | tf_op jit(solution)/shard_map/pallas_call | solution.py:74
  176.9 25.7 %shard_map.253 = (f32[1024,768]{1,0:T(8,128)}, f32[1024,768]{1,0:T(8,128)}, bf16[4,768,256]{2,1,0:T(8,128)(2,1)S(1)}, bf16[4,768,256]{2,1,0:T(8,128)(2,1)S(1)}, ...) custom-call(s32[14]{0:T(128)S(1)} %concatenate.97.info, bf16[1024,768]{1,0:T(8,128)(2,1)} %bitcast.71, ...), custom_call_target="tpu_custom_call" | custom-call | flops 14495514624 | bytes 18874368 | tf_op jit(solution)/shard_map/pallas_call | solution.py:74
  205.6 30.5 %shard_map.254 = (f32[128,768]{1,0:T(8,128)S(1)}, f32[128,768]{1,0:T(8,128)S(1)}, bf16[16,768,256]{2,1,0:T(8,128)(2,1)}, bf16[16,768,256]{2,1,0:T(8,128)(2,1)}, ...) custom-call(s32[14]{0:T(128)S(1)} %concatenate.97.info, bf16[128,768]{1,0:T(8,128)(2,1)S(1)} %bitcast.58, ...), custom_call_target="tpu_custom_call" | custom-call | flops 7247757312 | bytes 38928384 | tf_op jit(solution)/shard_map/pallas_call | solution.py:74
  237.7 11.6 %shard_map.255 = (bf16[2,512,768]{2,1,0:T(8,128)(2,1)}, f32[2,512,768]{2,1,0:T(8,128)}, bf16[2,512,512]{2,1,0:T(8,128)(2,1)S(1)}, bf16[2,64,768]{2,1,0:T(8,128)(...) custom-call(s32[14]{0:T(128)S(1)} %concatenate.97.info, ...), custom_call_target="tpu_custom_call" | custom-call | flops 3000000000 | bytes 22000000 | tf_op jit(solution)/shard_map/pallas_call | solution.py:74
  264.1 27.4 %collective-permute-done.15 = bf16[8,64,1536]{2,1,0:T(8,128)(2,1)} collective-permute-done((bf16[8,64,1536]{2,1,0:T(8,128)(2,1)S(1)}, bf16[8,64,1536]{2,1,0:T(8,128)(2,1)}, u32[]{:S(2)}, u32[]{:S(2)}) %collective-permute-start.15) | collective-permute-done | bytes 1572896 | tf_op jit(solution)/shard_map/ppermute | solution.py:863
  301.7 22.1 %shard_map.256 = (bf16[2,512,512]{2,1,0:T(8,128)(2,1)S(1)}, f32[2,512,1024]{2,1,0:T(8,128)}, bf16[2,128,1024]{2,1,0:T(8,128)(2,1)S(1)}, bf16[2,128,1024]{2,1,0:T(8,128)(2,1)S(1)}) custom-call(s32[14]{0:T(128)S(1)} %concatenate.97.info, bf16[2,512,1536]{2,1,0:T(8,128)(2,1)} %shard_map.248.qkv, bf16[2,128,1024]{2,1,0:T(8,128)(2,1)S(1)} %copy-done.45, ...), custom_call_target="tpu_custom_call" | custom-call | flops 10000000000 | bytes 14000000 | tf_op jit(solution)/shard_map/pallas_call | solution.py:74
  328.6 9.6 %collective-permute-done.17 = bf16[2,64,1536]{2,1,0:T(8,128)(2,1)S(1)} collective-permute-done((bf16[2,64,1536]{2,1,0:T(8,128)(2,1)S(1)}, bf16[2,64,1536]{2,1,0:T(8,128)(2,1)S(1)}, u32[]{:S(2)}, u32[]{:S(2)}) %collective-permute-start.17) | collective-permute-done | bytes 393248 | tf_op jit(solution)/shard_map/ppermute | solution.py:863
  350.4 8.7 %collective-permute-done.18 = bf16[1,64,1536]{2,1,0:T(8,128)(2,1)S(1)} collective-permute-done((bf16[1,64,1536]{2,1,0:T(8,128)(2,1)S(1)}, bf16[1,64,1536]{2,1,0:T(8,128)(2,1)S(1)}, u32[]{:S(2)}, u32[]{:S(2)}) %collective-permute-start.18) | collective-permute-done | bytes 196640 | tf_op jit(solution)/shard_map/ppermute | solution.py:863
  367.0 11.6 %collective-permute-start.68 = (bf16[8,10,48,256]{3,2,1,0:T(8,128)(2,1)S(1)}, bf16[8,10,48,256]{3,2,1,0:T(8,128)(2,1)}, u32[]{:S(2)}, u32[]{:S(2)}) collective-permute-start(bf16[8,10,48,256]{3,2,1,0:T(8,128)(2,1)S(1)} %get-tuple-element.145), channel_id=1, source_target_pairs={{0,8},{2,10},{4,12},{6,14},{8,0},{10,2},{12,4},{14,6},{16,24},{18,... | collective-permute-start | bytes 5898248 | tf_op jit(solution)/shard_map/ppermute | solution.py:863
  378.9 14.6 %shard_map.259 = (bf16[2,512,768]{2,1,0:T(8,128)(2,1)}, bf16[2,512,1536]{2,1,0:T(8,128)(2,1)}, f32[8,768]{1,0:T(8,128)S(1)}) custom-call(s32[14]{0:T(128)S(1)} %concatenate.97.info, bf16[2,512,768]{2,1,0:T(8,128)(2,1)} %bitcast.54, f32[2,512,768]{2,1,0:T(8,128)} %get-tuple-element.98.dy, bf16[2,512,512]{2,1,0:T(8,128)(2,1)S(1)} %get-tuple-element.101.dq, ...), custom_call_target="tpu_custom_call" | custom-call | flops 4000000000 | bytes 22000000 | tf_op jit(solution)/shard_map/pallas_call | solution.py:74
  393.5 13.0 %shard_map.260 = (bf16[10,768,256]{2,1,0:T(8,128)(2,1)}, bf16[10,768,256]{2,1,0:T(8,128)(2,1)}) custom-call(s32[14]{0:T(128)S(1)} %concatenate.97.info, bf16[2,512,768]{2,1,0:T(8,128)(2,1)S(1)} %bitcast.57, bf16[8,768]{1,0:T(8,128)(2,1)S(1)} %pad_maximum_fusion.27.small, bf16[2,512,1536]{2,1,0:T(8,128)(2,1)} %get-tuple-element.118.dl, ...), custom_call_target="tpu_custom_call" | custom-call | flops 3303014400 | bytes 20000000 | tf_op jit(solution)/shard_map/pallas_call | solution.py:74
  407.1 18.0 %collective-permute-done.68 = bf16[8,10,48,256]{3,2,1,0:T(8,128)(2,1)} collective-permute-done((bf16[8,10,48,256]{3,2,1,0:T(8,128)(2,1)S(1)}, bf16[8,10,48,256]{3,2,1,0:T(8,128)(2,1)}, u32[]{:S(2)}, u32[]{:S(2)}) %collective-permute-start.68) | collective-permute-done | bytes 1966112 | tf_op jit(solution)/shard_map/ppermute | solution.py:863
  452.2 46.3 %collective-permute-done.70 = bf16[2,10,48,256]{3,2,1,0:T(8,128)(2,1)S(1)} collective-permute-done((bf16[2,10,48,256]{3,2,1,0:T(8,128)(2,1)S(1)}, bf16[2,10,48,256]{3,2,1,0:T(8,128)(2,1)S(1)}, u32[]{:S(2)}, u32[]{:S(2)}) %collective-permute-start.70) | collective-permute-done | bytes 491552 | tf_op jit(solution)/shard_map/ppermute | solution.py:863
  501.0 10.5 %collective-permute-done.71 = bf16[1,10,48,256]{3,2,1,0:T(8,128)(2,1)S(1)} collective-permute-done((bf16[1,10,48,256]{3,2,1,0:T(8,128)(2,1)S(1)}, bf16[1,10,48,256]{3,2,1,0:T(8,128)(2,1)S(1)}, u32[]{:S(2)}, u32[]{:S(2)}) %collective-permute-start.71) | collective-permute-done | bytes 245792 | tf_op jit(solution)/shard_map/ppermute | solution.py:863
  536.3 10.4 %collective-permute-done.73 = bf16[2,10,48,256]{3,2,1,0:T(8,128)(2,1)S(1)} collective-permute-done((bf16[2,10,48,256]{3,2,1,0:T(8,128)(2,1)S(1)}, bf16[2,10,48,256]{3,2,1,0:T(8,128)(2,1)S(1)}, u32[]{:S(2)}, u32[]{:S(2)}) %collective-permute-start.73) | collective-permute-done | bytes 491552 | tf_op jit(solution)/shard_map/ppermute | solution.py:863
  549.1 12.3 %collective-permute-done.59 = bf16[4,10,48,256]{3,2,1,0:T(8,128)(2,1)S(1)} collective-permute-done((bf16[4,10,48,256]{3,2,1,0:T(8,128)(2,1)S(1)}, bf16[4,10,48,256]{3,2,1,0:T(8,128)(2,1)S(1)}, u32[]{:S(2)}, u32[]{:S(2)}) %collective-permute-start.59) | collective-permute-done | bytes 983072 | tf_op jit(solution)/shard_map/ppermute | solution.py:863
  596.2 10.3 %collective-permute-done.53 = bf16[1,10,48,256]{3,2,1,0:T(8,128)(2,1)S(1)} collective-permute-done((bf16[1,10,48,256]{3,2,1,0:T(8,128)(2,1)S(1)}, bf16[1,10,48,256]{3,2,1,0:T(8,128)(2,1)S(1)}, u32[]{:S(2)}, u32[]{:S(2)}) %collective-permute-start.53) | collective-permute-done | bytes 245792 | tf_op jit(solution)/shard_map/ppermute | solution.py:863
  668.8 27.2 %collective-permute-done.35 = bf16[1,3,48,256]{3,2,1,0:T(8,128)(2,1)S(1)} collective-permute-done((bf16[1,3,48,256]{3,2,1,0:T(8,128)(2,1)S(1)}, bf16[1,3,48,256]{3,2,1,0:T(8,128)(2,1)S(1)}, u32[]{:S(2)}, u32[]{:S(2)}) %collective-permute-start.35) | collective-permute-done | bytes 73760 | tf_op jit(solution)/shard_map/ppermute | solution.py:863
  732.5 41.3 %all-gather = f32[128,384]{1,0:T(8,128)S(1)} all-gather(f32[8,384]{1,0:T(8,128)S(1)} %dynamic-slice_add_fusion), channel_id=2, replica_groups=mesh['ctx'=16,'wsh'=2] {'ctx'}, dimensions={0}, use_global_device_ids=true | all-gather | bytes 208896 | tf_op jit(solution)/shard_map/all_gather | solution.py:1215
  794.0 13.3 %shard_map.271.unused = f32[384,8192]{1,0:T(8,128)} custom-call(s32[14]{0:T(128)} %copy-done.30, bf16[8,10,48,256]{3,2,1,0:T(8,128)(2,1)} %pad_maximum_fusion.1.near, bf16[8,10,48,256]{3,2,1,0:T(8,128)(2,1)} %collective-permute-done.65.far), custom_call_target="tpu_custom_call" | custom-call | bytes 9437184 | tf_op jit(solution)/shard_map/pallas_call | solution.py:942
  811.8 13.2 %shard_map.272 = f32[384,8192]{1,0:T(8,128)} custom-call(s32[14]{0:T(128)} %copy-done.30, bf16[8,10,48,256]{3,2,1,0:T(8,128)(2,1)} %pad_maximum_fusion.near, bf16[8,10,48,256]{3,2,1,0:T(8,128)(2,1)} %collective-permute-done.57.far, f32[384,8192]{1,0:T(8,128)} %shard_map.271.unused), custom_call_target="tpu_custom_call", output_to_operand_aliasing={{}: (3, {})} | custom-call | bytes 9437184 | tf_op jit(solution)/shard_map/pallas_call | solution.py:942
  (403 shorter events, 361.7 us)
Async XLA Ops:
  7.2 160.0 %all-gather.7.cloned.1.call-start = ((), (), s32[]{:S(2)}) async-start(), calls=%async_computation | async-start | bytes 1769472 | tf_op jit(solution)/shard_map/all_gather | solution.py:1118
  7.9 169.0 %all-gather.11.cloned.1.call-start = ((), (), s32[]{:S(2)}) async-start(), calls=%async_computation.2 | async-start | bytes 2359296 | tf_op jit(solution)/shard_map/all_gather | solution.py:1118
  8.7 168.2 %all-gather.9.cloned.1.call-start = ((), (), s32[]{:S(2)}) async-start(), calls=%async_computation.1 | async-start | bytes 4718592 | tf_op jit(solution)/shard_map/all_gather | solution.py:1118
  9.4 196.2 %all-gather.15.cloned.1.call-start = ((), (), s32[]{:S(2)}) async-start(), calls=%async_computation.4 | async-start | bytes 9437184 | tf_op jit(solution)/shard_map/all_gather | solution.py:1118
  10.1 195.5 %all-gather.13.cloned.1.call-start = ((), (), s32[]{:S(2)}) async-start(), calls=%async_computation.3 | async-start | bytes 18874368 | tf_op jit(solution)/shard_map/all_gather | solution.py:1118
  74.9 83.2 %collective-permute-start.8 = (bf16[512,1664]{1,0:T(8,128)(2,1)S(1)}, bf16[512,1664]{1,0:T(8,128)(2,1)S(1)}, u32[]{:S(2)}, u32[]{:S(2)}) collective-permute-start(bf16[512,1664]{1,0:T(8,128)(2,1)S(1)} %pad_maximum_fusion.3.kv_a), channel_id=1, source_target_pairs={{0,2},{2,0},{4,6},{6,4},{8,10},{10,8},{12,14},{14,12},{16,18},{18,... | collective-permute-start | bytes 5111816 | tf_op jit(solution)/shard_map/ppermute | solution.py:863
  84.9 77.3 %collective-permute-start.12 = (bf16[512,1664]{1,0:T(8,128)(2,1)S(1)}, bf16[512,1664]{1,0:T(8,128)(2,1)}, u32[]{:S(2)}, u32[]{:S(2)}) collective-permute-start(bf16[512,1664]{1,0:T(8,128)(2,1)S(1)} %pad_maximum_fusion.4.kv_a), channel_id=1, source_target_pairs={{0,4},{2,6},{4,0},{6,2},{8,12},{10,14},{12,8},{14,10},{16,20},{18,... | collective-permute-start | bytes 5111816 | tf_op jit(solution)/shard_map/ppermute | solution.py:863
  93.8 48.1 %collective-permute-start.3 = (bf16[2,128,1024]{2,1,0:T(8,128)(2,1)S(1)}, bf16[2,128,1024]{2,1,0:T(8,128)(2,1)S(1)}, u32[]{:S(2)}, u32[]{:S(2)}) collective-permute-start(bf16[2,128,1024]{2,1,0:T(8,128)(2,1)S(1)} %get-tuple-element.167), channel_id=1, source_target_pairs={{0,2},{2,4},{4,6},{6,8},{8,10},{10,12},{12,14},{14,16},{16,18},{18... | collective-permute-start | bytes 1572872 | tf_op jit(solution)/shard_map/ppermute | solution.py:1151
  97.2 45.6 %collective-permute-start.4 = (bf16[2,128,1024]{2,1,0:T(8,128)(2,1)S(1)}, bf16[2,128,1024]{2,1,0:T(8,128)(2,1)S(1)}, u32[]{:S(2)}, u32[]{:S(2)}) collective-permute-start(bf16[2,128,1024]{2,1,0:T(8,128)(2,1)S(1)} %get-tuple-element.166), channel_id=1, source_target_pairs={{2,0},{4,2},{6,4},{8,6},{10,8},{12,10},{14,12},{16,14},{18,16},{20... | collective-permute-start | bytes 1572872 | tf_op jit(solution)/shard_map/ppermute | solution.py:1152
  257.6 101.5 %collective-permute-start.67 = (bf16[2,768,256]{2,1,0:T(8,128)(2,1)S(1)}, bf16[2,768,256]{2,1,0:T(8,128)(2,1)S(1)}, u32[]{:S(2)}, u32[]{:S(2)}) collective-permute-start(bf16[2,768,256]{2,1,0:T(8,128)(2,1)S(1)} %copy-done.43), channel_id=1, source_target_pairs={{0,1},{1,0},{2,3},{3,2},{4,5},{5,4},{6,7},{7,6},{8,9},{9,8},{10,11... | collective-permute-start | bytes 2359304 | tf_op jit(solution)/shard_map/ppermute | solution.py:1166
  263.2 97.2 %collective-permute-start.66 = (bf16[8,768,256]{2,1,0:T(8,128)(2,1)}, bf16[8,768,256]{2,1,0:T(8,128)(2,1)}, u32[]{:S(2)}, u32[]{:S(2)}) collective-permute-start(bf16[8,768,256]{2,1,0:T(8,128)(2,1)} %get-tuple-element.141), channel_id=1, source_target_pairs={{0,1},{1,0},{2,3},{3,2},{4,5},{5,4},{6,7},{7,6},{8,9},{9,8},{10,11... | collective-permute-start | bytes 9437192 | tf_op jit(solution)/shard_map/ppermute | solution.py:1166
  263.8 163.4 %collective-permute-start.48 = (bf16[16,768,256]{2,1,0:T(8,128)(2,1)}, bf16[16,768,256]{2,1,0:T(8,128)(2,1)}, u32[]{:S(2)}, u32[]{:S(2)}) collective-permute-start(bf16[16,768,256]{2,1,0:T(8,128)(2,1)} %get-tuple-element.133), channel_id=1, source_target_pairs={{0,1},{1,0},{2,3},{3,2},{4,5},{5,4},{6,7},{7,6},{8,9},{9,8},{10,11... | collective-permute-start | bytes 18874376 | tf_op jit(solution)/shard_map/ppermute | solution.py:1166
  323.9 54.9 %collective-permute-start.13 = (bf16[2,128,1024]{2,1,0:T(8,128)(2,1)S(1)}, bf16[2,128,1024]{2,1,0:T(8,128)(2,1)S(1)}, u32[]{:S(2)}, u32[]{:S(2)}) collective-permute-start(bf16[2,128,1024]{2,1,0:T(8,128)(2,1)S(1)} %get-tuple-element.103), channel_id=1, source_target_pairs={{0,2},{2,4},{4,6},{6,8},{8,10},{10,12},{12,14},{14,16},{16,18},{18... | collective-permute-start | bytes 1572872 | tf_op jit(solution)/shard_map/ppermute | solution.py:1195
  367.0 58.0 %collective-permute-start.68 = (bf16[8,10,48,256]{3,2,1,0:T(8,128)(2,1)S(1)}, bf16[8,10,48,256]{3,2,1,0:T(8,128)(2,1)}, u32[]{:S(2)}, u32[]{:S(2)}) collective-permute-start(bf16[8,10,48,256]{3,2,1,0:T(8,128)(2,1)S(1)} %get-tuple-element.145), channel_id=1, source_target_pairs={{0,8},{2,10},{4,12},{6,14},{8,0},{10,2},{12,4},{14,6},{16,24},{18,... | collective-permute-start | bytes 5898248 | tf_op jit(solution)/shard_map/ppermute | solution.py:863
  406.5 105.1 %collective-permute-start.23 = (bf16[10,768,256]{2,1,0:T(8,128)(2,1)}, bf16[10,768,256]{2,1,0:T(8,128)(2,1)}, u32[]{:S(2)}, u32[]{:S(2)}) collective-permute-start(bf16[10,768,256]{2,1,0:T(8,128)(2,1)} %get-tuple-element.121), channel_id=1, source_target_pairs={{0,1},{1,0},{2,3},{3,2},{4,5},{5,4},{6,7},{7,6},{8,9},{9,8},{10,11... | collective-permute-start | bytes 11796488 | tf_op jit(solution)/shard_map/ppermute | solution.py:1205
  435.2 91.8 %collective-permute-start.58 = (bf16[8,10,48,256]{3,2,1,0:T(8,128)(2,1)}, bf16[8,10,48,256]{3,2,1,0:T(8,128)(2,1)}, u32[]{:S(2)}, u32[]{:S(2)}) collective-permute-start(bf16[8,10,48,256]{3,2,1,0:T(8,128)(2,1)} %get-tuple-element.139), channel_id=1, source_target_pairs={{0,2},{2,0},{4,6},{6,4},{8,10},{10,8},{12,14},{14,12},{16,18},{18,... | collective-permute-start | bytes 5898248 | tf_op jit(solution)/shard_map/ppermute | solution.py:863
  445.4 83.7 %collective-permute-start.50 = (bf16[8,10,48,256]{3,2,1,0:T(8,128)(2,1)}, bf16[8,10,48,256]{3,2,1,0:T(8,128)(2,1)}, u32[]{:S(2)}, u32[]{:S(2)}) collective-permute-start(bf16[8,10,48,256]{3,2,1,0:T(8,128)(2,1)} %get-tuple-element.137), channel_id=1, source_target_pairs={{0,4},{2,6},{4,0},{6,2},{8,12},{10,14},{12,8},{14,10},{16,20},{18,... | collective-permute-start | bytes 5898248 | tf_op jit(solution)/shard_map/ppermute | solution.py:863
  452.1 46.4 %collective-permute-start.70 = (bf16[2,10,48,256]{3,2,1,0:T(8,128)(2,1)S(1)}, bf16[2,10,48,256]{3,2,1,0:T(8,128)(2,1)S(1)}, u32[]{:S(2)}, u32[]{:S(2)}) collective-permute-start(bf16[2,10,48,256]{3,2,1,0:T(8,128)(2,1)S(1)} %get-tuple-element.169), channel_id=1, source_target_pairs={{0,4},{2,6},{4,0},{6,2},{8,12},{10,14},{12,8},{14,10},{16,20},{18,... | collective-permute-start | bytes 1474568 | tf_op jit(solution)/shard_map/ppermute | solution.py:863
  536.2 132.2 %collective-permute-start.76 = (f32[8,384]{1,0:T(8,128)S(1)}, f32[8,384]{1,0:T(8,128)S(1)}, u32[]{:S(2)}, u32[]{:S(2)}) collective-permute-start(f32[8,384]{1,0:T(8,128)S(1)} %constant_dynamic-slice_fusion), channel_id=1, source_target_pairs={{0,1},{1,0},{2,3},{3,2},{4,5},{5,4},{6,7},{7,6},{8,9},{9,8},{10,11... | collective-permute-start | bytes 36872 | tf_op jit(solution)/shard_map/ppermute | solution.py:1214
  561.4 94.9 %collective-permute-start.74 = (bf16[4,10,48,256]{3,2,1,0:T(8,128)(2,1)S(1)}, bf16[4,10,48,256]{3,2,1,0:T(8,128)(2,1)S(1)}, u32[]{:S(2)}, u32[]{:S(2)}) collective-permute-start(bf16[4,10,48,256]{3,2,1,0:T(8,128)(2,1)S(1)} %pad_maximum_fusion.7), channel_id=1, source_target_pairs={{0,2},{2,0},{4,6},{6,4},{8,10},{10,8},{12,14},{14,12},{16,18},{18,... | collective-permute-start | bytes 2949128 | tf_op jit(solution)/shard_map/ppermute | solution.py:863
  577.8 47.0 %collective-permute-start.25 = (bf16[4,4,48,256]{3,2,1,0:T(8,128)(2,1)S(1)}, bf16[4,4,48,256]{3,2,1,0:T(8,128)(2,1)S(1)}, u32[]{:S(2)}, u32[]{:S(2)}) collective-permute-start(bf16[4,4,48,256]{3,2,1,0:T(8,128)(2,1)S(1)} %get-tuple-element.175), channel_id=1, source_target_pairs={{0,4},{2,6},{4,0},{6,2},{8,12},{10,14},{12,8},{14,10},{16,20},{18,... | collective-permute-start | bytes 1179656 | tf_op jit(solution)/shard_map/ppermute | solution.py:863
  659.2 124.3 %collective-permute-start.75 = (bf16[8,10,48,256]{3,2,1,0:T(8,128)(2,1)}, bf16[8,10,48,256]{3,2,1,0:T(8,128)(2,1)}, u32[]{:S(2)}, u32[]{:S(2)}) collective-permute-start(bf16[8,10,48,256]{3,2,1,0:T(8,128)(2,1)} %pad_maximum_fusion.2.near), channel_id=1, source_target_pairs={{0,8},{2,10},{4,12},{6,14},{8,0},{10,2},{12,4},{14,6},{16,24},{18,... | collective-permute-start | bytes 5898248 | tf_op jit(solution)/shard_map/ppermute | solution.py:863
  663.4 130.6 %collective-permute-start.65 = (bf16[8,10,48,256]{3,2,1,0:T(8,128)(2,1)}, bf16[8,10,48,256]{3,2,1,0:T(8,128)(2,1)}, u32[]{:S(2)}, u32[]{:S(2)}) collective-permute-start(bf16[8,10,48,256]{3,2,1,0:T(8,128)(2,1)} %pad_maximum_fusion.1.near), channel_id=1, source_target_pairs={{0,2},{2,0},{4,6},{6,4},{8,10},{10,8},{12,14},{14,12},{16,18},{18,... | collective-permute-start | bytes 5898248 | tf_op jit(solution)/shard_map/ppermute | solution.py:863
  665.3 146.4 %collective-permute-start.57 = (bf16[8,10,48,256]{3,2,1,0:T(8,128)(2,1)}, bf16[8,10,48,256]{3,2,1,0:T(8,128)(2,1)}, u32[]{:S(2)}, u32[]{:S(2)}) collective-permute-start(bf16[8,10,48,256]{3,2,1,0:T(8,128)(2,1)} %pad_maximum_fusion.near), channel_id=1, source_target_pairs={{0,4},{2,6},{4,0},{6,2},{8,12},{10,14},{12,8},{14,10},{16,20},{18,... | collective-permute-start | bytes 5898248 | tf_op jit(solution)/shard_map/ppermute | solution.py:863
  (131 other events, 2872.8 us)
Sparse Core Ops, SparseCore 0:
  9.6 11.9 all-gather.6
  23.1 10.9 all-gather.10
  35.6 13.2 all-gather.8
  50.3 17.9 all-gather.14
  69.7 26.0 all-gather.12

commit v2 on v1

--- a/solution.py
+++ b/solution.py
@@ -70,9 +70,10 @@
     return jnp.concatenate([jnp.where(lower, own, other), jnp.where(lower, other, own)], axis=1)
 
 
-def call(body, outs, grid, in_specs, out_specs, args, scratch=(), flops=0, moved=0, limit=48):
+def call(body, outs, grid, in_specs, out_specs, args, scratch=(), flops=0, moved=0, limit=48, name=None):
     return pl.pallas_call(
         body,
+        name=name or getattr(body, "__name__", "kernel"),
         out_shape=outs,
         grid_spec=pltpu.PrefetchScalarGridSpec(
             num_scalar_prefetch=1,
@@ -863,26 +864,46 @@
     return lax.ppermute(value, "ctx", [(i, i ^ bit) for i in range(size)])
 
 
+def tied(*values):
+    return lax.optimization_barrier(values)
+
+
+def scatter_step(keep, got):
+    half = keep.shape[0] // 2
+    if half == 0:
+        return ((keep.astype(F32) + got.astype(F32)).astype(BF), None)
+    return (
+        (keep[:half].astype(F32) + got[:half].astype(F32)).astype(BF),
+        (keep[half:].astype(F32) + got[half:].astype(F32)).astype(BF),
+    )
+
+
+def scatter_start(chunks, orders, stage):
+    return [flipped(send, order[stage]) for (keep, send), order in zip(chunks, orders)]
+
+
+def scatter_end(chunks, got):
+    return [scatter_step(keep, g) for (keep, send), g in zip(chunks, got)]
+
+
 def scatter_sum(keep, send, order):
     for bit in order:
-        got = flipped(send, bit)
-        half = keep.shape[0] // 2
-        if half == 0:
-            return (keep.astype(F32) + got.astype(F32)).astype(BF)
-        send = (keep[half:].astype(F32) + got[half:].astype(F32)).astype(BF)
-        keep = (keep[:half].astype(F32) + got[:half].astype(F32)).astype(BF)
+        keep, send = scatter_step(keep, flipped(send, bit))
+    return keep
+
+
+def gather_start(values, orders, stage):
+    return [flipped(value, order[-1 - stage]) for value, order in zip(values, orders)]
+
+
+def gather_end(values, got):
+    return [jnp.concatenate([value, g], axis=0) for value, g in zip(values, got)]
 
 
 def gather_pair(value, order):
     for bit in order[:-1]:
         value = jnp.concatenate([value, flipped(value, bit)], axis=0)
     return (value, flipped(value, order[-1]))
-
-
-def reduced(info, order, parts):
-    keep, send = fold(info, order, parts)
-    own = scatter_sum(keep, send, order)
-    return gather_pair(own, tuple(reversed(order)))
 
 
 def place(info, order, near, far, block, part, half, write):
@@ -1137,21 +1158,43 @@
 
     q_pay, kv_pay, hq_in, kin, h1k, gate = routed_in(info, x, cols, small, h_own, h_got)
     kv_orders = ((8, 4, 2, 1), (8, 4, 1, 2))
-    pairs = []
-    for m in range(micros):
-        if direct:
-            pairs.append(gather_pair(kv_pay[m], kv_orders[m % 2]))
-        else:
+    upward = [(i, i + 1) for i in range(count - 1)]
+    downward = [(i + 1, i) for i in range(count - 1)]
+    inner = light_qkv.shape[1] // 3
+
+    def rims(qkv):
+        return (
+            lax.ppermute(qkv[:, tok - WIN :, inner:], "ctx", upward),
+            lax.ppermute(qkv[:, :WIN, inner:], "ctx", downward),
+        )
+
+    if direct:
+        back_orders = [tuple(reversed(order)) for order in kv_orders]
+        values = [kv_pay[m] for m in range(micros)]
+        got = gather_start(values, back_orders, 0)
+        qkv = light_in(info, x, small, l_own, l_got)
+        got, qkv, w_lout, w_hout = tied(got, qkv, w_lout, w_hout)
+        before, after = rims(qkv)
+        values = gather_end(values, got)
+        got = gather_start(values, back_orders, 1)
+        got, before, after = tied(got, before, after)
+        values = gather_end(values, got)
+        got = gather_start(values, back_orders, 2)
+        lo, light_lse = light_fwd(info, qkv, before, after)
+        got, lo, light_lse, w_hgu, w_hdown = tied(got, lo, light_lse, w_hgu, w_hdown)
+        values = gather_end(values, got)
+        got = gather_start(values, back_orders, 3)
+        pairs = list(zip(values, got))
+    else:
+        pairs = []
+        for m in range(micros):
             every = lax.all_gather(kv_pay[m], "ctx", axis=0, tiled=True)
             pairs.append((every[: every.shape[0] // 2], every[every.shape[0] // 2 :]))
-    qkv = light_in(info, x, small, l_own, l_got)
-    inner = qkv.shape[2] // 3
-    upward = [(i, i + 1) for i in range(count - 1)]
-    downward = [(i + 1, i) for i in range(count - 1)]
-    before = lax.ppermute(qkv[:, tok - WIN :, inner:], "ctx", upward)
-    after = lax.ppermute(qkv[:, :WIN, inner:], "ctx", downward)
-    lo, light_lse = light_fwd(info, qkv, before, after)
+        qkv = light_in(info, x, small, l_own, l_got)
+        before, after = rims(qkv)
+        lo, light_lse = light_fwd(info, qkv, before, after)
     heavy = [heavy_fwd(info, q_pay[m], *pairs[m]) for m in range(micros)]
+    heavy, w_lgu, w_ldown = tied(heavy, w_lgu, w_ldown)
     ho = jnp.stack([h[0] for h in heavy])
     y, low2, ffr, dzh, hy, gf = middle(info, x, up, cols, rows, small, gate, lo, w_lout, ho, w_hout)
     routed = ffr.shape[1]
@@ -1165,12 +1208,13 @@
         hgu_got, hdn_got, lgu_got, ldn_got = (
             lax.ppermute(part, "wsh", swap) for part in (hgu_send, hdn_send, lgu_send, ldn_send)
         )
-        orders = ((1, 2, 4, 8), (2, 1, 4, 8), (4, 1, 2, 8))
-        chunks = (
-            reduced(info, orders[0], [(hgu_own, hgu_got, 0, 8), (lgu_own, lgu_got, 0, 2)]),
-            reduced(info, orders[1], [(hgu_own, hgu_got, 8, 8), (lgu_own, lgu_got, 2, 2)]),
-            reduced(info, orders[2], [(hdn_own, hdn_got, 0, 8), (ldn_own, ldn_got, 0, 2)]),
-        )
+        orders = ((1, 2, 4, 8), (2, 4, 1, 8), (4, 1, 2, 8))
+        first = [
+            fold(info, orders[0], [(hgu_own, hgu_got, 0, 8), (lgu_own, lgu_got, 0, 2)]),
+            fold(info, orders[1], [(hgu_own, hgu_got, 8, 8), (lgu_own, lgu_got, 2, 2)]),
+            fold(info, orders[2], [(hdn_own, hdn_got, 0, 8), (ldn_own, ldn_got, 0, 2)]),
+        ]
+        got = scatter_start(first, orders, 0)
 
     def by_micro(value):
         return value.reshape(micros, -1, value.shape[-1])
@@ -1179,21 +1223,47 @@
         info, y, up, by_micro(z), by_micro(dh2), by_micro(zh), by_micro(dff), ffr, gf, cols, rows, small, gate, w_lout,
         w_hout, hy, hq_in,
     )
-    dhq, dhkv = ([], [])
+    dhq, partial = ([], [])
     for m in range(micros):
         dq, near, far = heavy_bwd(info, q_pay[m], *pairs[m], heavy[m][1], dho[m])
         dhq.append(dq)
-        if direct:
-            order = tuple(reversed(kv_orders[m % 2]))
-            shape = (count // 2, routed, 2 * width)
-            dhkv.append(scatter_sum(near.reshape(shape), far.reshape(shape), order)[0])
-        else:
-            every = jnp.concatenate([near, far], axis=0)
-            dhkv.append(lax.psum_scatter(every, "ctx", scatter_dimension=0, tiled=True))
-    dhq, dhkv = (jnp.stack(dhq), jnp.stack(dhkv))
+        partial.append((near, far))
+    dhq = jnp.stack(dhq)
+    if direct:
+        shape = (count // 2, routed, 2 * width)
+        back = [tuple(part.reshape(shape) for part in both) for both in partial]
+        got, back, dlo = tied(got, back, dlo)
+        first = scatter_end(first, got)
+        got = scatter_start(first, orders, 1)
+        got_back = scatter_start(back, back_orders, 0)
+    else:
+        dhkv = jnp.stack(
+            [
+                lax.psum_scatter(jnp.concatenate(both, axis=0), "ctx", scatter_dimension=0, tiled=True)
+                for both in partial
+            ]
+        )
     dlq, dl_own, rim_low, rim_high = light_bwd(info, qkv, before, after, light_lse, dlo)
+    if direct:
+        got, got_back, dlq, dl_own, rim_low, rim_high = tied(got, got_back, dlq, dl_own, rim_low, rim_high)
+        first, back = (scatter_end(first, got), scatter_end(back, got_back))
+        got, got_back = (scatter_start(first, orders, 2), scatter_start(back, back_orders, 1))
     got_low = lax.ppermute(rim_high, "ctx", upward)
     got_high = lax.ppermute(rim_low, "ctx", downward)
+    if direct:
+        for stage in (2, 3):
+            first, back = (scatter_end(first, got), scatter_end(back, got_back))
+            if stage == 2:
+                got = scatter_start(first, orders, 3)
+            else:
+                values = [keep for keep, send in first]
+                got = gather_start(values, orders, 0)
+            got_back = scatter_start(back, back_orders, stage)
+            got, got_back, got_low, got_high = tied(got, got_back, got_low, got_high)
+        back = scatter_end(back, got_back)
+        dhkv = jnp.concatenate([keep for keep, send in back], axis=0)
+        values = gather_end(values, got)
+        got = gather_start(values, orders, 1)
     grad_tokens, dl, part_one = in_back(
         info, x, dy, dlq, dl_own, got_low, got_high, dhq, dhkv, dsq, rows, small, gate, hq_in, kin, h1k, l_own, l_got,
         h_own, h_got,
@@ -1203,23 +1273,55 @@
     vector = part_one + part_two
     if direct:
         att_got = lax.ppermute(att_send, "wsh", swap)
-        pieces = ((0, 4), (4, 3), (7, 3))
-        sums = [
-            reduced(info, order, [(att_own, att_got, first, size)])
-            for order, (first, size) in zip(orders, pieces)
-        ]
         half = width // 2
         mine = lax.dynamic_slice_in_dim(vector, side * half, half, 1)
         given = lax.dynamic_slice_in_dim(vector, (1 - side) * half, half, 1)
-        mine = mine + lax.ppermute(given, "wsh", swap)
-        vector = jnp.sum(lax.all_gather(mine, "ctx", axis=0), axis=0)
+        vector = mine + lax.ppermute(given, "wsh", swap)
+        got, att_got, vector = tied(got, att_got, vector)
+        values = gather_end(values, got)
+        got = gather_start(values, orders, 2)
+        pieces = ((0, 4), (4, 3), (7, 3))
+        second = [
+            fold(info, order, [(att_own, att_got, start, size)])
+            for order, (start, size) in zip(orders, pieces)
+        ]
+        got, second, vector = tied(got, second, vector)
+        values = gather_end(values, got)
+        got = gather_start(values, orders, 3)
+        got_two = scatter_start(second, orders, 0)
+        got_vector = flipped(vector, 1)
+        got_two, second, vector, got_vector = tied(got_two, second, vector, got_vector)
+        second, vector = (scatter_end(second, got_two), vector + got_vector)
+        got_two, got_vector = (scatter_start(second, orders, 1), flipped(vector, 2))
+        got, got_two, vector, got_vector = tied(got, got_two, vector, got_vector)
+        second, vector = (scatter_end(second, got_two), vector + got_vector)
+        chunks = list(zip(values, got))
+        got_two, got_vector = (scatter_start(second, orders, 2), flipped(vector, 4))
+        g_hdown = unpack_dn(info, orders[2], chunks[2], 0, 8, 8, 0, None)
+        got_two, got_vector, vector, g_hdown = tied(got_two, got_vector, vector, g_hdown)
+        second, vector = (scatter_end(second, got_two), vector + got_vector)
+        got_two, got_vector = (scatter_start(second, orders, 3), flipped(vector, 8))
+        part = unpack_gu(info, orders[0], chunks[0], 0, 8, 16, 0, None)
+        got_two, got_vector, vector, part = tied(got_two, got_vector, vector, part)
+        second, vector = (scatter_end(second, got_two), vector + got_vector)
+        values = [keep for keep, send in second]
+        got = gather_start(values, orders, 0)
+        g_hgu = unpack_gu(info, orders[1], chunks[1], 0, 8, 16, 8, part)
+        got, g_hgu = tied(got, g_hgu)
+        values = gather_end(values, got)
+        got = gather_start(values, orders, 1)
+        part = unpack_gu(info, orders[0], chunks[0], 8, 2, 4, 0, None)
+        got, part = tied(got, part)
+        values = gather_end(values, got)
+        got = gather_start(values, orders, 2)
+        g_lgu = unpack_gu(info, orders[1], chunks[1], 8, 2, 4, 2, part)
+        got, g_lgu = tied(got, g_lgu)
+        values = gather_end(values, got)
+        got = gather_start(values, orders, 3)
+        g_ldown = unpack_dn(info, orders[2], chunks[2], 8, 2, 2, 0, None)
+        got, g_ldown = tied(got, g_ldown)
+        sums = list(zip(values, got))
         g_lqkv, g_hqkv, g_hout, g_lout = unpack_attention(info, orders, sums, widths, inner)
-        first = unpack_gu(info, orders[0], chunks[0], 0, 8, 16, 0, None)
-        g_hgu = unpack_gu(info, orders[1], chunks[1], 0, 8, 16, 8, first)
-        first = unpack_gu(info, orders[0], chunks[0], 8, 2, 4, 0, None)
-        g_lgu = unpack_gu(info, orders[1], chunks[1], 8, 2, 4, 2, first)
-        g_hdown = unpack_dn(info, orders[2], chunks[2], 0, 8, 8, 0, None)
-        g_ldown = unpack_dn(info, orders[2], chunks[2], 8, 2, 2, 0, None)
     else:
         g_lqkv, g_hqkv, g_hout = plain_units(att_own, att_send, widths)
         last = slice(att_own.shape[0] - 1, att_own.shape[0])

time: 847 us -> 751 us (0.89)
  waiting for transfers between devices: 392 us -> 308 us
  blocking collectives: 43.7 us -> 4.58 us
  other arithmetic: 21.8 us -> 38.4 us
  starting transfers between devices: 91 us -> 99.7 us
    ppermute x64 -> x68, waiting for transfers between devices: 347 us -> 291 us  [flipped(): return lax.ppermute(value, 'ctx', [(i, i ^ bit) for i in range(size)])]
    all_gather x1 -> x0, blocking collectives: 41.3 us -> none  [per_device(): vector = jnp.sum(lax.all_gather(mine, 'ctx', axis=0), axis=0)]
    ppermute x3, waiting for transfers between devices: 41.9 us -> 3.73 us  [the longest x1 3.72 us: per_device(): vector = mine + lax.ppermute(given, 'wsh', swap)]
    concatenate x24 -> x25, other arithmetic: 5.74 us -> 17.2 us  [the longest x24 17.1 us: gather_end(): jnp.concatenate([value, g], axis=0)]
    ppermute x64 -> x68, starting transfers between devices: 80 us -> 87.4 us  [flipped(): return lax.ppermute(value, 'ctx', [(i, i ^ bit) for i in range(size)])]
    unnamed x147 -> x175, local copies, waits for them, and re-layouts: 13.9 us -> 20.6 us
    convert_element_type x32 -> x31, other arithmetic: 13.2 us -> 19.1 us  [the longest x14 17.9 us: scatter_step(): (keep[:half].astype(F32) + got[:half].astype(F32)).astype(BF)]
  transfers between devices with their start and end apart: 82 -> 86, of which waited for: 41 -> 36; matrix products, arithmetic and copies ran while one was open for 3% -> 5% of each run, Pallas kernels for 23% -> 24%
where the time goes in v2:
time: 751 us; the launch traced here: 745 us
  waiting for transfers between devices  308 us (41%)
  Pallas kernels  255 us (34%)
  starting transfers between devices  99.7 us (13%)
  other arithmetic  38.4 us (5%)
  local copies, waits for them, and re-layouts  24.8 us (3%)
  between operations  15.3 us (2%)
    ppermute x68, waiting for transfers between devices, flipped(): return lax.ppermute(value, 'ctx', [(i, i ^ bit) for i in range(size)])  291 us
    pallas_call x21, Pallas kernels, call(): pl.pallas_call(body, name=name or getattr(body, '__name__', 'kernel'), ou...  209 us
    ppermute x68, starting transfers between devices, flipped(): return lax.ppermute(value, 'ctx', [(i, i ^ bit) for i in range(size)])  87.4 us
    pallas_call x4, Pallas kernels, unpack_gu(): pl.pallas_call(body, out_shape=out, grid_spec=pltpu.PrefetchScalarGridSpe...  35.3 us
    unnamed x175, local copies, waits for them, and re-layouts  20.6 us
    convert_element_type x14, other arithmetic, scatter_step(): (keep[:half].astype(F32) + got[:half].astype(F32)).astype(BF)  17.9 us
    concatenate x24, other arithmetic, gather_end(): jnp.concatenate([value, g], axis=0)  17.1 us
  transfers between devices with their start and end apart: 86, of which 36 were waited for; matrix products, arithmetic and copies ran while one was open for 5% of the time, Pallas kernels for 24%

profile of v2, /device:TPU:0, one launch (start us, length us, event | category | flops | bytes accessed | tf_op | source)
XLA Modules:
  0.0 745.5 jit_solution(4342361358880666841)
XLA Ops:
  62.7 19.1 %collective-permute-done.5 = bf16[128,1664]{1,0:T(8,128)(2,1)S(1)} collective-permute-done((bf16[128,1664]{1,0:T(8,128)(2,1)S(1)}, bf16[128,1664]{1,0:T(8,128)(2,1)S(1)}, u32[]{:S(2)}, u32[]{:S(2)}) %collective-permute-start.5) | collective-permute-done | bytes 426016 | tf_op jit(solution)/shard_map/ppermute | solution.py:864
  91.0 15.1 %light_fwd_body.1 = (bf16[2,512,512]{2,1,0:T(8,128)(2,1)S(1)}, f32[2,512,128]{2,1,0:T(8,128)S(1)}) custom-call(s32[14]{0:T(128)S(1)} %concatenate.100.info, bf16[2,512,1536]{2,1,0:T(8,128)(2,1)S(1)} %copy-done.19, bf16[2,128,1024]{2,1,0:T(8,128)(2,1)S(1)} %copy-done.35, bf16[2,128,1024]{2,1,0:T(8,128)(2,1)S(1)} %copy-done.38), custom_call_target="tpu_custom_call" | custom-call | flops 4000000000 | bytes 6000000 | tf_op jit(solution)/shard_map/light_fwd_body/pallas_call | solution.py:74
  113.6 33.8 %collective-permute-done.12.kv_b = bf16[512,1664]{1,0:T(8,128)(2,1)S(1)} collective-permute-done((bf16[512,1664]{1,0:T(8,128)(2,1)S(1)}, bf16[512,1664]{1,0:T(8,128)(2,1)S(1)}, u32[]{:S(2)}, u32[]{:S(2)}) %collective-permute-start.12) | collective-permute-done | bytes 1703968 | tf_op jit(solution)/shard_map/ppermute | solution.py:864
  163.5 30.4 %ffn_body.3 = (f32[128,768]{1,0:T(8,128)S(1)}, f32[128,768]{1,0:T(8,128)S(1)}, bf16[16,768,256]{2,1,0:T(8,128)(2,1)}, bf16[16,768,256]{2,1,0:T(8,128)(2,1)}, bf1...) custom-call(s32[14]{0:T(128)S(1)} %concatenate.100.info, bf16[128,768]{1,0:T(8,128)(2,1)S(1)} %bitcast.52, ...), custom_call_target="tpu_custom_call" | custom-call | flops 7247757312 | bytes 38928384 | tf_op jit(solution)/shard_map/ffn_body/pallas_call | solution.py:74
  196.1 26.0 %ffn_body.2 = (f32[1024,768]{1,0:T(8,128)}, f32[1024,768]{1,0:T(8,128)}, bf16[4,768,256]{2,1,0:T(8,128)(2,1)S(1)}, bf16[4,768,256]{2,1,0:T(8,128)(2,1)S(1)}, bf1...) custom-call(s32[14]{0:T(128)S(1)} %concatenate.100.info, bf16[1024,768]{1,0:T(8,128)(2,1)} %bitcast.65, ...), custom_call_target="tpu_custom_call" | custom-call | flops 14495514624 | bytes 18874368 | tf_op jit(solution)/shard_map/ffn_body/pallas_call | solution.py:74
  228.3 8.0 %kernel.9 = (bf16[8,10,48,256]{3,2,1,0:T(8,128)(2,1)S(1)}, bf16[8,10,48,256]{3,2,1,0:T(8,128)(2,1)}) custom-call(s32[14]{0:T(128)S(1)} %concatenate.100.info, bf16[8,768,256]{2,1,0:T(8,128)(2,1)} %copy-done.5, bf16[8,768,256]{2,1,0:T(8,128)(2,1)} %copy-done.59, bf16[2,768,256]{2,1,0:T(8,128)(2,1)S(1)} %get-tuple-element.240.refs_2_, ...), custom_call_target="tpu_custom_call" | custom-call | bytes 11796480 | tf_op jit(solution)/shard_map/kernel/pallas_call | solution.py:74
  239.1 8.0 %kernel.8 = (bf16[8,10,48,256]{3,2,1,0:T(8,128)(2,1)S(1)}, bf16[8,10,48,256]{3,2,1,0:T(8,128)(2,1)}) custom-call(s32[14]{0:T(128)S(1)} %concatenate.100.info, bf16[16,768,256]{2,1,0:T(8,128)(2,1)} %get-tuple-element.231.refs_0_, bf16[16,768,256]{2,1,0:T(8,128)(2,1)} %collective-permute-done.13.refs_1_, bf16[4,768,256]{2,1,0:T(8,128)(2,1)S(1)} %get-tuple-element.233.refs_2_, ...), custom_call_target="tpu_custom_call" | custom-call | bytes 11796480 | tf_op jit(solution)/shard_map/kernel/pallas_call | solution.py:74
  247.6 8.0 %kernel.7 = (bf16[8,10,48,256]{3,2,1,0:T(8,128)(2,1)S(1)}, bf16[8,10,48,256]{3,2,1,0:T(8,128)(2,1)}) custom-call(s32[14]{0:T(128)S(1)} %concatenate.100.info, bf16[16,768,256]{2,1,0:T(8,128)(2,1)} %get-tuple-element.231.refs_0_, bf16[16,768,256]{2,1,0:T(8,128)(2,1)} %collective-permute-done.13.refs_1_, bf16[4,768,256]{2,1,0:T(8,128)(2,1)S(1)} %get-tuple-element.233.refs_2_, ...), custom_call_target="tpu_custom_call" | custom-call | bytes 11796480 | tf_op jit(solution)/shard_map/kernel/pallas_call | solution.py:74
  256.4 11.3 %mid_back_body.1 = (bf16[2,512,768]{2,1,0:T(8,128)(2,1)}, f32[2,512,768]{2,1,0:T(8,128)}, bf16[2,512,512]{2,1,0:T(8,128)(2,1)S(1)}, bf16[2,64,768]{2,1,0:T(8,128...) custom-call(s32[14]{0:T(128)S(1)} %concatenate.100.info, ...), custom_call_target="tpu_custom_call" | custom-call | flops 3000000000 | bytes 22000000 | tf_op jit(solution)/shard_map/mid_back_body/pallas_call | solution.py:74
  282.5 9.5 %collective-permute-done.16 = bf16[8,10,48,256]{3,2,1,0:T(8,128)(2,1)} collective-permute-done((bf16[8,10,48,256]{3,2,1,0:T(8,128)(2,1)}, bf16[8,10,48,256]{3,2,1,0:T(8,128)(2,1)}, u32[]{:S(2)}, u32[]{:S(2)}) %collective-permute-start.16) | collective-permute-done | bytes 1966112 | tf_op jit(solution)/shard_map/ppermute | solution.py:864
  292.0 8.2 %collective-permute-done.15 = bf16[8,10,48,256]{3,2,1,0:T(8,128)(2,1)} collective-permute-done((bf16[8,10,48,256]{3,2,1,0:T(8,128)(2,1)}, bf16[8,10,48,256]{3,2,1,0:T(8,128)(2,1)}, u32[]{:S(2)}, u32[]{:S(2)}) %collective-permute-start.15) | collective-permute-done | bytes 1966112 | tf_op jit(solution)/shard_map/ppermute | solution.py:864
  313.8 22.0 %light_bwd_body.1 = (bf16[2,512,512]{2,1,0:T(8,128)(2,1)S(1)}, f32[2,512,1024]{2,1,0:T(8,128)}, bf16[2,128,1024]{2,1,0:T(8,128)(2,1)S(1)}, bf16[2,128,1024]{2,1,0:T(8,128)(2,1)S(1)}) custom-call(s32[14]{0:T(128)S(1)} %concatenate.100.info, bf16[2,512,1536]{2,1,0:T(8,128)(2,1)} %light_in_body.1.qkv, bf16[2,128,1024]{2,1,0:T(8,128)(2,1)S(1)} %copy-done.36, ...), custom_call_target="tpu_custom_call" | custom-call | flops 10000000000 | bytes 14000000 | tf_op jit(solution)/shard_map/light_bwd_body/pallas_call | solution.py:74
  335.8 25.1 %collective-permute-done.20 = bf16[4,10,48,256]{3,2,1,0:T(8,128)(2,1)} collective-permute-done((bf16[4,10,48,256]{3,2,1,0:T(8,128)(2,1)}, bf16[4,10,48,256]{3,2,1,0:T(8,128)(2,1)}, u32[]{:S(2)}, u32[]{:S(2)}) %collective-permute-start.20) | collective-permute-done | bytes 983072 | tf_op jit(solution)/shard_map/ppermute | solution.py:864
  373.8 18.5 %collective-permute-done.29 = bf16[2,10,48,256]{3,2,1,0:T(8,128)(2,1)S(1)} collective-permute-done((bf16[2,10,48,256]{3,2,1,0:T(8,128)(2,1)S(1)}, bf16[2,10,48,256]{3,2,1,0:T(8,128)(2,1)S(1)}, u32[]{:S(2)}, u32[]{:S(2)}) %collective-permute-start.29) | collective-permute-done | bytes 491552 | tf_op jit(solution)/shard_map/ppermute | solution.py:864
  448.2 23.8 %collective-permute-done.41 = bf16[1,64,1536]{2,1,0:T(8,128)(2,1)S(1)} collective-permute-done((bf16[1,64,1536]{2,1,0:T(8,128)(2,1)S(1)}, bf16[1,64,1536]{2,1,0:T(8,128)(2,1)S(1)}, u32[]{:S(2)}, u32[]{:S(2)}) %collective-permute-start.41) | collective-permute-done | bytes 196640 | tf_op jit(solution)/shard_map/ppermute | solution.py:864
  472.1 19.9 %collective-permute-done.40 = bf16[1,64,1536]{2,1,0:T(8,128)(2,1)S(1)} collective-permute-done((bf16[1,64,1536]{2,1,0:T(8,128)(2,1)S(1)}, bf16[1,64,1536]{2,1,0:T(8,128)(2,1)S(1)}, u32[]{:S(2)}, u32[]{:S(2)}) %collective-permute-start.40) | collective-permute-done | bytes 196640 | tf_op jit(solution)/shard_map/ppermute | solution.py:864
  492.3 15.1 %in_back_body.1 = (bf16[2,512,768]{2,1,0:T(8,128)(2,1)}, bf16[2,512,1536]{2,1,0:T(8,128)(2,1)}, f32[8,768]{1,0:T(8,128)S(1)}) custom-call(s32[14]{0:T(128)S(1)} %concatenate.100.info, bf16[2,512,768]{2,1,0:T(8,128)(2,1)} %bitcast.46, f32[2,512,768]{2,1,0:T(8,128)} %get-tuple-element.230.dy, bf16[2,512,512]{2,1,0:T(8,128)(2,1)S(1)} %get-tuple-element.264.dq, ...), custom_call_target="tpu_custom_call" | custom-call | flops 4000000000 | bytes 22000000 | tf_op jit(solution)/shard_map/in_back_body/pallas_call | solution.py:74
  507.5 13.1 %grads_body.1 = (bf16[10,768,256]{2,1,0:T(8,128)(2,1)}, bf16[10,768,256]{2,1,0:T(8,128)(2,1)}) custom-call(s32[14]{0:T(128)S(1)} %concatenate.100.info, bf16[2,512,768]{2,1,0:T(8,128)(2,1)S(1)} %bitcast.49, bf16[8,768]{1,0:T(8,128)(2,1)S(1)} %pad_maximum_fusion.27.small, bf16[2,512,1536]{2,1,0:T(8,128)(2,1)} %get-tuple-element.295.dl, ...), custom_call_target="tpu_custom_call" | custom-call | flops 3303014400 | bytes 20000000 | tf_op jit(solution)/shard_map/grads_body/pallas_call | solution.py:74
  551.3 10.5 %collective-permute-done.49 = bf16[4,10,48,256]{3,2,1,0:T(8,128)(2,1)} collective-permute-done((bf16[4,10,48,256]{3,2,1,0:T(8,128)(2,1)S(1)}, bf16[4,10,48,256]{3,2,1,0:T(8,128)(2,1)}, u32[]{:S(2)}, u32[]{:S(2)}) %collective-permute-start.49) | collective-permute-done | bytes 983072 | tf_op jit(solution)/shard_map/ppermute | solution.py:864
  571.1 41.2 %collective-permute-done.53 = f32[8,384]{1,0:T(8,128)S(1)} collective-permute-done((f32[8,384]{1,0:T(8,128)S(1)}, f32[8,384]{1,0:T(8,128)S(1)}, u32[]{:S(2)}, u32[]{:S(2)}) %collective-permute-start.53) | collective-permute-done | bytes 12320 | tf_op jit(solution)/shard_map/ppermute | solution.py:864
  613.7 9.9 %collective-permute-done.52 = bf16[8,3,48,256]{3,2,1,0:T(8,128)(2,1)S(1)} collective-permute-done((bf16[8,3,48,256]{3,2,1,0:T(8,128)(2,1)S(1)}, bf16[8,3,48,256]{3,2,1,0:T(8,128)(2,1)S(1)}, u32[]{:S(2)}, u32[]{:S(2)}) %collective-permute-start.52) | collective-permute-done | bytes 589856 | tf_op jit(solution)/shard_map/ppermute | solution.py:864
  664.9 13.3 %shard_map.248.unused = f32[384,8192]{1,0:T(8,128)} custom-call(s32[14]{0:T(128)} %copy-done.26, bf16[8,10,48,256]{3,2,1,0:T(8,128)(2,1)} %copy-done.49, bf16[8,10,48,256]{3,2,1,0:T(8,128)(2,1)} %copy-done.52), custom_call_target="tpu_custom_call" | custom-call | bytes 9437184 | tf_op jit(solution)/shard_map/pallas_call | solution.py:963
  681.6 13.2 %shard_map.249 = f32[384,8192]{1,0:T(8,128)} custom-call(s32[14]{0:T(128)} %copy-done.26, bf16[8,10,48,256]{3,2,1,0:T(8,128)(2,1)} %copy-done.50, bf16[8,10,48,256]{3,2,1,0:T(8,128)(2,1)} %copy-done.53, f32[384,8192]{1,0:T(8,128)} %shard_map.248.unused), custom_call_target="tpu_custom_call", output_to_operand_aliasing={{}: (3, {})} | custom-call | bytes 9437184 | tf_op jit(solution)/shard_map/pallas_call | solution.py:963
  730.5 8.3 %kernel.13 = (f32[384,1536]{1,0:T(8,128)}, f32[384,2304]{1,0:T(8,128)}, f32[384,768]{1,0:T(8,128)}, f32[256,768]{1,0:T(8,128)}) custom-call(s32[14]{0:T(128)S(1)} %copy-done.27, bf16[8,4,48,256]{3,2,1,0:T(8,128)(2,1)S(1)} %pad_maximum_fusion.10.refs_0_, bf16[8,4,48,256]{3,2,1,0:T(8,128)(2,1)S(1)} %collective-permute-done.78.refs_1_, ...), custom_call_target="tpu_custom_call" | custom-call | bytes 14000000 | tf_op jit(solution)/shard_map/kernel/pallas_call | solution.py:74
  (438 shorter events, 318.9 us)
Async XLA Ops:
  7.9 100.0 %all-gather.10.cloned.1.call-start = ((), (), s32[]{:S(2)}) async-start(), calls=%async_computation.2 | async-start | bytes 9437184 | tf_op jit(solution)/shard_map/all_gather | solution.py:1139
  8.7 99.3 %all-gather.8.cloned.1.call-start = ((), (), s32[]{:S(2)}) async-start(), calls=%async_computation.1 | async-start | bytes 18874368 | tf_op jit(solution)/shard_map/all_gather | solution.py:1139
  9.5 146.0 %all-gather.14.cloned.1.call-start = ((), (), s32[]{:S(2)}) async-start(), calls=%async_computation.4 | async-start | bytes 2359296 | tf_op jit(solution)/shard_map/all_gather | solution.py:1139
  11.9 143.6 %all-gather.12.cloned.1.call-start = ((), (), s32[]{:S(2)}) async-start(), calls=%async_computation.3 | async-start | bytes 4718592 | tf_op jit(solution)/shard_map/all_gather | solution.py:1139
  109.6 37.8 %collective-permute-start.12 = (bf16[512,1664]{1,0:T(8,128)(2,1)S(1)}, bf16[512,1664]{1,0:T(8,128)(2,1)S(1)}, u32[]{:S(2)}, u32[]{:S(2)}) collective-permute-start(bf16[512,1664]{1,0:T(8,128)(2,1)S(1)} %pad_maximum_fusion.4.kv_a), channel_id=1, source_target_pairs={{0,4},{2,6},{4,0},{6,2},{8,12},{10,14},{12,8},{14,10},{16,20},{18,... | collective-permute-start | bytes 5111816 | tf_op jit(solution)/shard_map/ppermute | solution.py:864
  111.9 38.9 %collective-permute-start.11 = (bf16[512,1664]{1,0:T(8,128)(2,1)S(1)}, bf16[512,1664]{1,0:T(8,128)(2,1)S(1)}, u32[]{:S(2)}, u32[]{:S(2)}) collective-permute-start(bf16[512,1664]{1,0:T(8,128)(2,1)S(1)} %pad_maximum_fusion.3.kv_a), channel_id=1, source_target_pairs={{0,2},{2,0},{4,6},{6,4},{8,10},{10,8},{12,14},{14,12},{16,18},{18,... | collective-permute-start | bytes 5111816 | tf_op jit(solution)/shard_map/ppermute | solution.py:864
  195.5 43.6 %collective-permute-start.13 = (bf16[16,768,256]{2,1,0:T(8,128)(2,1)}, bf16[16,768,256]{2,1,0:T(8,128)(2,1)}, u32[]{:S(2)}, u32[]{:S(2)}) collective-permute-start(bf16[16,768,256]{2,1,0:T(8,128)(2,1)} %get-tuple-element.232), channel_id=1, source_target_pairs={{0,1},{1,0},{2,3},{3,2},{4,5},{5,4},{6,7},{7,6},{8,9},{9,8},{10,11... | collective-permute-start | bytes 18874376 | tf_op jit(solution)/shard_map/ppermute | solution.py:1209
  236.3 46.2 %collective-permute-start.19 = (bf16[8,10,48,256]{3,2,1,0:T(8,128)(2,1)}, bf16[8,10,48,256]{3,2,1,0:T(8,128)(2,1)}, u32[]{:S(2)}, u32[]{:S(2)}) collective-permute-start(bf16[8,10,48,256]{3,2,1,0:T(8,128)(2,1)} %get-tuple-element.242), channel_id=1, source_target_pairs={{0,8},{2,10},{4,12},{6,14},{8,0},{10,2},{12,4},{14,6},{16,24},{18,... | collective-permute-start | bytes 5898248 | tf_op jit(solution)/shard_map/ppermute | solution.py:864
  247.1 44.9 %collective-permute-start.16 = (bf16[8,10,48,256]{3,2,1,0:T(8,128)(2,1)}, bf16[8,10,48,256]{3,2,1,0:T(8,128)(2,1)}, u32[]{:S(2)}, u32[]{:S(2)}) collective-permute-start(bf16[8,10,48,256]{3,2,1,0:T(8,128)(2,1)} %get-tuple-element.237), channel_id=1, source_target_pairs={{0,4},{2,6},{4,0},{6,2},{8,12},{10,14},{12,8},{14,10},{16,20},{18,... | collective-permute-start | bytes 5898248 | tf_op jit(solution)/shard_map/ppermute | solution.py:864
  255.6 44.6 %collective-permute-start.15 = (bf16[8,10,48,256]{3,2,1,0:T(8,128)(2,1)}, bf16[8,10,48,256]{3,2,1,0:T(8,128)(2,1)}, u32[]{:S(2)}, u32[]{:S(2)}) collective-permute-start(bf16[8,10,48,256]{3,2,1,0:T(8,128)(2,1)} %get-tuple-element.236), channel_id=1, source_target_pairs={{0,2},{2,0},{4,6},{6,4},{8,10},{10,8},{12,14},{14,12},{16,18},{18,... | collective-permute-start | bytes 5898248 | tf_op jit(solution)/shard_map/ppermute | solution.py:864
  304.1 56.8 %collective-permute-start.23 = (bf16[8,64,1536]{2,1,0:T(8,128)(2,1)S(1)}, bf16[8,64,1536]{2,1,0:T(8,128)(2,1)}, u32[]{:S(2)}, u32[]{:S(2)}) collective-permute-start(bf16[8,64,1536]{2,1,0:T(8,128)(2,1)S(1)} %bitcast.64), channel_id=1, source_target_pairs={{0,2},{2,0},{4,6},{6,4},{8,10},{10,8},{12,14},{14,12},{16,18},{18,... | collective-permute-start | bytes 4718600 | tf_op jit(solution)/shard_map/ppermute | solution.py:864
  305.3 55.6 %collective-permute-start.24 = (bf16[8,64,1536]{2,1,0:T(8,128)(2,1)S(1)}, bf16[8,64,1536]{2,1,0:T(8,128)(2,1)}, u32[]{:S(2)}, u32[]{:S(2)}) collective-permute-start(bf16[8,64,1536]{2,1,0:T(8,128)(2,1)S(1)} %bitcast.63), channel_id=1, source_target_pairs={{0,4},{2,6},{4,0},{6,2},{8,12},{10,14},{12,8},{14,10},{16,20},{18,... | collective-permute-start | bytes 4718600 | tf_op jit(solution)/shard_map/ppermute | solution.py:864
  313.3 47.6 %collective-permute-start.20 = (bf16[4,10,48,256]{3,2,1,0:T(8,128)(2,1)}, bf16[4,10,48,256]{3,2,1,0:T(8,128)(2,1)}, u32[]{:S(2)}, u32[]{:S(2)}) collective-permute-start(bf16[4,10,48,256]{3,2,1,0:T(8,128)(2,1)} %get-tuple-element.387), channel_id=1, source_target_pairs={{0,4},{2,6},{4,0},{6,2},{8,12},{10,14},{12,8},{14,10},{16,20},{18,... | collective-permute-start | bytes 2949128 | tf_op jit(solution)/shard_map/ppermute | solution.py:864
  365.4 38.0 %collective-permute-start.31 = (bf16[4,64,1536]{2,1,0:T(8,128)(2,1)S(1)}, bf16[4,64,1536]{2,1,0:T(8,128)(2,1)S(1)}, u32[]{:S(2)}, u32[]{:S(2)}) collective-permute-start(bf16[4,64,1536]{2,1,0:T(8,128)(2,1)S(1)} %get-tuple-element.391), channel_id=1, source_target_pairs={{0,4},{2,6},{4,0},{6,2},{8,12},{10,14},{12,8},{14,10},{16,20},{18,... | collective-permute-start | bytes 2359304 | tf_op jit(solution)/shard_map/ppermute | solution.py:864
  404.3 37.3 %collective-permute-start.32 = (bf16[2,64,1536]{2,1,0:T(8,128)(2,1)S(1)}, bf16[2,64,1536]{2,1,0:T(8,128)(2,1)S(1)}, u32[]{:S(2)}, u32[]{:S(2)}) collective-permute-start(bf16[2,64,1536]{2,1,0:T(8,128)(2,1)S(1)} %get-tuple-element.405), channel_id=1, source_target_pairs={{0,8},{2,10},{4,12},{6,14},{8,0},{10,2},{12,4},{14,6},{16,24},{18,... | collective-permute-start | bytes 1179656 | tf_op jit(solution)/shard_map/ppermute | solution.py:864
  441.8 50.2 %collective-permute-start.39 = (bf16[1,10,48,256]{3,2,1,0:T(8,128)(2,1)S(1)}, bf16[1,10,48,256]{3,2,1,0:T(8,128)(2,1)S(1)}, u32[]{:S(2)}, u32[]{:S(2)}) collective-permute-start(bf16[1,10,48,256]{3,2,1,0:T(8,128)(2,1)S(1)} %add_convert_fusion.26), channel_id=1, source_target_pairs={{0,16},{2,18},{4,20},{6,22},{8,24},{10,26},{12,28},{14,30},{16,0},... | collective-permute-start | bytes 737288 | tf_op jit(solution)/shard_map/ppermute | solution.py:864
  444.9 47.1 %collective-permute-start.38 = (bf16[1,10,48,256]{3,2,1,0:T(8,128)(2,1)S(1)}, bf16[1,10,48,256]{3,2,1,0:T(8,128)(2,1)S(1)}, u32[]{:S(2)}, u32[]{:S(2)}) collective-permute-start(bf16[1,10,48,256]{3,2,1,0:T(8,128)(2,1)S(1)} %add_convert_fusion.28), channel_id=1, source_target_pairs={{0,16},{2,18},{4,20},{6,22},{8,24},{10,26},{12,28},{14,30},{16,0},... | collective-permute-start | bytes 737288 | tf_op jit(solution)/shard_map/ppermute | solution.py:864
  445.1 46.9 %collective-permute-start.37 = (bf16[1,10,48,256]{3,2,1,0:T(8,128)(2,1)S(1)}, bf16[1,10,48,256]{3,2,1,0:T(8,128)(2,1)S(1)}, u32[]{:S(2)}, u32[]{:S(2)}) collective-permute-start(bf16[1,10,48,256]{3,2,1,0:T(8,128)(2,1)S(1)} %add_convert_fusion.30), channel_id=1, source_target_pairs={{0,16},{2,18},{4,20},{6,22},{8,24},{10,26},{12,28},{14,30},{16,0},... | collective-permute-start | bytes 737288 | tf_op jit(solution)/shard_map/ppermute | solution.py:864
  448.1 43.9 %collective-permute-start.40 = (bf16[1,64,1536]{2,1,0:T(8,128)(2,1)S(1)}, bf16[1,64,1536]{2,1,0:T(8,128)(2,1)S(1)}, u32[]{:S(2)}, u32[]{:S(2)}) collective-permute-start(bf16[1,64,1536]{2,1,0:T(8,128)(2,1)S(1)} %add_convert_fusion.42), channel_id=1, source_target_pairs={{0,16},{2,18},{4,20},{6,22},{8,24},{10,26},{12,28},{14,30},{16,0},... | collective-permute-start | bytes 589832 | tf_op jit(solution)/shard_map/ppermute | solution.py:864
  563.4 49.5 %collective-permute-start.51 = (bf16[8,3,48,256]{3,2,1,0:T(8,128)(2,1)S(1)}, bf16[8,3,48,256]{3,2,1,0:T(8,128)(2,1)S(1)}, u32[]{:S(2)}, u32[]{:S(2)}) collective-permute-start(bf16[8,3,48,256]{3,2,1,0:T(8,128)(2,1)S(1)} %get-tuple-element.313), channel_id=1, source_target_pairs={{0,4},{2,6},{4,0},{6,2},{8,12},{10,14},{12,8},{14,10},{16,20},{18,... | collective-permute-start | bytes 1769480 | tf_op jit(solution)/shard_map/ppermute | solution.py:864
  566.4 78.1 %collective-permute-start.56 = (bf16[8,10,48,256]{3,2,1,0:T(8,128)(2,1)S(1)}, bf16[8,10,48,256]{3,2,1,0:T(8,128)(2,1)S(1)}, u32[]{:S(2)}, u32[]{:S(2)}) collective-permute-start(bf16[8,10,48,256]{3,2,1,0:T(8,128)(2,1)S(1)} %pad_maximum_fusion.2.near), channel_id=1, source_target_pairs={{0,8},{2,10},{4,12},{6,14},{8,0},{10,2},{12,4},{14,6},{16,24},{18,... | collective-permute-start | bytes 5898248 | tf_op jit(solution)/shard_map/ppermute | solution.py:864
  568.1 76.4 %collective-permute-start.55 = (bf16[8,10,48,256]{3,2,1,0:T(8,128)(2,1)S(1)}, bf16[8,10,48,256]{3,2,1,0:T(8,128)(2,1)S(1)}, u32[]{:S(2)}, u32[]{:S(2)}) collective-permute-start(bf16[8,10,48,256]{3,2,1,0:T(8,128)(2,1)S(1)} %pad_maximum_fusion.1.near), channel_id=1, source_target_pairs={{0,4},{2,6},{4,0},{6,2},{8,12},{10,14},{12,8},{14,10},{16,20},{18,... | collective-permute-start | bytes 5898248 | tf_op jit(solution)/shard_map/ppermute | solution.py:864
  569.0 75.5 %collective-permute-start.54 = (bf16[8,10,48,256]{3,2,1,0:T(8,128)(2,1)S(1)}, bf16[8,10,48,256]{3,2,1,0:T(8,128)(2,1)S(1)}, u32[]{:S(2)}, u32[]{:S(2)}) collective-permute-start(bf16[8,10,48,256]{3,2,1,0:T(8,128)(2,1)S(1)} %pad_maximum_fusion.near), channel_id=1, source_target_pairs={{0,2},{2,0},{4,6},{6,4},{8,10},{10,8},{12,14},{14,12},{16,18},{18,... | collective-permute-start | bytes 5898248 | tf_op jit(solution)/shard_map/ppermute | solution.py:864
  569.7 42.6 %collective-permute-start.53 = (f32[8,384]{1,0:T(8,128)S(1)}, f32[8,384]{1,0:T(8,128)S(1)}, u32[]{:S(2)}, u32[]{:S(2)}) collective-permute-start(f32[8,384]{1,0:T(8,128)S(1)} %dynamic-slice_add_fusion), channel_id=1, source_target_pairs={{0,2},{2,0},{4,6},{6,4},{8,10},{10,8},{12,14},{14,12},{16,18},{18,... | collective-permute-start | bytes 36872 | tf_op jit(solution)/shard_map/ppermute | solution.py:864
  (149 other events, 2693.9 us)
Sparse Core Ops, SparseCore 0:
  9.6 11.9 all-gather.5
  23.1 17.9 all-gather.9
  42.6 26.0 all-gather.7
  70.1 10.9 all-gather.13
  89.0 13.3 all-gather.11

commit v3 on v2

--- a/solution.py
+++ b/solution.py
@@ -101,7 +101,7 @@
     return jax.ShapeDtypeStruct(tuple(shape), dtype)
 
 
-def routed_body(info, x, cols, small, w_own, w_got, q_out, kv_out, hq_out, kin_out, h1k_out, gate_out):
+def routed_body(info, x, cols, small, w_own, w_got, q_out, kin_out, hq_out, h1k_out, gate_out):
     micros, tok, width = x.shape
     rows = cols.shape[2]
     base = info[1]
@@ -124,20 +124,17 @@
     )
     kin = (h1k * gate_k).astype(BF)
     own_q, other_q = halves(info, low_q)
-    own_k, other_k = halves(info, kin)
-    query = mm(own_q, w_own[:, :width]) + mm(other_q, w_got[:, :width])
-    pair = mm(own_k, w_own[:, width:]) + mm(other_k, w_got[:, width:])
+    query = mm(own_q, w_own[...]) + mm(other_q, w_got[...])
     lane = iota((rows, LANES), 1)
     for m in range(micros):
         part = slice(m * rows, (m + 1) * rows)
         q_out[m, :, :width] = query[part].astype(BF)
-        kv_out[m, :, : 2 * width] = pair[part].astype(BF)
+        kin_out[m, :, :width] = kin[part]
         seg_q = segment(info, m, cols[0, m])
         seg_k = segment(info, m, cols[1, m])
         q_out[m, :, width:] = (lane == seg_q).astype(F32).astype(BF)
-        kv_out[m, :, 2 * width :] = jnp.where((lane < 8) & (lane != seg_k), FAR, 0.0).astype(BF)
+        kin_out[m, :, width:] = jnp.where((lane < 8) & (lane != seg_k), FAR, 0.0).astype(BF)
         hq_out[m] = low_q[part]
-        kin_out[m] = kin[part]
         h1k_out[m] = h1k[part]
         gate_out[m] = jnp.where(lane == 0, gate_q[part], gate_k[part])
 
@@ -147,8 +144,7 @@
     rows = cols.shape[2]
     shapes = [
         sds((micros, rows, width + LANES), BF),
-        sds((micros, rows, 2 * width + LANES), BF),
-        sds((micros, rows, width), BF),
+        sds((micros, rows, width + LANES), BF),
         sds((micros, rows, width), BF),
         sds((micros, rows, width), F32),
         sds((micros, rows, LANES), F32),
@@ -158,11 +154,11 @@
         routed_body,
         shapes,
         (1,),
-        [whole(a.shape) for a in args[1:]],
+        [whole(a.shape) for a in args[1:4]] + [whole((w_own.shape[0], width))] * 2,
         [whole(s.shape) for s in shapes],
         args,
-        flops=2 * micros * rows * width * 3 * width,
-        moved=9_000_000,
+        flops=2 * micros * rows * width * width,
+        moved=5_000_000,
     )
 
 
@@ -342,17 +338,40 @@
     )
 
 
+def key_body(info, kin, w_own, w_got, out):
+    half = w_own.shape[0]
+    width = 2 * half
+    own = kin[:, pl.ds(pl.multiple_of(info[0] * half, half), half)]
+    other = kin[:, pl.ds(pl.multiple_of((1 - info[0]) * half, half), half)]
+    out[...] = (mm(own, w_own[:, width:]) + mm(other, w_got[:, width:])).astype(BF)
+
+
+def key_project(info, kin, w_own, w_got):
+    shape = sds((kin.shape[0], 2 * (kin.shape[1] - LANES)), BF)
+    args = (info, kin, w_own, w_got)
+    return call(
+        key_body,
+        shape,
+        (1,),
+        [whole(a.shape) for a in args[1:]],
+        whole(shape.shape),
+        args,
+        flops=1_200_000_000,
+        moved=6_000_000,
+    )
+
+
 def heavy_scores(query, parts, bias, cut):
     return [mm_t(query, part[:, cut]) + b for part, b in zip(parts, bias)]
 
 
-def heavy_fwd_body(info, q, kv_a, kv_b, out, lse_out):
+def heavy_fwd_body(info, q, kin_a, kin_b, kv_a, kv_b, out, lse_out):
     rows, width = out.shape
     parts = (kv_a, kv_b)
     low_lane = iota((rows, LANES), 1) < HD
     lane = iota((rows, LANES), 1)
     feature = jnp.concatenate([q[:, width:]] * 2, axis=0)
-    bias = [mm_t(feature, part[:, 2 * width :]) for part in parts]
+    bias = [mm_t(feature, kin[:, width:]) for kin in (kin_a, kin_b)]
     stats = jnp.zeros((rows, LANES), F32)
     for pair in range(width // LANES):
         cut = slice(pair * LANES, (pair + 1) * LANES)
@@ -375,11 +394,11 @@
     lse_out[...] = stats
 
 
-def heavy_fwd(info, q, kv_a, kv_b):
+def heavy_fwd(info, q, kins, kvs):
     rows = q.shape[0]
     width = q.shape[1] - LANES
     shapes = [sds((rows, width), BF), sds((rows, LANES), F32)]
-    args = (info, q, kv_a, kv_b)
+    args = (info, q, *kins, *kvs)
     return call(
         heavy_fwd_body,
         shapes,
@@ -388,16 +407,16 @@
         [whole(s.shape) for s in shapes],
         args,
         flops=1_500_000_000,
-        moved=4_000_000,
-    )
-
-
-def heavy_bwd_body(info, q, kv_a, kv_b, lse, grad, dq_out, da_out, db_out):
+        moved=5_000_000,
+    )
+
+
+def heavy_bwd_body(info, q, kin_a, kin_b, kv_a, kv_b, lse, grad, w_own, w_got, dq_out, da_out, db_out, ia_out, ib_out):
     rows, width = grad.shape
     parts = (kv_a, kv_b)
     low_lane = iota((rows, LANES), 1) < HD
     feature = jnp.concatenate([q[:, width:]] * 2, axis=0)
-    bias = [mm_t(feature, part[:, 2 * width :]) for part in parts]
+    bias = [mm_t(feature, kin[:, width:]) for kin in (kin_a, kin_b)]
     for pair in range(width // LANES):
         cut = slice(pair * LANES, (pair + 1) * LANES)
         upcut = slice(width + pair * LANES, width + (pair + 1) * LANES)
@@ -415,13 +434,20 @@
         for target, slope, prob in zip((da_out, db_out), slopes, probs):
             target[:, cut] = t_mm(slope, query).astype(BF)
             target[:, upcut] = t_mm(prob.astype(BF), upper).astype(BF)
-
-
-def heavy_bwd(info, q, kv_a, kv_b, lse, grad):
+    half = width // 2
+    for target, source in ((ia_out, da_out), (ib_out, db_out)):
+        for weight, side in ((w_own, info[0]), (w_got, 1 - info[0])):
+            target[:, pl.ds(pl.multiple_of(side * half, half), half)] = mm_t(
+                source[...], weight[:, width:]
+            ).astype(BF)
+
+
+def heavy_bwd(info, q, kins, kvs, lse, grad, w_own, w_got):
     rows = q.shape[0]
     width = q.shape[1] - LANES
-    shapes = [sds((rows, width), BF)] + [sds((kv.shape[0], 2 * width), BF) for kv in (kv_a, kv_b)]
-    args = (info, q, kv_a, kv_b, lse, grad)
+    keys = kvs[0].shape[0]
+    shapes = [sds((rows, width), BF)] + [sds((keys, 2 * width), BF)] * 2 + [sds((keys, width), BF)] * 2
+    args = (info, q, *kins, *kvs, lse, grad, w_own, w_got)
     return call(
         heavy_bwd_body,
         shapes,
@@ -429,12 +455,57 @@
         [whole(a.shape) for a in args[1:]],
         [whole(s.shape) for s in shapes],
         args,
-        flops=4_000_000_000,
-        moved=8_000_000,
-    )
-
-
-def middle_body(info, x, up, cols, rows, small, gate, lo, lout, ho, hout, y_out, low_out, ffr_out, dzh_out, hy_out, gf_out):
+        flops=6_500_000_000,
+        moved=15_000_000,
+    )
+
+
+def heavy_grads_body(info, *refs):
+    micros = (len(refs) - 8) // 4
+    hq, dhq, ho, dhy, lo, dy = refs[:6]
+    kins, dkvs = (refs[6 : 6 + 2 * micros], refs[6 + 2 * micros : -2])
+    other_out, own_out = (refs[-1], refs[-2])
+    half = hq.shape[2] // 2
+    every = range(micros)
+    for target, side in ((other_out, 1 - info[0]), (own_out, info[0])):
+        cut = pl.ds(pl.multiple_of(side * half, half), half)
+
+        def put(unit, left, right, columns):
+            for block in range(columns // COLS):
+                at = unit + block
+                total = sum(
+                    t_mm(a, b[:, block * COLS : (block + 1) * COLS]) for a, b in zip(left, right)
+                )
+                target[at // 2, (at % 2) * half : (at % 2 + 1) * half] = total.astype(BF)
+            return unit + columns // COLS
+
+        unit = put(0, [hq[m, :, cut] for m in every], [dhq[m] for m in every], dhq.shape[2])
+        unit = put(unit, [kin[:, cut] for kin in kins], dkvs, dkvs[0].shape[1])
+        unit = put(unit, [ho[m, :, cut] for m in every], [dhy[m] for m in every], dhy.shape[2])
+        part = lo.shape[2] // 2
+        small_cut = pl.ds(pl.multiple_of(side * part, part), part)
+        total = sum(t_mm(lo[m, :, small_cut], dy[m].astype(BF)) for m in every)
+        pack_rows(target.at[pl.ds(unit // 2, 1)], total)
+
+
+def heavy_grads(info, hq, dhq, ho, dhy, lo, dy, kins, dkvs):
+    width = hq.shape[2]
+    units = (dhq.shape[2] + dkvs[0].shape[1] + dhy.shape[2]) // COLS
+    shapes = [sds((units // 2 + 1, width, COLS), BF)] * 2
+    args = (info, hq, dhq, ho, dhy, lo, dy, *kins, *dkvs)
+    return call(
+        heavy_grads_body,
+        shapes,
+        (1,),
+        [whole(a.shape) for a in args[1:]],
+        [whole(s.shape) for s in shapes],
+        args,
+        flops=6_500_000_000,
+        moved=28_000_000,
+    )
+
+
+def middle_body(info, x, up, cols, rows, small, gate, lo, lout, ho, hout, y_out, low_out, pay_out, hy_out, gf_out):
     tok = x.shape[1]
     base = info[1]
     hy = mm(ho[0], hout[...])
@@ -446,9 +517,10 @@
     low_out[0] = low
     take = onehot_cols(cols[2, 0], base, tok)
     taken = mm(take, low)
-    ffr_out[0] = taken.astype(BF)
+    width = x.shape[2]
+    pay_out[0, :, :width] = taken.astype(BF)
     gf = jax.nn.sigmoid(jnp.sum(taken * small[2:3].astype(F32), axis=-1, keepdims=True))
-    dzh_out[0] = (mm(take, up[0]) * gf).astype(BF)
+    pay_out[0, :, width:] = (mm(take, up[0]) * gf).astype(BF)
     gf_out[0] = jnp.broadcast_to(gf, gf_out.shape[1:])
 
 
@@ -465,8 +537,7 @@
     shapes = [
         sds((micros, tok, width), F32),
         sds((micros, tok, width), BF),
-        sds((micros, count, width), BF),
-        sds((micros, count, width), BF),
+        sds((micros, count, 2 * width), BF),
         sds((micros, count, width), F32),
         sds((micros, count, LANES), F32),
     ]
@@ -505,36 +576,50 @@
             ].astype(BF)
 
 
+def gelu_parts(g):
+    root = (2.0 / 3.141592653589793) ** 0.5
+    square = g * g
+    tanh = jnp.tanh(root * g * (1.0 + 0.044715 * square))
+    bell = 0.5 * (1.0 + tanh)
+    slope = bell + 0.5 * g * (1.0 - tanh * tanh) * (root * (1.0 + 3 * 0.044715 * square))
+    return (g * bell, slope)
+
+
+def hidden_both_ways(low, upstream, wg, wu, wd):
+    g, u = (mm(low, wg), mm(low, wu))
+    back = mm_t(upstream, wd)
+    gelu, slope = gelu_parts(g)
+    return ((gelu * u).astype(BF), (back * u * slope).astype(BF), (back * gelu).astype(BF))
+
+
+def add_steps(step, pairs):
+    @pl.when(step == 0)
+    def first():
+        for target, value in pairs:
+            target[...] = value
+
+    @pl.when(step > 0)
+    def later():
+        for target, value in pairs:
+            target[...] += value
+
+
+def ffn_local_body(info, a, ct, wg, wu, wd, z_out, dh_out):
+    hidden, dg, du = hidden_both_ways(a[...], ct[...], wg[...], wu[...], wd[...])
+    z = mm(hidden, wd[...])
+    dh = mm_t(dg, wg[...]) + mm_t(du, wu[...])
+    add_steps(pl.program_id(0), [(z_out, z), (dh_out, dh)])
+
+
 def ffn_body(info, a, ct, wg, wu, wd, z_out, dh_out, own_gu, other_gu, own_dn, other_dn):
     step = pl.program_id(0)
     half = pl.num_programs(0) // 2
     width = a.shape[1] // 2
-    low, upstream = (a[...], ct[...])
-    g, u = (mm(low, wg[...]), mm(low, wu[...]))
-    back = mm_t(upstream, wd[...])
-    root = (2.0 / 3.141592653589793) ** 0.5
-    square = g * g
-    tanh = jnp.tanh(root * g * (1.0 + 0.044715 * square))
-    bell = 0.5 * (1.0 + tanh)
-    gelu = g * bell
-    hidden = (gelu * u).astype(BF)
-    slope = bell + 0.5 * g * (1.0 - tanh * tanh) * (root * (1.0 + 3 * 0.044715 * square))
-    dg = (back * u * slope).astype(BF)
-    du = (back * gelu).astype(BF)
+    hidden, dg, du = hidden_both_ways(a[...], ct[...], wg[...], wu[...], wd[...])
     z = mm(hidden, wd[...])
     dh = mm_t(dg, wg[...]) + mm_t(du, wu[...])
-
-    @pl.when(step == 0)
-    def first():
-        z_out[...] = z
-        dh_out[...] = dh
-
-    @pl.when(step > 0)
-    def later():
-        z_out[...] += z
-        dh_out[...] += dh
-
-    down = t_mm(hidden, upstream)
+    add_steps(step, [(z_out, z), (dh_out, dh)])
+    down = t_mm(hidden, ct[...])
 
     @pl.when(step < half)
     def send():
@@ -550,6 +635,28 @@
     own_gu[0, width:] = t_mm(own, du).astype(BF)
     other_gu[0, :width] = t_mm(other, dg).astype(BF)
     other_gu[0, width:] = t_mm(other, du).astype(BF)
+
+
+def ffn_local(info, pay, w_gu, w_down, block):
+    rows = pay.shape[0]
+    hidden, width = w_down.shape
+    steps = hidden // block
+    return call(
+        ffn_local_body,
+        [sds((rows, width), F32)] * 2,
+        (steps,),
+        [
+            pl.BlockSpec((rows, width), lambda i, *u: (0, 0)),
+            pl.BlockSpec((rows, width), lambda i, *u: (0, 1)),
+            pl.BlockSpec((width, block), lambda i, *u: (0, i)),
+            pl.BlockSpec((width, block), lambda i, *u: (0, steps + i)),
+            pl.BlockSpec((block, width), lambda i, *u: (i, 0)),
+        ],
+        [whole((rows, width))] * 2,
+        (info, pay, pay, w_gu, w_gu, w_down),
+        flops=2 * 6 * rows * hidden * width,
+        moved=2 * 3 * hidden * width,
+    )
 
 
 def ffn(info, a, ct, w_gu, w_down):
@@ -593,6 +700,83 @@
         (info, a, ct, w_gu, w_gu, w_down),
         flops=2 * 9 * rows * hidden * width,
         moved=2 * 2 * 3 * hidden * width + rows * width * 12,
+    )
+
+
+def plane_grads_body(info, near, far, wg, wu, wd, own_gu, other_gu, dn):
+    width = wg.shape[0]
+    half = width // 2
+    sums = None
+    for part in (near, far):
+        low, upstream = (part[:, :width], part[:, width:])
+        hidden, dg, du = hidden_both_ways(low, upstream, wg[...], wu[...], wd[...])
+        own = part[:, pl.ds(pl.multiple_of(info[0] * half, half), half)]
+        other = part[:, pl.ds(pl.multiple_of((1 - info[0]) * half, half), half)]
+        terms = (t_mm(own, dg), t_mm(own, du), t_mm(other, dg), t_mm(other, du), t_mm(hidden, upstream))
+        sums = terms if sums is None else tuple(p + q for p, q in zip(sums, terms))
+    own_gu[0, :half] = sums[0].astype(BF)
+    own_gu[0, half:] = sums[1].astype(BF)
+    other_gu[0, :half] = sums[2].astype(BF)
+    other_gu[0, half:] = sums[3].astype(BF)
+    for cut in range(width // COLS):
+        dn[0, cut * COLS : (cut + 1) * COLS] = sums[4][:, cut * COLS : (cut + 1) * COLS].astype(BF)
+
+
+def plane_grads(info, near, far, w_gu, w_down):
+    hidden, width = w_down.shape
+    steps = hidden // COLS
+    turns = steps // 8
+
+    def block(i, info):
+        return info[0] * (steps // 2) + lax.rem(info[3], 4) * turns + i
+
+    unit = (1, width, COLS)
+    spec = pl.BlockSpec(unit, lambda i, *u: (i, 0, 0))
+    rows = 2 * near.shape[0]
+    return call(
+        plane_grads_body,
+        [sds((turns, width, COLS), BF)] * 3,
+        (turns,),
+        [
+            whole(near.shape),
+            whole(far.shape),
+            pl.BlockSpec((width, COLS), lambda i, info: (0, block(i, info))),
+            pl.BlockSpec((width, COLS), lambda i, info: (0, steps + block(i, info))),
+            pl.BlockSpec((COLS, width), lambda i, info: (block(i, info), 0)),
+        ],
+        [spec] * 3,
+        (info, near, far, w_gu, w_gu, w_down),
+        flops=2 * 6 * rows * turns * COLS * width,
+        moved=9_000_000,
+    )
+
+
+def column_fold_body(order, info, first, second, third, keep, send):
+    slots = 1 << len(order)
+    size = keep.shape[2]
+    place_z = info[3] // 4
+    for part, source in enumerate((first, second, third)):
+        for block in range(source.shape[0]):
+            for slot in range(slots):
+                owner = jnp.bitwise_xor(place_z, mask_of(slot, order))
+                at = pl.ds(pl.multiple_of(owner * size, size), size)
+                target = keep if slot < slots // 2 else send
+                target[slot % (slots // 2), part * source.shape[0] + block] = source[block, at, :]
+
+
+def column_fold(info, order, sources):
+    slots = 1 << len(order)
+    blocks, width, cols = sources[0].shape
+    shape = sds((slots // 2, 3 * blocks, width // slots, cols), BF)
+    return call(
+        functools.partial(column_fold_body, order),
+        [shape, shape],
+        (1,),
+        [whole(a.shape) for a in sources],
+        [whole(shape.shape)] * 2,
+        (info, *sources),
+        moved=10_000_000,
+        name="column_fold",
     )
 
 
@@ -663,7 +847,7 @@
             one_of(dh2.shape),
             one_of(zh.shape),
             one_of(dff.shape),
-            one_of(ffr.shape),
+            pl.BlockSpec((1, count, width), lambda i, *u: (i, 0, 0)),
             one_of(gf.shape),
             second_of(cols.shape),
             second_of(rows.shape),
@@ -681,29 +865,62 @@
     )
 
 
+def light_join_body(info, x, small, dq, own, got_low, got_high, dl_out, own_out, other_out, low):
+    tok, width = x.shape[1:]
+    micros = x.shape[0]
+    half = width // 2
+    inner = dq.shape[2]
+    for m in range(micros):
+        dl_out[m, :, :inner] = dq[m]
+        dl_out[m, WIN : tok - WIN, inner:] = own[m, WIN : tok - WIN].astype(BF)
+        dl_out[m, :WIN, inner:] = (own[m, :WIN] + got_low[m].astype(F32)).astype(BF)
+        dl_out[m, tok - WIN :, inner:] = (own[m, tok - WIN :] + got_high[m].astype(F32)).astype(BF)
+        values = x[m].astype(F32)
+        low[m] = (values * inverse_rms(values) * small[3:4].astype(F32)).astype(BF)
+    for target, side in ((other_out, 1 - info[0]), (own_out, info[0])):
+        cut = pl.ds(pl.multiple_of(side * half, half), half)
+        for block in range(dl_out.shape[2] // COLS):
+            total = sum(
+                t_mm(low[m, :, cut], dl_out[m, :, block * COLS : (block + 1) * COLS])
+                for m in range(micros)
+            )
+            target[block // 2, (block % 2) * half : (block % 2 + 1) * half] = total.astype(BF)
+
+
+def light_join(info, x, small, dq, own, got_low, got_high):
+    micros, tok, width = x.shape
+    columns = dq.shape[2] + own.shape[2]
+    shapes = [sds((micros, tok, columns), BF)] + [sds((columns // (2 * COLS), width, COLS), BF)] * 2
+    args = (info, x, small, dq, own, got_low, got_high)
+    return call(
+        light_join_body,
+        shapes,
+        (1,),
+        [whole(a.shape) for a in args[1:]],
+        [whole(s.shape) for s in shapes],
+        args,
+        scratch=[pltpu.VMEM(x.shape, BF)],
+        flops=2 * micros * tok * width * columns,
+        moved=20_000_000,
+    )
+
+
 def in_back_body(
-    info, x, dy, dq, own, got_low, got_high, dhq, dhkv, dsq, rows, small, gate, hq, kin, h1k, l_own, l_got, h_own, h_got,
-    grad_out, dl_out, part_out,
+    info, x, dy, dl, dhq, dkin, dsq, rows, small, gate, h1k, l_own, l_got, h_own, h_got,
+    grad_out, part_out,
 ):
     tok, width = x.shape[1:]
     micro = pl.program_id(0)
     base = info[1]
-    inner = dq.shape[2]
-    dl_out[0, :, :inner] = dq[0]
-    dl_out[0, WIN : tok - WIN, inner:] = own[0, WIN : tok - WIN].astype(BF)
-    dl_out[0, :WIN, inner:] = (own[0, :WIN] + got_low[0].astype(F32)).astype(BF)
-    dl_out[0, tok - WIN :, inner:] = (own[0, tok - WIN :] + got_high[0].astype(F32)).astype(BF)
-    light = dl_out[0]
+    light = dl[0]
     back = unhalved(info, mm_t(light, l_own[...]), mm_t(light, l_got[...]))
-    dkin = unhalved(
-        info, mm_t(dhkv[0], h_own[:, width:]), mm_t(dhkv[0], h_got[:, width:])
-    )
+    given = dkin[0].astype(F32)
     open_k = gate[0, :, 1:2]
     source = h1k[0]
-    dskv = jnp.sum(dkin * source, axis=-1, keepdims=True) * open_k * (1.0 - open_k)
-    to_q = unhalved(info, mm_t(dhq[0], h_own[:, :width]), mm_t(dhq[0], h_got[:, :width]))
+    dskv = jnp.sum(given * source, axis=-1, keepdims=True) * open_k * (1.0 - open_k)
+    to_q = unhalved(info, mm_t(dhq[0], h_own[...]), mm_t(dhq[0], h_got[...]))
     to_q += dsq[0, :, 0:1] * small[0:1].astype(F32)
-    to_k = dkin * open_k + dskv * small[1:2].astype(F32)
+    to_k = given * open_k + dskv * small[1:2].astype(F32)
     back += pick(onehot_rows(rows[0, 0], base, tok), to_q)
     back += pick(onehot_rows(rows[1, 0], base, tok), to_k)
     values = x[0].astype(F32)
@@ -725,74 +942,23 @@
         part_out[...] += part
 
 
-def in_back(info, x, dy, dq, own, got_low, got_high, dhq, dhkv, dsq, rows, small, gate, hq, kin, h1k, l_own, l_got, h_own, h_got):
+def in_back(info, x, dy, dl, dhq, dkin, dsq, rows, small, gate, h1k, l_own, l_got, h_own, h_got):
     micros, tok, width = x.shape
-    shapes = [
-        sds((micros, tok, width), BF),
-        sds((micros, tok, l_own.shape[1]), BF),
-        sds((8, width), F32),
-    ]
-    firsts = (x, dy, dq, own, got_low, got_high, dhq, dhkv, dsq)
+    shapes = [sds((micros, tok, width), BF), sds((8, width), F32)]
+    firsts = (x, dy, dl, dhq, dkin, dsq)
     return call(
         in_back_body,
         shapes,
         (micros,),
         [one_of(a.shape) for a in firsts]
         + [second_of(rows.shape), whole(small.shape)]
-        + [one_of(a.shape) for a in (gate, hq, kin, h1k)]
-        + [whole(a.shape) for a in (l_own, l_got, h_own, h_got)],
-        [one_of(s.shape) for s in shapes[:-1]] + [whole(shapes[-1].shape)],
-        (info,) + firsts + (rows, small, gate, hq, kin, h1k, l_own, l_got, h_own, h_got),
-        flops=4_000_000_000,
-        moved=22_000_000,
-    )
-
-
-def grads_body(info, x, small, dl, hq, dhq, kin, dhkv, lo, dy, ho, dhy, own_out, other_out, low):
-    micros, tok, width = x.shape
-    half = width // 2
-    for m in range(micros):
-        values = x[m].astype(F32)
-        low[m] = (values * inverse_rms(values) * small[3:4].astype(F32)).astype(BF)
-    inner = lo.shape[2]
-    for target, side in ((other_out, 1 - info[0]), (own_out, info[0])):
-        cut = pl.ds(pl.multiple_of(side * half, half), half)
-
-        def put(unit, left, right):
-            for block in range(right[0].shape[1] // COLS):
-                at = unit + block
-                total = sum(
-                    t_mm(a, b[:, block * COLS : (block + 1) * COLS]) for a, b in zip(left, right)
-                )
-                target[at // 2, (at % 2) * half : (at % 2 + 1) * half] = total.astype(BF)
-            return unit + right[0].shape[1] // COLS
-
-        every = range(micros)
-        unit = put(0, [low[m, :, cut] for m in every], [dl[m] for m in every])
-        unit = put(unit, [hq[m, :, cut] for m in every], [dhq[m] for m in every])
-        unit = put(unit, [kin[m, :, cut] for m in every], [dhkv[m] for m in every])
-        unit = put(unit, [ho[m, :, cut] for m in every], [dhy[m] for m in every])
-        part = inner // 2
-        small_cut = pl.ds(pl.multiple_of(side * part, part), part)
-        total = sum(t_mm(lo[m, :, small_cut], dy[m].astype(BF)) for m in every)
-        pack_rows(target.at[pl.ds(unit // 2, 1)], total)
-
-
-def attention_grads(info, x, small, dl, hq, dhq, kin, dhkv, lo, dy, ho, dhy):
-    micros, tok, width = x.shape
-    units = (dl.shape[2] + dhq.shape[2] + dhkv.shape[2] + dhy.shape[2]) // COLS
-    shapes = [sds((units // 2 + 1, width, COLS), BF)] * 2
-    args = (info, x, small, dl, hq, dhq, kin, dhkv, lo, dy, ho, dhy)
-    return call(
-        grads_body,
-        shapes,
-        (1,),
-        [whole(a.shape) for a in args[1:]],
-        [whole(s.shape) for s in shapes],
-        args,
-        scratch=[pltpu.VMEM(x.shape, BF)],
-        flops=2 * micros * tok * width * 2100,
-        moved=20_000_000,
+        + [one_of(a.shape) for a in (gate, h1k)]
+        + [whole(a.shape) for a in (l_own, l_got)]
+        + [whole((h_own.shape[0], width))] * 2,
+        [one_of(shapes[0].shape), whole(shapes[1].shape)],
+        (info,) + firsts + (rows, small, gate, h1k, l_own, l_got, h_own, h_got),
+        flops=2_600_000_000,
+        moved=14_000_000,
     )
 
 
@@ -906,159 +1072,208 @@
     return (value, flipped(value, order[-1]))
 
 
-def place(info, order, near, far, block, part, half, write):
+def from_owner(info, order, near, far, owner, write):
     slots = 1 << len(order)
-    back = tuple(reversed(order))
-    for slot in range(slots):
-        mask = sum(back[b] for b in range(len(order)) if (slot >> b) & 1)
-        owner = jnp.bitwise_xor(info[3], mask)
-        source = near if slot < slots // 2 else far
-        value = source[slot % (slots // 2), block].astype(F32)
-        write(owner, value)
-
-
-def unpack_gu_body(order, starts, info, near, far, out):
-    side = pl.program_id(1)
+    distance = jnp.bitwise_xor(info[3], owner)
+    slot = sum(
+        jnp.where(jnp.bitwise_and(distance, bit) != 0, 1 << place, 0)
+        for place, bit in enumerate(reversed(order))
+    )
+    inside = lax.rem(slot, slots // 2)
+
+    @pl.when(slot < slots // 2)
+    def close():
+        write(near.at[inside])
+
+    @pl.when(slot >= slots // 2)
+    def distant():
+        write(far.at[inside])
+
+
+def unpack_gu_body(order, info, near, far, *outs):
+    out = outs[-1]
     size = near.shape[2]
-
-    def write(owner, value):
-        per = out.shape[0] // size
-
-        @pl.when(owner // per == side)
-        def hit():
-            out[pl.ds(pl.multiple_of((owner % per) * size, size), size), :] = value
-
-    place(info, order, near, far, 0, None, None, write)
-
-
-def unpack_dn_body(order, info, near, far, out):
-    size = near.shape[2]
+    per = out.shape[0] // size
+    for turn in range(per):
+
+        def write(source, turn=turn):
+            for block in range(near.shape[1]):
+                out[turn * size : (turn + 1) * size, block * COLS : (block + 1) * COLS] = source[
+                    block
+                ].astype(F32)
+
+        from_owner(info, order, near, far, pl.program_id(1) * per + turn, write)
+
+
+def write_dn(out, source, first, size, owner, row):
     cuts = out.shape[1] // COLS
     rows = size // cuts
-
-    def write(owner, value):
-        for cut in range(cuts):
-            out[
-                pl.ds(pl.multiple_of(owner * rows, rows), rows), cut * COLS : (cut + 1) * COLS
-            ] = value[cut * rows : (cut + 1) * rows]
-
-    place(info, order, near, far, 0, None, None, write)
-
-
-def unpack_gu(info, order, pair, first, count, total, base, previous):
+    value = source[first].astype(F32)
+    for cut in range(cuts):
+        out[row + owner * rows : row + (owner + 1) * rows, cut * COLS : (cut + 1) * COLS] = value[
+            cut * rows : (cut + 1) * rows
+        ]
+
+
+def unpack_dn_body(order, info, near, far, *outs):
+    slots, blocks, size = near.shape[:3]
+    for owner in range(2 * slots):
+
+        def write(source, owner=owner):
+            for block in range(blocks):
+                write_dn(outs[-1], source, block, size, owner, block * COLS)
+
+        from_owner(info, order, near, far, owner, write)
+
+
+def unpack(body, info, order, pair, first, count, step, shape, grid_more, block, index, previous, name):
     near, far = pair
     slots, unused, size, unused_too = near.shape
-    rows = size * slots
-    spec = pl.BlockSpec((slots, 1, size, COLS), lambda i, s, *u: (0, first + i, 0, 0))
-    out = sds((rows, 2 * total * COLS), F32)
-    body = functools.partial(unpack_gu_body, order, None)
-    args, specs = ([info, near, far], [spec, spec])
-    aliases = {}
+    spec = pl.BlockSpec((slots, step, size, COLS), lambda i, *u: (0, first // step + i, 0, 0))
+    args, specs, aliases = ([info, near, far], [spec, spec], {})
     if previous is not None:
         args.append(previous)
         specs.append(pl.BlockSpec(memory_space=pl.ANY))
         aliases = {3: 0}
-        inner = body
-        body = lambda info, near, far, unused, out: inner(info, near, far, out)
     return pl.pallas_call(
-        body,
-        out_shape=out,
+        functools.partial(body, order),
+        out_shape=sds(shape, F32),
         grid_spec=pltpu.PrefetchScalarGridSpec(
             num_scalar_prefetch=1,
-            grid=(count, 2),
+            grid=(count // step,) + grid_more,
             in_specs=specs,
-            out_specs=pl.BlockSpec((rows, COLS), lambda i, s, *u: (0, s * total + base + i)),
+            out_specs=pl.BlockSpec(block, index),
         ),
         input_output_aliases=aliases,
-        cost_estimate=pl.CostEstimate(flops=0, bytes_accessed=count * rows * COLS * 12, transcendentals=0),
+        compiler_params=pltpu.CompilerParams(vmem_limit_bytes=32 * 1024 * 1024),
+        cost_estimate=pl.CostEstimate(
+            flops=0, bytes_accessed=count * 2 * slots * size * COLS * 6, transcendentals=0
+        ),
+        name=name,
     )(*args)
 
 
-def unpack_dn(info, order, pair, first, count, total, base, previous):
-    near, far = pair
-    slots, unused, size, unused_too = near.shape
-    width = 2 * slots * size
-    cuts = width // COLS
-    rows = width * COLS // width
-    spec = pl.BlockSpec((slots, 1, size, COLS), lambda i, *u: (0, first + i, 0, 0))
-    out = sds((total * rows, width), F32)
-    body = functools.partial(unpack_dn_body, order)
-    args, specs = ([info, near, far], [spec, spec])
-    aliases = {}
-    if previous is not None:
-        args.append(previous)
-        specs.append(pl.BlockSpec(memory_space=pl.ANY))
-        aliases = {3: 0}
-        inner = body
-        body = lambda info, near, far, unused, out: inner(info, near, far, out)
-    return pl.pallas_call(
-        body,
-        out_shape=out,
-        grid_spec=pltpu.PrefetchScalarGridSpec(
-            num_scalar_prefetch=1,
-            grid=(count,),
-            in_specs=specs,
-            out_specs=pl.BlockSpec((rows, width), lambda i, *u: (base + i, 0)),
-        ),
-        input_output_aliases=aliases,
-        cost_estimate=pl.CostEstimate(flops=0, bytes_accessed=count * rows * width * 6, transcendentals=0),
-    )(*args)
-
-
-def unpack_attention_body(orders, widths, info, *refs):
-    pairs, outs = (refs[: 2 * len(orders)], refs[2 * len(orders) :])
-    unit = 0
-    homes = []
-    for which, columns in enumerate(widths):
-        for block in range(columns // COLS):
-            homes.append((which, block))
-    start = 0
+def unpack_gu(info, order, pair, first, count, total, base, previous, step):
+    rows = pair[0].shape[0] * pair[0].shape[2]
+    return unpack(
+        unpack_gu_body, info, order, pair, first, count, step, (rows, 2 * total * COLS), (2,), (rows, step * COLS),
+        lambda i, s, *u: (0, (s * total + base) // step + i), previous, "unpack_gu",
+    )
+
+
+def unpack_dn(info, order, pair, first, count, total, base, previous, step):
+    width = 2 * pair[0].shape[0] * pair[0].shape[2]
+    return unpack(
+        unpack_dn_body, info, order, pair, first, count, step, (total * COLS, width), (), (step * COLS, width),
+        lambda i, *u: (base // step + i, 0), previous, "unpack_dn",
+    )
+
+
+def unpack_plane_gu_body(orders, info, *refs):
+    out = refs[-1]
+    side, plane = (pl.program_id(0), pl.program_id(2))
     for which, order in enumerate(orders):
-        near, far = pairs[2 * which : 2 * which + 2]
-        size = near.shape[2]
-        for block in range(near.shape[1]):
-            at = start + block
-
-            def write(owner, value, at=at):
-                if 2 * at >= len(homes):
-                    out = outs[len(widths)]
-                    cuts = out.shape[1] // COLS
-                    rows = size // cuts
-                    for cut in range(cuts):
-                        out[
-                            pl.ds(pl.multiple_of(owner * rows, rows), rows),
-                            cut * COLS : (cut + 1) * COLS,
-                        ] = value[cut * rows : (cut + 1) * rows]
-                    return
-                per = outs[0].shape[0] // size
-                for side in range(2):
-                    which_out, column = homes[2 * at + side]
-                    out = outs[which_out]
-
-                    @pl.when(owner // per == side)
-                    def hit(out=out, column=column):
-                        out[
-                            pl.ds(pl.multiple_of((owner % per) * size, size), size),
-                            column * COLS : (column + 1) * COLS,
-                        ] = value
-
-            place(info, order, near, far, block, None, None, write)
-        start += near.shape[1]
-
-
-def unpack_attention(info, orders, pairs, widths, inner):
-    slots, unused, size, unused_too = pairs[0][0].shape
-    half = slots * size
-    shapes = [sds((half, w), F32) for w in widths] + [sds((inner // 2, 2 * half), F32)]
+        near, far = refs[2 * which : 2 * which + 2]
+        blocks, size = near.shape[1:3]
+        per = out.shape[0] // 2
+        for level in range(2):
+            owner = (side * 2 + level) * 4 + plane
+            row = level * per + which * size
+
+            def write(source, row=row):
+                for block in range(blocks):
+                    out[row : row + size, block * COLS : (block + 1) * COLS] = source[block].astype(F32)
+
+            from_owner(info, order, near, far, owner, write)
+
+
+def unpack_plane_gu(info, orders, pairs, total):
+    slots, blocks, size, unused = pairs[0][0].shape
+    turns = blocks // 3
+    spec = pl.BlockSpec(
+        (slots, turns, size, COLS), lambda s, h, q, info: (0, jnp.bitwise_xor(h, info[0]), 0, 0)
+    )
+    rows = 2 * len(pairs) * size
     args = [info] + [part for pair in pairs for part in pair]
     return call(
-        functools.partial(unpack_attention_body, orders, widths),
+        functools.partial(unpack_plane_gu_body, orders),
+        sds((rows, 2 * total * COLS), F32),
+        (2, 2, 4),
+        [spec] * (len(args) - 1),
+        pl.BlockSpec((rows, turns * COLS), lambda s, h, q, *u: (0, s * 8 + h * 4 + q)),
+        args,
+        moved=2 * rows * total * COLS * 6,
+        name="unpack_plane_gu",
+    )
+
+
+def unpack_plane_dn_body(orders, info, *refs):
+    out = refs[-1]
+    plane = pl.program_id(0)
+    for which, order in enumerate(orders):
+        near, far = refs[2 * which : 2 * which + 2]
+        blocks, size = near.shape[1:3]
+        for level in range(4):
+            owner = level * 4 + plane
+            cut, row = divmod((level * len(orders) + which) * size, COLS)
+
+            def write(source, cut=cut, row=row):
+                for block in range(blocks):
+                    at = block * COLS + row
+                    out[at : at + size, cut * COLS : (cut + 1) * COLS] = source[block].astype(F32)
+
+            from_owner(info, order, near, far, owner, write)
+
+
+def unpack_plane_dn(info, orders, pairs):
+    slots, blocks, size, unused = pairs[0][0].shape
+    turns = blocks // 3
+    width = 4 * len(pairs) * size
+    spec = pl.BlockSpec((slots, turns, size, COLS), lambda q, *u: (0, 2, 0, 0))
+    args = [info] + [part for pair in pairs for part in pair]
+    return call(
+        functools.partial(unpack_plane_dn_body, orders),
+        sds((4 * turns * COLS, width), F32),
+        (4,),
+        [spec] * (len(args) - 1),
+        pl.BlockSpec((turns * COLS, width), lambda q, *u: (q, 0)),
+        args,
+        moved=4 * turns * COLS * width * 6,
+        name="unpack_plane_dn",
+    )
+
+
+def unpack_units_body(order, first, info, near, far, *outs):
+    slots, unused, size = near.shape[:3]
+    homes = [
+        (out, block * COLS) for out in outs for block in range(out.shape[1] // COLS)
+    ]
+    for owner in range(2 * slots):
+        side, turn = divmod(owner, slots)
+
+        def write(source, side=side, turn=turn):
+            for at in range(side, len(homes), 2):
+                out, column = homes[at]
+                out[turn * size : (turn + 1) * size, column : column + COLS] = source[
+                    first + at // 2
+                ].astype(F32)
+
+        from_owner(info, order, near, far, owner, write)
+
+
+def unpack_units(info, order, pair, first, widths):
+    slots, unused, size, unused_too = pair[0].shape
+    shapes = [sds((slots * size, w), F32) for w in widths]
+    args = [info, *pair]
+    return call(
+        functools.partial(unpack_units_body, order, first),
         shapes,
         (1,),
         [whole(a.shape) for a in args[1:]],
         [whole(s.shape) for s in shapes],
         args,
-        moved=14_000_000,
+        moved=sum(widths) * slots * size * 6,
+        name="unpack_units",
     )
 
 
@@ -1156,11 +1371,13 @@
     index = jnp.stack([q_index[:, 0], kv_index[:, 0], ff_index[:, 0]])
     cols, rows = (index[..., None], index[:, :, None, :])
 
-    q_pay, kv_pay, hq_in, kin, h1k, gate = routed_in(info, x, cols, small, h_own, h_got)
+    q_pay, kin_pay, hq_in, h1k, gate = routed_in(info, x, cols, small, h_own, h_got)
     kv_orders = ((8, 4, 2, 1), (8, 4, 1, 2))
+    back_orders = [tuple(reversed(order)) for order in kv_orders]
     upward = [(i, i + 1) for i in range(count - 1)]
     downward = [(i + 1, i) for i in range(count - 1)]
     inner = light_qkv.shape[1] // 3
+    every = range(micros)
 
     def rims(qkv):
         return (
@@ -1168,9 +1385,11 @@
             lax.ppermute(qkv[:, :WIN, inner:], "ctx", downward),
         )
 
+    def project(kin):
+        return key_project(info, kin, h_own, h_got)
+
     if direct:
-        back_orders = [tuple(reversed(order)) for order in kv_orders]
-        values = [kv_pay[m] for m in range(micros)]
+        values = [kin_pay[m] for m in every]
         got = gather_start(values, back_orders, 0)
         qkv = light_in(info, x, small, l_own, l_got)
         got, qkv, w_lout, w_hout = tied(got, qkv, w_lout, w_hout)
@@ -1184,151 +1403,154 @@
         got, lo, light_lse, w_hgu, w_hdown = tied(got, lo, light_lse, w_hgu, w_hdown)
         values = gather_end(values, got)
         got = gather_start(values, back_orders, 3)
-        pairs = list(zip(values, got))
+        near_kv = [project(v) for v in values]
+        got, near_kv = tied(got, near_kv)
+        kins = list(zip(values, got))
+        kvs = [(n, project(f)) for n, f in zip(near_kv, got)]
     else:
-        pairs = []
-        for m in range(micros):
-            every = lax.all_gather(kv_pay[m], "ctx", axis=0, tiled=True)
-            pairs.append((every[: every.shape[0] // 2], every[every.shape[0] // 2 :]))
+        kins = []
+        for m in every:
+            full = lax.all_gather(kin_pay[m], "ctx", axis=0, tiled=True)
+            kins.append((full[: full.shape[0] // 2], full[full.shape[0] // 2 :]))
+        kvs = [tuple(project(k) for k in pair) for pair in kins]
         qkv = light_in(info, x, small, l_own, l_got)
         before, after = rims(qkv)
         lo, light_lse = light_fwd(info, qkv, before, after)
-    heavy = [heavy_fwd(info, q_pay[m], *pairs[m]) for m in range(micros)]
+    heavy = [heavy_fwd(info, q_pay[m], kins[m], kvs[m]) for m in every]
     heavy, w_lgu, w_ldown = tied(heavy, w_lgu, w_ldown)
     ho = jnp.stack([h[0] for h in heavy])
-    y, low2, ffr, dzh, hy, gf = middle(info, x, up, cols, rows, small, gate, lo, w_lout, ho, w_hout)
-    routed = ffr.shape[1]
+    y, low2, pay, hy, gf = middle(info, x, up, cols, rows, small, gate, lo, w_lout, ho, w_hout)
 
     def flat(value):
         return value.reshape(-1, value.shape[-1])
 
-    zh, dff, hgu_own, hgu_send, hdn_own, hdn_send = ffn(info, flat(ffr), flat(dzh), w_hgu, w_hdown)
+    orders = ((1, 2, 4, 8), (2, 4, 1, 8), (4, 1, 2, 8))
+    if direct:
+        mine = flat(pay)
+        plane = [flipped(mine, bit) for bit in (1, 2, 3)]
+        zh, dff = ffn_local(info, mine, w_hgu, w_hdown, 2 * COLS)
+        plane, zh, dff = tied(plane, zh, dff)
+        near = jnp.concatenate([mine, *plane], axis=0)
+        far = lax.ppermute(near, "wsh", swap)
+    else:
+        zh, dff, hgu_own, hgu_send, hdn_own, hdn_send = ffn(
+            info, flat(pay[..., :width]), flat(pay[..., width:]), w_hgu, w_hdown
+        )
     z, dh2, lgu_own, lgu_send, ldn_own, ldn_send = ffn(info, flat(low2), flat(up), w_lgu, w_ldown)
     if direct:
-        hgu_got, hdn_got, lgu_got, ldn_got = (
-            lax.ppermute(part, "wsh", swap) for part in (hgu_send, hdn_send, lgu_send, ldn_send)
-        )
-        orders = ((1, 2, 4, 8), (2, 4, 1, 8), (4, 1, 2, 8))
-        first = [
-            fold(info, orders[0], [(hgu_own, hgu_got, 0, 8), (lgu_own, lgu_got, 0, 2)]),
-            fold(info, orders[1], [(hgu_own, hgu_got, 8, 8), (lgu_own, lgu_got, 2, 2)]),
-            fold(info, orders[2], [(hdn_own, hdn_got, 0, 8), (ldn_own, ldn_got, 0, 2)]),
-        ]
-        got = scatter_start(first, orders, 0)
+        far, z, dh2 = tied(far, z, dh2)
+        lgu_got, ldn_got = (lax.ppermute(part, "wsh", swap) for part in (lgu_send, ldn_send))
+        plane_own, plane_send, plane_dn = plane_grads(info, near, far, w_hgu, w_hdown)
+        plane_got = lax.ppermute(plane_send, "wsh", swap)
+        keep, send = column_fold(info, (1, 2), (plane_own, plane_got, plane_dn))
+        got = flipped(send, 4)
 
     def by_micro(value):
         return value.reshape(micros, -1, value.shape[-1])
 
     out_tokens, dy, dlo, dho, dhy, dsq, part_two = mid_back(
-        info, y, up, by_micro(z), by_micro(dh2), by_micro(zh), by_micro(dff), ffr, gf, cols, rows, small, gate, w_lout,
+        info, y, up, by_micro(z), by_micro(dh2), by_micro(zh), by_micro(dff), pay, gf, cols, rows, small, gate, w_lout,
         w_hout, hy, hq_in,
     )
-    dhq, partial = ([], [])
-    for m in range(micros):
-        dq, near, far = heavy_bwd(info, q_pay[m], *pairs[m], heavy[m][1], dho[m])
-        dhq.append(dq)
-        partial.append((near, far))
-    dhq = jnp.stack(dhq)
+    backs = [
+        heavy_bwd(info, q_pay[m], kins[m], kvs[m], heavy[m][1], dho[m], h_own, h_got) for m in every
+    ]
+    dhq = jnp.stack([b[0] for b in backs])
+    shape = (count // 2, q_index.shape[2], width)
+    back = [tuple(part.reshape(shape) for part in b[3:5]) for b in backs]
+    dkvs = [part for b in backs for part in b[1:3]]
     if direct:
-        shape = (count // 2, routed, 2 * width)
-        back = [tuple(part.reshape(shape) for part in both) for both in partial]
-        got, back, dlo = tied(got, back, dlo)
-        first = scatter_end(first, got)
-        got = scatter_start(first, orders, 1)
+        got, back, dlo, dkvs = tied(got, back, dlo, dkvs)
+        keep, send = scatter_step(keep, got)
+        got = flipped(send, 8)
         got_back = scatter_start(back, back_orders, 0)
-    else:
-        dhkv = jnp.stack(
-            [
-                lax.psum_scatter(jnp.concatenate(both, axis=0), "ctx", scatter_dimension=0, tiled=True)
-                for both in partial
-            ]
-        )
     dlq, dl_own, rim_low, rim_high = light_bwd(info, qkv, before, after, light_lse, dlo)
     if direct:
         got, got_back, dlq, dl_own, rim_low, rim_high = tied(got, got_back, dlq, dl_own, rim_low, rim_high)
-        first, back = (scatter_end(first, got), scatter_end(back, got_back))
-        got, got_back = (scatter_start(first, orders, 2), scatter_start(back, back_orders, 1))
     got_low = lax.ppermute(rim_high, "ctx", upward)
     got_high = lax.ppermute(rim_low, "ctx", downward)
     if direct:
-        for stage in (2, 3):
-            first, back = (scatter_end(first, got), scatter_end(back, got_back))
-            if stage == 2:
-                got = scatter_start(first, orders, 3)
-            else:
-                values = [keep for keep, send in first]
-                got = gather_start(values, orders, 0)
-            got_back = scatter_start(back, back_orders, stage)
-            got, got_back, got_low, got_high = tied(got, got_back, got_low, got_high)
+        keep, send = scatter_step(keep, got)
+        third = keep.shape[2] // 3
+        values = [keep[:, :, t * third : (t + 1) * third] for t in range(3)]
         back = scatter_end(back, got_back)
-        dhkv = jnp.concatenate([keep for keep, send in back], axis=0)
-        values = gather_end(values, got)
-        got = gather_start(values, orders, 1)
-    grad_tokens, dl, part_one = in_back(
-        info, x, dy, dlq, dl_own, got_low, got_high, dhq, dhkv, dsq, rows, small, gate, hq_in, kin, h1k, l_own, l_got,
-        h_own, h_got,
-    )
-    att_own, att_send = attention_grads(info, x, small, dl, hq_in, dhq, kin, dhkv, lo, dy, ho, dhy)
-    widths = (light_qkv.shape[1], heavy_qkv.shape[1], heavy_out.shape[1])
+        got, got_back = (gather_start(values, orders, 0), scatter_start(back, back_orders, 1))
+    kin_all = [part for pair in kins for part in pair]
+    ha_own, ha_send = heavy_grads(info, hq_in, dhq, ho, dhy, lo, dy, kin_all, dkvs)
+    if direct:
+        got, got_back, got_low, got_high, ha_own, ha_send = tied(got, got_back, got_low, got_high, ha_own, ha_send)
+        ha_got = lax.ppermute(ha_send, "wsh", swap)
+        values, back = (gather_end(values, got), scatter_end(back, got_back))
+        got, got_back = (gather_start(values, orders, 1), scatter_start(back, back_orders, 2))
+    dl, la_own, la_send = light_join(info, x, small, dlq, dl_own, got_low, got_high)
+    if direct:
+        la_got = lax.ppermute(la_send, "wsh", swap)
+        got, got_back, ha_got, la_got, dl = tied(got, got_back, ha_got, la_got, dl)
+        values, back = (gather_end(values, got), scatter_end(back, got_back))
+        got, got_back = (gather_start(values, orders, 2), scatter_start(back, back_orders, 3))
+        second = [
+            fold(info, orders[0], [(ha_own, ha_got, 0, 6)]),
+            fold(info, orders[1], [(lgu_own, lgu_got, 0, 4), (ha_own, ha_got, 6, 1)]),
+            fold(info, orders[2], [(la_own, la_got, 0, 3), (ldn_own, ldn_got, 0, 2)]),
+        ]
+        got_two = scatter_start(second, orders, 0)
+        got, got_back, got_two = tied(got, got_back, got_two)
+        values, second, back = (
+            gather_end(values, got), scatter_end(second, got_two), scatter_end(back, got_back)
+        )
+        dkin = jnp.concatenate([keep for keep, send in back], axis=0)
+        got = gather_start(values, orders, 3)
+        got_two = scatter_start(second, orders, 1)
+    else:
+        dkin = jnp.stack(
+            [
+                lax.psum_scatter(jnp.concatenate(b[3:5], axis=0), "ctx", scatter_dimension=0, tiled=True)
+                for b in backs
+            ]
+        )
+    grad_tokens, part_one = in_back(
+        info, x, dy, dl, dhq, dkin, dsq, rows, small, gate, h1k, l_own, l_got, h_own, h_got
+    )
+    widths = (heavy_qkv.shape[1], heavy_out.shape[1])
     vector = part_one + part_two
     if direct:
-        att_got = lax.ppermute(att_send, "wsh", swap)
         half = width // 2
         mine = lax.dynamic_slice_in_dim(vector, side * half, half, 1)
         given = lax.dynamic_slice_in_dim(vector, (1 - side) * half, half, 1)
         vector = mine + lax.ppermute(given, "wsh", swap)
-        got, att_got, vector = tied(got, att_got, vector)
-        values = gather_end(values, got)
-        got = gather_start(values, orders, 2)
-        pieces = ((0, 4), (4, 3), (7, 3))
-        second = [
-            fold(info, order, [(att_own, att_got, start, size)])
-            for order, (start, size) in zip(orders, pieces)
-        ]
-        got, second, vector = tied(got, second, vector)
-        values = gather_end(values, got)
-        got = gather_start(values, orders, 3)
-        got_two = scatter_start(second, orders, 0)
-        got_vector = flipped(vector, 1)
-        got_two, second, vector, got_vector = tied(got_two, second, vector, got_vector)
+        got_two, vector = tied(got_two, vector)
+        second = scatter_end(second, got_two)
+        got_two, got_vector = (scatter_start(second, orders, 2), flipped(vector, 1))
+        got, got_two, vector, got_vector = tied(got, got_two, vector, got_vector)
+        chunks = list(zip(values, got))
         second, vector = (scatter_end(second, got_two), vector + got_vector)
-        got_two, got_vector = (scatter_start(second, orders, 1), flipped(vector, 2))
-        got, got_two, vector, got_vector = tied(got, got_two, vector, got_vector)
+        got_two, got_vector = (scatter_start(second, orders, 3), flipped(vector, 2))
+        g_hgu = unpack_plane_gu(info, orders, chunks, heavy_gu.shape[1] // (2 * COLS))
+        got_two, vector, got_vector, g_hgu = tied(got_two, vector, got_vector, g_hgu)
         second, vector = (scatter_end(second, got_two), vector + got_vector)
-        chunks = list(zip(values, got))
-        got_two, got_vector = (scatter_start(second, orders, 2), flipped(vector, 4))
-        g_hdown = unpack_dn(info, orders[2], chunks[2], 0, 8, 8, 0, None)
-        got_two, got_vector, vector, g_hdown = tied(got_two, got_vector, vector, g_hdown)
-        second, vector = (scatter_end(second, got_two), vector + got_vector)
-        got_two, got_vector = (scatter_start(second, orders, 3), flipped(vector, 8))
-        part = unpack_gu(info, orders[0], chunks[0], 0, 8, 16, 0, None)
-        got_two, got_vector, vector, part = tied(got_two, got_vector, vector, part)
-        second, vector = (scatter_end(second, got_two), vector + got_vector)
-        values = [keep for keep, send in second]
-        got = gather_start(values, orders, 0)
-        g_hgu = unpack_gu(info, orders[1], chunks[1], 0, 8, 16, 8, part)
-        got, g_hgu = tied(got, g_hgu)
-        values = gather_end(values, got)
-        got = gather_start(values, orders, 1)
-        part = unpack_gu(info, orders[0], chunks[0], 8, 2, 4, 0, None)
-        got, part = tied(got, part)
-        values = gather_end(values, got)
-        got = gather_start(values, orders, 2)
-        g_lgu = unpack_gu(info, orders[1], chunks[1], 8, 2, 4, 2, part)
-        got, g_lgu = tied(got, g_lgu)
-        values = gather_end(values, got)
-        got = gather_start(values, orders, 3)
-        g_ldown = unpack_dn(info, orders[2], chunks[2], 8, 2, 2, 0, None)
-        got, g_ldown = tied(got, g_ldown)
-        sums = list(zip(values, got))
-        g_lqkv, g_hqkv, g_hout, g_lout = unpack_attention(info, orders, sums, widths, inner)
+        tails = [keep for keep, send in second]
+        got_two, got_vector = (gather_start(tails, orders, 0), flipped(vector, 4))
+        g_hdown = unpack_plane_dn(info, orders, chunks)
+        got_two, vector, got_vector, g_hdown = tied(got_two, vector, got_vector, g_hdown)
+        tails, vector = (gather_end(tails, got_two), vector + got_vector)
+        got_two, got_vector = (gather_start(tails, orders, 1), flipped(vector, 8))
+        got_two, vector, got_vector = tied(got_two, vector, got_vector)
+        tails, vector = (gather_end(tails, got_two), vector + got_vector)
+        tails = gather_end(tails, gather_start(tails, orders, 2))
+        sums = list(zip(tails, gather_start(tails, orders, 3)))
+        g_hqkv, g_hout = unpack_units(info, orders[0], sums[0], 0, widths)
+        g_lgu = unpack_gu(info, orders[1], sums[1], 0, 4, 4, 0, None, 4)
+        g_lout = unpack_dn(info, orders[1], sums[1], 4, 1, 1, 0, None, 1)
+        (g_lqkv,) = unpack_units(info, orders[2], sums[2], 0, (light_qkv.shape[1],))
+        g_ldown = unpack_dn(info, orders[2], sums[2], 3, 2, 2, 0, None, 1)
     else:
-        g_lqkv, g_hqkv, g_hout = plain_units(att_own, att_send, widths)
-        last = slice(att_own.shape[0] - 1, att_own.shape[0])
+        g_hqkv, g_hout = plain_units(ha_own, ha_send, widths)
+        (g_lqkv,) = plain_units(la_own, la_send, (light_qkv.shape[1],))
+        last = slice(ha_own.shape[0] - 1, ha_own.shape[0])
         g_lqkv, g_lout, g_hqkv, g_hout, g_lgu, g_ldown, g_hgu, g_hdown = plain_sum(
             [
                 g_lqkv,
-                plain_dn(att_own[last], att_send[last]),
+                plain_dn(ha_own[last], ha_send[last]),
                 g_hqkv,
                 g_hout,
                 plain_gu(lgu_own, lgu_send),

time: 751 us -> 609 us (0.81)
  waiting for transfers between devices: 308 us -> 200 us
  Pallas kernels: 255 us -> 229 us
    ppermute x68 -> x61, waiting for transfers between devices: 291 us -> 191 us  [flipped(): return lax.ppermute(value, 'ctx', [(i, i ^ bit) for i in range(size)])]
    pallas_call x6 -> x3, Pallas kernels: 45.8 us -> 6.6 us  [unpack(): pl.pallas_call(functools.partial(body, order), out_shape=sds(shape, F32),...]
    pallas_call x21 -> x28, Pallas kernels: 209 us -> 223 us  [call(): pl.pallas_call(body, name=name or getattr(body, '__name__', 'kernel'), ou...]
    convert_element_type x14 -> x8, other arithmetic: 17.9 us -> 13 us  [scatter_step(): (keep[:half].astype(F32) + got[:half].astype(F32)).astype(BF)]
    ppermute x68 -> x61, starting transfers between devices: 87.4 us -> 82.6 us  [flipped(): return lax.ppermute(value, 'ctx', [(i, i ^ bit) for i in range(size)])]
    unnamed x175 -> x237, local copies, waits for them, and re-layouts: 20.6 us -> 17.8 us
  transfers between devices with their start and end apart: 86 -> 80, of which waited for: 36 -> 31; matrix products, arithmetic and copies ran while one was open for 5% -> 6% of each run, Pallas kernels for 24% -> 33%
where the time goes in v3:
time: 609 us; the launch traced here: 604 us
  Pallas kernels  229 us (38%)
  waiting for transfers between devices  200 us (33%)
  starting transfers between devices  94.2 us (15%)
  other arithmetic  37.6 us (6%)
  local copies, waits for them, and re-layouts  23.4 us (4%)
  between operations  15.5 us (3%)
    pallas_call x28, Pallas kernels, call(): pl.pallas_call(body, name=name or getattr(body, '__name__', 'kernel'), ou...  223 us
    ppermute x61, waiting for transfers between devices, flipped(): return lax.ppermute(value, 'ctx', [(i, i ^ bit) for i in range(size)])  191 us
    ppermute x61, starting transfers between devices, flipped(): return lax.ppermute(value, 'ctx', [(i, i ^ bit) for i in range(size)])  82.6 us
    unnamed x237, local copies, waits for them, and re-layouts  17.8 us
    convert_element_type x8, other arithmetic, scatter_step(): (keep[:half].astype(F32) + got[:half].astype(F32)).astype(BF)  13 us
  transfers between devices with their start and end apart: 80, of which 31 were waited for; matrix products, arithmetic and copies ran while one was open for 6% of the time, Pallas kernels for 33%

profile of v3, /device:TPU:0, one launch (start us, length us, event | category | flops | bytes accessed | tf_op | source)
XLA Modules:
  0.0 604.0 jit_solution(16293500897429169591)
XLA Ops:
  36.2 7.2 %light_in_body.1.qkv = bf16[2,512,1536]{2,1,0:T(8,128)(2,1)} custom-call(s32[14]{0:T(128)S(1)} %concatenate.103.info, bf16[2,512,768]{2,1,0:T(8,128)(2,1)S(1)} %bitcast.52, bf16[8,768]{1,0:T(8,128)(2,1)S(1)} %pad_maximum_fusion.28.small, bf16[384,1536]{1,0:T(8,128)(2,1)S(1)} %copy-done.17, bf16[384,1536]{1,0:T(8,128)(2,1)} %collective-permute-done.4.w_got.l_got), custom_call_target="tpu_custom_call" | custom-call | flops 2415919104 | bytes 8000000 | tf_op jit(solution)/shard_map/light_in_body/pallas_call | solution.py:74
  57.2 17.3 %collective-permute-done.6 = bf16[128,896]{1,0:T(8,128)(2,1)S(1)} collective-permute-done((bf16[128,896]{1,0:T(8,128)(2,1)S(1)}, bf16[128,896]{1,0:T(8,128)(2,1)S(1)}, u32[]{:S(2)}, u32[]{:S(2)}) %collective-permute-start.6) | collective-permute-done | bytes 229408 | tf_op jit(solution)/shard_map/ppermute | solution.py:1030
  78.9 15.1 %light_fwd_body.1 = (bf16[2,512,512]{2,1,0:T(8,128)(2,1)S(1)}, f32[2,512,128]{2,1,0:T(8,128)S(1)}) custom-call(s32[14]{0:T(128)S(1)} %concatenate.103.info, bf16[2,512,1536]{2,1,0:T(8,128)(2,1)S(1)} %copy-done.32, bf16[2,128,1024]{2,1,0:T(8,128)(2,1)S(1)} %collective-permute-done.7.before, bf16[2,128,1024]{2,1,0:T(8,128)(2,1)S(1)} %collective-permute-done.8.after), custom_call_target="tpu_custom_call" | custom-call | flops 4000000000 | bytes 6000000 | tf_op jit(solution)/shard_map/light_fwd_body/pallas_call | solution.py:74
  107.1 12.8 %collective-permute-done.12.kin.kin_b.refs_9_ = bf16[512,896]{1,0:T(8,128)(2,1)S(1)} collective-permute-done((bf16[512,896]{1,0:T(8,128)(2,1)S(1)}, bf16[512,896]{1,0:T(8,128)(2,1)S(1)}, u32[]{:S(2)}, u32[]{:S(2)}) %collective-permute-start.12) | collective-permute-done | bytes 917536 | tf_op jit(solution)/shard_map/ppermute | solution.py:1030
  135.1 6.9 %middle_body.1 = (f32[2,512,768]{2,1,0:T(8,128)}, bf16[2,512,768]{2,1,0:T(8,128)(2,1)S(1)}, bf16[2,64,1536]{2,1,0:T(8,128)(2,1)S(1)}, f32[2,64,768]{2,1,0:T(8,128)S(1)}, f32[2,64,128]{2,1,0:T(8,128)S(1)}) custom-call(s32[14]{0:T(128)S(1)} %concatenate.103.info, bf16[2,512,768]{2,1,0:T(8,128)(2,1)} %bitcast.50, bf16[2,512,768]{2,1,0:T(8,128)(2,1)} %bitcast.71, ...), custom_call_target="tpu_custom_call" | custom-call | flops 2000000000 | bytes 12000000 | tf_op jit(solution)/shard_map/middle_body/pallas_call | solution.py:74
  145.5 14.1 %ffn_local_body.1 = (f32[128,768]{1,0:T(8,128)S(1)}, f32[128,768]{1,0:T(8,128)S(1)}) custom-call(s32[14]{0:T(128)S(1)} %concatenate.103.info, bf16[128,1536]{1,0:T(8,128)(2,1)S(1)} %bitcast.47, bf16[128,1536]{1,0:T(8,128)(2,1)S(1)} %bitcast.48, bf16[768,8192]{1,0:T(8,128)(2,1)} %all-gather.8.cloned.1.call-done.wg.wu, ...), custom_call_target="tpu_custom_call" | custom-call | flops 4831838208 | bytes 18874368 | tf_op jit(solution)/shard_map/ffn_local_body/pallas_call | solution.py:74
  159.8 26.3 %ffn_body.1 = (f32[1024,768]{1,0:T(8,128)}, f32[1024,768]{1,0:T(8,128)}, bf16[4,768,256]{2,1,0:T(8,128)(2,1)S(1)}, bf16[4,768,256]{2,1,0:T(8,128)(2,1)}, bf16[2,...) custom-call(s32[14]{0:T(128)S(1)} %concatenate.103.info, bf16[1024,768]{1,0:T(8,128)(2,1)} %bitcast.68, ...), custom_call_target="tpu_custom_call" | custom-call | flops 14495514624 | bytes 18874368 | tf_op jit(solution)/shard_map/ffn_body/pallas_call | solution.py:74
  186.2 8.8 %plane_grads_body.1 = (bf16[2,768,256]{2,1,0:T(8,128)(2,1)S(1)}, bf16[2,768,256]{2,1,0:T(8,128)(2,1)}, bf16[2,768,256]{2,1,0:T(8,128)(2,1)S(1)}) custom-call(s32[14]{0:T(128)S(1)} %concatenate.103.info, bf16[512,1536]{1,0:T(8,128)(2,1)S(1)} %pad_maximum_fusion.near, bf16[512,1536]{1,0:T(8,128)(2,1)S(1)} %collective-permute-done.16.far, ...), custom_call_target="tpu_custom_call" | custom-call | flops 4831838208 | bytes 9000000 | tf_op jit(solution)/shard_map/plane_grads_body/pallas_call | solution.py:74
  195.5 11.3 %mid_back_body.1 = (bf16[2,512,768]{2,1,0:T(8,128)(2,1)}, f32[2,512,768]{2,1,0:T(8,128)}, bf16[2,512,512]{2,1,0:T(8,128)(2,1)S(1)}, bf16[2,64,768]{2,1,0:T(8,128...) custom-call(s32[14]{0:T(128)S(1)} %concatenate.103.info, ...), custom_call_target="tpu_custom_call" | custom-call | flops 3000000000 | bytes 22000000 | tf_op jit(solution)/shard_map/mid_back_body/pallas_call | solution.py:74
  210.8 10.3 %heavy_bwd_body.3 = (bf16[64,768]{1,0:T(8,128)(2,1)S(1)}, bf16[512,1536]{1,0:T(8,128)(2,1)S(1)}, bf16[512,1536]{1,0:T(8,128)(2,1)}, bf16[512,768]{1,0:T(8,128)(2,1)S(1)}, bf16[512,768]{1,0:T(8,128)(2,1)S(1)}) custom-call(s32[14]{0:T(128)S(1)} %concatenate.103.info, bf16[64,896]{1,0:T(8,128)(2,1)S(1)} %copy-done.42, bf16[512,896]{1,0:T(8,128)(2,1)S(1)} %copy-done.7, ...), custom_call_target="tpu_custom_call" | custom-call | flops 6499999744 | bytes 15000000 | tf_op jit(solution)/shard_map/heavy_bwd_body/pallas_call | solution.py:74
  222.3 10.3 %heavy_bwd_body.2 = (bf16[64,768]{1,0:T(8,128)(2,1)S(1)}, bf16[512,1536]{1,0:T(8,128)(2,1)S(1)}, bf16[512,1536]{1,0:T(8,128)(2,1)}, bf16[512,768]{1,0:T(8,128)(2,1)S(1)}, bf16[512,768]{1,0:T(8,128)(2,1)S(1)}) custom-call(s32[14]{0:T(128)S(1)} %concatenate.103.info, bf16[64,896]{1,0:T(8,128)(2,1)S(1)} %copy-done.40, bf16[512,896]{1,0:T(8,128)(2,1)S(1)} %copy-done.9, ...), custom_call_target="tpu_custom_call" | custom-call | flops 6499999744 | bytes 15000000 | tf_op jit(solution)/shard_map/heavy_bwd_body/pallas_call | solution.py:74
  245.0 22.4 %light_bwd_body.1 = (bf16[2,512,512]{2,1,0:T(8,128)(2,1)S(1)}, f32[2,512,1024]{2,1,0:T(8,128)}, bf16[2,128,1024]{2,1,0:T(8,128)(2,1)S(1)}, bf16[2,128,1024]{2,1,0:T(8,128)(2,1)S(1)}) custom-call(s32[14]{0:T(128)S(1)} %concatenate.103.info, bf16[2,512,1536]{2,1,0:T(8,128)(2,1)} %light_in_body.1.qkv, bf16[2,128,1024]{2,1,0:T(8,128)(2,1)S(1)} %copy-done.55, ...), custom_call_target="tpu_custom_call" | custom-call | flops 10000000000 | bytes 14000000 | tf_op jit(solution)/shard_map/light_bwd_body/pallas_call | solution.py:74
  279.7 14.3 %collective-permute-done.22 = bf16[1,6,64,256]{3,2,1,0:T(8,128)(2,1)S(1)} collective-permute-done((bf16[1,6,64,256]{3,2,1,0:T(8,128)(2,1)S(1)}, bf16[1,6,64,256]{3,2,1,0:T(8,128)(2,1)S(1)}, u32[]{:S(2)}, u32[]{:S(2)}) %collective-permute-start.22) | collective-permute-done | bytes 196640 | tf_op jit(solution)/shard_map/ppermute | solution.py:1030
  299.5 13.4 %heavy_grads_body.1 = (bf16[7,768,256]{2,1,0:T(8,128)(2,1)}, bf16[7,768,256]{2,1,0:T(8,128)(2,1)}) custom-call(s32[14]{0:T(128)S(1)} %concatenate.103.info, bf16[2,64,768]{2,1,0:T(8,128)(2,1)S(1)} %copy-done.38, bf16[2,64,768]{2,1,0:T(8,128)(2,1)S(1)} %pad_maximum_fusion.26.refs_1_.dhq, bf16[2,64,768]{2,1,0:T(8,128)(2,1)S(1)} %pad_maximum_fusion.25.ho.refs_2_, ...), custom_call_target="tpu_custom_call" | custom-call | flops 6499999744 | bytes 28000000 | tf_op jit(solution)/shard_map/heavy_grads_body/pallas_call | solution.py:74
  319.9 6.8 %light_join_body.1 = (bf16[2,512,1536]{2,1,0:T(8,128)(2,1)}, bf16[3,768,256]{2,1,0:T(8,128)(2,1)S(1)}, bf16[3,768,256]{2,1,0:T(8,128)(2,1)S(1)}) custom-call(s32[14]{0:T(128)S(1)} %concatenate.103.info, bf16[2,512,768]{2,1,0:T(8,128)(2,1)S(1)} %bitcast.53, bf16[8,768]{1,0:T(8,128)(2,1)S(1)} %pad_maximum_fusion.28.small, ...), custom_call_target="tpu_custom_call" | custom-call | flops 2415919104 | bytes 20000000 | tf_op jit(solution)/shard_map/light_join_body/pallas_call | solution.py:74
  335.6 6.1 %collective-permute-done.32 = bf16[2,64,768]{2,1,0:T(8,128)(2,1)S(1)} collective-permute-done((bf16[2,64,768]{2,1,0:T(8,128)(2,1)S(1)}, bf16[2,64,768]{2,1,0:T(8,128)(2,1)S(1)}, u32[]{:S(2)}, u32[]{:S(2)}) %collective-permute-start.32) | collective-permute-done | bytes 196640 | tf_op jit(solution)/shard_map/ppermute | solution.py:1030
  343.6 7.9 %collective-permute-done.30 = bf16[2,6,64,256]{3,2,1,0:T(8,128)(2,1)S(1)} collective-permute-done((bf16[2,6,64,256]{3,2,1,0:T(8,128)(2,1)S(1)}, bf16[2,6,64,256]{3,2,1,0:T(8,128)(2,1)S(1)}, u32[]{:S(2)}, u32[]{:S(2)}) %collective-permute-start.30) | collective-permute-done | bytes 393248 | tf_op jit(solution)/shard_map/ppermute | solution.py:1030
  352.2 8.1 %collective-permute-done.29 = bf16[2,6,64,256]{3,2,1,0:T(8,128)(2,1)S(1)} collective-permute-done((bf16[2,6,64,256]{3,2,1,0:T(8,128)(2,1)S(1)}, bf16[2,6,64,256]{3,2,1,0:T(8,128)(2,1)S(1)}, u32[]{:S(2)}, u32[]{:S(2)}) %collective-permute-start.29) | collective-permute-done | bytes 393248 | tf_op jit(solution)/shard_map/ppermute | solution.py:1030
  402.2 10.0 %collective-permute-done.37 = bf16[4,6,64,256]{3,2,1,0:T(8,128)(2,1)} collective-permute-done((bf16[4,6,64,256]{3,2,1,0:T(8,128)(2,1)}, bf16[4,6,64,256]{3,2,1,0:T(8,128)(2,1)}, u32[]{:S(2)}, u32[]{:S(2)}) %collective-permute-start.37) | collective-permute-done | bytes 786464 | tf_op jit(solution)/shard_map/ppermute | solution.py:1030
  417.6 11.7 %in_back_body.1 = (bf16[2,512,768]{2,1,0:T(8,128)(2,1)}, f32[8,768]{1,0:T(8,128)S(1)}) custom-call(s32[14]{0:T(128)S(1)} %concatenate.103.info, bf16[2,512,768]{2,1,0:T(8,128)(2,1)S(1)} %bitcast.54, f32[2,512,768]{2,1,0:T(8,128)} %get-tuple-element.230.refs_5_.dy, bf16[2,512,1536]{2,1,0:T(8,128)(2,1)} %get-tuple-element.286.dl, ...), custom_call_target="tpu_custom_call" | custom-call | flops 2600000000 | bytes 14000000 | tf_op jit(solution)/shard_map/in_back_body/pallas_call | solution.py:74
  448.2 37.1 %collective-permute-done.47 = bf16[4,5,48,256]{3,2,1,0:T(8,128)(2,1)} collective-permute-done((bf16[4,5,48,256]{3,2,1,0:T(8,128)(2,1)}, bf16[4,5,48,256]{3,2,1,0:T(8,128)(2,1)}, u32[]{:S(2)}, u32[]{:S(2)}) %collective-permute-start.47) | collective-permute-done | bytes 491552 | tf_op jit(solution)/shard_map/ppermute | solution.py:1030
  508.9 14.3 %unpack_plane_gu.1 = f32[384,8192]{1,0:T(8,128)} custom-call(s32[14]{0:T(128)S(1)} %concatenate.103.info, bf16[8,6,64,256]{3,2,1,0:T(8,128)(2,1)S(1)} %pad_maximum_fusion.1.refs_0_, bf16[8,6,64,256]{3,2,1,0:T(8,128)(2,1)} %collective-permute-done.50.refs_1_, bf16[8,6,64,256]{3,2,1,0:T(8,128)(2,1)S(1)} %pad_maximum_fusion.2.refs_2_, ...), custom_call_target="tpu_custom_call" | custom-call | bytes 18874368 | tf_op jit(solution)/shard_map/unpack_plane_gu/pallas_call | solution.py:74
  551.9 11.4 %collective-permute-done.73 = bf16[4,6,48,256]{3,2,1,0:T(8,128)(2,1)S(1)} collective-permute-done((bf16[4,6,48,256]{3,2,1,0:T(8,128)(2,1)S(1)}, bf16[4,6,48,256]{3,2,1,0:T(8,128)(2,1)S(1)}, u32[]{:S(2)}, u32[]{:S(2)}) %collective-permute-start.73) | collective-permute-done | bytes 589856 | tf_op jit(solution)/shard_map/ppermute | solution.py:1030
  566.4 18.7 %collective-permute-done.72.far = bf16[8,5,48,256]{3,2,1,0:T(8,128)(2,1)S(1)} collective-permute-done((bf16[8,5,48,256]{3,2,1,0:T(8,128)(2,1)S(1)}, bf16[8,5,48,256]{3,2,1,0:T(8,128)(2,1)S(1)}, u32[]{:S(2)}, u32[]{:S(2)}) %collective-permute-start.72) | collective-permute-done | bytes 983072 | tf_op jit(solution)/shard_map/ppermute | solution.py:1030
  (484 shorter events, 265.8 us)
Async XLA Ops:
  7.2 36.2 %all-gather.6.cloned.1.call-start = ((), (), s32[]{:S(2)}) async-start(), calls=%async_computation | async-start | bytes 1769472 | tf_op jit(solution)/shard_map/all_gather | solution.py:1354
  7.9 88.0 %all-gather.10.cloned.1.call-start = ((), (), s32[]{:S(2)}) async-start(), calls=%async_computation.2 | async-start | bytes 9437184 | tf_op jit(solution)/shard_map/all_gather | solution.py:1354
  8.7 87.2 %all-gather.8.cloned.1.call-start = ((), (), s32[]{:S(2)}) async-start(), calls=%async_computation.1 | async-start | bytes 18874368 | tf_op jit(solution)/shard_map/all_gather | solution.py:1354
  9.4 124.3 %all-gather.14.cloned.1.call-start = ((), (), s32[]{:S(2)}) async-start(), calls=%async_computation.4 | async-start | bytes 2359296 | tf_op jit(solution)/shard_map/all_gather | solution.py:1354
  10.0 123.7 %all-gather.12.cloned.1.call-start = ((), (), s32[]{:S(2)}) async-start(), calls=%async_computation.3 | async-start | bytes 4718592 | tf_op jit(solution)/shard_map/all_gather | solution.py:1354
  48.4 29.8 %collective-permute-start.7 = (bf16[2,128,1024]{2,1,0:T(8,128)(2,1)S(1)}, bf16[2,128,1024]{2,1,0:T(8,128)(2,1)S(1)}, u32[]{:S(2)}, u32[]{:S(2)}) collective-permute-start(bf16[2,128,1024]{2,1,0:T(8,128)(2,1)S(1)} %get-tuple-element.363), channel_id=1, source_target_pairs={{0,2},{2,4},{4,6},{6,8},{8,10},{10,12},{12,14},{14,16},{16,18},{18... | collective-permute-start | bytes 1572872 | tf_op jit(solution)/shard_map/ppermute | solution.py:1384
  209.7 28.1 %collective-permute-start.18 = (bf16[2,6,192,256]{3,2,1,0:T(8,128)(2,1)S(1)}, bf16[2,6,192,256]{3,2,1,0:T(8,128)(2,1)}, u32[]{:S(2)}, u32[]{:S(2)}) collective-permute-start(bf16[2,6,192,256]{3,2,1,0:T(8,128)(2,1)S(1)} %get-tuple-element.236), channel_id=1, source_target_pairs={{0,8},{2,10},{4,12},{6,14},{8,0},{10,2},{12,4},{14,6},{16,24},{18,... | collective-permute-start | bytes 3538952 | tf_op jit(solution)/shard_map/ppermute | solution.py:1030
  239.9 29.0 %collective-permute-start.19 = (bf16[1,6,192,256]{3,2,1,0:T(8,128)(2,1)}, bf16[1,6,192,256]{3,2,1,0:T(8,128)(2,1)}, u32[]{:S(2)}, u32[]{:S(2)}) collective-permute-start(bf16[1,6,192,256]{3,2,1,0:T(8,128)(2,1)} %add_convert_fusion.3), channel_id=1, source_target_pairs={{0,16},{2,18},{4,20},{6,22},{8,24},{10,26},{12,28},{14,30},{16,0},... | collective-permute-start | bytes 1769480 | tf_op jit(solution)/shard_map/ppermute | solution.py:1030
  271.3 41.7 %collective-permute-start.26 = (bf16[4,64,768]{2,1,0:T(8,128)(2,1)S(1)}, bf16[4,64,768]{2,1,0:T(8,128)(2,1)S(1)}, u32[]{:S(2)}, u32[]{:S(2)}) collective-permute-start(bf16[4,64,768]{2,1,0:T(8,128)(2,1)S(1)} %get-tuple-element.371), channel_id=1, source_target_pairs={{0,2},{2,0},{4,6},{6,4},{8,10},{10,8},{12,14},{14,12},{16,18},{18,... | collective-permute-start | bytes 1179656 | tf_op jit(solution)/shard_map/ppermute | solution.py:1030
  279.3 33.8 %collective-permute-start.25 = (bf16[4,64,768]{2,1,0:T(8,128)(2,1)S(1)}, bf16[4,64,768]{2,1,0:T(8,128)(2,1)S(1)}, u32[]{:S(2)}, u32[]{:S(2)}) collective-permute-start(bf16[4,64,768]{2,1,0:T(8,128)(2,1)S(1)} %get-tuple-element.373), channel_id=1, source_target_pairs={{0,4},{2,6},{4,0},{6,2},{8,12},{10,14},{12,8},{14,10},{16,20},{18,... | collective-permute-start | bytes 1179656 | tf_op jit(solution)/shard_map/ppermute | solution.py:1030
  279.6 33.4 %collective-permute-start.24 = (bf16[1,6,64,256]{3,2,1,0:T(8,128)(2,1)S(1)}, bf16[1,6,64,256]{3,2,1,0:T(8,128)(2,1)S(1)}, u32[]{:S(2)}, u32[]{:S(2)}) collective-permute-start(bf16[1,6,64,256]{3,2,1,0:T(8,128)(2,1)S(1)} %get-tuple-element.384), channel_id=1, source_target_pairs={{0,16},{2,18},{4,20},{6,22},{8,24},{10,26},{12,28},{14,30},{16,0},... | collective-permute-start | bytes 589832 | tf_op jit(solution)/shard_map/ppermute | solution.py:1030
  319.4 41.0 %collective-permute-start.34 = (bf16[7,768,256]{2,1,0:T(8,128)(2,1)}, bf16[7,768,256]{2,1,0:T(8,128)(2,1)}, u32[]{:S(2)}, u32[]{:S(2)}) collective-permute-start(bf16[7,768,256]{2,1,0:T(8,128)(2,1)} %get-tuple-element.279), channel_id=1, source_target_pairs={{0,1},{1,0},{2,3},{3,2},{4,5},{5,4},{6,7},{7,6},{8,9},{9,8},{10,11... | collective-permute-start | bytes 8257544 | tf_op jit(solution)/shard_map/ppermute | solution.py:1482
  319.4 54.2 %collective-permute-start.42 = (bf16[4,768,256]{2,1,0:T(8,128)(2,1)}, bf16[4,768,256]{2,1,0:T(8,128)(2,1)S(1)}, u32[]{:S(2)}, u32[]{:S(2)}) collective-permute-start(bf16[4,768,256]{2,1,0:T(8,128)(2,1)} %get-tuple-element.296), channel_id=1, source_target_pairs={{0,1},{1,0},{2,3},{3,2},{4,5},{5,4},{6,7},{7,6},{8,9},{9,8},{10,11... | collective-permute-start | bytes 4718600 | tf_op jit(solution)/shard_map/ppermute | solution.py:1442
  326.7 33.7 %collective-permute-start.35 = (bf16[3,768,256]{2,1,0:T(8,128)(2,1)S(1)}, bf16[3,768,256]{2,1,0:T(8,128)(2,1)S(1)}, u32[]{:S(2)}, u32[]{:S(2)}) collective-permute-start(bf16[3,768,256]{2,1,0:T(8,128)(2,1)S(1)} %get-tuple-element.284), channel_id=1, source_target_pairs={{0,1},{1,0},{2,3},{3,2},{4,5},{5,4},{6,7},{7,6},{8,9},{9,8},{10,11... | collective-permute-start | bytes 3538952 | tf_op jit(solution)/shard_map/ppermute | solution.py:1487
  361.4 36.6 %collective-permute-start.38 = (bf16[4,6,64,256]{3,2,1,0:T(8,128)(2,1)}, bf16[4,6,64,256]{3,2,1,0:T(8,128)(2,1)}, u32[]{:S(2)}, u32[]{:S(2)}) collective-permute-start(bf16[4,6,64,256]{3,2,1,0:T(8,128)(2,1)} %pad_maximum_fusion.11), channel_id=1, source_target_pairs={{0,2},{2,0},{4,6},{6,4},{8,10},{10,8},{12,14},{14,12},{16,18},{18,... | collective-permute-start | bytes 2359304 | tf_op jit(solution)/shard_map/ppermute | solution.py:1030
  367.2 48.1 %collective-permute-start.45 = (bf16[8,5,48,256]{3,2,1,0:T(8,128)(2,1)}, bf16[8,5,48,256]{3,2,1,0:T(8,128)(2,1)}, u32[]{:S(2)}, u32[]{:S(2)}) collective-permute-start(bf16[8,5,48,256]{3,2,1,0:T(8,128)(2,1)} %get-tuple-element.302), channel_id=1, source_target_pairs={{0,8},{2,10},{4,12},{6,14},{8,0},{10,2},{12,4},{14,6},{16,24},{18,... | collective-permute-start | bytes 2949128 | tf_op jit(solution)/shard_map/ppermute | solution.py:1030
  377.8 37.5 %collective-permute-start.43 = (bf16[8,5,48,256]{3,2,1,0:T(8,128)(2,1)}, bf16[8,5,48,256]{3,2,1,0:T(8,128)(2,1)}, u32[]{:S(2)}, u32[]{:S(2)}) collective-permute-start(bf16[8,5,48,256]{3,2,1,0:T(8,128)(2,1)} %get-tuple-element.297), channel_id=1, source_target_pairs={{0,4},{2,6},{4,0},{6,2},{8,12},{10,14},{12,8},{14,10},{16,20},{18,... | collective-permute-start | bytes 2949128 | tf_op jit(solution)/shard_map/ppermute | solution.py:1030
  378.0 37.3 %collective-permute-start.41 = (bf16[8,6,48,256]{3,2,1,0:T(8,128)(2,1)}, bf16[8,6,48,256]{3,2,1,0:T(8,128)(2,1)}, u32[]{:S(2)}, u32[]{:S(2)}) collective-permute-start(bf16[8,6,48,256]{3,2,1,0:T(8,128)(2,1)} %get-tuple-element.294), channel_id=1, source_target_pairs={{0,2},{2,0},{4,6},{6,4},{8,10},{10,8},{12,14},{14,12},{16,18},{18,... | collective-permute-start | bytes 3538952 | tf_op jit(solution)/shard_map/ppermute | solution.py:1030
  434.7 50.6 %collective-permute-start.46 = (bf16[4,6,48,256]{3,2,1,0:T(8,128)(2,1)}, bf16[4,6,48,256]{3,2,1,0:T(8,128)(2,1)}, u32[]{:S(2)}, u32[]{:S(2)}) collective-permute-start(bf16[4,6,48,256]{3,2,1,0:T(8,128)(2,1)} %get-tuple-element.364), channel_id=1, source_target_pairs={{0,4},{2,6},{4,0},{6,2},{8,12},{10,14},{12,8},{14,10},{16,20},{18,... | collective-permute-start | bytes 1769480 | tf_op jit(solution)/shard_map/ppermute | solution.py:1030
  438.3 61.6 %collective-permute-start.52 = (bf16[8,6,64,256]{3,2,1,0:T(8,128)(2,1)}, bf16[8,6,64,256]{3,2,1,0:T(8,128)(2,1)}, u32[]{:S(2)}, u32[]{:S(2)}) collective-permute-start(bf16[8,6,64,256]{3,2,1,0:T(8,128)(2,1)} %pad_maximum_fusion.3.refs_4_), channel_id=1, source_target_pairs={{0,8},{2,10},{4,12},{6,14},{8,0},{10,2},{12,4},{14,6},{16,24},{18,... | collective-permute-start | bytes 4718600 | tf_op jit(solution)/shard_map/ppermute | solution.py:1030
  440.8 59.1 %collective-permute-start.51 = (bf16[8,6,64,256]{3,2,1,0:T(8,128)(2,1)S(1)}, bf16[8,6,64,256]{3,2,1,0:T(8,128)(2,1)}, u32[]{:S(2)}, u32[]{:S(2)}) collective-permute-start(bf16[8,6,64,256]{3,2,1,0:T(8,128)(2,1)S(1)} %pad_maximum_fusion.2.refs_2_), channel_id=1, source_target_pairs={{0,4},{2,6},{4,0},{6,2},{8,12},{10,14},{12,8},{14,10},{16,20},{18,... | collective-permute-start | bytes 4718600 | tf_op jit(solution)/shard_map/ppermute | solution.py:1030
  442.8 57.2 %collective-permute-start.50 = (bf16[8,6,64,256]{3,2,1,0:T(8,128)(2,1)S(1)}, bf16[8,6,64,256]{3,2,1,0:T(8,128)(2,1)}, u32[]{:S(2)}, u32[]{:S(2)}) collective-permute-start(bf16[8,6,64,256]{3,2,1,0:T(8,128)(2,1)S(1)} %pad_maximum_fusion.1.refs_0_), channel_id=1, source_target_pairs={{0,2},{2,0},{4,6},{6,4},{8,10},{10,8},{12,14},{14,12},{16,18},{18,... | collective-permute-start | bytes 4718600 | tf_op jit(solution)/shard_map/ppermute | solution.py:1030
  447.0 38.4 %collective-permute-start.47 = (bf16[4,5,48,256]{3,2,1,0:T(8,128)(2,1)}, bf16[4,5,48,256]{3,2,1,0:T(8,128)(2,1)}, u32[]{:S(2)}, u32[]{:S(2)}) collective-permute-start(bf16[4,5,48,256]{3,2,1,0:T(8,128)(2,1)} %get-tuple-element.369), channel_id=1, source_target_pairs={{0,8},{2,10},{4,12},{6,14},{8,0},{10,2},{12,4},{14,6},{16,24},{18,... | collective-permute-start | bytes 1474568 | tf_op jit(solution)/shard_map/ppermute | solution.py:1030
  563.5 30.5 %collective-permute-start.74 = (bf16[8,6,48,256]{3,2,1,0:T(8,128)(2,1)S(1)}, bf16[8,6,48,256]{3,2,1,0:T(8,128)(2,1)S(1)}, u32[]{:S(2)}, u32[]{:S(2)}) collective-permute-start(bf16[8,6,48,256]{3,2,1,0:T(8,128)(2,1)S(1)} %pad_maximum_fusion.4.near), channel_id=1, source_target_pairs={{0,2},{2,0},{4,6},{6,4},{8,10},{10,8},{12,14},{14,12},{16,18},{18,... | collective-permute-start | bytes 3538952 | tf_op jit(solution)/shard_map/ppermute | solution.py:1030
  (174 other events, 2452.6 us)
Sparse Core Ops, SparseCore 0:
  9.6 11.9 all-gather.5
  23.1 17.9 all-gather.9
  42.6 26.0 all-gather.7
  70.1 10.9 all-gather.13
  82.5 13.2 all-gather.11

commit v4 on v3

--- a/solution.py
+++ b/solution.py
@@ -101,64 +101,76 @@
     return jax.ShapeDtypeStruct(tuple(shape), dtype)
 
 
-def routed_body(info, x, cols, small, w_own, w_got, q_out, kin_out, hq_out, h1k_out, gate_out):
+def routed_body(info, x, cols, small, q_out, kin_out, h1k_out, gate_out):
     micros, tok, width = x.shape
     rows = cols.shape[2]
     base = info[1]
     gain = small[3:4].astype(F32)
-    taken_q, taken_k = ([], [])
+    lane = iota((rows, LANES), 1)
     for m in range(micros):
         both = jnp.concatenate([cols[0, m], cols[1, m]], axis=0)
         got = mm(onehot_cols(both, base, tok), x[m])
-        taken_q.append(got[:rows])
-        taken_k.append(got[rows:])
-    xq, xk = (jnp.concatenate(taken_q, axis=0), jnp.concatenate(taken_k, axis=0))
-    low_q = (xq * inverse_rms(xq) * gain).astype(BF)
-    h1k = xk * inverse_rms(xk) * gain
-    low_k = h1k.astype(BF)
-    gate_q = jax.nn.sigmoid(
-        jnp.sum(low_q.astype(F32) * small[0:1].astype(F32), axis=-1, keepdims=True)
-    )
-    gate_k = jax.nn.sigmoid(
-        jnp.sum(low_k.astype(F32) * small[1:2].astype(F32), axis=-1, keepdims=True)
-    )
-    kin = (h1k * gate_k).astype(BF)
-    own_q, other_q = halves(info, low_q)
-    query = mm(own_q, w_own[...]) + mm(other_q, w_got[...])
-    lane = iota((rows, LANES), 1)
-    for m in range(micros):
-        part = slice(m * rows, (m + 1) * rows)
-        q_out[m, :, :width] = query[part].astype(BF)
-        kin_out[m, :, :width] = kin[part]
+        xq, xk = (got[:rows], got[rows:])
+        low_q = (xq * inverse_rms(xq) * gain).astype(BF)
+        h1k = xk * inverse_rms(xk) * gain
+        low_k = h1k.astype(BF)
+        gate_q = jax.nn.sigmoid(
+            jnp.sum(low_q.astype(F32) * small[0:1].astype(F32), axis=-1, keepdims=True)
+        )
+        gate_k = jax.nn.sigmoid(
+            jnp.sum(low_k.astype(F32) * small[1:2].astype(F32), axis=-1, keepdims=True)
+        )
         seg_q = segment(info, m, cols[0, m])
         seg_k = segment(info, m, cols[1, m])
+        q_out[m, :, :width] = low_q
         q_out[m, :, width:] = (lane == seg_q).astype(F32).astype(BF)
+        kin_out[m, :, :width] = (h1k * gate_k).astype(BF)
         kin_out[m, :, width:] = jnp.where((lane < 8) & (lane != seg_k), FAR, 0.0).astype(BF)
-        hq_out[m] = low_q[part]
-        h1k_out[m] = h1k[part]
-        gate_out[m] = jnp.where(lane == 0, gate_q[part], gate_k[part])
-
-
-def routed_in(info, x, cols, small, w_own, w_got):
+        h1k_out[m] = h1k
+        gate_out[m] = jnp.where(lane == 0, gate_q, gate_k)
+
+
+def routed_in(info, x, cols, small):
     micros, unused, width = x.shape
     rows = cols.shape[2]
     shapes = [
         sds((micros, rows, width + LANES), BF),
         sds((micros, rows, width + LANES), BF),
-        sds((micros, rows, width), BF),
         sds((micros, rows, width), F32),
         sds((micros, rows, LANES), F32),
     ]
-    args = (info, x, cols, small, w_own, w_got)
+    args = (info, x, cols, small)
     return call(
         routed_body,
         shapes,
         (1,),
-        [whole(a.shape) for a in args[1:4]] + [whole((w_own.shape[0], width))] * 2,
+        [whole(a.shape) for a in args[1:]],
         [whole(s.shape) for s in shapes],
         args,
-        flops=2 * micros * rows * width * width,
-        moved=5_000_000,
+        flops=200_000_000,
+        moved=3_000_000,
+    )
+
+
+def query_body(info, low, w_own, w_got, out):
+    width = 2 * w_own.shape[0]
+    for m in range(low.shape[0]):
+        own, other = halves(info, low[m, :, :width])
+        out[m, :, :width] = (mm(own, w_own[...]) + mm(other, w_got[...])).astype(BF)
+        out[m, :, width:] = low[m, :, width:]
+
+
+def query_project(info, low, w_own, w_got):
+    half = w_own.shape[0]
+    return call(
+        query_body,
+        sds(low.shape, BF),
+        (1,),
+        [whole(low.shape)] + [whole((half, 2 * half))] * 2,
+        whole(low.shape),
+        (info, low, w_own, w_got),
+        flops=2 * low.shape[0] * low.shape[1] * 4 * half * half,
+        moved=2_000_000,
     )
 
 
@@ -249,7 +261,7 @@
         lse_out[0, at, :] = stats
         return carry
 
-    lax.fori_loop(0, tok // WIN, block_step, 0)
+    [block_step(b, 0) for b in range(tok // WIN)]
 
 
 def light_fwd(info, qkv, before, after):
@@ -302,7 +314,7 @@
             dv[around, cut] += t_mm(probs.astype(BF), upper)
         return carry
 
-    lax.fori_loop(0, tok // WIN, block_step, 0)
+    [block_step(b, 0) for b in range(tok // WIN)]
     own_out[0, :, :inner] = dk[WIN : WIN + tok]
     own_out[0, :, inner:] = dv[WIN : WIN + tok]
     low_out[0, :, :inner] = dk[:WIN].astype(BF)
@@ -489,7 +501,7 @@
 
 
 def heavy_grads(info, hq, dhq, ho, dhy, lo, dy, kins, dkvs):
-    width = hq.shape[2]
+    width = dhq.shape[2]
     units = (dhq.shape[2] + dkvs[0].shape[1] + dhy.shape[2]) // COLS
     shapes = [sds((units // 2 + 1, width, COLS), BF)] * 2
     args = (info, hq, dhq, ho, dhy, lo, dy, *kins, *dkvs)
@@ -497,7 +509,7 @@
         heavy_grads_body,
         shapes,
         (1,),
-        [whole(a.shape) for a in args[1:]],
+        [whole(dhq.shape)] + [whole(a.shape) for a in args[2:]],
         [whole(s.shape) for s in shapes],
         args,
         flops=6_500_000_000,
@@ -505,13 +517,17 @@
     )
 
 
-def middle_body(info, x, up, cols, rows, small, gate, lo, lout, ho, hout, y_out, low_out, pay_out, hy_out, gf_out):
+def middle_body(info, x, up, cols, rows, small, gate, lo, lout, lout_got, ho, hout, y_out, low_out, pay_out, hy_out, gf_out):
     tok = x.shape[1]
     base = info[1]
     hy = mm(ho[0], hout[...])
     hy_out[0] = hy
     spread = onehot_rows(rows[0, 0], base, tok)
-    y = x[0].astype(F32) + mm(lo[0], lout[...]) + pick(spread, hy * gate[0, :, 0:1])
+    part = lout.shape[0]
+    own = lo[0, :, pl.ds(pl.multiple_of(info[0] * part, part), part)]
+    other = lo[0, :, pl.ds(pl.multiple_of((1 - info[0]) * part, part), part)]
+    light = mm(own, lout[...]) + mm(other, lout_got[...])
+    y = x[0].astype(F32) + light + pick(spread, hy * gate[0, :, 0:1])
     y_out[0] = y
     low = (y * inverse_rms(y) * small[4:5].astype(F32)).astype(BF)
     low_out[0] = low
@@ -531,7 +547,7 @@
     )
 
 
-def middle(info, x, up, cols, rows, small, gate, lo, lout, ho, hout):
+def middle(info, x, up, cols, rows, small, gate, lo, lout, lout_got, ho, hout):
     micros, tok, width = x.shape
     count = cols.shape[2]
     shapes = [
@@ -541,7 +557,7 @@
         sds((micros, count, width), F32),
         sds((micros, count, LANES), F32),
     ]
-    args = (info, x, up, cols, rows, small, gate, lo, lout, ho, hout)
+    args = (info, x, up, cols, rows, small, gate, lo, lout, lout_got, ho, hout)
     return call(
         middle_body,
         shapes,
@@ -555,6 +571,7 @@
             one_of(gate.shape),
             one_of(lo.shape),
             whole(lout.shape),
+            whole(lout_got.shape),
             one_of(ho.shape),
             whole(hout.shape),
         ],
@@ -703,6 +720,89 @@
     )
 
 
+def ffn_all_body(info, a, ct, w_gu, w_down, z_out, dh_out, own_gu, other_gu, own_dn, other_dn, turned, hid, slopes):
+    step = pl.program_id(0)
+    hidden, whole_width = w_down.shape
+    steps = hidden // COLS
+    half = steps // 2
+    width = whole_width // 2
+
+    @pl.when(step == 0)
+    def turn():
+        turned[...] = a[...].T
+
+    @pl.when(step < steps)
+    def block():
+        at = jnp.where(step < half, (1 - info[0]) * half + step, info[0] * half + step - half)
+        gate = pl.ds(pl.multiple_of(at * COLS, COLS), COLS)
+        upper = pl.ds(pl.multiple_of(hidden + at * COLS, COLS), COLS)
+        mixed, dg, du = hidden_both_ways(a[...], ct[...], w_gu[:, gate], w_gu[:, upper], w_down[gate])
+        hid[:, gate] = mixed
+        slopes[:, gate] = dg
+        slopes[:, upper] = du
+        down = t_mm(mixed, ct[...])
+
+        @pl.when(step < half)
+        def send():
+            pack_rows(other_dn, down)
+
+        @pl.when(step >= half)
+        def keep():
+            pack_rows(own_dn, down)
+
+        for target, side in ((own_gu, info[0]), (other_gu, 1 - info[0])):
+            rows = turned[pl.ds(pl.multiple_of(side * width, width), width)]
+            target[0, :width] = mm(rows, dg).astype(BF)
+            target[0, width:] = mm(rows, du).astype(BF)
+
+    @pl.when(step == steps)
+    def last():
+        z_out[...] = mm(hid[...], w_down[...]).astype(BF)
+        dh_out[...] = mm_t(slopes[...], w_gu[...]).astype(BF)
+
+
+def ffn_all(info, a, ct, w_gu, w_down):
+    rows, width = a.shape
+    hidden = w_down.shape[0]
+    steps = hidden // COLS
+    half = steps // 2
+
+    def natural(i, info):
+        return jnp.where(i < half, (1 - info[0]) * half + i, info[0] * half + jnp.minimum(i - half, half - 1))
+
+    unit = (1, width, COLS)
+    shapes = [
+        sds((rows, width), BF),
+        sds((rows, width), BF),
+        sds((steps,) + unit[1:], BF),
+        sds((steps,) + unit[1:], BF),
+        sds((half,) + unit[1:], BF),
+        sds((half,) + unit[1:], BF),
+    ]
+    return call(
+        ffn_all_body,
+        shapes,
+        (steps + 1,),
+        [whole(a.shape), whole(ct.shape), whole(w_gu.shape), whole(w_down.shape)],
+        [
+            whole((rows, width)),
+            whole((rows, width)),
+            pl.BlockSpec(unit, lambda i, info: (natural(i, info), 0, 0)),
+            pl.BlockSpec(unit, lambda i, info: (natural(i, info), 0, 0)),
+            pl.BlockSpec(unit, lambda i, info: (jnp.minimum(jnp.maximum(i - half, 0), half - 1), 0, 0)),
+            pl.BlockSpec(unit, lambda i, info: (jnp.minimum(i, half - 1), 0, 0)),
+        ],
+        (info, a, ct, w_gu, w_down),
+        scratch=[
+            pltpu.VMEM((width, rows), BF),
+            pltpu.VMEM((rows, hidden), BF),
+            pltpu.VMEM((rows, 2 * hidden), BF),
+        ],
+        flops=2 * 9 * rows * hidden * width,
+        moved=2 * 2 * 3 * hidden * width + rows * width * 12,
+    )
+
+
 def plane_grads_body(info, near, far, wg, wu, wd, own_gu, other_gu, dn):
     width = wg.shape[0]
     half = width // 2
@@ -781,7 +881,7 @@
 
 
 def mid_back_body(
-    info, y, up, z, dh2, zh, dff, ffr, gf, cols, rows, small, gate, lout, hout, hy, hq,
+    info, y, up, z, dh2, zh, dff, ffr, gf, cols, rows, small, gate, lout, lout_got, hout, hy, hq,
     out, dy_out, dlo_out, dho_out, dhy_out, dsq_out, part_out,
 ):
     tok = y.shape[1]
@@ -792,10 +892,10 @@
     values, top = (y[0], up[0].astype(F32))
     open_f = gf[0, :, 0:1]
     zhv = zh[0]
-    out[0] = (values + z[0] + pick(spread, zhv * open_f)).astype(BF)
+    out[0] = (values + z[0].astype(F32) + pick(spread, zhv * open_f)).astype(BF)
     taken = mm(take, up[0])
     dsf = jnp.sum(taken * zhv, axis=-1, keepdims=True) * open_f * (1.0 - open_f)
-    back = dh2[0] + pick(spread, dff[0] + dsf * small[2:3].astype(F32))
+    back = dh2[0].astype(F32) + pick(spread, dff[0] + dsf * small[2:3].astype(F32))
     inv = inverse_rms(values)
     scaled = back * small[4:5].astype(F32)
     mean = jnp.mean(values * scaled, axis=-1, keepdims=True)
@@ -803,7 +903,10 @@
     dy_out[0] = dy
     dgain = jnp.sum(back * values * inv, axis=0, keepdims=True)
     drf = jnp.sum(dsf * ffr[0].astype(F32), axis=0, keepdims=True)
-    dlo_out[0] = mm_t(dy.astype(BF), lout[...]).astype(BF)
+    part_in = lout.shape[0]
+    for weight, side in ((lout, info[0]), (lout_got, 1 - info[0])):
+        at = pl.ds(pl.multiple_of(side * part_in, part_in), part_in)
+        dlo_out[0, :, at] = mm_t(dy.astype(BF), weight[...]).astype(BF)
     dyq = pick(onehot_cols(cols[0, 0], base, tok), dy)
     open_q = gate[0, :, 0:1]
     dhy = (dyq * open_q).astype(BF)
@@ -824,13 +927,13 @@
         part_out[...] += part
 
 
-def mid_back(info, y, up, z, dh2, zh, dff, ffr, gf, cols, rows, small, gate, lout, hout, hy, hq):
+def mid_back(info, y, up, z, dh2, zh, dff, ffr, gf, cols, rows, small, gate, lout, lout_got, hout, hy, hq):
     micros, tok, width = y.shape
     count = cols.shape[2]
     shapes = [
         sds((micros, tok, width), BF),
         sds((micros, tok, width), F32),
-        sds((micros, tok, lout.shape[0]), BF),
+        sds((micros, tok, 2 * lout.shape[0]), BF),
         sds((micros, count, width), BF),
         sds((micros, count, width), BF),
         sds((micros, count, LANES), F32),
@@ -854,12 +957,13 @@
             whole(small.shape),
             one_of(gate.shape),
             whole(lout.shape),
+            whole(lout_got.shape),
             whole(hout.shape),
             one_of(hy.shape),
-            one_of(hq.shape),
+            pl.BlockSpec((1, count, width), lambda i, *u: (i, 0, 0)),
         ],
         [one_of(s.shape) for s in shapes[:-1]] + [whole(shapes[-1].shape)],
-        (info, y, up, z, dh2, zh, dff, ffr, gf, cols, rows, small, gate, lout, hout, hy, hq),
+        (info, y, up, z, dh2, zh, dff, ffr, gf, cols, rows, small, gate, lout, lout_got, hout, hy, hq),
         flops=3_000_000_000,
         moved=22_000_000,
     )
@@ -1169,76 +1273,64 @@
     )
 
 
-def unpack_plane_gu_body(orders, info, *refs):
-    out = refs[-1]
-    side, plane = (pl.program_id(0), pl.program_id(2))
-    for which, order in enumerate(orders):
-        near, far = refs[2 * which : 2 * which + 2]
-        blocks, size = near.shape[1:3]
-        per = out.shape[0] // 2
-        for level in range(2):
-            owner = (side * 2 + level) * 4 + plane
-            row = level * per + which * size
-
-            def write(source, row=row):
-                for block in range(blocks):
-                    out[row : row + size, block * COLS : (block + 1) * COLS] = source[block].astype(F32)
-
-            from_owner(info, order, near, far, owner, write)
-
-
-def unpack_plane_gu(info, orders, pairs, total):
-    slots, blocks, size, unused = pairs[0][0].shape
+def unpack_plane_gu_body(info, full, out):
+    sides, unused, planes, blocks, size, cols = full.shape
     turns = blocks // 3
-    spec = pl.BlockSpec(
-        (slots, turns, size, COLS), lambda s, h, q, info: (0, jnp.bitwise_xor(h, info[0]), 0, 0)
-    )
-    rows = 2 * len(pairs) * size
-    args = [info] + [part for pair in pairs for part in pair]
-    return call(
-        functools.partial(unpack_plane_gu_body, orders),
+    columns = out.shape[1] // sides
+    for side in range(sides):
+        for half in range(2):
+            first = jnp.bitwise_xor(half, info[0]) * turns
+            for plane in range(planes):
+                for turn in range(turns):
+                    at = side * columns + ((half * planes + plane) * turns + turn) * cols
+                    out[:, at : at + cols] = full[side, 0, plane, first + turn].astype(F32)
+
+
+def unpack_plane_gu(info, full, total):
+    levels, planes, blocks, size, unused = full.shape
+    rows, step = (2 * size, 48)
+    turns = size // step
+    view = full.reshape((2, levels // 2) + full.shape[1:])
+    return call(
+        unpack_plane_gu_body,
         sds((rows, 2 * total * COLS), F32),
-        (2, 2, 4),
-        [spec] * (len(args) - 1),
-        pl.BlockSpec((rows, turns * COLS), lambda s, h, q, *u: (0, s * 8 + h * 4 + q)),
-        args,
+        (rows // step,),
+        [
+            pl.BlockSpec(
+                (2, 1, planes, blocks, step, COLS), lambda r, *u: (0, r // turns, 0, 0, r % turns, 0)
+            )
+        ],
+        pl.BlockSpec((step, 2 * total * COLS), lambda r, *u: (r, 0)),
+        (info, view),
         moved=2 * rows * total * COLS * 6,
         name="unpack_plane_gu",
     )
 
 
-def unpack_plane_dn_body(orders, info, *refs):
-    out = refs[-1]
-    plane = pl.program_id(0)
-    for which, order in enumerate(orders):
-        near, far = refs[2 * which : 2 * which + 2]
-        blocks, size = near.shape[1:3]
-        for level in range(4):
-            owner = level * 4 + plane
-            cut, row = divmod((level * len(orders) + which) * size, COLS)
-
-            def write(source, cut=cut, row=row):
-                for block in range(blocks):
-                    at = block * COLS + row
-                    out[at : at + size, cut * COLS : (cut + 1) * COLS] = source[block].astype(F32)
-
-            from_owner(info, order, near, far, owner, write)
-
-
-def unpack_plane_dn(info, orders, pairs):
-    slots, blocks, size, unused = pairs[0][0].shape
+def unpack_plane_dn_body(info, full, out):
+    levels, unused, blocks, size, cols = full.shape
+    for level in range(levels):
+        for block in range(blocks):
+            for part in range(size // 64):
+                cut, row = divmod(level * size + part * 64, COLS)
+                at = block * COLS + row
+                out[at : at + 64, cut * COLS : (cut + 1) * COLS] = full[
+                    level, 0, block, part * 64 : (part + 1) * 64
+                ].astype(F32)
+
+
+def unpack_plane_dn(info, full):
+    levels, planes, blocks, size, unused = full.shape
     turns = blocks // 3
-    width = 4 * len(pairs) * size
-    spec = pl.BlockSpec((slots, turns, size, COLS), lambda q, *u: (0, 2, 0, 0))
-    args = [info] + [part for pair in pairs for part in pair]
-    return call(
-        functools.partial(unpack_plane_dn_body, orders),
-        sds((4 * turns * COLS, width), F32),
-        (4,),
-        [spec] * (len(args) - 1),
+    width = levels * size
+    return call(
+        unpack_plane_dn_body,
+        sds((planes * turns * COLS, width), F32),
+        (planes,),
+        [pl.BlockSpec((levels, 1, turns, size, COLS), lambda q, *u: (0, q, 2, 0, 0))],
         pl.BlockSpec((turns * COLS, width), lambda q, *u: (q, 0)),
-        args,
-        moved=4 * turns * COLS * width * 6,
+        (info, full),
+        moved=planes * turns * COLS * width * 6,
         name="unpack_plane_dn",
     )
 
@@ -1361,18 +1453,16 @@
         )
     else:
         small = full_of(vectors, 1)
-    h_own, h_got = pair_of(heavy_qkv)
-    l_own, l_got = pair_of(light_qkv)
-    w_lout, w_hout = (full_of(light_out), full_of(heavy_out))
-    w_hgu, w_hdown = (full_of(heavy_gu), full_of(heavy_down))
-    w_lgu, w_ldown = (full_of(light_gu), full_of(light_down))
-
     x, up = (tokens[:, 0], cotangent[:, 0])
     index = jnp.stack([q_index[:, 0], kv_index[:, 0], ff_index[:, 0]])
     cols, rows = (index[..., None], index[:, :, None, :])
-
-    q_pay, kin_pay, hq_in, h1k, gate = routed_in(info, x, cols, small, h_own, h_got)
-    kv_orders = ((8, 4, 2, 1), (8, 4, 1, 2))
+    hq_in, kin_pay, h1k, gate = routed_in(info, x, cols, small)
+    l_own, l_got = pair_of(light_qkv)
+    h_own, h_got = pair_of(heavy_qkv)
+    o_own, o_got = pair_of(light_out)
+    w_hout, w_hgu, w_hdown = (full_of(heavy_out), full_of(heavy_gu), full_of(heavy_down))
+    w_lgu, w_ldown = (full_of(light_gu), full_of(light_down))
+    kv_orders = ((8, 4, 1, 2), (8, 1, 2, 4))
     back_orders = [tuple(reversed(order)) for order in kv_orders]
     upward = [(i, i + 1) for i in range(count - 1)]
     downward = [(i + 1, i) for i in range(count - 1)]
@@ -1392,19 +1482,20 @@
         values = [kin_pay[m] for m in every]
         got = gather_start(values, back_orders, 0)
         qkv = light_in(info, x, small, l_own, l_got)
-        got, qkv, w_lout, w_hout = tied(got, qkv, w_lout, w_hout)
+        got, qkv = tied(got, qkv)
         before, after = rims(qkv)
         values = gather_end(values, got)
         got = gather_start(values, back_orders, 1)
-        got, before, after = tied(got, before, after)
+        q_pay = query_project(info, hq_in, h_own, h_got)
+        got, q_pay, w_hout = tied(got, q_pay, w_hout)
         values = gather_end(values, got)
         got = gather_start(values, back_orders, 2)
-        lo, light_lse = light_fwd(info, qkv, before, after)
-        got, lo, light_lse, w_hgu, w_hdown = tied(got, lo, light_lse, w_hgu, w_hdown)
+        got, before, after = tied(got, before, after)
         values = gather_end(values, got)
         got = gather_start(values, back_orders, 3)
         near_kv = [project(v) for v in values]
-        got, near_kv = tied(got, near_kv)
+        lo, light_lse = light_fwd(info, qkv, before, after)
+        got, near_kv, lo, light_lse, w_hgu, w_hdown = tied(got, near_kv, lo, light_lse, w_hgu, w_hdown)
         kins = list(zip(values, got))
         kvs = [(n, project(f)) for n, f in zip(near_kv, got)]
     else:
@@ -1416,10 +1507,11 @@
         qkv = light_in(info, x, small, l_own, l_got)
         before, after = rims(qkv)
         lo, light_lse = light_fwd(info, qkv, before, after)
+        q_pay = query_project(info, hq_in, h_own, h_got)
     heavy = [heavy_fwd(info, q_pay[m], kins[m], kvs[m]) for m in every]
     heavy, w_lgu, w_ldown = tied(heavy, w_lgu, w_ldown)
     ho = jnp.stack([h[0] for h in heavy])
-    y, low2, pay, hy, gf = middle(info, x, up, cols, rows, small, gate, lo, w_lout, ho, w_hout)
+    y, low2, pay, hy, gf = middle(info, x, up, cols, rows, small, gate, lo, o_own, o_got, ho, w_hout)
 
     def flat(value):
         return value.reshape(-1, value.shape[-1])
@@ -1436,7 +1528,7 @@
         zh, dff, hgu_own, hgu_send, hdn_own, hdn_send = ffn(
             info, flat(pay[..., :width]), flat(pay[..., width:]), w_hgu, w_hdown
         )
-    z, dh2, lgu_own, lgu_send, ldn_own, ldn_send = ffn(info, flat(low2), flat(up), w_lgu, w_ldown)
+    z, dh2, lgu_own, lgu_send, ldn_own, ldn_send = ffn_all(info, flat(low2), flat(up), w_lgu, w_ldown)
     if direct:
         far, z, dh2 = tied(far, z, dh2)
         lgu_got, ldn_got = (lax.ppermute(part, "wsh", swap) for part in (lgu_send, ldn_send))
@@ -1449,8 +1541,8 @@
         return value.reshape(micros, -1, value.shape[-1])
 
     out_tokens, dy, dlo, dho, dhy, dsq, part_two = mid_back(
-        info, y, up, by_micro(z), by_micro(dh2), by_micro(zh), by_micro(dff), pay, gf, cols, rows, small, gate, w_lout,
-        w_hout, hy, hq_in,
+        info, y, up, by_micro(z), by_micro(dh2), by_micro(zh), by_micro(dff), pay, gf, cols, rows, small, gate, o_own,
+        o_got, w_hout, hy, hq_in,
     )
     backs = [
         heavy_bwd(info, q_pay[m], kins[m], kvs[m], heavy[m][1], dho[m], h_own, h_got) for m in every
@@ -1467,40 +1559,37 @@
     dlq, dl_own, rim_low, rim_high = light_bwd(info, qkv, before, after, light_lse, dlo)
     if direct:
         got, got_back, dlq, dl_own, rim_low, rim_high = tied(got, got_back, dlq, dl_own, rim_low, rim_high)
+        keep, send = scatter_step(keep, got)
+        plane_full = lax.all_gather(keep[0], "ctx", axis=0, tiled=False)
+        plane_full = plane_full.reshape((count // 4, 4) + plane_full.shape[1:])
     got_low = lax.ppermute(rim_high, "ctx", upward)
     got_high = lax.ppermute(rim_low, "ctx", downward)
+    kin_all = [part for pair in kins for part in pair]
     if direct:
-        keep, send = scatter_step(keep, got)
-        third = keep.shape[2] // 3
-        values = [keep[:, :, t * third : (t + 1) * third] for t in range(3)]
         back = scatter_end(back, got_back)
-        got, got_back = (gather_start(values, orders, 0), scatter_start(back, back_orders, 1))
-    kin_all = [part for pair in kins for part in pair]
+        got_back = scatter_start(back, back_orders, 1)
     ha_own, ha_send = heavy_grads(info, hq_in, dhq, ho, dhy, lo, dy, kin_all, dkvs)
     if direct:
-        got, got_back, got_low, got_high, ha_own, ha_send = tied(got, got_back, got_low, got_high, ha_own, ha_send)
+        got_back, got_low, got_high, ha_own, ha_send = tied(got_back, got_low, got_high, ha_own, ha_send)
+        back = scatter_end(back, got_back)
+        got_back = scatter_start(back, back_orders, 2)
         ha_got = lax.ppermute(ha_send, "wsh", swap)
-        values, back = (gather_end(values, got), scatter_end(back, got_back))
-        got, got_back = (gather_start(values, orders, 1), scatter_start(back, back_orders, 2))
     dl, la_own, la_send = light_join(info, x, small, dlq, dl_own, got_low, got_high)
     if direct:
         la_got = lax.ppermute(la_send, "wsh", swap)
-        got, got_back, ha_got, la_got, dl = tied(got, got_back, ha_got, la_got, dl)
-        values, back = (gather_end(values, got), scatter_end(back, got_back))
-        got, got_back = (gather_start(values, orders, 2), scatter_start(back, back_orders, 3))
         second = [
             fold(info, orders[0], [(ha_own, ha_got, 0, 6)]),
             fold(info, orders[1], [(lgu_own, lgu_got, 0, 4), (ha_own, ha_got, 6, 1)]),
             fold(info, orders[2], [(la_own, la_got, 0, 3), (ldn_own, ldn_got, 0, 2)]),
         ]
+        got_back, second, dl = tied(got_back, second, dl)
         got_two = scatter_start(second, orders, 0)
-        got, got_back, got_two = tied(got, got_back, got_two)
-        values, second, back = (
-            gather_end(values, got), scatter_end(second, got_two), scatter_end(back, got_back)
-        )
+        back = scatter_end(back, got_back)
+        got_back = scatter_start(back, back_orders, 3)
+        got_two, got_back = tied(got_two, got_back)
+        second, back = (scatter_end(second, got_two), scatter_end(back, got_back))
+        got_two = scatter_start(second, orders, 1)
         dkin = jnp.concatenate([keep for keep, send in back], axis=0)
-        got = gather_start(values, orders, 3)
-        got_two = scatter_start(second, orders, 1)
     else:
         dkin = jnp.stack(
             [
@@ -1517,27 +1606,30 @@
         half = width // 2
         mine = lax.dynamic_slice_in_dim(vector, side * half, half, 1)
         given = lax.dynamic_slice_in_dim(vector, (1 - side) * half, half, 1)
+        got_two, mine, given = tied(got_two, mine, given)
+        second = scatter_end(second, got_two)
+        got_two = scatter_start(second, orders, 2)
         vector = mine + lax.ppermute(given, "wsh", swap)
         got_two, vector = tied(got_two, vector)
         second = scatter_end(second, got_two)
-        got_two, got_vector = (scatter_start(second, orders, 2), flipped(vector, 1))
-        got, got_two, vector, got_vector = tied(got, got_two, vector, got_vector)
-        chunks = list(zip(values, got))
-        second, vector = (scatter_end(second, got_two), vector + got_vector)
-        got_two, got_vector = (scatter_start(second, orders, 3), flipped(vector, 2))
-        g_hgu = unpack_plane_gu(info, orders, chunks, heavy_gu.shape[1] // (2 * COLS))
-        got_two, vector, got_vector, g_hgu = tied(got_two, vector, got_vector, g_hgu)
+        got_two, got_vector = (scatter_start(second, orders, 3), flipped(vector, 1))
+        got_two, vector, got_vector = tied(got_two, vector, got_vector)
         second, vector = (scatter_end(second, got_two), vector + got_vector)
         tails = [keep for keep, send in second]
-        got_two, got_vector = (gather_start(tails, orders, 0), flipped(vector, 4))
-        g_hdown = unpack_plane_dn(info, orders, chunks)
-        got_two, vector, got_vector, g_hdown = tied(got_two, vector, got_vector, g_hdown)
-        tails, vector = (gather_end(tails, got_two), vector + got_vector)
-        got_two, got_vector = (gather_start(tails, orders, 1), flipped(vector, 8))
+        got_two, got_vector = (gather_start(tails, orders, 0), flipped(vector, 2))
         got_two, vector, got_vector = tied(got_two, vector, got_vector)
         tails, vector = (gather_end(tails, got_two), vector + got_vector)
-        tails = gather_end(tails, gather_start(tails, orders, 2))
-        sums = list(zip(tails, gather_start(tails, orders, 3)))
+        got_two, got_vector = (gather_start(tails, orders, 1), flipped(vector, 4))
+        got_two, vector, got_vector = tied(got_two, vector, got_vector)
+        tails, vector = (gather_end(tails, got_two), vector + got_vector)
+        got_two, got_vector = (gather_start(tails, orders, 2), flipped(vector, 8))
+        g_hdown = unpack_plane_dn(info, plane_full)
+        got_two, vector, got_vector, g_hdown, plane_full = tied(got_two, vector, got_vector, g_hdown, plane_full)
+        tails, vector = (gather_end(tails, got_two), vector + got_vector)
+        got_two = gather_start(tails, orders, 3)
+        g_hgu = unpack_plane_gu(info, plane_full, heavy_gu.shape[1] // (2 * COLS))
+        got_two, g_hgu = tied(got_two, g_hgu)
+        sums = list(zip(tails, got_two))
         g_hqkv, g_hout = unpack_units(info, orders[0], sums[0], 0, widths)
         g_lgu = unpack_gu(info, orders[1], sums[1], 0, 4, 4, 0, None, 4)
         g_lout = unpack_dn(info, orders[1], sums[1], 4, 1, 1, 0, None, 1)

time: 609 us -> 553 us (0.908)
  waiting for transfers between devices: 200 us -> 170 us
  starting transfers between devices: 94.2 us -> 78.5 us
  other arithmetic: 37.6 us -> 26.5 us
  local copies, waits for them, and re-layouts: 23.4 us -> 30.8 us
  Pallas kernels: 229 us -> 222 us
    ppermute x61 -> x49, waiting for transfers between devices: 191 us -> 141 us  [flipped(): return lax.ppermute(value, 'ctx', [(i, i ^ bit) for i in range(size)])]
    ppermute x61 -> x49, starting transfers between devices: 82.6 us -> 65.2 us  [flipped(): return lax.ppermute(value, 'ctx', [(i, i ^ bit) for i in range(size)])]
    ppermute x1, waiting for transfers between devices: 0.01 us -> 9.67 us  [rims(): lax.ppermute(qkv[:, tok - WIN:, inner:], 'ctx', upward)]
    convert_element_type x8 -> x7, other arithmetic: 13 us -> 5.16 us  [scatter_step(): (keep[:half].astype(F32) + got[:half].astype(F32)).astype(BF)]
    pallas_call x28 -> x29, Pallas kernels: 223 us -> 216 us  [call(): pl.pallas_call(body, name=name or getattr(body, '__name__', 'kernel'), ou...]
    ppermute x1, waiting for transfers between devices: 5.63 us -> 11.8 us  [per_device(): got_low = lax.ppermute(rim_high, 'ctx', upward)]
    unnamed x237 -> x229, local copies, waits for them, and re-layouts: 17.8 us -> 23.8 us
  transfers between devices with their start and end apart: 80 -> 70, of which waited for: 31 -> 34; matrix products, arithmetic and copies ran while one was open for 6% -> 6% of each run, Pallas kernels for 33% -> 35%
where the time goes in v4:
time: 553 us; the launch traced here: 544 us
  Pallas kernels  222 us (40%)
  waiting for transfers between devices  170 us (31%)
  starting transfers between devices  78.5 us (14%)
  local copies, waits for them, and re-layouts  30.8 us (6%)
  other arithmetic  26.5 us (5%)
  between operations  16 us (3%)
    pallas_call x29, Pallas kernels, call(): pl.pallas_call(body, name=name or getattr(body, '__name__', 'kernel'), ou...  216 us
    ppermute x49, waiting for transfers between devices, flipped(): return lax.ppermute(value, 'ctx', [(i, i ^ bit) for i in range(size)])  141 us
    ppermute x49, starting transfers between devices, flipped(): return lax.ppermute(value, 'ctx', [(i, i ^ bit) for i in range(size)])  65.2 us
    unnamed x229, local copies, waits for them, and re-layouts  23.8 us
    ppermute x1, waiting for transfers between devices, per_device(): got_low = lax.ppermute(rim_high, 'ctx', upward)  11.8 us
  transfers between devices with their start and end apart: 70, of which 34 were waited for; matrix products, arithmetic and copies ran while one was open for 6% of the time, Pallas kernels for 35%

profile of v4, /device:TPU:0, one launch (start us, length us, event | category | flops | bytes accessed | tf_op | source)
XLA Modules:
  0.0 543.6 jit_solution(10960278335089270000)
XLA Ops:
  27.6 7.4 %light_in_body.1.qkv = bf16[2,512,1536]{2,1,0:T(8,128)(2,1)} custom-call(s32[14]{0:T(128)S(1)} %concatenate.70.info, bf16[2,512,768]{2,1,0:T(8,128)(2,1)S(1)} %bitcast.54, bf16[8,768]{1,0:T(8,128)(2,1)S(1)} %pad_maximum_fusion.19.small, bf16[384,1536]{1,0:T(8,128)(2,1)} %l_own.1, bf16[384,1536]{1,0:T(8,128)(2,1)} %collective-permute-done.3.w_got.l_got), custom_call_target="tpu_custom_call" | custom-call | flops 2415919104 | bytes 8000000 | tf_op jit(solution)/shard_map/light_in_body/pallas_call | solution.py:74
  61.5 9.7 %collective-permute-done.9.before = bf16[2,128,1024]{2,1,0:T(8,128)(2,1)} collective-permute-done((bf16[2,128,1024]{2,1,0:T(8,128)(2,1)}, bf16[2,128,1024]{2,1,0:T(8,128)(2,1)}, u32[]{:S(2)}, u32[]{:S(2)}) %collective-permute-start.9) | collective-permute-done | bytes 524320 | tf_op jit(solution)/shard_map/ppermute | solution.py:1474
  71.2 5.4 collective-permute-done.8
  92.8 15.4 %light_fwd_body.1 = (bf16[2,512,512]{2,1,0:T(8,128)(2,1)S(1)}, f32[2,512,128]{2,1,0:T(8,128)S(1)}) custom-call(s32[14]{0:T(128)S(1)} %concatenate.70.info, bf16[2,512,1536]{2,1,0:T(8,128)(2,1)S(1)} %copy-done.45, bf16[2,128,1024]{2,1,0:T(8,128)(2,1)} %collective-permute-done.9.before, bf16[2,128,1024]{2,1,0:T(8,128)(2,1)} %collective-permute-done.10.after), custom_call_target="tpu_custom_call" | custom-call | flops 4000000000 | bytes 6000000 | tf_op jit(solution)/shard_map/light_fwd_body/pallas_call | solution.py:74
  126.9 6.9 %middle_body.1 = (f32[2,512,768]{2,1,0:T(8,128)}, bf16[2,512,768]{2,1,0:T(8,128)(2,1)S(1)}, bf16[2,64,1536]{2,1,0:T(8,128)(2,1)S(1)}, f32[2,64,768]{2,1,0:T(8,128)S(1)}, f32[2,64,128]{2,1,0:T(8,128)S(1)}) custom-call(s32[14]{0:T(128)S(1)} %concatenate.70.info, bf16[2,512,768]{2,1,0:T(8,128)(2,1)} %bitcast.52, bf16[2,512,768]{2,1,0:T(8,128)(2,1)} %bitcast.75, ...), custom_call_target="tpu_custom_call" | custom-call | flops 2000000000 | bytes 12000000 | tf_op jit(solution)/shard_map/middle_body/pallas_call | solution.py:74
  138.5 14.1 %ffn_local_body.1 = (f32[128,768]{1,0:T(8,128)S(1)}, f32[128,768]{1,0:T(8,128)S(1)}) custom-call(s32[14]{0:T(128)S(1)} %concatenate.70.info, bf16[128,1536]{1,0:T(8,128)(2,1)S(1)} %bitcast.49, bf16[128,1536]{1,0:T(8,128)(2,1)S(1)} %bitcast.50, bf16[768,8192]{1,0:T(8,128)(2,1)} %all-gather.9.cloned.1.call-done.wg.wu, ...), custom_call_target="tpu_custom_call" | custom-call | flops 4831838208 | bytes 18874368 | tf_op jit(solution)/shard_map/ffn_local_body/pallas_call | solution.py:74
  154.9 23.3 %ffn_all_body.1 = (bf16[1024,768]{1,0:T(8,128)(2,1)S(1)}, bf16[1024,768]{1,0:T(8,128)(2,1)S(1)}, bf16[4,768,256]{2,1,0:T(8,128)(2,1)}, bf16[4,768,256]{2,1,0:T(8...) custom-call(s32[14]{0:T(128)S(1)} %concatenate.70.info, bf16[1024,768]{1,0:T(8,128)(2,1)} %bitcast.72, ...), custom_call_target="tpu_custom_call" | custom-call | flops 14495514624 | bytes 18874368 | tf_op jit(solution)/shard_map/ffn_all_body/pallas_call | solution.py:74
  178.2 9.4 %plane_grads_body.1 = (bf16[2,768,256]{2,1,0:T(8,128)(2,1)S(1)}, bf16[2,768,256]{2,1,0:T(8,128)(2,1)S(1)}, bf16[2,768,256]{2,1,0:T(8,128)(2,1)S(1)}) custom-call(s32[14]{0:T(128)S(1)} %concatenate.70.info, bf16[512,1536]{1,0:T(8,128)(2,1)S(1)} %pad_maximum_fusion.near, bf16[512,1536]{1,0:T(8,128)(2,1)S(1)} %collective-permute-done.17.far, ...), custom_call_target="tpu_custom_call" | custom-call | flops 4831838208 | bytes 9000000 | tf_op jit(solution)/shard_map/plane_grads_body/pallas_call | solution.py:74
  188.3 11.3 %mid_back_body.1 = (bf16[2,512,768]{2,1,0:T(8,128)(2,1)}, f32[2,512,768]{2,1,0:T(8,128)}, bf16[2,512,512]{2,1,0:T(8,128)(2,1)S(1)}, bf16[2,64,768]{2,1,0:T(8,128...) custom-call(s32[14]{0:T(128)S(1)} %concatenate.70.info, ...), custom_call_target="tpu_custom_call" | custom-call | flops 3000000000 | bytes 22000000 | tf_op jit(solution)/shard_map/mid_back_body/pallas_call | solution.py:74
  202.8 10.3 %heavy_bwd_body.3 = (bf16[64,768]{1,0:T(8,128)(2,1)S(1)}, bf16[512,1536]{1,0:T(8,128)(2,1)S(1)}, bf16[512,1536]{1,0:T(8,128)(2,1)}, bf16[512,768]{1,0:T(8,128)(2,1)S(1)}, bf16[512,768]{1,0:T(8,128)(2,1)S(1)}) custom-call(s32[14]{0:T(128)S(1)} %concatenate.70.info, bf16[64,896]{1,0:T(8,128)(2,1)S(1)} %copy-done.53, bf16[512,896]{1,0:T(8,128)(2,1)S(1)} %copy-done.6, ...), custom_call_target="tpu_custom_call" | custom-call | flops 6499999744 | bytes 15000000 | tf_op jit(solution)/shard_map/heavy_bwd_body/pallas_call | solution.py:74
  214.9 10.3 %heavy_bwd_body.2 = (bf16[64,768]{1,0:T(8,128)(2,1)S(1)}, bf16[512,1536]{1,0:T(8,128)(2,1)S(1)}, bf16[512,1536]{1,0:T(8,128)(2,1)}, bf16[512,768]{1,0:T(8,128)(2,1)S(1)}, bf16[512,768]{1,0:T(8,128)(2,1)S(1)}) custom-call(s32[14]{0:T(128)S(1)} %concatenate.70.info, bf16[64,896]{1,0:T(8,128)(2,1)S(1)} %copy-done.51, bf16[512,896]{1,0:T(8,128)(2,1)S(1)} %copy-done.9, ...), custom_call_target="tpu_custom_call" | custom-call | flops 6499999744 | bytes 15000000 | tf_op jit(solution)/shard_map/heavy_bwd_body/pallas_call | solution.py:74
  235.0 20.5 %light_bwd_body.1 = (bf16[2,512,512]{2,1,0:T(8,128)(2,1)S(1)}, f32[2,512,1024]{2,1,0:T(8,128)}, bf16[2,128,1024]{2,1,0:T(8,128)(2,1)S(1)}, bf16[2,128,1024]{2,1,0:T(8,128)(2,1)S(1)}) custom-call(s32[14]{0:T(128)S(1)} %concatenate.70.info, bf16[2,512,1536]{2,1,0:T(8,128)(2,1)} %light_in_body.1.qkv, bf16[2,128,1024]{2,1,0:T(8,128)(2,1)} %collective-permute-done.9.before, ...), custom_call_target="tpu_custom_call" | custom-call | flops 10000000000 | bytes 14000000 | tf_op jit(solution)/shard_map/light_bwd_body/pallas_call | solution.py:74
  277.1 13.7 %heavy_grads_body.1 = (bf16[7,768,256]{2,1,0:T(8,128)(2,1)}, bf16[7,768,256]{2,1,0:T(8,128)(2,1)}) custom-call(s32[14]{0:T(128)S(1)} %concatenate.70.info, bf16[2,64,896]{2,1,0:T(8,128)(2,1)S(1)} %copy-done.38, bf16[2,64,768]{2,1,0:T(8,128)(2,1)S(1)} %pad_maximum_fusion.17.refs_1_.dhq, bf16[2,64,768]{2,1,0:T(8,128)(2,1)S(1)} %copy-done.49, ...), custom_call_target="tpu_custom_call" | custom-call | flops 6499999744 | bytes 28000000 | tf_op jit(solution)/shard_map/heavy_grads_body/pallas_call | solution.py:74
  294.9 11.8 %collective-permute-done.25.got_low = bf16[2,128,1024]{2,1,0:T(8,128)(2,1)S(1)} collective-permute-done((bf16[2,128,1024]{2,1,0:T(8,128)(2,1)S(1)}, bf16[2,128,1024]{2,1,0:T(8,128)(2,1)S(1)}, u32[]{:S(2)}, u32[]{:S(2)}) %collective-permute-start.25) | collective-permute-done | bytes 524320 | tf_op jit(solution)/shard_map/ppermute | solution.py:1565
  307.2 6.8 %light_join_body.1 = (bf16[2,512,1536]{2,1,0:T(8,128)(2,1)}, bf16[3,768,256]{2,1,0:T(8,128)(2,1)S(1)}, bf16[3,768,256]{2,1,0:T(8,128)(2,1)S(1)}) custom-call(s32[14]{0:T(128)S(1)} %concatenate.70.info, bf16[2,512,768]{2,1,0:T(8,128)(2,1)S(1)} %bitcast.55, bf16[8,768]{1,0:T(8,128)(2,1)S(1)} %pad_maximum_fusion.19.small, bf16[2,512,512]{2,1,0:T(8,128)(2,1)S(1)} %copy-done.75, ...), custom_call_target="tpu_custom_call" | custom-call | flops 2415919104 | bytes 20000000 | tf_op jit(solution)/shard_map/light_join_body/pallas_call | solution.py:74
  323.2 5.4 kernel.3
  340.2 33.0 %collective-permute-done.37 = bf16[1,64,768]{2,1,0:T(8,128)(2,1)S(1)} collective-permute-done((bf16[1,64,768]{2,1,0:T(8,128)(2,1)S(1)}, bf16[1,64,768]{2,1,0:T(8,128)(2,1)S(1)}, u32[]{:S(2)}, u32[]{:S(2)}) %collective-permute-start.37) | collective-permute-done | bytes 98336 | tf_op jit(solution)/shard_map/ppermute | solution.py:1134
  376.8 18.4 %collective-permute-done.35 = bf16[8,5,48,256]{3,2,1,0:T(8,128)(2,1)} collective-permute-done((bf16[8,5,48,256]{3,2,1,0:T(8,128)(2,1)}, bf16[8,5,48,256]{3,2,1,0:T(8,128)(2,1)}, u32[]{:S(2)}, u32[]{:S(2)}) %collective-permute-start.35) | collective-permute-done | bytes 983072 | tf_op jit(solution)/shard_map/ppermute | solution.py:1134
  402.4 12.1 %in_back_body.1 = (bf16[2,512,768]{2,1,0:T(8,128)(2,1)}, f32[8,768]{1,0:T(8,128)S(1)}) custom-call(s32[14]{0:T(128)S(1)} %concatenate.70.info, bf16[2,512,768]{2,1,0:T(8,128)(2,1)S(1)} %bitcast.56, f32[2,512,768]{2,1,0:T(8,128)} %get-tuple-element.229.refs_5_.dy, bf16[2,512,1536]{2,1,0:T(8,128)(2,1)} %get-tuple-element.293.dl, ...), custom_call_target="tpu_custom_call" | custom-call | flops 2600000000 | bytes 14000000 | tf_op jit(solution)/shard_map/in_back_body/pallas_call | solution.py:74
  414.5 11.7 %collective-permute-done.39 = bf16[4,5,48,256]{3,2,1,0:T(8,128)(2,1)S(1)} collective-permute-done((bf16[4,5,48,256]{3,2,1,0:T(8,128)(2,1)S(1)}, bf16[4,5,48,256]{3,2,1,0:T(8,128)(2,1)S(1)}, u32[]{:S(2)}, u32[]{:S(2)}) %collective-permute-start.39) | collective-permute-done | bytes 491552 | tf_op jit(solution)/shard_map/ppermute | solution.py:1134
  461.1 10.4 %collective-permute-done.51 = bf16[1,5,48,256]{3,2,1,0:T(8,128)(2,1)S(1)} collective-permute-done((bf16[1,5,48,256]{3,2,1,0:T(8,128)(2,1)S(1)}, bf16[1,5,48,256]{3,2,1,0:T(8,128)(2,1)S(1)}, u32[]{:S(2)}, u32[]{:S(2)}) %collective-permute-start.51) | collective-permute-done | bytes 122912 | tf_op jit(solution)/shard_map/ppermute | solution.py:1134
  489.8 5.6 %unpack_plane_dn.1 = f32[2048,768]{1,0:T(8,128)} custom-call(s32[14]{0:T(128)S(1)} %concatenate.70.info, bf16[4,4,6,192,256]{4,3,2,1,0:T(8,128)(2,1)} %bitcast.73), custom_call_target="tpu_custom_call" | custom-call | bytes 9437184 | tf_op jit(solution)/shard_map/unpack_plane_dn/pallas_call | solution.py:74
  505.0 10.8 %unpack_plane_gu.1 = f32[384,8192]{1,0:T(8,128)} custom-call(s32[14]{0:T(128)S(1)} %concatenate.70.info, bf16[2,2,4,6,192,256]{5,4,3,2,1,0:T(8,128)(2,1)} %bitcast.74), custom_call_target="tpu_custom_call" | custom-call | bytes 18874368 | tf_op jit(solution)/shard_map/unpack_plane_gu/pallas_call | solution.py:74
  515.7 7.4 %collective-permute-done.62.far = bf16[8,5,48,256]{3,2,1,0:T(8,128)(2,1)S(1)} collective-permute-done((bf16[8,5,48,256]{3,2,1,0:T(8,128)(2,1)S(1)}, bf16[8,5,48,256]{3,2,1,0:T(8,128)(2,1)S(1)}, u32[]{:S(2)}, u32[]{:S(2)}) %collective-permute-start.62) | collective-permute-done | bytes 983072 | tf_op jit(solution)/shard_map/ppermute | solution.py:1134
  (447 shorter events, 236.5 us)
Async XLA Ops:
  7.2 45.7 %all-gather.7.cloned.1.call-start = ((), (), s32[]{:S(2)}) async-start(), calls=%async_computation | async-start | bytes 1769472 | tf_op jit(solution)/shard_map/all_gather | solution.py:1446
  7.9 104.0 %all-gather.11.cloned.1.call-start = ((), (), s32[]{:S(2)}) async-start(), calls=%async_computation.2 | async-start | bytes 9437184 | tf_op jit(solution)/shard_map/all_gather | solution.py:1446
  8.7 103.2 %all-gather.9.cloned.1.call-start = ((), (), s32[]{:S(2)}) async-start(), calls=%async_computation.1 | async-start | bytes 18874368 | tf_op jit(solution)/shard_map/all_gather | solution.py:1446
  9.4 116.2 %all-gather.15.cloned.1.call-start = ((), (), s32[]{:S(2)}) async-start(), calls=%async_computation.4 | async-start | bytes 2359296 | tf_op jit(solution)/shard_map/all_gather | solution.py:1446
  10.0 115.6 %all-gather.13.cloned.1.call-start = ((), (), s32[]{:S(2)}) async-start(), calls=%async_computation.3 | async-start | bytes 4718592 | tf_op jit(solution)/shard_map/all_gather | solution.py:1446
  10.6 40.5 %collective-permute-start.6 = (bf16[384,2304]{1,0:T(8,128)(2,1)S(1)}, bf16[384,2304]{1,0:T(8,128)(2,1)S(1)}, u32[]{:S(2)}, u32[]{:S(2)}) collective-permute-start(bf16[384,2304]{1,0:T(8,128)(2,1)S(1)} %copy-done), channel_id=1, source_target_pairs={{0,1},{1,0},{2,3},{3,2},{4,5},{5,4},{6,7},{7,6},{8,9},{9,8},{10,11... | collective-permute-start | bytes 5308424 | tf_op jit(solution)/shard_map/ppermute | solution.py:1441
  11.9 478.0 %all-gather.17.cloned.1.call-start = ((), (), s32[]{:S(2)}) async-start(), calls=%async_computation.5 | async-start | bytes 10027008 | tf_op jit(solution)/shard_map/all_gather | solution.py:1563
  59.0 66.7 %collective-permute-start.13 = (bf16[256,768]{1,0:T(8,128)(2,1)}, bf16[256,768]{1,0:T(8,128)(2,1)}, u32[]{:S(2)}, u32[]{:S(2)}) collective-permute-start(bf16[256,768]{1,0:T(8,128)(2,1)} %lout.3), channel_id=1, source_target_pairs={{0,1},{1,0},{2,3},{3,2},{4,5},{5,4},{6,7},{7,6},{8,9},{9,8},{10,11... | collective-permute-start | bytes 1179656 | tf_op jit(solution)/shard_map/ppermute | solution.py:1441
  82.0 28.0 %collective-permute-start.12 = (bf16[512,896]{1,0:T(8,128)(2,1)S(1)}, bf16[512,896]{1,0:T(8,128)(2,1)S(1)}, u32[]{:S(2)}, u32[]{:S(2)}) collective-permute-start(bf16[512,896]{1,0:T(8,128)(2,1)S(1)} %pad_maximum_fusion.5.kin.kin_a.refs_8_), channel_id=1, source_target_pairs={{0,8},{2,10},{4,12},{6,14},{8,0},{10,2},{12,4},{14,6},{16,24},{18,... | collective-permute-start | bytes 2752520 | tf_op jit(solution)/shard_map/ppermute | solution.py:1134
  84.2 26.7 %collective-permute-start.11 = (bf16[512,896]{1,0:T(8,128)(2,1)S(1)}, bf16[512,896]{1,0:T(8,128)(2,1)S(1)}, u32[]{:S(2)}, u32[]{:S(2)}) collective-permute-start(bf16[512,896]{1,0:T(8,128)(2,1)S(1)} %pad_maximum_fusion.4.kin.kin_a.refs_6_), channel_id=1, source_target_pairs={{0,4},{2,6},{4,0},{6,2},{8,12},{10,14},{12,8},{14,10},{16,20},{18,... | collective-permute-start | bytes 2752520 | tf_op jit(solution)/shard_map/ppermute | solution.py:1134
  201.9 28.0 %collective-permute-start.19 = (bf16[2,6,192,256]{3,2,1,0:T(8,128)(2,1)S(1)}, bf16[2,6,192,256]{3,2,1,0:T(8,128)(2,1)S(1)}, u32[]{:S(2)}, u32[]{:S(2)}) collective-permute-start(bf16[2,6,192,256]{3,2,1,0:T(8,128)(2,1)S(1)} %get-tuple-element.234), channel_id=1, source_target_pairs={{0,8},{2,10},{4,12},{6,14},{8,0},{10,2},{12,4},{14,6},{16,24},{18,... | collective-permute-start | bytes 3538952 | tf_op jit(solution)/shard_map/ppermute | solution.py:1134
  230.1 28.3 %collective-permute-start.20 = (bf16[1,6,192,256]{3,2,1,0:T(8,128)(2,1)S(1)}, bf16[1,6,192,256]{3,2,1,0:T(8,128)(2,1)}, u32[]{:S(2)}, u32[]{:S(2)}) collective-permute-start(bf16[1,6,192,256]{3,2,1,0:T(8,128)(2,1)S(1)} %add_convert_fusion.4), channel_id=1, source_target_pairs={{0,16},{2,18},{4,20},{6,22},{8,24},{10,26},{12,28},{14,30},{16,0},... | collective-permute-start | bytes 1769480 | tf_op jit(solution)/shard_map/ppermute | solution.py:1134
  232.8 25.5 %collective-permute-start.21 = (bf16[8,64,768]{2,1,0:T(8,128)(2,1)S(1)}, bf16[8,64,768]{2,1,0:T(8,128)(2,1)S(1)}, u32[]{:S(2)}, u32[]{:S(2)}) collective-permute-start(bf16[8,64,768]{2,1,0:T(8,128)(2,1)S(1)} %bitcast.71), channel_id=1, source_target_pairs={{0,4},{2,6},{4,0},{6,2},{8,12},{10,14},{12,8},{14,10},{16,20},{18,... | collective-permute-start | bytes 2359304 | tf_op jit(solution)/shard_map/ppermute | solution.py:1134
  233.5 29.7 %collective-permute-start.22 = (bf16[8,64,768]{2,1,0:T(8,128)(2,1)S(1)}, bf16[8,64,768]{2,1,0:T(8,128)(2,1)S(1)}, u32[]{:S(2)}, u32[]{:S(2)}) collective-permute-start(bf16[8,64,768]{2,1,0:T(8,128)(2,1)S(1)} %bitcast.70), channel_id=1, source_target_pairs={{0,8},{2,10},{4,12},{6,14},{8,0},{10,2},{12,4},{14,6},{16,24},{18,... | collective-permute-start | bytes 2359304 | tf_op jit(solution)/shard_map/ppermute | solution.py:1134
  273.3 33.3 %collective-permute-start.25 = (bf16[2,128,1024]{2,1,0:T(8,128)(2,1)S(1)}, bf16[2,128,1024]{2,1,0:T(8,128)(2,1)S(1)}, u32[]{:S(2)}, u32[]{:S(2)}) collective-permute-start(bf16[2,128,1024]{2,1,0:T(8,128)(2,1)S(1)} %copy-done.67), channel_id=1, source_target_pairs={{0,2},{2,4},{4,6},{6,8},{8,10},{10,12},{12,14},{14,16},{16,18},{18... | collective-permute-start | bytes 1572872 | tf_op jit(solution)/shard_map/ppermute | solution.py:1565
  275.5 31.2 %collective-permute-start.26 = (bf16[2,128,1024]{2,1,0:T(8,128)(2,1)S(1)}, bf16[2,128,1024]{2,1,0:T(8,128)(2,1)S(1)}, u32[]{:S(2)}, u32[]{:S(2)}) collective-permute-start(bf16[2,128,1024]{2,1,0:T(8,128)(2,1)S(1)} %copy-done.65), channel_id=1, source_target_pairs={{2,0},{4,2},{6,4},{8,6},{10,8},{12,10},{14,12},{16,14},{18,16},{20... | collective-permute-start | bytes 1572872 | tf_op jit(solution)/shard_map/ppermute | solution.py:1566
  333.6 61.6 %collective-permute-start.33 = (bf16[8,6,48,256]{3,2,1,0:T(8,128)(2,1)}, bf16[8,6,48,256]{3,2,1,0:T(8,128)(2,1)}, u32[]{:S(2)}, u32[]{:S(2)}) collective-permute-start(bf16[8,6,48,256]{3,2,1,0:T(8,128)(2,1)} %get-tuple-element.295), channel_id=1, source_target_pairs={{0,2},{2,0},{4,6},{6,4},{8,10},{10,8},{12,14},{14,12},{16,18},{18,... | collective-permute-start | bytes 3538952 | tf_op jit(solution)/shard_map/ppermute | solution.py:1134
  336.0 40.8 %collective-permute-start.34 = (bf16[8,5,48,256]{3,2,1,0:T(8,128)(2,1)}, bf16[8,5,48,256]{3,2,1,0:T(8,128)(2,1)}, u32[]{:S(2)}, u32[]{:S(2)}) collective-permute-start(bf16[8,5,48,256]{3,2,1,0:T(8,128)(2,1)} %get-tuple-element.296), channel_id=1, source_target_pairs={{0,4},{2,6},{4,0},{6,2},{8,12},{10,14},{12,8},{14,10},{16,20},{18,... | collective-permute-start | bytes 2949128 | tf_op jit(solution)/shard_map/ppermute | solution.py:1134
  336.0 59.2 %collective-permute-start.35 = (bf16[8,5,48,256]{3,2,1,0:T(8,128)(2,1)}, bf16[8,5,48,256]{3,2,1,0:T(8,128)(2,1)}, u32[]{:S(2)}, u32[]{:S(2)}) collective-permute-start(bf16[8,5,48,256]{3,2,1,0:T(8,128)(2,1)} %get-tuple-element.297), channel_id=1, source_target_pairs={{0,8},{2,10},{4,12},{6,14},{8,0},{10,2},{12,4},{14,6},{16,24},{18,... | collective-permute-start | bytes 2949128 | tf_op jit(solution)/shard_map/ppermute | solution.py:1134
  337.1 36.1 %collective-permute-start.37 = (bf16[1,64,768]{2,1,0:T(8,128)(2,1)S(1)}, bf16[1,64,768]{2,1,0:T(8,128)(2,1)S(1)}, u32[]{:S(2)}, u32[]{:S(2)}) collective-permute-start(bf16[1,64,768]{2,1,0:T(8,128)(2,1)S(1)} %add_convert_fusion.35), channel_id=1, source_target_pairs={{0,16},{2,18},{4,20},{6,22},{8,24},{10,26},{12,28},{14,30},{16,0},... | collective-permute-start | bytes 294920 | tf_op jit(solution)/shard_map/ppermute | solution.py:1134
  338.2 38.6 %collective-permute-start.36 = (bf16[1,64,768]{2,1,0:T(8,128)(2,1)S(1)}, bf16[1,64,768]{2,1,0:T(8,128)(2,1)S(1)}, u32[]{:S(2)}, u32[]{:S(2)}) collective-permute-start(bf16[1,64,768]{2,1,0:T(8,128)(2,1)S(1)} %add_convert_fusion.36), channel_id=1, source_target_pairs={{0,16},{2,18},{4,20},{6,22},{8,24},{10,26},{12,28},{14,30},{16,0},... | collective-permute-start | bytes 294920 | tf_op jit(solution)/shard_map/ppermute | solution.py:1134
  397.0 29.2 %collective-permute-start.39 = (bf16[4,5,48,256]{3,2,1,0:T(8,128)(2,1)S(1)}, bf16[4,5,48,256]{3,2,1,0:T(8,128)(2,1)S(1)}, u32[]{:S(2)}, u32[]{:S(2)}) collective-permute-start(bf16[4,5,48,256]{3,2,1,0:T(8,128)(2,1)S(1)} %get-tuple-element.381), channel_id=1, source_target_pairs={{0,8},{2,10},{4,12},{6,14},{8,0},{10,2},{12,4},{14,6},{16,24},{18,... | collective-permute-start | bytes 1474568 | tf_op jit(solution)/shard_map/ppermute | solution.py:1134
  398.7 27.5 %collective-permute-start.40 = (bf16[4,5,48,256]{3,2,1,0:T(8,128)(2,1)S(1)}, bf16[4,5,48,256]{3,2,1,0:T(8,128)(2,1)S(1)}, u32[]{:S(2)}, u32[]{:S(2)}) collective-permute-start(bf16[4,5,48,256]{3,2,1,0:T(8,128)(2,1)S(1)} %get-tuple-element.379), channel_id=1, source_target_pairs={{0,2},{2,0},{4,6},{6,4},{8,10},{10,8},{12,14},{14,12},{16,18},{18,... | collective-permute-start | bytes 1474568 | tf_op jit(solution)/shard_map/ppermute | solution.py:1134
  400.5 25.7 %collective-permute-start.38 = (bf16[4,6,48,256]{3,2,1,0:T(8,128)(2,1)S(1)}, bf16[4,6,48,256]{3,2,1,0:T(8,128)(2,1)S(1)}, u32[]{:S(2)}, u32[]{:S(2)}) collective-permute-start(bf16[4,6,48,256]{3,2,1,0:T(8,128)(2,1)S(1)} %get-tuple-element.376), channel_id=1, source_target_pairs={{0,4},{2,6},{4,0},{6,2},{8,12},{10,14},{12,8},{14,10},{16,20},{18,... | collective-permute-start | bytes 1769480 | tf_op jit(solution)/shard_map/ppermute | solution.py:1134
  (160 other events, 1729.0 us)
Sparse Core Ops, SparseCore 0:
  9.6 11.9 all-gather.6
  23.1 17.9 all-gather.10
  42.6 26.6 all-gather.8
  70.7 10.4 all-gather.14
  82.5 13.2 all-gather.12
  266.4 158.7 all-gather.16

commit v5 on v4

--- a/solution.py
+++ b/solution.py
@@ -232,17 +232,14 @@
     return jnp.where(low_lane, values[:rows], values[rows:])
 
 
-def light_fwd_body(info, qkv, before, after, out, lse_out, near):
+def light_fwd_blocks(info, qkv, near, blocks, emit):
     micro = pl.program_id(0)
-    tok = qkv.shape[1]
-    inner = out.shape[2]
-    fill_near(near, qkv, before, after)
+    inner = near.shape[1] // 2
     low_lane = iota((WIN, LANES), 1) < HD
     lane = iota((WIN, LANES), 1)
-
-    def block_step(block, carry):
-        at = pl.ds(pl.multiple_of(block * WIN, WIN), WIN)
-        around = pl.ds(pl.multiple_of(block * WIN, WIN), 3 * WIN)
+    for place, block in enumerate(blocks):
+        at = slice(block * WIN, (block + 1) * WIN)
+        around = slice(block * WIN, (block + 3) * WIN)
         bias = light_bias(info, micro, block)
         stats = jnp.zeros((WIN, LANES), F32)
         for pair in range(inner // LANES):
@@ -254,46 +251,87 @@
             total = jnp.sum(weights, axis=-1, keepdims=True)
             value = near[around, inner + pair * LANES : inner + (pair + 1) * LANES]
             mixed = mm((weights * (1.0 / total)).astype(BF), value)
-            out[0, at, cut] = merged(mixed, low_lane).astype(BF)
+            emit(place, cut, merged(mixed, low_lane).astype(BF))
             lse = top + jnp.log(total)
             stats = jnp.where(lane == 2 * pair, lse[:WIN], stats)
             stats = jnp.where(lane == 2 * pair + 1, lse[WIN:], stats)
-        lse_out[0, at, :] = stats
-        return carry
-
-    [block_step(b, 0) for b in range(tok // WIN)]
-
-
-def light_fwd(info, qkv, before, after):
+        emit(place, None, stats)
+
+
+def light_inner_body(info, qkv, out, lse_out, near):
+    tok = qkv.shape[1]
+    inner = out.shape[2]
+    near[WIN : WIN + tok] = qkv[0, :, inner:]
+
+    def emit(place, cut, value):
+        rows = slice(place * WIN, (place + 1) * WIN)
+        if cut is None:
+            lse_out[0, rows] = value
+        else:
+            out[0, rows, cut] = value
+
+    light_fwd_blocks(info, qkv, near, range(1, tok // WIN - 1), emit)
+
+
+def light_outer_body(info, qkv, before, after, done, lse_done, out, lse_out, near):
+    tok = qkv.shape[1]
+    fill_near(near, qkv, before, after)
+    out[0, WIN : tok - WIN] = done[0]
+    lse_out[0, WIN : tok - WIN] = lse_done[0]
+    blocks = (0, tok // WIN - 1)
+
+    def emit(place, cut, value):
+        rows = slice(blocks[place] * WIN, (blocks[place] + 1) * WIN)
+        if cut is None:
+            lse_out[0, rows] = value
+        else:
+            out[0, rows, cut] = value
+
+    light_fwd_blocks(info, qkv, near, blocks, emit)
+
+
+def light_inner(info, qkv):
+    micros, tok, columns = qkv.shape
+    inner = columns // 3
+    shapes = [sds((micros, tok - 2 * WIN, inner), BF), sds((micros, tok - 2 * WIN, LANES), F32)]
+    return call(
+        light_inner_body,
+        shapes,
+        (micros,),
+        [one_of(qkv.shape)],
+        [one_of(a.shape) for a in shapes],
+        (info, qkv),
+        scratch=[pltpu.VMEM((tok + 2 * WIN, 2 * inner), BF)],
+        flops=2_000_000_000,
+        moved=4_000_000,
+    )
+
+
+def light_outer(info, qkv, before, after, done):
     micros, tok, columns = qkv.shape
     inner = columns // 3
     shapes = [sds((micros, tok, inner), BF), sds((micros, tok, LANES), F32)]
-    args = (info, qkv, before, after)
-    return call(
-        light_fwd_body,
+    args = (info, qkv, before, after, *done)
+    return call(
+        light_outer_body,
         shapes,
         (micros,),
         [one_of(a.shape) for a in args[1:]],
-        [one_of(s.shape) for s in shapes],
+        [one_of(a.shape) for a in shapes],
         args,
         scratch=[pltpu.VMEM((tok + 2 * WIN, 2 * inner), BF)],
-        flops=4_000_000_000,
+        flops=2_000_000_000,
         moved=6_000_000,
     )
 
 
-def light_bwd_body(info, qkv, before, after, lse, grad, dq_out, own_out, low_out, high_out, near, dk, dv):
+def light_bwd_blocks(info, qkv, lse, grad, near, dk, dv, blocks, emit):
     micro = pl.program_id(0)
-    tok = qkv.shape[1]
     inner = grad.shape[2]
-    fill_near(near, qkv, before, after)
-    dk[...] = jnp.zeros_like(dk)
-    dv[...] = jnp.zeros_like(dv)
     low_lane = iota((WIN, LANES), 1) < HD
-
-    def block_step(block, carry):
-        at = pl.ds(pl.multiple_of(block * WIN, WIN), WIN)
-        around = pl.ds(pl.multiple_of(block * WIN, WIN), 3 * WIN)
+    for place, block in enumerate(blocks):
+        at = slice(block * WIN, (block + 1) * WIN)
+        around = slice(block * WIN, (block + 3) * WIN)
         bias = light_bias(info, micro, block)
         stats = lse[0, at, :]
         for pair in range(inner // LANES):
@@ -309,43 +347,92 @@
             grad_probs = mm_t(upper, value)
             center = jnp.sum(probs * grad_probs, axis=-1, keepdims=True)
             slope = (probs * (grad_probs - center)).astype(BF)
-            dq_out[0, at, cut] = (merged(mm(slope, key), low_lane) * HD**-0.5).astype(BF)
+            emit(place, cut, (merged(mm(slope, key), low_lane) * HD**-0.5).astype(BF))
             dk[around, cut] += t_mm(slope, query)
             dv[around, cut] += t_mm(probs.astype(BF), upper)
-        return carry
-
-    [block_step(b, 0) for b in range(tok // WIN)]
+
+
+def light_bwd_outer_body(info, qkv, before, after, lse, grad, dq_out, own_out, low_out, high_out, near, dk, dv):
+    tok = qkv.shape[1]
+    inner = grad.shape[2]
+    fill_near(near, qkv, before, after)
+    dk[...] = jnp.zeros_like(dk)
+    dv[...] = jnp.zeros_like(dv)
+
+    def emit(place, cut, value):
+        dq_out[0, place * WIN : (place + 1) * WIN, cut] = value
+
+    light_bwd_blocks(info, qkv, lse, grad, near, dk, dv, (0, tok // WIN - 1), emit)
+    for first, source in ((0, dk), (inner, dv)):
+        to = slice(first, first + inner)
+        own_out[0, :, to] = source[WIN : WIN + tok]
+        low_out[0, :, to] = source[:WIN].astype(BF)
+        high_out[0, :, to] = source[WIN + tok :].astype(BF)
+
+
+def light_bwd_inner_body(info, qkv, lse, grad, dq_in, own_in, dq_out, own_out, near, dk, dv):
+    tok = qkv.shape[1]
+    inner = grad.shape[2]
+    near[WIN : WIN + tok] = qkv[0, :, inner:]
+    dk[WIN : WIN + tok] = own_in[0, :, :inner]
+    dv[WIN : WIN + tok] = own_in[0, :, inner:]
+    dq_out[0, :WIN] = dq_in[0, :WIN]
+    dq_out[0, tok - WIN :] = dq_in[0, WIN:]
+    blocks = range(1, tok // WIN - 1)
+
+    def emit(place, cut, value):
+        dq_out[0, blocks[place] * WIN : (blocks[place] + 1) * WIN, cut] = value
+
+    light_bwd_blocks(info, qkv, lse, grad, near, dk, dv, blocks, emit)
     own_out[0, :, :inner] = dk[WIN : WIN + tok]
     own_out[0, :, inner:] = dv[WIN : WIN + tok]
-    low_out[0, :, :inner] = dk[:WIN].astype(BF)
-    low_out[0, :, inner:] = dv[:WIN].astype(BF)
-    high_out[0, :, :inner] = dk[WIN + tok :].astype(BF)
-    high_out[0, :, inner:] = dv[WIN + tok :].astype(BF)
-
-
-def light_bwd(info, qkv, before, after, lse, grad):
+
+
+def light_bwd_scratch(tok, inner):
+    return [
+        pltpu.VMEM((tok + 2 * WIN, 2 * inner), BF),
+        pltpu.VMEM((tok + 2 * WIN, inner), F32),
+        pltpu.VMEM((tok + 2 * WIN, inner), F32),
+    ]
+
+
+def light_bwd_outer(info, qkv, before, after, lse, grad):
     micros, tok, columns = qkv.shape
     inner = columns // 3
     shapes = [
-        sds((micros, tok, inner), BF),
+        sds((micros, 2 * WIN, inner), BF),
         sds((micros, tok, 2 * inner), F32),
         sds((micros, WIN, 2 * inner), BF),
         sds((micros, WIN, 2 * inner), BF),
     ]
     args = (info, qkv, before, after, lse, grad)
     return call(
-        light_bwd_body,
+        light_bwd_outer_body,
         shapes,
         (micros,),
         [one_of(a.shape) for a in args[1:]],
-        [one_of(s.shape) for s in shapes],
+        [one_of(a.shape) for a in shapes],
         args,
-        scratch=[
-            pltpu.VMEM((tok + 2 * WIN, 2 * inner), BF),
-            pltpu.VMEM((tok + 2 * WIN, inner), F32),
-            pltpu.VMEM((tok + 2 * WIN, inner), F32),
-        ],
-        flops=10_000_000_000,
+        scratch=light_bwd_scratch(tok, inner),
+        flops=5_000_000_000,
+        moved=12_000_000,
+    )
+
+
+def light_bwd_inner(info, qkv, lse, grad, dq, own):
+    micros, tok, columns = qkv.shape
+    inner = columns // 3
+    shapes = [sds((micros, tok, inner), BF), sds((micros, tok, 2 * inner), F32)]
+    args = (info, qkv, lse, grad, dq, own)
+    return call(
+        light_bwd_inner_body,
+        shapes,
+        (micros,),
+        [one_of(a.shape) for a in args[1:]],
+        [one_of(a.shape) for a in shapes],
+        args,
+        scratch=light_bwd_scratch(tok, inner),
+        flops=5_000_000_000,
         moved=14_000_000,
     )
 
@@ -1462,7 +1549,7 @@
     o_own, o_got = pair_of(light_out)
     w_hout, w_hgu, w_hdown = (full_of(heavy_out), full_of(heavy_gu), full_of(heavy_down))
     w_lgu, w_ldown = (full_of(light_gu), full_of(light_down))
-    kv_orders = ((8, 4, 1, 2), (8, 1, 2, 4))
+    kv_orders = ((8, 4, 2, 1), (8, 1, 4, 2))
     back_orders = [tuple(reversed(order)) for order in kv_orders]
     upward = [(i, i + 1) for i in range(count - 1)]
     downward = [(i + 1, i) for i in range(count - 1)]
@@ -1490,11 +1577,12 @@
         got, q_pay, w_hout = tied(got, q_pay, w_hout)
         values = gather_end(values, got)
         got = gather_start(values, back_orders, 2)
-        got, before, after = tied(got, before, after)
+        done = light_inner(info, qkv)
+        got, before, after, done = tied(got, before, after, done)
         values = gather_end(values, got)
         got = gather_start(values, back_orders, 3)
+        lo, light_lse = light_outer(info, qkv, before, after, done)
         near_kv = [project(v) for v in values]
-        lo, light_lse = light_fwd(info, qkv, before, after)
         got, near_kv, lo, light_lse, w_hgu, w_hdown = tied(got, near_kv, lo, light_lse, w_hgu, w_hdown)
         kins = list(zip(values, got))
         kvs = [(n, project(f)) for n, f in zip(near_kv, got)]
@@ -1506,7 +1594,7 @@
         kvs = [tuple(project(k) for k in pair) for pair in kins]
         qkv = light_in(info, x, small, l_own, l_got)
         before, after = rims(qkv)
-        lo, light_lse = light_fwd(info, qkv, before, after)
+        lo, light_lse = light_outer(info, qkv, before, after, light_inner(info, qkv))
         q_pay = query_project(info, hq_in, h_own, h_got)
     heavy = [heavy_fwd(info, q_pay[m], kins[m], kvs[m]) for m in every]
     heavy, w_lgu, w_ldown = tied(heavy, w_lgu, w_ldown)
@@ -1528,14 +1616,18 @@
         zh, dff, hgu_own, hgu_send, hdn_own, hdn_send = ffn(
             info, flat(pay[..., :width]), flat(pay[..., width:]), w_hgu, w_hdown
         )
-    z, dh2, lgu_own, lgu_send, ldn_own, ldn_send = ffn_all(info, flat(low2), flat(up), w_lgu, w_ldown)
     if direct:
-        far, z, dh2 = tied(far, z, dh2)
-        lgu_got, ldn_got = (lax.ppermute(part, "wsh", swap) for part in (lgu_send, ldn_send))
         plane_own, plane_send, plane_dn = plane_grads(info, near, far, w_hgu, w_hdown)
         plane_got = lax.ppermute(plane_send, "wsh", swap)
         keep, send = column_fold(info, (1, 2), (plane_own, plane_got, plane_dn))
+        send, low2 = tied(send, low2)
         got = flipped(send, 4)
+    z, dh2, lgu_own, lgu_send, ldn_own, ldn_send = ffn_all(info, flat(low2), flat(up), w_lgu, w_ldown)
+    if direct:
+        got, z, dh2, lgu_send, ldn_send = tied(got, z, dh2, lgu_send, ldn_send)
+        keep, send = scatter_step(keep, got)
+        got = flipped(send, 8)
+        lgu_got, ldn_got = (lax.ppermute(part, "wsh", swap) for part in (lgu_send, ldn_send))
 
     def by_micro(value):
         return value.reshape(micros, -1, value.shape[-1])
@@ -1544,36 +1636,36 @@
         info, y, up, by_micro(z), by_micro(dh2), by_micro(zh), by_micro(dff), pay, gf, cols, rows, small, gate, o_own,
         o_got, w_hout, hy, hq_in,
     )
-    backs = [
-        heavy_bwd(info, q_pay[m], kins[m], kvs[m], heavy[m][1], dho[m], h_own, h_got) for m in every
-    ]
+    backs = []
+    for m in every:
+        backs.append(heavy_bwd(info, q_pay[m], kins[m], kvs[m], heavy[m][1], dho[m], h_own, h_got))
+        if direct and m == 0:
+            got, backs[0], dho = tied(got, backs[0], dho)
+            keep, send = scatter_step(keep, got)
+            plane_full = lax.all_gather(keep[0], "ctx", axis=0, tiled=False)
+            plane_full = plane_full.reshape((count // 4, 4) + plane_full.shape[1:])
     dhq = jnp.stack([b[0] for b in backs])
     shape = (count // 2, q_index.shape[2], width)
     back = [tuple(part.reshape(shape) for part in b[3:5]) for b in backs]
     dkvs = [part for b in backs for part in b[1:3]]
     if direct:
-        got, back, dlo, dkvs = tied(got, back, dlo, dkvs)
-        keep, send = scatter_step(keep, got)
-        got = flipped(send, 8)
+        back, dlo, dkvs = tied(back, dlo, dkvs)
         got_back = scatter_start(back, back_orders, 0)
-    dlq, dl_own, rim_low, rim_high = light_bwd(info, qkv, before, after, light_lse, dlo)
-    if direct:
-        got, got_back, dlq, dl_own, rim_low, rim_high = tied(got, got_back, dlq, dl_own, rim_low, rim_high)
-        keep, send = scatter_step(keep, got)
-        plane_full = lax.all_gather(keep[0], "ctx", axis=0, tiled=False)
-        plane_full = plane_full.reshape((count // 4, 4) + plane_full.shape[1:])
+    dlq, dl_own, rim_low, rim_high = light_bwd_outer(info, qkv, before, after, light_lse, dlo)
     got_low = lax.ppermute(rim_high, "ctx", upward)
     got_high = lax.ppermute(rim_low, "ctx", downward)
-    kin_all = [part for pair in kins for part in pair]
+    dlq, dl_own = light_bwd_inner(info, qkv, light_lse, dlo, dlq, dl_own)
     if direct:
+        got_back, dlq, dl_own = tied(got_back, dlq, dl_own)
         back = scatter_end(back, got_back)
         got_back = scatter_start(back, back_orders, 1)
+    kin_all = [part for pair in kins for part in pair]
     ha_own, ha_send = heavy_grads(info, hq_in, dhq, ho, dhy, lo, dy, kin_all, dkvs)
     if direct:
         got_back, got_low, got_high, ha_own, ha_send = tied(got_back, got_low, got_high, ha_own, ha_send)
+        ha_got = lax.ppermute(ha_send, "wsh", swap)
         back = scatter_end(back, got_back)
         got_back = scatter_start(back, back_orders, 2)
-        ha_got = lax.ppermute(ha_send, "wsh", swap)
     dl, la_own, la_send = light_join(info, x, small, dlq, dl_own, got_low, got_high)
     if direct:
         la_got = lax.ppermute(la_send, "wsh", swap)
@@ -1586,9 +1678,11 @@
         got_two = scatter_start(second, orders, 0)
         back = scatter_end(back, got_back)
         got_back = scatter_start(back, back_orders, 3)
-        got_two, got_back = tied(got_two, got_back)
-        second, back = (scatter_end(second, got_two), scatter_end(back, got_back))
+        (got_two,) = tied(got_two)
+        second = scatter_end(second, got_two)
         got_two = scatter_start(second, orders, 1)
+        back, got_back, second = tied(back, got_back, second)
+        back = scatter_end(back, got_back)
         dkin = jnp.concatenate([keep for keep, send in back], axis=0)
     else:
         dkin = jnp.stack(

time: 553 us -> 537 us (0.971)
  waiting for transfers between devices: 170 us -> 143 us
  local copies, waits for them, and re-layouts: 30.8 us -> 38.4 us
  Pallas kernels: 222 us -> 228 us
    ppermute x49, waiting for transfers between devices: 141 us -> 120 us  [flipped(): return lax.ppermute(value, 'ctx', [(i, i ^ bit) for i in range(size)])]
    ppermute x1, waiting for transfers between devices: 11.8 us -> 0.01 us  [per_device(): got_low = lax.ppermute(rim_high, 'ctx', upward)]
    ppermute x1, waiting for transfers between devices: 0.05 us -> 8.26 us  [per_device(): got_high = lax.ppermute(rim_low, 'ctx', downward)]
    unnamed x229 -> x203, local copies, waits for them, and re-layouts: 23.8 us -> 31.4 us
    ppermute x1, waiting for transfers between devices: 9.67 us -> 3.54 us  [rims(): lax.ppermute(qkv[:, tok - WIN:, inner:], 'ctx', upward)]
    pallas_call x29 -> x31, Pallas kernels: 216 us -> 222 us  [call(): pl.pallas_call(body, name=name or getattr(body, '__name__', 'kernel'), ou...]
  transfers between devices with their start and end apart: 70 -> 70, of which waited for: 34 -> 30; matrix products, arithmetic and copies ran while one was open for 6% -> 6% of each run, Pallas kernels for 35% -> 36%
where the time goes in v5:
time: 537 us; the launch traced here: 527 us
  Pallas kernels  228 us (42%)
  waiting for transfers between devices  143 us (27%)
  starting transfers between devices  78.2 us (15%)
  local copies, waits for them, and re-layouts  38.4 us (7%)
  other arithmetic  23.8 us (4%)
  between operations  15.8 us (3%)
    pallas_call x31, Pallas kernels, call(): pl.pallas_call(body, name=name or getattr(body, '__name__', 'kernel'), ou...  222 us
    ppermute x49, waiting for transfers between devices, flipped(): return lax.ppermute(value, 'ctx', [(i, i ^ bit) for i in range(size)])  120 us
    ppermute x49, starting transfers between devices, flipped(): return lax.ppermute(value, 'ctx', [(i, i ^ bit) for i in range(size)])  65.1 us
    unnamed x203, local copies, waits for them, and re-layouts  31.4 us
  transfers between devices with their start and end apart: 70, of which 30 were waited for; matrix products, arithmetic and copies ran while one was open for 6% of the time, Pallas kernels for 36%

profile of v5, /device:TPU:0, one launch (start us, length us, event | category | flops | bytes accessed | tf_op | source)
XLA Modules:
  0.0 527.4 jit_solution(16844430104515548210)
XLA Ops:
  27.7 7.4 %light_in_body.1.qkv = bf16[2,512,1536]{2,1,0:T(8,128)(2,1)} custom-call(s32[14]{0:T(128)S(1)} %concatenate.70.info, bf16[2,512,768]{2,1,0:T(8,128)(2,1)S(1)} %bitcast.54, bf16[8,768]{1,0:T(8,128)(2,1)S(1)} %pad_maximum_fusion.19.small, bf16[384,1536]{1,0:T(8,128)(2,1)} %l_own.1, bf16[384,1536]{1,0:T(8,128)(2,1)} %collective-permute-done.3.w_got.l_got), custom_call_target="tpu_custom_call" | custom-call | flops 2415919104 | bytes 8000000 | tf_op jit(solution)/shard_map/light_in_body/pallas_call | solution.py:74
  60.0 7.5 %light_inner_body.1 = (bf16[2,256,512]{2,1,0:T(8,128)(2,1)S(1)}, f32[2,256,128]{2,1,0:T(8,128)S(1)}) custom-call(s32[14]{0:T(128)S(1)} %concatenate.70.info, bf16[2,512,1536]{2,1,0:T(8,128)(2,1)S(1)} %copy-done.49), custom_call_target="tpu_custom_call" | custom-call | flops 2000000000 | bytes 4000000 | tf_op jit(solution)/shard_map/light_inner_body/pallas_call | solution.py:74
  71.1 6.1 %collective-permute-done.7 = bf16[256,896]{1,0:T(8,128)(2,1)S(1)} collective-permute-done((bf16[256,896]{1,0:T(8,128)(2,1)S(1)}, bf16[256,896]{1,0:T(8,128)(2,1)S(1)}, u32[]{:S(2)}, u32[]{:S(2)}) %collective-permute-start.7) | collective-permute-done | bytes 458784 | tf_op jit(solution)/shard_map/ppermute | solution.py:1221
  88.3 9.5 %light_outer_body.1 = (bf16[2,512,512]{2,1,0:T(8,128)(2,1)S(1)}, f32[2,512,128]{2,1,0:T(8,128)S(1)}) custom-call(s32[14]{0:T(128)S(1)} %concatenate.70.info, bf16[2,512,1536]{2,1,0:T(8,128)(2,1)} %light_in_body.1.qkv, bf16[2,128,1024]{2,1,0:T(8,128)(2,1)} %collective-permute-done.9.before, bf16[2,128,1024]{2,1,0:T(8,128)(2,1)} %collective-permute-done.10.after, ...), custom_call_target="tpu_custom_call" | custom-call | flops 2000000000 | bytes 6000000 | tf_op jit(solution)/shard_map/light_outer_body/pallas_call | solution.py:74
  119.5 6.9 %middle_body.1 = (f32[2,512,768]{2,1,0:T(8,128)}, bf16[2,512,768]{2,1,0:T(8,128)(2,1)S(1)}, bf16[2,64,1536]{2,1,0:T(8,128)(2,1)S(1)}, f32[2,64,768]{2,1,0:T(8,128)S(1)}, f32[2,64,128]{2,1,0:T(8,128)S(1)}) custom-call(s32[14]{0:T(128)S(1)} %concatenate.70.info, bf16[2,512,768]{2,1,0:T(8,128)(2,1)} %bitcast.52, bf16[2,512,768]{2,1,0:T(8,128)(2,1)} %bitcast.75, ...), custom_call_target="tpu_custom_call" | custom-call | flops 2000000000 | bytes 12000000 | tf_op jit(solution)/shard_map/middle_body/pallas_call | solution.py:74
  130.0 14.1 %ffn_local_body.1 = (f32[128,768]{1,0:T(8,128)S(1)}, f32[128,768]{1,0:T(8,128)S(1)}) custom-call(s32[14]{0:T(128)S(1)} %concatenate.70.info, bf16[128,1536]{1,0:T(8,128)(2,1)S(1)} %bitcast.49, bf16[128,1536]{1,0:T(8,128)(2,1)S(1)} %bitcast.50, bf16[768,8192]{1,0:T(8,128)(2,1)} %all-gather.9.cloned.1.call-done.wg.wu, ...), custom_call_target="tpu_custom_call" | custom-call | flops 4831838208 | bytes 18874368 | tf_op jit(solution)/shard_map/ffn_local_body/pallas_call | solution.py:74
  150.1 8.7 %plane_grads_body.1 = (bf16[2,768,256]{2,1,0:T(8,128)(2,1)S(1)}, bf16[2,768,256]{2,1,0:T(8,128)(2,1)S(1)}, bf16[2,768,256]{2,1,0:T(8,128)(2,1)S(1)}) custom-call(s32[14]{0:T(128)S(1)} %concatenate.70.info, bf16[512,1536]{1,0:T(8,128)(2,1)S(1)} %pad_maximum_fusion.near, bf16[512,1536]{1,0:T(8,128)(2,1)S(1)} %collective-permute-done.17.far, ...), custom_call_target="tpu_custom_call" | custom-call | flops 4831838208 | bytes 9000000 | tf_op jit(solution)/shard_map/plane_grads_body/pallas_call | solution.py:74
  162.9 23.1 %ffn_all_body.1 = (bf16[1024,768]{1,0:T(8,128)(2,1)S(1)}, bf16[1024,768]{1,0:T(8,128)(2,1)S(1)}, bf16[4,768,256]{2,1,0:T(8,128)(2,1)}, bf16[4,768,256]{2,1,0:T(8...) custom-call(s32[14]{0:T(128)S(1)} %concatenate.70.info, bf16[1024,768]{1,0:T(8,128)(2,1)} %bitcast.72, ...), custom_call_target="tpu_custom_call" | custom-call | flops 14495514624 | bytes 18874368 | tf_op jit(solution)/shard_map/ffn_all_body/pallas_call | solution.py:74
  190.1 11.4 %mid_back_body.1 = (bf16[2,512,768]{2,1,0:T(8,128)(2,1)}, f32[2,512,768]{2,1,0:T(8,128)}, bf16[2,512,512]{2,1,0:T(8,128)(2,1)S(1)}, bf16[2,64,768]{2,1,0:T(8,128...) custom-call(s32[14]{0:T(128)S(1)} %concatenate.70.info, ...), custom_call_target="tpu_custom_call" | custom-call | flops 3000000000 | bytes 22000000 | tf_op jit(solution)/shard_map/mid_back_body/pallas_call | solution.py:74
  206.6 10.3 %heavy_bwd_body.2 = (bf16[64,768]{1,0:T(8,128)(2,1)S(1)}, bf16[512,1536]{1,0:T(8,128)(2,1)S(1)}, bf16[512,1536]{1,0:T(8,128)(2,1)}, bf16[512,768]{1,0:T(8,128)(2,1)S(1)}, bf16[512,768]{1,0:T(8,128)(2,1)S(1)}) custom-call(s32[14]{0:T(128)S(1)} %concatenate.70.info, bf16[64,896]{1,0:T(8,128)(2,1)S(1)} %copy-done.58, bf16[512,896]{1,0:T(8,128)(2,1)S(1)} %copy-done.9, ...), custom_call_target="tpu_custom_call" | custom-call | flops 6499999744 | bytes 15000000 | tf_op jit(solution)/shard_map/heavy_bwd_body/pallas_call | solution.py:74
  220.5 12.1 %collective-permute-done.20 = bf16[1,6,192,256]{3,2,1,0:T(8,128)(2,1)S(1)} collective-permute-done((bf16[1,6,192,256]{3,2,1,0:T(8,128)(2,1)S(1)}, bf16[1,6,192,256]{3,2,1,0:T(8,128)(2,1)S(1)}, u32[]{:S(2)}, u32[]{:S(2)}) %collective-permute-start.20) | collective-permute-done | bytes 589856 | tf_op jit(solution)/shard_map/ppermute | solution.py:1221
  235.0 10.4 %heavy_bwd_body.3 = (bf16[64,768]{1,0:T(8,128)(2,1)S(1)}, bf16[512,1536]{1,0:T(8,128)(2,1)S(1)}, bf16[512,1536]{1,0:T(8,128)(2,1)}, bf16[512,768]{1,0:T(8,128)(2,1)S(1)}, bf16[512,768]{1,0:T(8,128)(2,1)S(1)}) custom-call(s32[14]{0:T(128)S(1)} %concatenate.70.info, bf16[64,896]{1,0:T(8,128)(2,1)S(1)} %copy-done.57, bf16[512,896]{1,0:T(8,128)(2,1)S(1)} %copy-done.7, ...), custom_call_target="tpu_custom_call" | custom-call | flops 6499999744 | bytes 15000000 | tf_op jit(solution)/shard_map/heavy_bwd_body/pallas_call | solution.py:74
  248.4 12.2 %light_bwd_outer_body.1 = (bf16[2,256,512]{2,1,0:T(8,128)(2,1)S(1)}, f32[2,512,1024]{2,1,0:T(8,128)}, bf16[2,128,1024]{2,1,0:T(8,128)(2,1)S(1)}, bf16[2,128,1024]{2,1,0:T(8,128)(2,1)S(1)}) custom-call(s32[14]{0:T(128)S(1)} %concatenate.70.info, bf16[2,512,1536]{2,1,0:T(8,128)(2,1)} %light_in_body.1.qkv, bf16[2,128,1024]{2,1,0:T(8,128)(2,1)} %collective-permute-done.9.before, ...), custom_call_target="tpu_custom_call" | custom-call | flops 5000000000 | bytes 12000000 | tf_op jit(solution)/shard_map/light_bwd_outer_body/pallas_call | solution.py:74
  264.4 13.1 %light_bwd_inner_body.1 = (bf16[2,512,512]{2,1,0:T(8,128)(2,1)S(1)}, f32[2,512,1024]{2,1,0:T(8,128)}) custom-call(s32[14]{0:T(128)S(1)} %concatenate.70.info, bf16[2,512,1536]{2,1,0:T(8,128)(2,1)} %light_in_body.1.qkv, f32[2,512,128]{2,1,0:T(8,128)S(1)} %copy-done.82, bf16[2,512,512]{2,1,0:T(8,128)(2,1)S(1)} %copy-done.66, ...), custom_call_target="tpu_custom_call" | custom-call | flops 5000000000 | bytes 14000000 | tf_op jit(solution)/shard_map/light_bwd_inner_body/pallas_call | solution.py:74
  283.2 13.7 %heavy_grads_body.1 = (bf16[7,768,256]{2,1,0:T(8,128)(2,1)}, bf16[7,768,256]{2,1,0:T(8,128)(2,1)}) custom-call(s32[14]{0:T(128)S(1)} %concatenate.70.info, bf16[2,64,896]{2,1,0:T(8,128)(2,1)S(1)} %copy-done.40, bf16[2,64,768]{2,1,0:T(8,128)(2,1)S(1)} %pad_maximum_fusion.17.refs_1_.dhq, bf16[2,64,768]{2,1,0:T(8,128)(2,1)S(1)} %copy-done.53, ...), custom_call_target="tpu_custom_call" | custom-call | flops 6499999744 | bytes 28000000 | tf_op jit(solution)/shard_map/heavy_grads_body/pallas_call | solution.py:74
  296.9 8.3 %collective-permute-done.26.got_high = bf16[2,128,1024]{2,1,0:T(8,128)(2,1)S(1)} collective-permute-done((bf16[2,128,1024]{2,1,0:T(8,128)(2,1)S(1)}, bf16[2,128,1024]{2,1,0:T(8,128)(2,1)S(1)}, u32[]{:S(2)}, u32[]{:S(2)}) %collective-permute-start.26) | collective-permute-done | bytes 524320 | tf_op jit(solution)/shard_map/ppermute | solution.py:1656
  305.7 6.8 %light_join_body.1 = (bf16[2,512,1536]{2,1,0:T(8,128)(2,1)}, bf16[3,768,256]{2,1,0:T(8,128)(2,1)S(1)}, bf16[3,768,256]{2,1,0:T(8,128)(2,1)S(1)}) custom-call(s32[14]{0:T(128)S(1)} %concatenate.70.info, bf16[2,512,768]{2,1,0:T(8,128)(2,1)S(1)} %bitcast.55, bf16[8,768]{1,0:T(8,128)(2,1)S(1)} %pad_maximum_fusion.19.small, bf16[2,512,512]{2,1,0:T(8,128)(2,1)S(1)} %copy-done.78, ...), custom_call_target="tpu_custom_call" | custom-call | flops 2415919104 | bytes 20000000 | tf_op jit(solution)/shard_map/light_join_body/pallas_call | solution.py:74
  321.9 5.8 %kernel.3 = (bf16[8,6,48,256]{3,2,1,0:T(8,128)(2,1)S(1)}, bf16[8,6,48,256]{3,2,1,0:T(8,128)(2,1)}) custom-call(s32[14]{0:T(128)S(1)} %concatenate.70.info, bf16[7,768,256]{2,1,0:T(8,128)(2,1)S(1)} %copy-done.2, bf16[7,768,256]{2,1,0:T(8,128)(2,1)} %collective-permute-done.29.refs_1_.refs_3_), custom_call_target="tpu_custom_call" | custom-call | bytes 7077888 | tf_op jit(solution)/shard_map/kernel/pallas_call | solution.py:74
  341.5 36.9 %collective-permute-done.36 = bf16[8,5,48,256]{3,2,1,0:T(8,128)(2,1)} collective-permute-done((bf16[8,5,48,256]{3,2,1,0:T(8,128)(2,1)}, bf16[8,5,48,256]{3,2,1,0:T(8,128)(2,1)}, u32[]{:S(2)}, u32[]{:S(2)}) %collective-permute-start.36) | collective-permute-done | bytes 983072 | tf_op jit(solution)/shard_map/ppermute | solution.py:1221
  378.4 6.5 %collective-permute-done.37 = bf16[8,5,48,256]{3,2,1,0:T(8,128)(2,1)} collective-permute-done((bf16[8,5,48,256]{3,2,1,0:T(8,128)(2,1)}, bf16[8,5,48,256]{3,2,1,0:T(8,128)(2,1)}, u32[]{:S(2)}, u32[]{:S(2)}) %collective-permute-start.37) | collective-permute-done | bytes 983072 | tf_op jit(solution)/shard_map/ppermute | solution.py:1221
  391.7 12.1 %in_back_body.1 = (bf16[2,512,768]{2,1,0:T(8,128)(2,1)}, f32[8,768]{1,0:T(8,128)S(1)}) custom-call(s32[14]{0:T(128)S(1)} %concatenate.70.info, bf16[2,512,768]{2,1,0:T(8,128)(2,1)S(1)} %bitcast.56, f32[2,512,768]{2,1,0:T(8,128)} %get-tuple-element.259.refs_5_.dy, bf16[2,512,1536]{2,1,0:T(8,128)(2,1)} %get-tuple-element.324.dl, ...), custom_call_target="tpu_custom_call" | custom-call | flops 2600000000 | bytes 14000000 | tf_op jit(solution)/shard_map/in_back_body/pallas_call | solution.py:74
  403.9 6.0 %collective-permute-done.39 = bf16[4,5,48,256]{3,2,1,0:T(8,128)(2,1)S(1)} collective-permute-done((bf16[4,5,48,256]{3,2,1,0:T(8,128)(2,1)S(1)}, bf16[4,5,48,256]{3,2,1,0:T(8,128)(2,1)S(1)}, u32[]{:S(2)}, u32[]{:S(2)}) %collective-permute-start.39) | collective-permute-done | bytes 491552 | tf_op jit(solution)/shard_map/ppermute | solution.py:1221
  446.5 8.0 %collective-permute-done.51 = bf16[1,5,48,256]{3,2,1,0:T(8,128)(2,1)S(1)} collective-permute-done((bf16[1,5,48,256]{3,2,1,0:T(8,128)(2,1)S(1)}, bf16[1,5,48,256]{3,2,1,0:T(8,128)(2,1)S(1)}, u32[]{:S(2)}, u32[]{:S(2)}) %collective-permute-start.51) | collective-permute-done | bytes 122912 | tf_op jit(solution)/shard_map/ppermute | solution.py:1221
  490.4 10.8 %unpack_plane_gu.1 = f32[384,8192]{1,0:T(8,128)} custom-call(s32[14]{0:T(128)S(1)} %concatenate.70.info, bf16[2,2,4,6,192,256]{5,4,3,2,1,0:T(8,128)(2,1)} %bitcast.74), custom_call_target="tpu_custom_call" | custom-call | bytes 18874368 | tf_op jit(solution)/shard_map/unpack_plane_gu/pallas_call | solution.py:74
  (424 shorter events, 243.9 us)
Async XLA Ops:
  7.2 45.7 %all-gather.7.cloned.1.call-start = ((), (), s32[]{:S(2)}) async-start(), calls=%async_computation | async-start | bytes 1769472 | tf_op jit(solution)/shard_map/all_gather | solution.py:1533
  7.9 95.2 %all-gather.11.cloned.1.call-start = ((), (), s32[]{:S(2)}) async-start(), calls=%async_computation.2 | async-start | bytes 9437184 | tf_op jit(solution)/shard_map/all_gather | solution.py:1533
  8.7 94.5 %all-gather.9.cloned.1.call-start = ((), (), s32[]{:S(2)}) async-start(), calls=%async_computation.1 | async-start | bytes 18874368 | tf_op jit(solution)/shard_map/all_gather | solution.py:1533
  9.4 107.4 %all-gather.15.cloned.1.call-start = ((), (), s32[]{:S(2)}) async-start(), calls=%async_computation.4 | async-start | bytes 2359296 | tf_op jit(solution)/shard_map/all_gather | solution.py:1533
  10.0 106.9 %all-gather.13.cloned.1.call-start = ((), (), s32[]{:S(2)}) async-start(), calls=%async_computation.3 | async-start | bytes 4718592 | tf_op jit(solution)/shard_map/all_gather | solution.py:1533
  10.6 40.5 %collective-permute-start.6 = (bf16[384,2304]{1,0:T(8,128)(2,1)S(1)}, bf16[384,2304]{1,0:T(8,128)(2,1)S(1)}, u32[]{:S(2)}, u32[]{:S(2)}) collective-permute-start(bf16[384,2304]{1,0:T(8,128)(2,1)S(1)} %copy-done), channel_id=1, source_target_pairs={{0,1},{1,0},{2,3},{3,2},{4,5},{5,4},{6,7},{7,6},{8,9},{9,8},{10,11... | collective-permute-start | bytes 5308424 | tf_op jit(solution)/shard_map/ppermute | solution.py:1528
  11.9 462.7 %all-gather.17.cloned.1.call-start = ((), (), s32[]{:S(2)}) async-start(), calls=%async_computation.5 | async-start | bytes 10027008 | tf_op jit(solution)/shard_map/all_gather | solution.py:1645
  44.4 23.1 %collective-permute-start.10 = (bf16[2,128,1024]{2,1,0:T(8,128)(2,1)}, bf16[2,128,1024]{2,1,0:T(8,128)(2,1)}, u32[]{:S(2)}, u32[]{:S(2)}) collective-permute-start(bf16[2,128,1024]{2,1,0:T(8,128)(2,1)} %get-tuple-element.410), channel_id=1, source_target_pairs={{2,0},{4,2},{6,4},{8,6},{10,8},{12,10},{14,12},{16,14},{18,16},{20... | collective-permute-start | bytes 1572872 | tf_op jit(solution)/shard_map/ppermute | solution.py:1562
  45.7 25.4 %collective-permute-start.9 = (bf16[2,128,1024]{2,1,0:T(8,128)(2,1)}, bf16[2,128,1024]{2,1,0:T(8,128)(2,1)}, u32[]{:S(2)}, u32[]{:S(2)}) collective-permute-start(bf16[2,128,1024]{2,1,0:T(8,128)(2,1)} %get-tuple-element.411), channel_id=1, source_target_pairs={{0,2},{2,4},{4,6},{6,8},{8,10},{10,12},{12,14},{14,16},{16,18},{18... | collective-permute-start | bytes 1572872 | tf_op jit(solution)/shard_map/ppermute | solution.py:1561
  82.2 34.7 %collective-permute-start.13 = (bf16[256,768]{1,0:T(8,128)(2,1)}, bf16[256,768]{1,0:T(8,128)(2,1)}, u32[]{:S(2)}, u32[]{:S(2)}) collective-permute-start(bf16[256,768]{1,0:T(8,128)(2,1)} %lout.3), channel_id=1, source_target_pairs={{0,1},{1,0},{2,3},{3,2},{4,5},{5,4},{6,7},{7,6},{8,9},{9,8},{10,11... | collective-permute-start | bytes 1179656 | tf_op jit(solution)/shard_map/ppermute | solution.py:1528
  161.9 28.2 %collective-permute-start.19 = (bf16[2,6,192,256]{3,2,1,0:T(8,128)(2,1)S(1)}, bf16[2,6,192,256]{3,2,1,0:T(8,128)(2,1)S(1)}, u32[]{:S(2)}, u32[]{:S(2)}) collective-permute-start(bf16[2,6,192,256]{3,2,1,0:T(8,128)(2,1)S(1)} %get-tuple-element.244), channel_id=1, source_target_pairs={{0,8},{2,10},{4,12},{6,14},{8,0},{10,2},{12,4},{14,6},{16,24},{18,... | collective-permute-start | bytes 3538952 | tf_op jit(solution)/shard_map/ppermute | solution.py:1221
  203.1 29.4 %collective-permute-start.20 = (bf16[1,6,192,256]{3,2,1,0:T(8,128)(2,1)S(1)}, bf16[1,6,192,256]{3,2,1,0:T(8,128)(2,1)S(1)}, u32[]{:S(2)}, u32[]{:S(2)}) collective-permute-start(bf16[1,6,192,256]{3,2,1,0:T(8,128)(2,1)S(1)} %add_convert_fusion.4), channel_id=1, source_target_pairs={{0,16},{2,18},{4,20},{6,22},{8,24},{10,26},{12,28},{14,30},{16,0},... | collective-permute-start | bytes 1769480 | tf_op jit(solution)/shard_map/ppermute | solution.py:1221
  246.6 31.8 %collective-permute-start.21 = (bf16[8,64,768]{2,1,0:T(8,128)(2,1)S(1)}, bf16[8,64,768]{2,1,0:T(8,128)(2,1)S(1)}, u32[]{:S(2)}, u32[]{:S(2)}) collective-permute-start(bf16[8,64,768]{2,1,0:T(8,128)(2,1)S(1)} %bitcast.70), channel_id=1, source_target_pairs={{0,2},{2,0},{4,6},{6,4},{8,10},{10,8},{12,14},{14,12},{16,18},{18,... | collective-permute-start | bytes 2359304 | tf_op jit(solution)/shard_map/ppermute | solution.py:1221
  247.0 31.5 %collective-permute-start.22 = (bf16[8,64,768]{2,1,0:T(8,128)(2,1)S(1)}, bf16[8,64,768]{2,1,0:T(8,128)(2,1)S(1)}, u32[]{:S(2)}, u32[]{:S(2)}) collective-permute-start(bf16[8,64,768]{2,1,0:T(8,128)(2,1)S(1)} %bitcast.71), channel_id=1, source_target_pairs={{0,4},{2,6},{4,0},{6,2},{8,12},{10,14},{12,8},{14,10},{16,20},{18,... | collective-permute-start | bytes 2359304 | tf_op jit(solution)/shard_map/ppermute | solution.py:1221
  260.5 36.4 %collective-permute-start.25 = (bf16[2,128,1024]{2,1,0:T(8,128)(2,1)S(1)}, bf16[2,128,1024]{2,1,0:T(8,128)(2,1)S(1)}, u32[]{:S(2)}, u32[]{:S(2)}) collective-permute-start(bf16[2,128,1024]{2,1,0:T(8,128)(2,1)S(1)} %get-tuple-element.292), channel_id=1, source_target_pairs={{0,2},{2,4},{4,6},{6,8},{8,10},{10,12},{12,14},{14,16},{16,18},{18... | collective-permute-start | bytes 1572872 | tf_op jit(solution)/shard_map/ppermute | solution.py:1655
  263.0 42.1 %collective-permute-start.26 = (bf16[2,128,1024]{2,1,0:T(8,128)(2,1)S(1)}, bf16[2,128,1024]{2,1,0:T(8,128)(2,1)S(1)}, u32[]{:S(2)}, u32[]{:S(2)}) collective-permute-start(bf16[2,128,1024]{2,1,0:T(8,128)(2,1)S(1)} %get-tuple-element.293), channel_id=1, source_target_pairs={{2,0},{4,2},{6,4},{8,6},{10,8},{12,10},{14,12},{16,14},{18,16},{20... | collective-permute-start | bytes 1572872 | tf_op jit(solution)/shard_map/ppermute | solution.py:1656
  278.7 26.4 %collective-permute-start.24 = (bf16[4,64,768]{2,1,0:T(8,128)(2,1)S(1)}, bf16[4,64,768]{2,1,0:T(8,128)(2,1)S(1)}, u32[]{:S(2)}, u32[]{:S(2)}) collective-permute-start(bf16[4,64,768]{2,1,0:T(8,128)(2,1)S(1)} %get-tuple-element.419), channel_id=1, source_target_pairs={{0,8},{2,10},{4,12},{6,14},{8,0},{10,2},{12,4},{14,6},{16,24},{18,... | collective-permute-start | bytes 1179656 | tf_op jit(solution)/shard_map/ppermute | solution.py:1221
  305.2 22.5 %collective-permute-start.30 = (bf16[4,768,256]{2,1,0:T(8,128)(2,1)}, bf16[4,768,256]{2,1,0:T(8,128)(2,1)S(1)}, u32[]{:S(2)}, u32[]{:S(2)}) collective-permute-start(bf16[4,768,256]{2,1,0:T(8,128)(2,1)} %get-tuple-element.310), channel_id=1, source_target_pairs={{0,1},{1,0},{2,3},{3,2},{4,5},{5,4},{6,7},{7,6},{8,9},{9,8},{10,11... | collective-permute-start | bytes 4718600 | tf_op jit(solution)/shard_map/ppermute | solution.py:1630
  334.3 50.6 %collective-permute-start.35 = (bf16[8,6,48,256]{3,2,1,0:T(8,128)(2,1)}, bf16[8,6,48,256]{3,2,1,0:T(8,128)(2,1)}, u32[]{:S(2)}, u32[]{:S(2)}) collective-permute-start(bf16[8,6,48,256]{3,2,1,0:T(8,128)(2,1)} %get-tuple-element.328), channel_id=1, source_target_pairs={{0,2},{2,0},{4,6},{6,4},{8,10},{10,8},{12,14},{14,12},{16,18},{18,... | collective-permute-start | bytes 3538952 | tf_op jit(solution)/shard_map/ppermute | solution.py:1221
  335.8 42.6 %collective-permute-start.36 = (bf16[8,5,48,256]{3,2,1,0:T(8,128)(2,1)}, bf16[8,5,48,256]{3,2,1,0:T(8,128)(2,1)}, u32[]{:S(2)}, u32[]{:S(2)}) collective-permute-start(bf16[8,5,48,256]{3,2,1,0:T(8,128)(2,1)} %get-tuple-element.329), channel_id=1, source_target_pairs={{0,4},{2,6},{4,0},{6,2},{8,12},{10,14},{12,8},{14,10},{16,20},{18,... | collective-permute-start | bytes 2949128 | tf_op jit(solution)/shard_map/ppermute | solution.py:1221
  335.8 49.1 %collective-permute-start.37 = (bf16[8,5,48,256]{3,2,1,0:T(8,128)(2,1)}, bf16[8,5,48,256]{3,2,1,0:T(8,128)(2,1)}, u32[]{:S(2)}, u32[]{:S(2)}) collective-permute-start(bf16[8,5,48,256]{3,2,1,0:T(8,128)(2,1)} %get-tuple-element.330), channel_id=1, source_target_pairs={{0,8},{2,10},{4,12},{6,14},{8,0},{10,2},{12,4},{14,6},{16,24},{18,... | collective-permute-start | bytes 2949128 | tf_op jit(solution)/shard_map/ppermute | solution.py:1221
  337.4 54.2 %collective-permute-start.34 = (bf16[1,64,768]{2,1,0:T(8,128)(2,1)S(1)}, bf16[1,64,768]{2,1,0:T(8,128)(2,1)S(1)}, u32[]{:S(2)}, u32[]{:S(2)}) collective-permute-start(bf16[1,64,768]{2,1,0:T(8,128)(2,1)S(1)} %get-tuple-element.432), channel_id=1, source_target_pairs={{0,16},{2,18},{4,20},{6,22},{8,24},{10,26},{12,28},{14,30},{16,0},... | collective-permute-start | bytes 294920 | tf_op jit(solution)/shard_map/ppermute | solution.py:1221
  340.9 50.7 %collective-permute-start.33 = (bf16[1,64,768]{2,1,0:T(8,128)(2,1)S(1)}, bf16[1,64,768]{2,1,0:T(8,128)(2,1)S(1)}, u32[]{:S(2)}, u32[]{:S(2)}) collective-permute-start(bf16[1,64,768]{2,1,0:T(8,128)(2,1)S(1)} %get-tuple-element.434), channel_id=1, source_target_pairs={{0,16},{2,18},{4,20},{6,22},{8,24},{10,26},{12,28},{14,30},{16,0},... | collective-permute-start | bytes 294920 | tf_op jit(solution)/shard_map/ppermute | solution.py:1221
  482.2 25.6 %collective-permute-start.61 = (bf16[8,6,48,256]{3,2,1,0:T(8,128)(2,1)S(1)}, bf16[8,6,48,256]{3,2,1,0:T(8,128)(2,1)S(1)}, u32[]{:S(2)}, u32[]{:S(2)}) collective-permute-start(bf16[8,6,48,256]{3,2,1,0:T(8,128)(2,1)S(1)} %pad_maximum_fusion.1.near), channel_id=1, source_target_pairs={{0,2},{2,0},{4,6},{6,4},{8,10},{10,8},{12,14},{14,12},{16,18},{18,... | collective-permute-start | bytes 3538952 | tf_op jit(solution)/shard_map/ppermute | solution.py:1221
  (147 other events, 1345.0 us)
Sparse Core Ops, SparseCore 0:
  9.6 11.9 all-gather.6
  23.1 17.9 all-gather.10
  42.6 26.0 all-gather.8
  70.1 10.9 all-gather.14
  82.5 13.2 all-gather.12
  233.8 173.4 all-gather.16

commit v6 on v5

--- a/solution.py
+++ b/solution.py
@@ -1605,6 +1605,7 @@
         return value.reshape(-1, value.shape[-1])
 
     orders = ((1, 2, 4, 8), (2, 4, 1, 8), (4, 1, 2, 8))
+    back_two = ((1, 2, 4, 8), (2, 1, 4, 8), (4, 1, 2, 8))
     if direct:
         mine = flat(pay)
         plane = [flipped(mine, bit) for bit in (1, 2, 3)]
@@ -1636,51 +1637,52 @@
         info, y, up, by_micro(z), by_micro(dh2), by_micro(zh), by_micro(dff), pay, gf, cols, rows, small, gate, o_own,
         o_got, w_hout, hy, hq_in,
     )
-    backs = []
-    for m in every:
-        backs.append(heavy_bwd(info, q_pay[m], kins[m], kvs[m], heavy[m][1], dho[m], h_own, h_got))
-        if direct and m == 0:
-            got, backs[0], dho = tied(got, backs[0], dho)
-            keep, send = scatter_step(keep, got)
-            plane_full = lax.all_gather(keep[0], "ctx", axis=0, tiled=False)
-            plane_full = plane_full.reshape((count // 4, 4) + plane_full.shape[1:])
+    dlq, dl_own, rim_low, rim_high = light_bwd_outer(info, qkv, before, after, light_lse, dlo)
+    if direct:
+        got, dlq, dl_own, rim_low, rim_high, dho = tied(got, dlq, dl_own, rim_low, rim_high, dho)
+        keep, send = scatter_step(keep, got)
+        plane_full = lax.all_gather(keep[0], "ctx", axis=0, tiled=False)
+        plane_full = plane_full.reshape((count // 4, 4) + plane_full.shape[1:])
+    got_low = lax.ppermute(rim_high, "ctx", upward)
+    got_high = lax.ppermute(rim_low, "ctx", downward)
+    backs = [
+        heavy_bwd(info, q_pay[m], kins[m], kvs[m], heavy[m][1], dho[m], h_own, h_got) for m in every
+    ]
     dhq = jnp.stack([b[0] for b in backs])
     shape = (count // 2, q_index.shape[2], width)
     back = [tuple(part.reshape(shape) for part in b[3:5]) for b in backs]
     dkvs = [part for b in backs for part in b[1:3]]
     if direct:
-        back, dlo, dkvs = tied(back, dlo, dkvs)
+        back, dlo, dkvs, got_low, got_high = tied(back, dlo, dkvs, got_low, got_high)
         got_back = scatter_start(back, back_orders, 0)
-    dlq, dl_own, rim_low, rim_high = light_bwd_outer(info, qkv, before, after, light_lse, dlo)
-    got_low = lax.ppermute(rim_high, "ctx", upward)
-    got_high = lax.ppermute(rim_low, "ctx", downward)
     dlq, dl_own = light_bwd_inner(info, qkv, light_lse, dlo, dlq, dl_own)
     if direct:
         got_back, dlq, dl_own = tied(got_back, dlq, dl_own)
         back = scatter_end(back, got_back)
         got_back = scatter_start(back, back_orders, 1)
     kin_all = [part for pair in kins for part in pair]
+    dl, la_own, la_send = light_join(info, x, small, dlq, dl_own, got_low, got_high)
+    if direct:
+        la_got = lax.ppermute(la_send, "wsh", swap)
     ha_own, ha_send = heavy_grads(info, hq_in, dhq, ho, dhy, lo, dy, kin_all, dkvs)
     if direct:
-        got_back, got_low, got_high, ha_own, ha_send = tied(got_back, got_low, got_high, ha_own, ha_send)
+        got_back, ha_own, ha_send, la_got, dl = tied(got_back, ha_own, ha_send, la_got, dl)
         ha_got = lax.ppermute(ha_send, "wsh", swap)
         back = scatter_end(back, got_back)
         got_back = scatter_start(back, back_orders, 2)
-    dl, la_own, la_send = light_join(info, x, small, dlq, dl_own, got_low, got_high)
-    if direct:
-        la_got = lax.ppermute(la_send, "wsh", swap)
         second = [
             fold(info, orders[0], [(ha_own, ha_got, 0, 6)]),
-            fold(info, orders[1], [(lgu_own, lgu_got, 0, 4), (ha_own, ha_got, 6, 1)]),
+            fold(info, back_two[1], [(lgu_own, lgu_got, 0, 4), (ha_own, ha_got, 6, 1)]),
             fold(info, orders[2], [(la_own, la_got, 0, 3), (ldn_own, ldn_got, 0, 2)]),
         ]
         got_back, second, dl = tied(got_back, second, dl)
-        got_two = scatter_start(second, orders, 0)
+        *got_two, got_last = scatter_start(second, back_two, 0)
         back = scatter_end(back, got_back)
         got_back = scatter_start(back, back_orders, 3)
         (got_two,) = tied(got_two)
+        *second, last = second
         second = scatter_end(second, got_two)
-        got_two = scatter_start(second, orders, 1)
+        got_two = scatter_start(second, back_two, 1)
         back, got_back, second = tied(back, got_back, second)
         back = scatter_end(back, got_back)
         dkin = jnp.concatenate([keep for keep, send in back], axis=0)
@@ -1700,15 +1702,20 @@
         half = width // 2
         mine = lax.dynamic_slice_in_dim(vector, side * half, half, 1)
         given = lax.dynamic_slice_in_dim(vector, (1 - side) * half, half, 1)
-        got_two, mine, given = tied(got_two, mine, given)
-        second = scatter_end(second, got_two)
-        got_two = scatter_start(second, orders, 2)
+        got_two, got_last, mine, given = tied(got_two, got_last, mine, given)
+        second, last = (scatter_end(second, got_two), scatter_step(last[0], got_last))
+        got_two, got_last = (scatter_start(second, back_two, 2), flipped(last[1], back_two[2][1]))
         vector = mine + lax.ppermute(given, "wsh", swap)
-        got_two, vector = tied(got_two, vector)
-        second = scatter_end(second, got_two)
-        got_two, got_vector = (scatter_start(second, orders, 3), flipped(vector, 1))
-        got_two, vector, got_vector = tied(got_two, vector, got_vector)
-        second, vector = (scatter_end(second, got_two), vector + got_vector)
+        got_two, got_last, vector = tied(got_two, got_last, vector)
+        second, last = (scatter_end(second, got_two), scatter_step(last[0], got_last))
+        got_two, got_last = (scatter_start(second, back_two, 3), flipped(last[1], back_two[2][2]))
+        got_vector = flipped(vector, 1)
+        got_two, got_last, vector, got_vector = tied(got_two, got_last, vector, got_vector)
+        second, last = (scatter_end(second, got_two), scatter_step(last[0], got_last))
+        got_last = flipped(last[1], back_two[2][3])
+        second, got_last, got_vector = tied(second, got_last, got_vector)
+        vector = vector + got_vector
+        second = [*second, scatter_step(last[0], got_last)]
         tails = [keep for keep, send in second]
         got_two, got_vector = (gather_start(tails, orders, 0), flipped(vector, 2))
         got_two, vector, got_vector = tied(got_two, vector, got_vector)

time: 537 us -> 526 us (0.980)
  waiting for transfers between devices: 143 us -> 132 us
    ppermute x49, waiting for transfers between devices: 120 us -> 110 us  [flipped(): return lax.ppermute(value, 'ctx', [(i, i ^ bit) for i in range(size)])]
    unnamed x203 -> x207, local copies, waits for them, and re-layouts: 31.4 us -> 30.6 us
  transfers between devices with their start and end apart: 70 -> 70, of which waited for: 30 -> 34; matrix products, arithmetic and copies ran while one was open for 6% -> 6% of each run, Pallas kernels for 36% -> 38%
where the time goes in v6:
time: 526 us; the launch traced here: 516 us
  Pallas kernels  226 us (43%)
  waiting for transfers between devices  132 us (25%)
  starting transfers between devices  78.3 us (15%)
  local copies, waits for them, and re-layouts  39.9 us (8%)
  other arithmetic  23.8 us (5%)
  between operations  15.6 us (3%)
    pallas_call x31, Pallas kernels, call(): pl.pallas_call(body, name=name or getattr(body, '__name__', 'kernel'), ou...  219 us
    ppermute x49, waiting for transfers between devices, flipped(): return lax.ppermute(value, 'ctx', [(i, i ^ bit) for i in range(size)])  110 us
    ppermute x49, starting transfers between devices, flipped(): return lax.ppermute(value, 'ctx', [(i, i ^ bit) for i in range(size)])  67.5 us
    unnamed x207, local copies, waits for them, and re-layouts  30.6 us
  transfers between devices with their start and end apart: 70, of which 34 were waited for; matrix products, arithmetic and copies ran while one was open for 6% of the time, Pallas kernels for 38%

profile of v6, /device:TPU:0, one launch (start us, length us, event | category | flops | bytes accessed | tf_op | source)
XLA Modules:
  0.0 515.5 jit_solution(10452114671294466562)
XLA Ops:
  27.6 7.4 %light_in_body.1.qkv = bf16[2,512,1536]{2,1,0:T(8,128)(2,1)} custom-call(s32[14]{0:T(128)S(1)} %concatenate.70.info, bf16[2,512,768]{2,1,0:T(8,128)(2,1)S(1)} %bitcast.54, bf16[8,768]{1,0:T(8,128)(2,1)S(1)} %pad_maximum_fusion.17.small, bf16[384,1536]{1,0:T(8,128)(2,1)} %l_own.1, bf16[384,1536]{1,0:T(8,128)(2,1)} %collective-permute-done.3.w_got.l_got), custom_call_target="tpu_custom_call" | custom-call | flops 2415919104 | bytes 8000000 | tf_op jit(solution)/shard_map/light_in_body/pallas_call | solution.py:74
  61.3 7.4 %light_inner_body.1 = (bf16[2,256,512]{2,1,0:T(8,128)(2,1)S(1)}, f32[2,256,128]{2,1,0:T(8,128)S(1)}) custom-call(s32[14]{0:T(128)S(1)} %concatenate.70.info, bf16[2,512,1536]{2,1,0:T(8,128)(2,1)S(1)} %copy-done.45), custom_call_target="tpu_custom_call" | custom-call | flops 2000000000 | bytes 4000000 | tf_op jit(solution)/shard_map/light_inner_body/pallas_call | solution.py:74
  87.0 9.2 %light_outer_body.1 = (bf16[2,512,512]{2,1,0:T(8,128)(2,1)S(1)}, f32[2,512,128]{2,1,0:T(8,128)S(1)}) custom-call(s32[14]{0:T(128)S(1)} %concatenate.70.info, bf16[2,512,1536]{2,1,0:T(8,128)(2,1)} %light_in_body.1.qkv, bf16[2,128,1024]{2,1,0:T(8,128)(2,1)} %collective-permute-done.9.before, bf16[2,128,1024]{2,1,0:T(8,128)(2,1)} %collective-permute-done.10.after, ...), custom_call_target="tpu_custom_call" | custom-call | flops 2000000000 | bytes 6000000 | tf_op jit(solution)/shard_map/light_outer_body/pallas_call | solution.py:74
  116.9 6.9 %middle_body.1 = (f32[2,512,768]{2,1,0:T(8,128)}, bf16[2,512,768]{2,1,0:T(8,128)(2,1)S(1)}, bf16[2,64,1536]{2,1,0:T(8,128)(2,1)S(1)}, f32[2,64,768]{2,1,0:T(8,128)S(1)}, f32[2,64,128]{2,1,0:T(8,128)S(1)}) custom-call(s32[14]{0:T(128)S(1)} %concatenate.70.info, bf16[2,512,768]{2,1,0:T(8,128)(2,1)} %bitcast.52, bf16[2,512,768]{2,1,0:T(8,128)(2,1)} %bitcast.75, ...), custom_call_target="tpu_custom_call" | custom-call | flops 2000000000 | bytes 12000000 | tf_op jit(solution)/shard_map/middle_body/pallas_call | solution.py:74
  127.4 14.1 %ffn_local_body.1 = (f32[128,768]{1,0:T(8,128)S(1)}, f32[128,768]{1,0:T(8,128)S(1)}) custom-call(s32[14]{0:T(128)S(1)} %concatenate.70.info, bf16[128,1536]{1,0:T(8,128)(2,1)S(1)} %bitcast.49, bf16[128,1536]{1,0:T(8,128)(2,1)S(1)} %bitcast.50, bf16[768,8192]{1,0:T(8,128)(2,1)} %all-gather.9.cloned.1.call-done.wg.wu, ...), custom_call_target="tpu_custom_call" | custom-call | flops 4831838208 | bytes 18874368 | tf_op jit(solution)/shard_map/ffn_local_body/pallas_call | solution.py:74
  148.0 8.7 %plane_grads_body.1 = (bf16[2,768,256]{2,1,0:T(8,128)(2,1)S(1)}, bf16[2,768,256]{2,1,0:T(8,128)(2,1)S(1)}, bf16[2,768,256]{2,1,0:T(8,128)(2,1)S(1)}) custom-call(s32[14]{0:T(128)S(1)} %concatenate.70.info, bf16[512,1536]{1,0:T(8,128)(2,1)S(1)} %pad_maximum_fusion.near, bf16[512,1536]{1,0:T(8,128)(2,1)S(1)} %collective-permute-done.17.far, ...), custom_call_target="tpu_custom_call" | custom-call | flops 4831838208 | bytes 9000000 | tf_op jit(solution)/shard_map/plane_grads_body/pallas_call | solution.py:74
  162.1 23.1 %ffn_all_body.1 = (bf16[1024,768]{1,0:T(8,128)(2,1)S(1)}, bf16[1024,768]{1,0:T(8,128)(2,1)S(1)}, bf16[4,768,256]{2,1,0:T(8,128)(2,1)}, bf16[4,768,256]{2,1,0:T(8...) custom-call(s32[14]{0:T(128)S(1)} %concatenate.70.info, bf16[1024,768]{1,0:T(8,128)(2,1)} %bitcast.72, ...), custom_call_target="tpu_custom_call" | custom-call | flops 14495514624 | bytes 18874368 | tf_op jit(solution)/shard_map/ffn_all_body/pallas_call | solution.py:74
  191.7 11.4 %mid_back_body.1 = (bf16[2,512,768]{2,1,0:T(8,128)(2,1)}, f32[2,512,768]{2,1,0:T(8,128)}, bf16[2,512,512]{2,1,0:T(8,128)(2,1)S(1)}, bf16[2,64,768]{2,1,0:T(8,128...) custom-call(s32[14]{0:T(128)S(1)} %concatenate.70.info, ...), custom_call_target="tpu_custom_call" | custom-call | flops 3000000000 | bytes 22000000 | tf_op jit(solution)/shard_map/mid_back_body/pallas_call | solution.py:74
  204.4 12.0 %light_bwd_outer_body.1 = (bf16[2,256,512]{2,1,0:T(8,128)(2,1)S(1)}, f32[2,512,1024]{2,1,0:T(8,128)}, bf16[2,128,1024]{2,1,0:T(8,128)(2,1)S(1)}, bf16[2,128,1024]{2,1,0:T(8,128)(2,1)S(1)}) custom-call(s32[14]{0:T(128)S(1)} %concatenate.70.info, bf16[2,512,1536]{2,1,0:T(8,128)(2,1)} %light_in_body.1.qkv, bf16[2,128,1024]{2,1,0:T(8,128)(2,1)} %collective-permute-done.9.before, ...), custom_call_target="tpu_custom_call" | custom-call | flops 5000000000 | bytes 12000000 | tf_op jit(solution)/shard_map/light_bwd_outer_body/pallas_call | solution.py:74
  224.5 10.7 %heavy_bwd_body.2 = (bf16[64,768]{1,0:T(8,128)(2,1)S(1)}, bf16[512,1536]{1,0:T(8,128)(2,1)S(1)}, bf16[512,1536]{1,0:T(8,128)(2,1)}, bf16[512,768]{1,0:T(8,128)(2,1)S(1)}, bf16[512,768]{1,0:T(8,128)(2,1)S(1)}) custom-call(s32[14]{0:T(128)S(1)} %concatenate.70.info, bf16[64,896]{1,0:T(8,128)(2,1)S(1)} %copy-done.53, bf16[512,896]{1,0:T(8,128)(2,1)S(1)} %copy-done.7, ...), custom_call_target="tpu_custom_call" | custom-call | flops 6499999744 | bytes 15000000 | tf_op jit(solution)/shard_map/heavy_bwd_body/pallas_call | solution.py:74
  236.5 10.4 %heavy_bwd_body.3 = (bf16[64,768]{1,0:T(8,128)(2,1)S(1)}, bf16[512,1536]{1,0:T(8,128)(2,1)S(1)}, bf16[512,1536]{1,0:T(8,128)(2,1)}, bf16[512,768]{1,0:T(8,128)(2,1)S(1)}, bf16[512,768]{1,0:T(8,128)(2,1)S(1)}) custom-call(s32[14]{0:T(128)S(1)} %concatenate.70.info, bf16[64,896]{1,0:T(8,128)(2,1)S(1)} %copy-done.51, bf16[512,896]{1,0:T(8,128)(2,1)S(1)} %copy-done.9, ...), custom_call_target="tpu_custom_call" | custom-call | flops 6499999744 | bytes 15000000 | tf_op jit(solution)/shard_map/heavy_bwd_body/pallas_call | solution.py:74
  254.3 13.0 %light_bwd_inner_body.1 = (bf16[2,512,512]{2,1,0:T(8,128)(2,1)S(1)}, f32[2,512,1024]{2,1,0:T(8,128)}) custom-call(s32[14]{0:T(128)S(1)} %concatenate.70.info, bf16[2,512,1536]{2,1,0:T(8,128)(2,1)} %light_in_body.1.qkv, f32[2,512,128]{2,1,0:T(8,128)S(1)} %copy-done.77, bf16[2,512,512]{2,1,0:T(8,128)(2,1)S(1)} %copy-done.59, ...), custom_call_target="tpu_custom_call" | custom-call | flops 5000000000 | bytes 14000000 | tf_op jit(solution)/shard_map/light_bwd_inner_body/pallas_call | solution.py:74
  267.3 10.7 %collective-permute-done.23 = bf16[8,64,768]{2,1,0:T(8,128)(2,1)} collective-permute-done((bf16[8,64,768]{2,1,0:T(8,128)(2,1)S(1)}, bf16[8,64,768]{2,1,0:T(8,128)(2,1)}, u32[]{:S(2)}, u32[]{:S(2)}) %collective-permute-start.23) | collective-permute-done | bytes 786464 | tf_op jit(solution)/shard_map/ppermute | solution.py:1221
  278.9 6.8 %light_join_body.1 = (bf16[2,512,1536]{2,1,0:T(8,128)(2,1)}, bf16[3,768,256]{2,1,0:T(8,128)(2,1)S(1)}, bf16[3,768,256]{2,1,0:T(8,128)(2,1)S(1)}) custom-call(s32[14]{0:T(128)S(1)} %concatenate.70.info, bf16[2,512,768]{2,1,0:T(8,128)(2,1)S(1)} %bitcast.55, bf16[8,768]{1,0:T(8,128)(2,1)S(1)} %pad_maximum_fusion.17.small, ...), custom_call_target="tpu_custom_call" | custom-call | flops 2415919104 | bytes 20000000 | tf_op jit(solution)/shard_map/light_join_body/pallas_call | solution.py:74
  292.0 13.5 %heavy_grads_body.1 = (bf16[7,768,256]{2,1,0:T(8,128)(2,1)}, bf16[7,768,256]{2,1,0:T(8,128)(2,1)}) custom-call(s32[14]{0:T(128)S(1)} %concatenate.70.info, bf16[2,64,896]{2,1,0:T(8,128)(2,1)S(1)} %copy-done.38, bf16[2,64,768]{2,1,0:T(8,128)(2,1)S(1)} %pad_maximum_fusion.15.refs_1_.dhq, bf16[2,64,768]{2,1,0:T(8,128)(2,1)S(1)} %copy-done.49, ...), custom_call_target="tpu_custom_call" | custom-call | flops 6499999744 | bytes 28000000 | tf_op jit(solution)/shard_map/heavy_grads_body/pallas_call | solution.py:74
  307.7 6.3 %collective-permute-done.32.refs_3_ = bf16[2,768,256]{2,1,0:T(8,128)(2,1)S(1)} collective-permute-done((bf16[2,768,256]{2,1,0:T(8,128)(2,1)S(1)}, bf16[2,768,256]{2,1,0:T(8,128)(2,1)S(1)}, u32[]{:S(2)}, u32[]{:S(2)}) %collective-permute-start.32) | collective-permute-done | bytes 786464 | tf_op jit(solution)/shard_map/ppermute | solution.py:1631
  336.5 29.4 %collective-permute-done.36 = bf16[8,5,48,256]{3,2,1,0:T(8,128)(2,1)} collective-permute-done((bf16[8,5,48,256]{3,2,1,0:T(8,128)(2,1)}, bf16[8,5,48,256]{3,2,1,0:T(8,128)(2,1)}, u32[]{:S(2)}, u32[]{:S(2)}) %collective-permute-start.36) | collective-permute-done | bytes 983072 | tf_op jit(solution)/shard_map/ppermute | solution.py:1221
  365.9 6.8 %collective-permute-done.35 = bf16[8,6,48,256]{3,2,1,0:T(8,128)(2,1)} collective-permute-done((bf16[8,6,48,256]{3,2,1,0:T(8,128)(2,1)}, bf16[8,6,48,256]{3,2,1,0:T(8,128)(2,1)}, u32[]{:S(2)}, u32[]{:S(2)}) %collective-permute-start.35) | collective-permute-done | bytes 1179680 | tf_op jit(solution)/shard_map/ppermute | solution.py:1221
  378.3 12.1 %in_back_body.1 = (bf16[2,512,768]{2,1,0:T(8,128)(2,1)}, f32[8,768]{1,0:T(8,128)S(1)}) custom-call(s32[14]{0:T(128)S(1)} %concatenate.70.info, bf16[2,512,768]{2,1,0:T(8,128)(2,1)S(1)} %bitcast.56, f32[2,512,768]{2,1,0:T(8,128)} %get-tuple-element.262.refs_5_.dy, bf16[2,512,1536]{2,1,0:T(8,128)(2,1)} %get-tuple-element.328.dl, ...), custom_call_target="tpu_custom_call" | custom-call | flops 2600000000 | bytes 14000000 | tf_op jit(solution)/shard_map/in_back_body/pallas_call | solution.py:74
  396.8 7.4 %collective-permute-done.41 = bf16[2,5,48,256]{3,2,1,0:T(8,128)(2,1)S(1)} collective-permute-done((bf16[2,5,48,256]{3,2,1,0:T(8,128)(2,1)S(1)}, bf16[2,5,48,256]{3,2,1,0:T(8,128)(2,1)S(1)}, u32[]{:S(2)}, u32[]{:S(2)}) %collective-permute-start.41) | collective-permute-done | bytes 245792 | tf_op jit(solution)/shard_map/ppermute | solution.py:1221
  418.4 8.9 %collective-permute-done.48 = bf16[1,5,48,256]{3,2,1,0:T(8,128)(2,1)S(1)} collective-permute-done((bf16[1,5,48,256]{3,2,1,0:T(8,128)(2,1)S(1)}, bf16[1,5,48,256]{3,2,1,0:T(8,128)(2,1)S(1)}, u32[]{:S(2)}, u32[]{:S(2)}) %collective-permute-start.48) | collective-permute-done | bytes 122912 | tf_op jit(solution)/shard_map/ppermute | solution.py:1221
  434.1 7.6 %collective-permute-done.50 = bf16[1,5,48,256]{3,2,1,0:T(8,128)(2,1)S(1)} collective-permute-done((bf16[1,5,48,256]{3,2,1,0:T(8,128)(2,1)S(1)}, bf16[1,5,48,256]{3,2,1,0:T(8,128)(2,1)S(1)}, u32[]{:S(2)}, u32[]{:S(2)}) %collective-permute-start.50) | collective-permute-done | bytes 122912 | tf_op jit(solution)/shard_map/ppermute | solution.py:1221
  476.2 10.8 %unpack_plane_gu.1 = f32[384,8192]{1,0:T(8,128)} custom-call(s32[14]{0:T(128)S(1)} %concatenate.70.info, bf16[2,2,4,6,192,256]{5,4,3,2,1,0:T(8,128)(2,1)} %bitcast.74), custom_call_target="tpu_custom_call" | custom-call | bytes 18874368 | tf_op jit(solution)/shard_map/unpack_plane_gu/pallas_call | solution.py:74
  487.0 7.5 %collective-permute-done.62.far = bf16[8,5,48,256]{3,2,1,0:T(8,128)(2,1)S(1)} collective-permute-done((bf16[8,5,48,256]{3,2,1,0:T(8,128)(2,1)S(1)}, bf16[8,5,48,256]{3,2,1,0:T(8,128)(2,1)S(1)}, u32[]{:S(2)}, u32[]{:S(2)}) %collective-permute-start.62) | collective-permute-done | bytes 983072 | tf_op jit(solution)/shard_map/ppermute | solution.py:1221
  (427 shorter events, 237.7 us)
Async XLA Ops:
  7.2 43.6 %all-gather.7.cloned.1.call-start = ((), (), s32[]{:S(2)}) async-start(), calls=%async_computation | async-start | bytes 1769472 | tf_op jit(solution)/shard_map/all_gather | solution.py:1533
  7.9 92.7 %all-gather.11.cloned.1.call-start = ((), (), s32[]{:S(2)}) async-start(), calls=%async_computation.2 | async-start | bytes 9437184 | tf_op jit(solution)/shard_map/all_gather | solution.py:1533
  8.7 91.9 %all-gather.9.cloned.1.call-start = ((), (), s32[]{:S(2)}) async-start(), calls=%async_computation.1 | async-start | bytes 18874368 | tf_op jit(solution)/shard_map/all_gather | solution.py:1533
  9.4 104.8 %all-gather.15.cloned.1.call-start = ((), (), s32[]{:S(2)}) async-start(), calls=%async_computation.4 | async-start | bytes 2359296 | tf_op jit(solution)/shard_map/all_gather | solution.py:1533
  10.0 104.3 %all-gather.13.cloned.1.call-start = ((), (), s32[]{:S(2)}) async-start(), calls=%async_computation.3 | async-start | bytes 4718592 | tf_op jit(solution)/shard_map/all_gather | solution.py:1533
  10.6 38.4 %collective-permute-start.6 = (bf16[384,2304]{1,0:T(8,128)(2,1)S(1)}, bf16[384,2304]{1,0:T(8,128)(2,1)S(1)}, u32[]{:S(2)}, u32[]{:S(2)}) collective-permute-start(bf16[384,2304]{1,0:T(8,128)(2,1)S(1)} %copy-done), channel_id=1, source_target_pairs={{0,1},{1,0},{2,3},{3,2},{4,5},{5,4},{6,7},{7,6},{8,9},{9,8},{10,11... | collective-permute-start | bytes 5308424 | tf_op jit(solution)/shard_map/ppermute | solution.py:1528
  11.9 448.2 %all-gather.17.cloned.1.call-start = ((), (), s32[]{:S(2)}) async-start(), calls=%async_computation.5 | async-start | bytes 10027008 | tf_op jit(solution)/shard_map/all_gather | solution.py:1644
  44.4 25.3 %collective-permute-start.9 = (bf16[2,128,1024]{2,1,0:T(8,128)(2,1)}, bf16[2,128,1024]{2,1,0:T(8,128)(2,1)}, u32[]{:S(2)}, u32[]{:S(2)}) collective-permute-start(bf16[2,128,1024]{2,1,0:T(8,128)(2,1)} %get-tuple-element.417), channel_id=1, source_target_pairs={{0,2},{2,4},{4,6},{6,8},{8,10},{10,12},{12,14},{14,16},{16,18},{18... | collective-permute-start | bytes 1572872 | tf_op jit(solution)/shard_map/ppermute | solution.py:1561
  47.6 24.5 %collective-permute-start.10 = (bf16[2,128,1024]{2,1,0:T(8,128)(2,1)}, bf16[2,128,1024]{2,1,0:T(8,128)(2,1)}, u32[]{:S(2)}, u32[]{:S(2)}) collective-permute-start(bf16[2,128,1024]{2,1,0:T(8,128)(2,1)} %get-tuple-element.416), channel_id=1, source_target_pairs={{2,0},{4,2},{6,4},{8,6},{10,8},{12,10},{14,12},{16,14},{18,16},{20... | collective-permute-start | bytes 1572872 | tf_op jit(solution)/shard_map/ppermute | solution.py:1562
  75.3 22.8 %collective-permute-start.11 = (bf16[512,896]{1,0:T(8,128)(2,1)S(1)}, bf16[512,896]{1,0:T(8,128)(2,1)S(1)}, u32[]{:S(2)}, u32[]{:S(2)}) collective-permute-start(bf16[512,896]{1,0:T(8,128)(2,1)S(1)} %pad_maximum_fusion.2.kin.kin_a.refs_6_), channel_id=1, source_target_pairs={{0,2},{2,0},{4,6},{6,4},{8,10},{10,8},{12,14},{14,12},{16,18},{18,... | collective-permute-start | bytes 2752520 | tf_op jit(solution)/shard_map/ppermute | solution.py:1221
  79.6 34.7 %collective-permute-start.13 = (bf16[256,768]{1,0:T(8,128)(2,1)}, bf16[256,768]{1,0:T(8,128)(2,1)}, u32[]{:S(2)}, u32[]{:S(2)}) collective-permute-start(bf16[256,768]{1,0:T(8,128)(2,1)} %lout.3), channel_id=1, source_target_pairs={{0,1},{1,0},{2,3},{3,2},{4,5},{5,4},{6,7},{7,6},{8,9},{9,8},{10,11... | collective-permute-start | bytes 1179656 | tf_op jit(solution)/shard_map/ppermute | solution.py:1528
  159.8 28.6 %collective-permute-start.19 = (bf16[2,6,192,256]{3,2,1,0:T(8,128)(2,1)S(1)}, bf16[2,6,192,256]{3,2,1,0:T(8,128)(2,1)S(1)}, u32[]{:S(2)}, u32[]{:S(2)}) collective-permute-start(bf16[2,6,192,256]{3,2,1,0:T(8,128)(2,1)S(1)} %get-tuple-element.247), channel_id=1, source_target_pairs={{0,8},{2,10},{4,12},{6,14},{8,0},{10,2},{12,4},{14,6},{16,24},{18,... | collective-permute-start | bytes 3538952 | tf_op jit(solution)/shard_map/ppermute | solution.py:1221
  188.6 28.7 %collective-permute-start.20 = (bf16[1,6,192,256]{3,2,1,0:T(8,128)(2,1)S(1)}, bf16[1,6,192,256]{3,2,1,0:T(8,128)(2,1)S(1)}, u32[]{:S(2)}, u32[]{:S(2)}) collective-permute-start(bf16[1,6,192,256]{3,2,1,0:T(8,128)(2,1)S(1)} %add_convert_fusion.4), channel_id=1, source_target_pairs={{0,16},{2,18},{4,20},{6,22},{8,24},{10,26},{12,28},{14,30},{16,0},... | collective-permute-start | bytes 1769480 | tf_op jit(solution)/shard_map/ppermute | solution.py:1221
  219.3 27.6 %collective-permute-start.21 = (bf16[2,128,1024]{2,1,0:T(8,128)(2,1)}, bf16[2,128,1024]{2,1,0:T(8,128)(2,1)S(1)}, u32[]{:S(2)}, u32[]{:S(2)}) collective-permute-start(bf16[2,128,1024]{2,1,0:T(8,128)(2,1)} %copy-done.64), channel_id=1, source_target_pairs={{0,2},{2,4},{4,6},{6,8},{8,10},{10,12},{12,14},{14,16},{16,18},{18... | collective-permute-start | bytes 1572872 | tf_op jit(solution)/shard_map/ppermute | solution.py:1646
  221.8 28.0 %collective-permute-start.22 = (bf16[2,128,1024]{2,1,0:T(8,128)(2,1)}, bf16[2,128,1024]{2,1,0:T(8,128)(2,1)S(1)}, u32[]{:S(2)}, u32[]{:S(2)}) collective-permute-start(bf16[2,128,1024]{2,1,0:T(8,128)(2,1)} %copy-done.63), channel_id=1, source_target_pairs={{2,0},{4,2},{6,4},{8,6},{10,8},{12,10},{14,12},{16,14},{18,16},{20... | collective-permute-start | bytes 1572872 | tf_op jit(solution)/shard_map/ppermute | solution.py:1647
  249.8 28.2 %collective-permute-start.23 = (bf16[8,64,768]{2,1,0:T(8,128)(2,1)S(1)}, bf16[8,64,768]{2,1,0:T(8,128)(2,1)}, u32[]{:S(2)}, u32[]{:S(2)}) collective-permute-start(bf16[8,64,768]{2,1,0:T(8,128)(2,1)S(1)} %bitcast.70), channel_id=1, source_target_pairs={{0,2},{2,0},{4,6},{6,4},{8,10},{10,8},{12,14},{14,12},{16,18},{18,... | collective-permute-start | bytes 2359304 | tf_op jit(solution)/shard_map/ppermute | solution.py:1221
  251.5 26.5 %collective-permute-start.24 = (bf16[8,64,768]{2,1,0:T(8,128)(2,1)S(1)}, bf16[8,64,768]{2,1,0:T(8,128)(2,1)S(1)}, u32[]{:S(2)}, u32[]{:S(2)}) collective-permute-start(bf16[8,64,768]{2,1,0:T(8,128)(2,1)S(1)} %bitcast.71), channel_id=1, source_target_pairs={{0,4},{2,6},{4,0},{6,2},{8,12},{10,14},{12,8},{14,10},{16,20},{18,... | collective-permute-start | bytes 2359304 | tf_op jit(solution)/shard_map/ppermute | solution.py:1221
  306.2 21.5 %collective-permute-start.28 = (bf16[2,64,768]{2,1,0:T(8,128)(2,1)S(1)}, bf16[2,64,768]{2,1,0:T(8,128)(2,1)S(1)}, u32[]{:S(2)}, u32[]{:S(2)}) collective-permute-start(bf16[2,64,768]{2,1,0:T(8,128)(2,1)S(1)} %get-tuple-element.437), channel_id=1, source_target_pairs={{0,8},{2,10},{4,12},{6,14},{8,0},{10,2},{12,4},{14,6},{16,24},{18,... | collective-permute-start | bytes 589832 | tf_op jit(solution)/shard_map/ppermute | solution.py:1221
  329.1 43.7 %collective-permute-start.35 = (bf16[8,6,48,256]{3,2,1,0:T(8,128)(2,1)}, bf16[8,6,48,256]{3,2,1,0:T(8,128)(2,1)}, u32[]{:S(2)}, u32[]{:S(2)}) collective-permute-start(bf16[8,6,48,256]{3,2,1,0:T(8,128)(2,1)} %get-tuple-element.332), channel_id=1, source_target_pairs={{0,2},{2,0},{4,6},{6,4},{8,10},{10,8},{12,14},{14,12},{16,18},{18,... | collective-permute-start | bytes 3538952 | tf_op jit(solution)/shard_map/ppermute | solution.py:1221
  329.5 36.4 %collective-permute-start.36 = (bf16[8,5,48,256]{3,2,1,0:T(8,128)(2,1)}, bf16[8,5,48,256]{3,2,1,0:T(8,128)(2,1)}, u32[]{:S(2)}, u32[]{:S(2)}) collective-permute-start(bf16[8,5,48,256]{3,2,1,0:T(8,128)(2,1)} %get-tuple-element.333), channel_id=1, source_target_pairs={{0,4},{2,6},{4,0},{6,2},{8,12},{10,14},{12,8},{14,10},{16,20},{18,... | collective-permute-start | bytes 2949128 | tf_op jit(solution)/shard_map/ppermute | solution.py:1221
  332.1 46.1 %collective-permute-start.33 = (bf16[1,64,768]{2,1,0:T(8,128)(2,1)S(1)}, bf16[1,64,768]{2,1,0:T(8,128)(2,1)S(1)}, u32[]{:S(2)}, u32[]{:S(2)}) collective-permute-start(bf16[1,64,768]{2,1,0:T(8,128)(2,1)S(1)} %get-tuple-element.440), channel_id=1, source_target_pairs={{0,16},{2,18},{4,20},{6,22},{8,24},{10,26},{12,28},{14,30},{16,0},... | collective-permute-start | bytes 294920 | tf_op jit(solution)/shard_map/ppermute | solution.py:1221
  335.3 42.9 %collective-permute-start.34 = (bf16[1,64,768]{2,1,0:T(8,128)(2,1)S(1)}, bf16[1,64,768]{2,1,0:T(8,128)(2,1)S(1)}, u32[]{:S(2)}, u32[]{:S(2)}) collective-permute-start(bf16[1,64,768]{2,1,0:T(8,128)(2,1)S(1)} %get-tuple-element.438), channel_id=1, source_target_pairs={{0,16},{2,18},{4,20},{6,22},{8,24},{10,26},{12,28},{14,30},{16,0},... | collective-permute-start | bytes 294920 | tf_op jit(solution)/shard_map/ppermute | solution.py:1221
  336.1 54.4 %collective-permute-start.39 = (bf16[8,5,48,256]{3,2,1,0:T(8,128)(2,1)}, bf16[8,5,48,256]{3,2,1,0:T(8,128)(2,1)S(1)}, u32[]{:S(2)}, u32[]{:S(2)}) collective-permute-start(bf16[8,5,48,256]{3,2,1,0:T(8,128)(2,1)} %copy-done.60), channel_id=1, source_target_pairs={{0,8},{2,10},{4,12},{6,14},{8,0},{10,2},{12,4},{14,6},{16,24},{18,... | collective-permute-start | bytes 2949128 | tf_op jit(solution)/shard_map/ppermute | solution.py:1221
  470.6 25.6 %collective-permute-start.61 = (bf16[8,6,48,256]{3,2,1,0:T(8,128)(2,1)S(1)}, bf16[8,6,48,256]{3,2,1,0:T(8,128)(2,1)S(1)}, u32[]{:S(2)}, u32[]{:S(2)}) collective-permute-start(bf16[8,6,48,256]{3,2,1,0:T(8,128)(2,1)S(1)} %constant_dynamic-update-slice_fusion.near), channel_id=1, source_target_pairs={{0,2},{2,0},{4,6},{6,4},{8,10},{10,8},{12,14},{14,12},{16,18},{18,... | collective-permute-start | bytes 3538952 | tf_op jit(solution)/shard_map/ppermute | solution.py:1221
  (146 other events, 1234.1 us)
Sparse Core Ops, SparseCore 0:
  9.6 11.9 all-gather.6
  23.1 17.9 all-gather.10
  42.6 26.0 all-gather.8
  70.1 11.1 all-gather.14
  82.7 13.3 all-gather.12
  219.4 170.5 all-gather.16

commit v7 on v6

--- a/solution.py
+++ b/solution.py
@@ -1453,6 +1453,60 @@
         args,
         moved=sum(widths) * slots * size * 6,
         name="unpack_units",
+    )
+
+
+def unpack_second_body(orders, info, *refs):
+    pairs, outs = ([refs[i : i + 2] for i in (0, 2, 4)], refs[6:])
+    qkv_out, hout_out, gu_out, lout_out, light_out, dn_out = outs
+    slots, unused, size = refs[0].shape[:3]
+    half = gu_out.shape[1] // 2
+    blocks = half // COLS
+
+    def homes(targets):
+        return [(out, block * COLS) for out in targets for block in range(out.shape[1] // COLS)]
+
+    def put_units(source, targets, side, rows):
+        every = homes(targets)
+        for at in range(side, len(every), 2):
+            out, column = every[at]
+            out[rows, column : column + COLS] = source[at // 2].astype(F32)
+
+    for owner in range(2 * slots):
+        side, turn = divmod(owner, slots)
+        rows = slice(turn * size, (turn + 1) * size)
+
+        def first(source, side=side, rows=rows):
+            put_units(source, (qkv_out, hout_out), side, rows)
+
+        def second(source, side=side, rows=rows, owner=owner):
+            for block in range(blocks):
+                at = side * half + block * COLS
+                gu_out[rows, at : at + COLS] = source[block].astype(F32)
+            write_dn(lout_out, source, blocks, size, owner, 0)
+
+        def third(source, side=side, rows=rows, owner=owner):
+            put_units(source, (light_out,), side, rows)
+            used = light_out.shape[1] // (2 * COLS)
+            for block in range(dn_out.shape[0] // COLS):
+                write_dn(dn_out, source, used + block, size, owner, block * COLS)
+
+        for order, (near, far), write in zip(orders, pairs, (first, second, third)):
+            from_owner(info, order, near, far, owner, write)
+
+
+def unpack_second(info, orders, pairs, shapes):
+    args = [info] + [part for pair in pairs for part in pair]
+    outs = [sds(shape, F32) for shape in shapes]
+    return call(
+        functools.partial(unpack_second_body, orders),
+        outs,
+        (1,),
+        [whole(a.shape) for a in args[1:]],
+        [whole(out.shape) for out in outs],
+        args,
+        moved=20_000_000,
+        name="unpack_second",
     )
 
 
@@ -1731,11 +1785,15 @@
         g_hgu = unpack_plane_gu(info, plane_full, heavy_gu.shape[1] // (2 * COLS))
         got_two, g_hgu = tied(got_two, g_hgu)
         sums = list(zip(tails, got_two))
-        g_hqkv, g_hout = unpack_units(info, orders[0], sums[0], 0, widths)
-        g_lgu = unpack_gu(info, orders[1], sums[1], 0, 4, 4, 0, None, 4)
-        g_lout = unpack_dn(info, orders[1], sums[1], 4, 1, 1, 0, None, 1)
-        (g_lqkv,) = unpack_units(info, orders[2], sums[2], 0, (light_qkv.shape[1],))
-        g_ldown = unpack_dn(info, orders[2], sums[2], 3, 2, 2, 0, None, 1)
+        g_hqkv, g_hout, g_lgu, g_lout, g_lqkv, g_ldown = unpack_second(
+            info,
+            orders,
+            sums,
+            [
+                weight.shape
+                for weight in (heavy_qkv, heavy_out, light_gu, light_out, light_qkv, light_down)
+            ],
+        )
     else:
         g_hqkv, g_hout = plain_units(ha_own, ha_send, widths)
         (g_lqkv,) = plain_units(la_own, la_send, (light_qkv.shape[1],))

time: 526 us -> 521 us (level)
    pallas_call x3 -> x0, Pallas kernels: 6.6 us -> none  [unpack(): pl.pallas_call(functools.partial(body, order), out_shape=sds(shape, F32),...]
    pallas_call x31 -> x30, Pallas kernels: 219 us -> 221 us  [call(): pl.pallas_call(body, name=name or getattr(body, '__name__', 'kernel'), ou...]
    unnamed x207 -> x211, local copies, waits for them, and re-layouts: 30.6 us -> 31.2 us
  transfers between devices with their start and end apart: 70 -> 70, of which waited for: 34 -> 33; matrix products, arithmetic and copies ran while one was open for 6% -> 6% of each run, Pallas kernels for 38% -> 39%
where the time goes in v7:
time: 521 us; the launch traced here: 512 us
  Pallas kernels  221 us (42%)
  waiting for transfers between devices  132 us (25%)
  starting transfers between devices  80 us (15%)
  local copies, waits for them, and re-layouts  39.8 us (8%)
  other arithmetic  23.2 us (4%)
  between operations  15.6 us (3%)
    pallas_call x30, Pallas kernels, call(): pl.pallas_call(body, name=name or getattr(body, '__name__', 'kernel'), ou...  221 us
    ppermute x49, waiting for transfers between devices, flipped(): return lax.ppermute(value, 'ctx', [(i, i ^ bit) for i in range(size)])  109 us
    ppermute x49, starting transfers between devices, flipped(): return lax.ppermute(value, 'ctx', [(i, i ^ bit) for i in range(size)])  69.2 us
    unnamed x211, local copies, waits for them, and re-layouts  31.2 us
  transfers between devices with their start and end apart: 70, of which 33 were waited for; matrix products, arithmetic and copies ran while one was open for 6% of the time, Pallas kernels for 39%

profile of v7, /device:TPU:0, one launch (start us, length us, event | category | flops | bytes accessed | tf_op | source)
XLA Modules:
  0.0 511.6 jit_solution(4634158107415479373)
XLA Ops:
  26.4 7.4 %light_in_body.1.qkv = bf16[2,512,1536]{2,1,0:T(8,128)(2,1)} custom-call(s32[14]{0:T(128)S(1)} %concatenate.70.info, bf16[2,512,768]{2,1,0:T(8,128)(2,1)S(1)} %bitcast.54, bf16[8,768]{1,0:T(8,128)(2,1)S(1)} %pad_maximum_fusion.17.small, bf16[384,1536]{1,0:T(8,128)(2,1)} %l_own.1, bf16[384,1536]{1,0:T(8,128)(2,1)} %collective-permute-done.3.w_got.l_got), custom_call_target="tpu_custom_call" | custom-call | flops 2415919104 | bytes 8000000 | tf_op jit(solution)/shard_map/light_in_body/pallas_call | solution.py:74
  59.7 7.5 %light_inner_body.1 = (bf16[2,256,512]{2,1,0:T(8,128)(2,1)S(1)}, f32[2,256,128]{2,1,0:T(8,128)S(1)}) custom-call(s32[14]{0:T(128)S(1)} %concatenate.70.info, bf16[2,512,1536]{2,1,0:T(8,128)(2,1)S(1)} %copy-done.45), custom_call_target="tpu_custom_call" | custom-call | flops 2000000000 | bytes 4000000 | tf_op jit(solution)/shard_map/light_inner_body/pallas_call | solution.py:74
  85.9 9.2 %light_outer_body.1 = (bf16[2,512,512]{2,1,0:T(8,128)(2,1)S(1)}, f32[2,512,128]{2,1,0:T(8,128)S(1)}) custom-call(s32[14]{0:T(128)S(1)} %concatenate.70.info, bf16[2,512,1536]{2,1,0:T(8,128)(2,1)} %light_in_body.1.qkv, bf16[2,128,1024]{2,1,0:T(8,128)(2,1)} %collective-permute-done.9.before, bf16[2,128,1024]{2,1,0:T(8,128)(2,1)} %collective-permute-done.10.after, ...), custom_call_target="tpu_custom_call" | custom-call | flops 2000000000 | bytes 6000000 | tf_op jit(solution)/shard_map/light_outer_body/pallas_call | solution.py:74
  115.7 6.9 %middle_body.1 = (f32[2,512,768]{2,1,0:T(8,128)}, bf16[2,512,768]{2,1,0:T(8,128)(2,1)S(1)}, bf16[2,64,1536]{2,1,0:T(8,128)(2,1)S(1)}, f32[2,64,768]{2,1,0:T(8,128)S(1)}, f32[2,64,128]{2,1,0:T(8,128)S(1)}) custom-call(s32[14]{0:T(128)S(1)} %concatenate.70.info, bf16[2,512,768]{2,1,0:T(8,128)(2,1)} %bitcast.52, bf16[2,512,768]{2,1,0:T(8,128)(2,1)} %bitcast.75, ...), custom_call_target="tpu_custom_call" | custom-call | flops 2000000000 | bytes 12000000 | tf_op jit(solution)/shard_map/middle_body/pallas_call | solution.py:74
  126.2 14.1 %ffn_local_body.1 = (f32[128,768]{1,0:T(8,128)S(1)}, f32[128,768]{1,0:T(8,128)S(1)}) custom-call(s32[14]{0:T(128)S(1)} %concatenate.70.info, bf16[128,1536]{1,0:T(8,128)(2,1)S(1)} %bitcast.49, bf16[128,1536]{1,0:T(8,128)(2,1)S(1)} %bitcast.50, bf16[768,8192]{1,0:T(8,128)(2,1)} %all-gather.9.cloned.1.call-done.wg.wu, ...), custom_call_target="tpu_custom_call" | custom-call | flops 4831838208 | bytes 18874368 | tf_op jit(solution)/shard_map/ffn_local_body/pallas_call | solution.py:74
  146.9 8.7 %plane_grads_body.1 = (bf16[2,768,256]{2,1,0:T(8,128)(2,1)S(1)}, bf16[2,768,256]{2,1,0:T(8,128)(2,1)S(1)}, bf16[2,768,256]{2,1,0:T(8,128)(2,1)S(1)}) custom-call(s32[14]{0:T(128)S(1)} %concatenate.70.info, bf16[512,1536]{1,0:T(8,128)(2,1)S(1)} %pad_maximum_fusion.near, bf16[512,1536]{1,0:T(8,128)(2,1)S(1)} %collective-permute-done.17.far, ...), custom_call_target="tpu_custom_call" | custom-call | flops 4831838208 | bytes 9000000 | tf_op jit(solution)/shard_map/plane_grads_body/pallas_call | solution.py:74
  160.9 23.1 %ffn_all_body.1 = (bf16[1024,768]{1,0:T(8,128)(2,1)S(1)}, bf16[1024,768]{1,0:T(8,128)(2,1)S(1)}, bf16[4,768,256]{2,1,0:T(8,128)(2,1)}, bf16[4,768,256]{2,1,0:T(8...) custom-call(s32[14]{0:T(128)S(1)} %concatenate.70.info, bf16[1024,768]{1,0:T(8,128)(2,1)} %bitcast.72, ...), custom_call_target="tpu_custom_call" | custom-call | flops 14495514624 | bytes 18874368 | tf_op jit(solution)/shard_map/ffn_all_body/pallas_call | solution.py:74
  190.4 11.4 %mid_back_body.1 = (bf16[2,512,768]{2,1,0:T(8,128)(2,1)}, f32[2,512,768]{2,1,0:T(8,128)}, bf16[2,512,512]{2,1,0:T(8,128)(2,1)S(1)}, bf16[2,64,768]{2,1,0:T(8,128...) custom-call(s32[14]{0:T(128)S(1)} %concatenate.70.info, ...), custom_call_target="tpu_custom_call" | custom-call | flops 3000000000 | bytes 22000000 | tf_op jit(solution)/shard_map/mid_back_body/pallas_call | solution.py:74
  203.1 12.0 %light_bwd_outer_body.1 = (bf16[2,256,512]{2,1,0:T(8,128)(2,1)S(1)}, f32[2,512,1024]{2,1,0:T(8,128)}, bf16[2,128,1024]{2,1,0:T(8,128)(2,1)S(1)}, bf16[2,128,1024]{2,1,0:T(8,128)(2,1)S(1)}) custom-call(s32[14]{0:T(128)S(1)} %concatenate.70.info, bf16[2,512,1536]{2,1,0:T(8,128)(2,1)} %light_in_body.1.qkv, bf16[2,128,1024]{2,1,0:T(8,128)(2,1)} %collective-permute-done.9.before, ...), custom_call_target="tpu_custom_call" | custom-call | flops 5000000000 | bytes 12000000 | tf_op jit(solution)/shard_map/light_bwd_outer_body/pallas_call | solution.py:74
  223.2 10.7 %heavy_bwd_body.2 = (bf16[64,768]{1,0:T(8,128)(2,1)S(1)}, bf16[512,1536]{1,0:T(8,128)(2,1)S(1)}, bf16[512,1536]{1,0:T(8,128)(2,1)}, bf16[512,768]{1,0:T(8,128)(2,1)S(1)}, bf16[512,768]{1,0:T(8,128)(2,1)S(1)}) custom-call(s32[14]{0:T(128)S(1)} %concatenate.70.info, bf16[64,896]{1,0:T(8,128)(2,1)S(1)} %copy-done.53, bf16[512,896]{1,0:T(8,128)(2,1)S(1)} %copy-done.7, ...), custom_call_target="tpu_custom_call" | custom-call | flops 6499999744 | bytes 15000000 | tf_op jit(solution)/shard_map/heavy_bwd_body/pallas_call | solution.py:74
  235.1 10.4 %heavy_bwd_body.3 = (bf16[64,768]{1,0:T(8,128)(2,1)S(1)}, bf16[512,1536]{1,0:T(8,128)(2,1)S(1)}, bf16[512,1536]{1,0:T(8,128)(2,1)}, bf16[512,768]{1,0:T(8,128)(2,1)S(1)}, bf16[512,768]{1,0:T(8,128)(2,1)S(1)}) custom-call(s32[14]{0:T(128)S(1)} %concatenate.70.info, bf16[64,896]{1,0:T(8,128)(2,1)S(1)} %copy-done.51, bf16[512,896]{1,0:T(8,128)(2,1)S(1)} %copy-done.9, ...), custom_call_target="tpu_custom_call" | custom-call | flops 6499999744 | bytes 15000000 | tf_op jit(solution)/shard_map/heavy_bwd_body/pallas_call | solution.py:74
  252.9 13.0 %light_bwd_inner_body.1 = (bf16[2,512,512]{2,1,0:T(8,128)(2,1)S(1)}, f32[2,512,1024]{2,1,0:T(8,128)}) custom-call(s32[14]{0:T(128)S(1)} %concatenate.70.info, bf16[2,512,1536]{2,1,0:T(8,128)(2,1)} %light_in_body.1.qkv, f32[2,512,128]{2,1,0:T(8,128)S(1)} %copy-done.77, bf16[2,512,512]{2,1,0:T(8,128)(2,1)S(1)} %copy-done.59, ...), custom_call_target="tpu_custom_call" | custom-call | flops 5000000000 | bytes 14000000 | tf_op jit(solution)/shard_map/light_bwd_inner_body/pallas_call | solution.py:74
  265.9 10.7 %collective-permute-done.23 = bf16[8,64,768]{2,1,0:T(8,128)(2,1)} collective-permute-done((bf16[8,64,768]{2,1,0:T(8,128)(2,1)S(1)}, bf16[8,64,768]{2,1,0:T(8,128)(2,1)}, u32[]{:S(2)}, u32[]{:S(2)}) %collective-permute-start.23) | collective-permute-done | bytes 786464 | tf_op jit(solution)/shard_map/ppermute | solution.py:1221
  277.5 6.8 %light_join_body.1 = (bf16[2,512,1536]{2,1,0:T(8,128)(2,1)}, bf16[3,768,256]{2,1,0:T(8,128)(2,1)S(1)}, bf16[3,768,256]{2,1,0:T(8,128)(2,1)S(1)}) custom-call(s32[14]{0:T(128)S(1)} %concatenate.70.info, bf16[2,512,768]{2,1,0:T(8,128)(2,1)S(1)} %bitcast.55, bf16[8,768]{1,0:T(8,128)(2,1)S(1)} %pad_maximum_fusion.17.small, ...), custom_call_target="tpu_custom_call" | custom-call | flops 2415919104 | bytes 20000000 | tf_op jit(solution)/shard_map/light_join_body/pallas_call | solution.py:74
  290.5 13.5 %heavy_grads_body.1 = (bf16[7,768,256]{2,1,0:T(8,128)(2,1)}, bf16[7,768,256]{2,1,0:T(8,128)(2,1)}) custom-call(s32[14]{0:T(128)S(1)} %concatenate.70.info, bf16[2,64,896]{2,1,0:T(8,128)(2,1)S(1)} %copy-done.38, bf16[2,64,768]{2,1,0:T(8,128)(2,1)S(1)} %pad_maximum_fusion.15.refs_1_.dhq, bf16[2,64,768]{2,1,0:T(8,128)(2,1)S(1)} %copy-done.49, ...), custom_call_target="tpu_custom_call" | custom-call | flops 6499999744 | bytes 28000000 | tf_op jit(solution)/shard_map/heavy_grads_body/pallas_call | solution.py:74
  306.2 6.3 %collective-permute-done.32.refs_3_ = bf16[2,768,256]{2,1,0:T(8,128)(2,1)S(1)} collective-permute-done((bf16[2,768,256]{2,1,0:T(8,128)(2,1)S(1)}, bf16[2,768,256]{2,1,0:T(8,128)(2,1)S(1)}, u32[]{:S(2)}, u32[]{:S(2)}) %collective-permute-start.32) | collective-permute-done | bytes 786464 | tf_op jit(solution)/shard_map/ppermute | solution.py:1685
  335.1 29.5 %collective-permute-done.36 = bf16[8,5,48,256]{3,2,1,0:T(8,128)(2,1)} collective-permute-done((bf16[8,5,48,256]{3,2,1,0:T(8,128)(2,1)}, bf16[8,5,48,256]{3,2,1,0:T(8,128)(2,1)}, u32[]{:S(2)}, u32[]{:S(2)}) %collective-permute-start.36) | collective-permute-done | bytes 983072 | tf_op jit(solution)/shard_map/ppermute | solution.py:1221
  364.6 6.7 %collective-permute-done.35 = bf16[8,6,48,256]{3,2,1,0:T(8,128)(2,1)} collective-permute-done((bf16[8,6,48,256]{3,2,1,0:T(8,128)(2,1)}, bf16[8,6,48,256]{3,2,1,0:T(8,128)(2,1)}, u32[]{:S(2)}, u32[]{:S(2)}) %collective-permute-start.35) | collective-permute-done | bytes 1179680 | tf_op jit(solution)/shard_map/ppermute | solution.py:1221
  376.9 12.1 %in_back_body.1 = (bf16[2,512,768]{2,1,0:T(8,128)(2,1)}, f32[8,768]{1,0:T(8,128)S(1)}) custom-call(s32[14]{0:T(128)S(1)} %concatenate.70.info, bf16[2,512,768]{2,1,0:T(8,128)(2,1)S(1)} %bitcast.56, f32[2,512,768]{2,1,0:T(8,128)} %get-tuple-element.266.refs_5_.dy, bf16[2,512,1536]{2,1,0:T(8,128)(2,1)} %get-tuple-element.332.dl, ...), custom_call_target="tpu_custom_call" | custom-call | flops 2600000000 | bytes 14000000 | tf_op jit(solution)/shard_map/in_back_body/pallas_call | solution.py:74
  395.4 7.4 %collective-permute-done.41 = bf16[2,5,48,256]{3,2,1,0:T(8,128)(2,1)S(1)} collective-permute-done((bf16[2,5,48,256]{3,2,1,0:T(8,128)(2,1)S(1)}, bf16[2,5,48,256]{3,2,1,0:T(8,128)(2,1)S(1)}, u32[]{:S(2)}, u32[]{:S(2)}) %collective-permute-start.41) | collective-permute-done | bytes 245792 | tf_op jit(solution)/shard_map/ppermute | solution.py:1221
  417.0 8.8 %collective-permute-done.48 = bf16[1,5,48,256]{3,2,1,0:T(8,128)(2,1)S(1)} collective-permute-done((bf16[1,5,48,256]{3,2,1,0:T(8,128)(2,1)S(1)}, bf16[1,5,48,256]{3,2,1,0:T(8,128)(2,1)S(1)}, u32[]{:S(2)}, u32[]{:S(2)}) %collective-permute-start.48) | collective-permute-done | bytes 122912 | tf_op jit(solution)/shard_map/ppermute | solution.py:1221
  432.6 7.7 %collective-permute-done.50 = bf16[1,5,48,256]{3,2,1,0:T(8,128)(2,1)S(1)} collective-permute-done((bf16[1,5,48,256]{3,2,1,0:T(8,128)(2,1)S(1)}, bf16[1,5,48,256]{3,2,1,0:T(8,128)(2,1)S(1)}, u32[]{:S(2)}, u32[]{:S(2)}) %collective-permute-start.50) | collective-permute-done | bytes 122912 | tf_op jit(solution)/shard_map/ppermute | solution.py:1221
  476.6 10.8 %unpack_plane_gu.1 = f32[384,8192]{1,0:T(8,128)} custom-call(s32[14]{0:T(128)S(1)} %concatenate.70.info, bf16[2,2,4,6,192,256]{5,4,3,2,1,0:T(8,128)(2,1)} %bitcast.74), custom_call_target="tpu_custom_call" | custom-call | bytes 18874368 | tf_op jit(solution)/shard_map/unpack_plane_gu/pallas_call | solution.py:74
  496.5 8.1 %unpack_second.1 = (f32[384,2304]{1,0:T(8,128)}, f32[384,768]{1,0:T(8,128)}, f32[384,2048]{1,0:T(8,128)}, f32[256,768]{1,0:T(8,128)}, f32[384,1536]{1,0:T(8,128)}, /*index=5*/f32[512,768]{1,0:T(8,128)}) custom-call(s32[14]{0:T(128)S(1)} %concatenate.70.info, bf16[8,6,48,256]{3,2,1,0:T(8,128)(2,1)S(1)} %constant_dynamic-update-slice_fusion.refs_0_, ...), custom_call_target="tpu_custom_call" | custom-call | bytes 20000000 | tf_op jit(solution)/shard_map/unpack_second/pallas_call | solution.py:74
  (427 shorter events, 233.2 us)
Async XLA Ops:
  7.2 42.5 %all-gather.7.cloned.1.call-start = ((), (), s32[]{:S(2)}) async-start(), calls=%async_computation | async-start | bytes 1769472 | tf_op jit(solution)/shard_map/all_gather | solution.py:1587
  7.9 91.5 %all-gather.11.cloned.1.call-start = ((), (), s32[]{:S(2)}) async-start(), calls=%async_computation.2 | async-start | bytes 9437184 | tf_op jit(solution)/shard_map/all_gather | solution.py:1587
  8.7 90.7 %all-gather.9.cloned.1.call-start = ((), (), s32[]{:S(2)}) async-start(), calls=%async_computation.1 | async-start | bytes 18874368 | tf_op jit(solution)/shard_map/all_gather | solution.py:1587
  9.4 103.7 %all-gather.15.cloned.1.call-start = ((), (), s32[]{:S(2)}) async-start(), calls=%async_computation.4 | async-start | bytes 2359296 | tf_op jit(solution)/shard_map/all_gather | solution.py:1587
  10.0 103.1 %all-gather.13.cloned.1.call-start = ((), (), s32[]{:S(2)}) async-start(), calls=%async_computation.3 | async-start | bytes 4718592 | tf_op jit(solution)/shard_map/all_gather | solution.py:1587
  10.6 37.2 %collective-permute-start.6 = (bf16[384,2304]{1,0:T(8,128)(2,1)S(1)}, bf16[384,2304]{1,0:T(8,128)(2,1)S(1)}, u32[]{:S(2)}, u32[]{:S(2)}) collective-permute-start(bf16[384,2304]{1,0:T(8,128)(2,1)S(1)} %copy-done), channel_id=1, source_target_pairs={{0,1},{1,0},{2,3},{3,2},{4,5},{5,4},{6,7},{7,6},{8,9},{9,8},{10,11... | collective-permute-start | bytes 5308424 | tf_op jit(solution)/shard_map/ppermute | solution.py:1582
  11.9 448.3 %all-gather.17.cloned.1.call-start = ((), (), s32[]{:S(2)}) async-start(), calls=%async_computation.5 | async-start | bytes 10027008 | tf_op jit(solution)/shard_map/all_gather | solution.py:1698
  43.3 25.3 %collective-permute-start.9 = (bf16[2,128,1024]{2,1,0:T(8,128)(2,1)}, bf16[2,128,1024]{2,1,0:T(8,128)(2,1)}, u32[]{:S(2)}, u32[]{:S(2)}) collective-permute-start(bf16[2,128,1024]{2,1,0:T(8,128)(2,1)} %get-tuple-element.425), channel_id=1, source_target_pairs={{0,2},{2,4},{4,6},{6,8},{8,10},{10,12},{12,14},{14,16},{16,18},{18... | collective-permute-start | bytes 1572872 | tf_op jit(solution)/shard_map/ppermute | solution.py:1615
  46.5 24.5 %collective-permute-start.10 = (bf16[2,128,1024]{2,1,0:T(8,128)(2,1)}, bf16[2,128,1024]{2,1,0:T(8,128)(2,1)}, u32[]{:S(2)}, u32[]{:S(2)}) collective-permute-start(bf16[2,128,1024]{2,1,0:T(8,128)(2,1)} %get-tuple-element.424), channel_id=1, source_target_pairs={{2,0},{4,2},{6,4},{8,6},{10,8},{12,10},{14,12},{16,14},{18,16},{20... | collective-permute-start | bytes 1572872 | tf_op jit(solution)/shard_map/ppermute | solution.py:1616
  74.0 23.0 %collective-permute-start.11 = (bf16[512,896]{1,0:T(8,128)(2,1)S(1)}, bf16[512,896]{1,0:T(8,128)(2,1)S(1)}, u32[]{:S(2)}, u32[]{:S(2)}) collective-permute-start(bf16[512,896]{1,0:T(8,128)(2,1)S(1)} %pad_maximum_fusion.2.kin.kin_a.refs_6_), channel_id=1, source_target_pairs={{0,2},{2,0},{4,6},{6,4},{8,10},{10,8},{12,14},{14,12},{16,18},{18,... | collective-permute-start | bytes 2752520 | tf_op jit(solution)/shard_map/ppermute | solution.py:1221
  78.6 34.6 %collective-permute-start.13 = (bf16[256,768]{1,0:T(8,128)(2,1)}, bf16[256,768]{1,0:T(8,128)(2,1)}, u32[]{:S(2)}, u32[]{:S(2)}) collective-permute-start(bf16[256,768]{1,0:T(8,128)(2,1)} %lout.3), channel_id=1, source_target_pairs={{0,1},{1,0},{2,3},{3,2},{4,5},{5,4},{6,7},{7,6},{8,9},{9,8},{10,11... | collective-permute-start | bytes 1179656 | tf_op jit(solution)/shard_map/ppermute | solution.py:1582
  158.7 28.4 %collective-permute-start.19 = (bf16[2,6,192,256]{3,2,1,0:T(8,128)(2,1)S(1)}, bf16[2,6,192,256]{3,2,1,0:T(8,128)(2,1)S(1)}, u32[]{:S(2)}, u32[]{:S(2)}) collective-permute-start(bf16[2,6,192,256]{3,2,1,0:T(8,128)(2,1)S(1)} %get-tuple-element.251), channel_id=1, source_target_pairs={{0,8},{2,10},{4,12},{6,14},{8,0},{10,2},{12,4},{14,6},{16,24},{18,... | collective-permute-start | bytes 3538952 | tf_op jit(solution)/shard_map/ppermute | solution.py:1221
  187.3 28.7 %collective-permute-start.20 = (bf16[1,6,192,256]{3,2,1,0:T(8,128)(2,1)S(1)}, bf16[1,6,192,256]{3,2,1,0:T(8,128)(2,1)S(1)}, u32[]{:S(2)}, u32[]{:S(2)}) collective-permute-start(bf16[1,6,192,256]{3,2,1,0:T(8,128)(2,1)S(1)} %add_convert_fusion.4), channel_id=1, source_target_pairs={{0,16},{2,18},{4,20},{6,22},{8,24},{10,26},{12,28},{14,30},{16,0},... | collective-permute-start | bytes 1769480 | tf_op jit(solution)/shard_map/ppermute | solution.py:1221
  217.9 27.6 %collective-permute-start.21 = (bf16[2,128,1024]{2,1,0:T(8,128)(2,1)}, bf16[2,128,1024]{2,1,0:T(8,128)(2,1)S(1)}, u32[]{:S(2)}, u32[]{:S(2)}) collective-permute-start(bf16[2,128,1024]{2,1,0:T(8,128)(2,1)} %copy-done.64), channel_id=1, source_target_pairs={{0,2},{2,4},{4,6},{6,8},{8,10},{10,12},{12,14},{14,16},{16,18},{18... | collective-permute-start | bytes 1572872 | tf_op jit(solution)/shard_map/ppermute | solution.py:1700
  220.4 28.0 %collective-permute-start.22 = (bf16[2,128,1024]{2,1,0:T(8,128)(2,1)}, bf16[2,128,1024]{2,1,0:T(8,128)(2,1)S(1)}, u32[]{:S(2)}, u32[]{:S(2)}) collective-permute-start(bf16[2,128,1024]{2,1,0:T(8,128)(2,1)} %copy-done.63), channel_id=1, source_target_pairs={{2,0},{4,2},{6,4},{8,6},{10,8},{12,10},{14,12},{16,14},{18,16},{20... | collective-permute-start | bytes 1572872 | tf_op jit(solution)/shard_map/ppermute | solution.py:1701
  248.4 28.2 %collective-permute-start.23 = (bf16[8,64,768]{2,1,0:T(8,128)(2,1)S(1)}, bf16[8,64,768]{2,1,0:T(8,128)(2,1)}, u32[]{:S(2)}, u32[]{:S(2)}) collective-permute-start(bf16[8,64,768]{2,1,0:T(8,128)(2,1)S(1)} %bitcast.70), channel_id=1, source_target_pairs={{0,2},{2,0},{4,6},{6,4},{8,10},{10,8},{12,14},{14,12},{16,18},{18,... | collective-permute-start | bytes 2359304 | tf_op jit(solution)/shard_map/ppermute | solution.py:1221
  250.1 26.5 %collective-permute-start.24 = (bf16[8,64,768]{2,1,0:T(8,128)(2,1)S(1)}, bf16[8,64,768]{2,1,0:T(8,128)(2,1)S(1)}, u32[]{:S(2)}, u32[]{:S(2)}) collective-permute-start(bf16[8,64,768]{2,1,0:T(8,128)(2,1)S(1)} %bitcast.71), channel_id=1, source_target_pairs={{0,4},{2,6},{4,0},{6,2},{8,12},{10,14},{12,8},{14,10},{16,20},{18,... | collective-permute-start | bytes 2359304 | tf_op jit(solution)/shard_map/ppermute | solution.py:1221
  304.7 21.6 %collective-permute-start.28 = (bf16[2,64,768]{2,1,0:T(8,128)(2,1)S(1)}, bf16[2,64,768]{2,1,0:T(8,128)(2,1)S(1)}, u32[]{:S(2)}, u32[]{:S(2)}) collective-permute-start(bf16[2,64,768]{2,1,0:T(8,128)(2,1)S(1)} %get-tuple-element.445), channel_id=1, source_target_pairs={{0,8},{2,10},{4,12},{6,14},{8,0},{10,2},{12,4},{14,6},{16,24},{18,... | collective-permute-start | bytes 589832 | tf_op jit(solution)/shard_map/ppermute | solution.py:1221
  327.7 43.6 %collective-permute-start.35 = (bf16[8,6,48,256]{3,2,1,0:T(8,128)(2,1)}, bf16[8,6,48,256]{3,2,1,0:T(8,128)(2,1)}, u32[]{:S(2)}, u32[]{:S(2)}) collective-permute-start(bf16[8,6,48,256]{3,2,1,0:T(8,128)(2,1)} %get-tuple-element.336), channel_id=1, source_target_pairs={{0,2},{2,0},{4,6},{6,4},{8,10},{10,8},{12,14},{14,12},{16,18},{18,... | collective-permute-start | bytes 3538952 | tf_op jit(solution)/shard_map/ppermute | solution.py:1221
  328.1 36.5 %collective-permute-start.36 = (bf16[8,5,48,256]{3,2,1,0:T(8,128)(2,1)}, bf16[8,5,48,256]{3,2,1,0:T(8,128)(2,1)}, u32[]{:S(2)}, u32[]{:S(2)}) collective-permute-start(bf16[8,5,48,256]{3,2,1,0:T(8,128)(2,1)} %get-tuple-element.337), channel_id=1, source_target_pairs={{0,4},{2,6},{4,0},{6,2},{8,12},{10,14},{12,8},{14,10},{16,20},{18,... | collective-permute-start | bytes 2949128 | tf_op jit(solution)/shard_map/ppermute | solution.py:1221
  330.7 46.1 %collective-permute-start.33 = (bf16[1,64,768]{2,1,0:T(8,128)(2,1)S(1)}, bf16[1,64,768]{2,1,0:T(8,128)(2,1)S(1)}, u32[]{:S(2)}, u32[]{:S(2)}) collective-permute-start(bf16[1,64,768]{2,1,0:T(8,128)(2,1)S(1)} %get-tuple-element.448), channel_id=1, source_target_pairs={{0,16},{2,18},{4,20},{6,22},{8,24},{10,26},{12,28},{14,30},{16,0},... | collective-permute-start | bytes 294920 | tf_op jit(solution)/shard_map/ppermute | solution.py:1221
  333.8 43.0 %collective-permute-start.34 = (bf16[1,64,768]{2,1,0:T(8,128)(2,1)S(1)}, bf16[1,64,768]{2,1,0:T(8,128)(2,1)S(1)}, u32[]{:S(2)}, u32[]{:S(2)}) collective-permute-start(bf16[1,64,768]{2,1,0:T(8,128)(2,1)S(1)} %get-tuple-element.446), channel_id=1, source_target_pairs={{0,16},{2,18},{4,20},{6,22},{8,24},{10,26},{12,28},{14,30},{16,0},... | collective-permute-start | bytes 294920 | tf_op jit(solution)/shard_map/ppermute | solution.py:1221
  334.8 54.3 %collective-permute-start.39 = (bf16[8,5,48,256]{3,2,1,0:T(8,128)(2,1)}, bf16[8,5,48,256]{3,2,1,0:T(8,128)(2,1)S(1)}, u32[]{:S(2)}, u32[]{:S(2)}) collective-permute-start(bf16[8,5,48,256]{3,2,1,0:T(8,128)(2,1)} %copy-done.60), channel_id=1, source_target_pairs={{0,8},{2,10},{4,12},{6,14},{8,0},{10,2},{12,4},{14,6},{16,24},{18,... | collective-permute-start | bytes 2949128 | tf_op jit(solution)/shard_map/ppermute | solution.py:1221
  470.4 25.1 %collective-permute-start.61 = (bf16[8,6,48,256]{3,2,1,0:T(8,128)(2,1)S(1)}, bf16[8,6,48,256]{3,2,1,0:T(8,128)(2,1)S(1)}, u32[]{:S(2)}, u32[]{:S(2)}) collective-permute-start(bf16[8,6,48,256]{3,2,1,0:T(8,128)(2,1)S(1)} %constant_dynamic-update-slice_fusion.refs_0_), channel_id=1, source_target_pairs={{0,2},{2,0},{4,6},{6,4},{8,10},{10,8},{12,14},{14,12},{16,18},{18,... | collective-permute-start | bytes 3538952 | tf_op jit(solution)/shard_map/ppermute | solution.py:1221
  (148 other events, 1243.1 us)
Sparse Core Ops, SparseCore 0:
  9.6 11.9 all-gather.6
  23.1 17.9 all-gather.10
  42.6 26.0 all-gather.8
  70.1 11.4 all-gather.14
  82.9 12.8 all-gather.12
  218.0 170.5 all-gather.16

commit v8 on v7

--- a/solution.py
+++ b/solution.py
@@ -1663,7 +1663,7 @@
     if direct:
         mine = flat(pay)
         plane = [flipped(mine, bit) for bit in (1, 2, 3)]
-        zh, dff = ffn_local(info, mine, w_hgu, w_hdown, 2 * COLS)
+        zh, dff = ffn_local(info, mine, w_hgu, w_hdown, 4 * COLS)
         plane, zh, dff = tied(plane, zh, dff)
         near = jnp.concatenate([mine, *plane], axis=0)
         far = lax.ppermute(near, "wsh", swap)

time: 521 us -> 521 us (level)
  transfers between devices with their start and end apart: 70 -> 70, of which waited for: 33 -> 33; matrix products, arithmetic and copies ran while one was open for 6% -> 6% of each run, Pallas kernels for 39% -> 38%
where the time goes in v8:
time: 521 us; the launch traced here: 512 us
  Pallas kernels  220 us (42%)
  waiting for transfers between devices  133 us (26%)
  starting transfers between devices  80 us (15%)
  local copies, waits for them, and re-layouts  39.8 us (8%)
  other arithmetic  23.2 us (4%)
  between operations  15.6 us (3%)
    pallas_call x30, Pallas kernels, call(): pl.pallas_call(body, name=name or getattr(body, '__name__', 'kernel'), ou...  220 us
    ppermute x49, waiting for transfers between devices, flipped(): return lax.ppermute(value, 'ctx', [(i, i ^ bit) for i in range(size)])  110 us
    ppermute x49, starting transfers between devices, flipped(): return lax.ppermute(value, 'ctx', [(i, i ^ bit) for i in range(size)])  69.2 us
    unnamed x211, local copies, waits for them, and re-layouts  31.2 us
  transfers between devices with their start and end apart: 70, of which 33 were waited for; matrix products, arithmetic and copies ran while one was open for 6% of the time, Pallas kernels for 38%

profile of v8, /device:TPU:0, one launch (start us, length us, event | category | flops | bytes accessed | tf_op | source)
XLA Modules:
  0.0 511.6 jit_solution(7405851657376497387)
XLA Ops:
  26.4 7.4 %light_in_body.1.qkv = bf16[2,512,1536]{2,1,0:T(8,128)(2,1)} custom-call(s32[14]{0:T(128)S(1)} %concatenate.70.info, bf16[2,512,768]{2,1,0:T(8,128)(2,1)S(1)} %bitcast.54, bf16[8,768]{1,0:T(8,128)(2,1)S(1)} %pad_maximum_fusion.17.small, bf16[384,1536]{1,0:T(8,128)(2,1)} %l_own.1, bf16[384,1536]{1,0:T(8,128)(2,1)} %collective-permute-done.3.w_got.l_got), custom_call_target="tpu_custom_call" | custom-call | flops 2415919104 | bytes 8000000 | tf_op jit(solution)/shard_map/light_in_body/pallas_call | solution.py:74
  59.7 7.5 %light_inner_body.1 = (bf16[2,256,512]{2,1,0:T(8,128)(2,1)S(1)}, f32[2,256,128]{2,1,0:T(8,128)S(1)}) custom-call(s32[14]{0:T(128)S(1)} %concatenate.70.info, bf16[2,512,1536]{2,1,0:T(8,128)(2,1)S(1)} %copy-done.45), custom_call_target="tpu_custom_call" | custom-call | flops 2000000000 | bytes 4000000 | tf_op jit(solution)/shard_map/light_inner_body/pallas_call | solution.py:74
  85.9 9.2 %light_outer_body.1 = (bf16[2,512,512]{2,1,0:T(8,128)(2,1)S(1)}, f32[2,512,128]{2,1,0:T(8,128)S(1)}) custom-call(s32[14]{0:T(128)S(1)} %concatenate.70.info, bf16[2,512,1536]{2,1,0:T(8,128)(2,1)} %light_in_body.1.qkv, bf16[2,128,1024]{2,1,0:T(8,128)(2,1)} %collective-permute-done.9.before, bf16[2,128,1024]{2,1,0:T(8,128)(2,1)} %collective-permute-done.10.after, ...), custom_call_target="tpu_custom_call" | custom-call | flops 2000000000 | bytes 6000000 | tf_op jit(solution)/shard_map/light_outer_body/pallas_call | solution.py:74
  115.7 6.9 %middle_body.1 = (f32[2,512,768]{2,1,0:T(8,128)}, bf16[2,512,768]{2,1,0:T(8,128)(2,1)S(1)}, bf16[2,64,1536]{2,1,0:T(8,128)(2,1)S(1)}, f32[2,64,768]{2,1,0:T(8,128)S(1)}, f32[2,64,128]{2,1,0:T(8,128)S(1)}) custom-call(s32[14]{0:T(128)S(1)} %concatenate.70.info, bf16[2,512,768]{2,1,0:T(8,128)(2,1)} %bitcast.52, bf16[2,512,768]{2,1,0:T(8,128)(2,1)} %bitcast.75, ...), custom_call_target="tpu_custom_call" | custom-call | flops 2000000000 | bytes 12000000 | tf_op jit(solution)/shard_map/middle_body/pallas_call | solution.py:74
  126.2 12.9 %ffn_local_body.1 = (f32[128,768]{1,0:T(8,128)S(1)}, f32[128,768]{1,0:T(8,128)S(1)}) custom-call(s32[14]{0:T(128)S(1)} %concatenate.70.info, bf16[128,1536]{1,0:T(8,128)(2,1)S(1)} %bitcast.49, bf16[128,1536]{1,0:T(8,128)(2,1)S(1)} %bitcast.50, bf16[768,8192]{1,0:T(8,128)(2,1)} %all-gather.9.cloned.1.call-done.wg.wu, ...), custom_call_target="tpu_custom_call" | custom-call | flops 4831838208 | bytes 18874368 | tf_op jit(solution)/shard_map/ffn_local_body/pallas_call | solution.py:74
  146.9 8.7 %plane_grads_body.1 = (bf16[2,768,256]{2,1,0:T(8,128)(2,1)S(1)}, bf16[2,768,256]{2,1,0:T(8,128)(2,1)S(1)}, bf16[2,768,256]{2,1,0:T(8,128)(2,1)S(1)}) custom-call(s32[14]{0:T(128)S(1)} %concatenate.70.info, bf16[512,1536]{1,0:T(8,128)(2,1)S(1)} %pad_maximum_fusion.near, bf16[512,1536]{1,0:T(8,128)(2,1)S(1)} %collective-permute-done.17.far, ...), custom_call_target="tpu_custom_call" | custom-call | flops 4831838208 | bytes 9000000 | tf_op jit(solution)/shard_map/plane_grads_body/pallas_call | solution.py:74
  160.9 23.1 %ffn_all_body.1 = (bf16[1024,768]{1,0:T(8,128)(2,1)S(1)}, bf16[1024,768]{1,0:T(8,128)(2,1)S(1)}, bf16[4,768,256]{2,1,0:T(8,128)(2,1)}, bf16[4,768,256]{2,1,0:T(8...) custom-call(s32[14]{0:T(128)S(1)} %concatenate.70.info, bf16[1024,768]{1,0:T(8,128)(2,1)} %bitcast.72, ...), custom_call_target="tpu_custom_call" | custom-call | flops 14495514624 | bytes 18874368 | tf_op jit(solution)/shard_map/ffn_all_body/pallas_call | solution.py:74
  190.4 11.4 %mid_back_body.1 = (bf16[2,512,768]{2,1,0:T(8,128)(2,1)}, f32[2,512,768]{2,1,0:T(8,128)}, bf16[2,512,512]{2,1,0:T(8,128)(2,1)S(1)}, bf16[2,64,768]{2,1,0:T(8,128...) custom-call(s32[14]{0:T(128)S(1)} %concatenate.70.info, ...), custom_call_target="tpu_custom_call" | custom-call | flops 3000000000 | bytes 22000000 | tf_op jit(solution)/shard_map/mid_back_body/pallas_call | solution.py:74
  203.1 12.0 %light_bwd_outer_body.1 = (bf16[2,256,512]{2,1,0:T(8,128)(2,1)S(1)}, f32[2,512,1024]{2,1,0:T(8,128)}, bf16[2,128,1024]{2,1,0:T(8,128)(2,1)S(1)}, bf16[2,128,1024]{2,1,0:T(8,128)(2,1)S(1)}) custom-call(s32[14]{0:T(128)S(1)} %concatenate.70.info, bf16[2,512,1536]{2,1,0:T(8,128)(2,1)} %light_in_body.1.qkv, bf16[2,128,1024]{2,1,0:T(8,128)(2,1)} %collective-permute-done.9.before, ...), custom_call_target="tpu_custom_call" | custom-call | flops 5000000000 | bytes 12000000 | tf_op jit(solution)/shard_map/light_bwd_outer_body/pallas_call | solution.py:74
  223.2 10.7 %heavy_bwd_body.2 = (bf16[64,768]{1,0:T(8,128)(2,1)S(1)}, bf16[512,1536]{1,0:T(8,128)(2,1)S(1)}, bf16[512,1536]{1,0:T(8,128)(2,1)}, bf16[512,768]{1,0:T(8,128)(2,1)S(1)}, bf16[512,768]{1,0:T(8,128)(2,1)S(1)}) custom-call(s32[14]{0:T(128)S(1)} %concatenate.70.info, bf16[64,896]{1,0:T(8,128)(2,1)S(1)} %copy-done.53, bf16[512,896]{1,0:T(8,128)(2,1)S(1)} %copy-done.7, ...), custom_call_target="tpu_custom_call" | custom-call | flops 6499999744 | bytes 15000000 | tf_op jit(solution)/shard_map/heavy_bwd_body/pallas_call | solution.py:74
  235.1 10.4 %heavy_bwd_body.3 = (bf16[64,768]{1,0:T(8,128)(2,1)S(1)}, bf16[512,1536]{1,0:T(8,128)(2,1)S(1)}, bf16[512,1536]{1,0:T(8,128)(2,1)}, bf16[512,768]{1,0:T(8,128)(2,1)S(1)}, bf16[512,768]{1,0:T(8,128)(2,1)S(1)}) custom-call(s32[14]{0:T(128)S(1)} %concatenate.70.info, bf16[64,896]{1,0:T(8,128)(2,1)S(1)} %copy-done.51, bf16[512,896]{1,0:T(8,128)(2,1)S(1)} %copy-done.9, ...), custom_call_target="tpu_custom_call" | custom-call | flops 6499999744 | bytes 15000000 | tf_op jit(solution)/shard_map/heavy_bwd_body/pallas_call | solution.py:74
  252.9 13.0 %light_bwd_inner_body.1 = (bf16[2,512,512]{2,1,0:T(8,128)(2,1)S(1)}, f32[2,512,1024]{2,1,0:T(8,128)}) custom-call(s32[14]{0:T(128)S(1)} %concatenate.70.info, bf16[2,512,1536]{2,1,0:T(8,128)(2,1)} %light_in_body.1.qkv, f32[2,512,128]{2,1,0:T(8,128)S(1)} %copy-done.77, bf16[2,512,512]{2,1,0:T(8,128)(2,1)S(1)} %copy-done.59, ...), custom_call_target="tpu_custom_call" | custom-call | flops 5000000000 | bytes 14000000 | tf_op jit(solution)/shard_map/light_bwd_inner_body/pallas_call | solution.py:74
  265.9 10.7 %collective-permute-done.23 = bf16[8,64,768]{2,1,0:T(8,128)(2,1)} collective-permute-done((bf16[8,64,768]{2,1,0:T(8,128)(2,1)S(1)}, bf16[8,64,768]{2,1,0:T(8,128)(2,1)}, u32[]{:S(2)}, u32[]{:S(2)}) %collective-permute-start.23) | collective-permute-done | bytes 786464 | tf_op jit(solution)/shard_map/ppermute | solution.py:1221
  277.5 6.8 %light_join_body.1 = (bf16[2,512,1536]{2,1,0:T(8,128)(2,1)}, bf16[3,768,256]{2,1,0:T(8,128)(2,1)S(1)}, bf16[3,768,256]{2,1,0:T(8,128)(2,1)S(1)}) custom-call(s32[14]{0:T(128)S(1)} %concatenate.70.info, bf16[2,512,768]{2,1,0:T(8,128)(2,1)S(1)} %bitcast.55, bf16[8,768]{1,0:T(8,128)(2,1)S(1)} %pad_maximum_fusion.17.small, ...), custom_call_target="tpu_custom_call" | custom-call | flops 2415919104 | bytes 20000000 | tf_op jit(solution)/shard_map/light_join_body/pallas_call | solution.py:74
  290.5 13.5 %heavy_grads_body.1 = (bf16[7,768,256]{2,1,0:T(8,128)(2,1)}, bf16[7,768,256]{2,1,0:T(8,128)(2,1)}) custom-call(s32[14]{0:T(128)S(1)} %concatenate.70.info, bf16[2,64,896]{2,1,0:T(8,128)(2,1)S(1)} %copy-done.38, bf16[2,64,768]{2,1,0:T(8,128)(2,1)S(1)} %pad_maximum_fusion.15.refs_1_.dhq, bf16[2,64,768]{2,1,0:T(8,128)(2,1)S(1)} %copy-done.49, ...), custom_call_target="tpu_custom_call" | custom-call | flops 6499999744 | bytes 28000000 | tf_op jit(solution)/shard_map/heavy_grads_body/pallas_call | solution.py:74
  306.2 6.3 %collective-permute-done.32.refs_3_ = bf16[2,768,256]{2,1,0:T(8,128)(2,1)S(1)} collective-permute-done((bf16[2,768,256]{2,1,0:T(8,128)(2,1)S(1)}, bf16[2,768,256]{2,1,0:T(8,128)(2,1)S(1)}, u32[]{:S(2)}, u32[]{:S(2)}) %collective-permute-start.32) | collective-permute-done | bytes 786464 | tf_op jit(solution)/shard_map/ppermute | solution.py:1685
  335.1 29.5 %collective-permute-done.36 = bf16[8,5,48,256]{3,2,1,0:T(8,128)(2,1)} collective-permute-done((bf16[8,5,48,256]{3,2,1,0:T(8,128)(2,1)}, bf16[8,5,48,256]{3,2,1,0:T(8,128)(2,1)}, u32[]{:S(2)}, u32[]{:S(2)}) %collective-permute-start.36) | collective-permute-done | bytes 983072 | tf_op jit(solution)/shard_map/ppermute | solution.py:1221
  364.6 6.7 %collective-permute-done.35 = bf16[8,6,48,256]{3,2,1,0:T(8,128)(2,1)} collective-permute-done((bf16[8,6,48,256]{3,2,1,0:T(8,128)(2,1)}, bf16[8,6,48,256]{3,2,1,0:T(8,128)(2,1)}, u32[]{:S(2)}, u32[]{:S(2)}) %collective-permute-start.35) | collective-permute-done | bytes 1179680 | tf_op jit(solution)/shard_map/ppermute | solution.py:1221
  376.9 12.1 %in_back_body.1 = (bf16[2,512,768]{2,1,0:T(8,128)(2,1)}, f32[8,768]{1,0:T(8,128)S(1)}) custom-call(s32[14]{0:T(128)S(1)} %concatenate.70.info, bf16[2,512,768]{2,1,0:T(8,128)(2,1)S(1)} %bitcast.56, f32[2,512,768]{2,1,0:T(8,128)} %get-tuple-element.266.refs_5_.dy, bf16[2,512,1536]{2,1,0:T(8,128)(2,1)} %get-tuple-element.332.dl, ...), custom_call_target="tpu_custom_call" | custom-call | flops 2600000000 | bytes 14000000 | tf_op jit(solution)/shard_map/in_back_body/pallas_call | solution.py:74
  395.4 7.4 %collective-permute-done.41 = bf16[2,5,48,256]{3,2,1,0:T(8,128)(2,1)S(1)} collective-permute-done((bf16[2,5,48,256]{3,2,1,0:T(8,128)(2,1)S(1)}, bf16[2,5,48,256]{3,2,1,0:T(8,128)(2,1)S(1)}, u32[]{:S(2)}, u32[]{:S(2)}) %collective-permute-start.41) | collective-permute-done | bytes 245792 | tf_op jit(solution)/shard_map/ppermute | solution.py:1221
  417.0 8.8 %collective-permute-done.48 = bf16[1,5,48,256]{3,2,1,0:T(8,128)(2,1)S(1)} collective-permute-done((bf16[1,5,48,256]{3,2,1,0:T(8,128)(2,1)S(1)}, bf16[1,5,48,256]{3,2,1,0:T(8,128)(2,1)S(1)}, u32[]{:S(2)}, u32[]{:S(2)}) %collective-permute-start.48) | collective-permute-done | bytes 122912 | tf_op jit(solution)/shard_map/ppermute | solution.py:1221
  432.6 7.7 %collective-permute-done.50 = bf16[1,5,48,256]{3,2,1,0:T(8,128)(2,1)S(1)} collective-permute-done((bf16[1,5,48,256]{3,2,1,0:T(8,128)(2,1)S(1)}, bf16[1,5,48,256]{3,2,1,0:T(8,128)(2,1)S(1)}, u32[]{:S(2)}, u32[]{:S(2)}) %collective-permute-start.50) | collective-permute-done | bytes 122912 | tf_op jit(solution)/shard_map/ppermute | solution.py:1221
  476.6 10.8 %unpack_plane_gu.1 = f32[384,8192]{1,0:T(8,128)} custom-call(s32[14]{0:T(128)S(1)} %concatenate.70.info, bf16[2,2,4,6,192,256]{5,4,3,2,1,0:T(8,128)(2,1)} %bitcast.74), custom_call_target="tpu_custom_call" | custom-call | bytes 18874368 | tf_op jit(solution)/shard_map/unpack_plane_gu/pallas_call | solution.py:74
  496.5 8.1 %unpack_second.1 = (f32[384,2304]{1,0:T(8,128)}, f32[384,768]{1,0:T(8,128)}, f32[384,2048]{1,0:T(8,128)}, f32[256,768]{1,0:T(8,128)}, f32[384,1536]{1,0:T(8,128)}, /*index=5*/f32[512,768]{1,0:T(8,128)}) custom-call(s32[14]{0:T(128)S(1)} %concatenate.70.info, bf16[8,6,48,256]{3,2,1,0:T(8,128)(2,1)S(1)} %constant_dynamic-update-slice_fusion.refs_0_, ...), custom_call_target="tpu_custom_call" | custom-call | bytes 20000000 | tf_op jit(solution)/shard_map/unpack_second/pallas_call | solution.py:74
  (427 shorter events, 234.4 us)
Async XLA Ops:
  7.2 42.5 %all-gather.7.cloned.1.call-start = ((), (), s32[]{:S(2)}) async-start(), calls=%async_computation | async-start | bytes 1769472 | tf_op jit(solution)/shard_map/all_gather | solution.py:1587
  7.9 91.5 %all-gather.11.cloned.1.call-start = ((), (), s32[]{:S(2)}) async-start(), calls=%async_computation.2 | async-start | bytes 9437184 | tf_op jit(solution)/shard_map/all_gather | solution.py:1587
  8.7 90.7 %all-gather.9.cloned.1.call-start = ((), (), s32[]{:S(2)}) async-start(), calls=%async_computation.1 | async-start | bytes 18874368 | tf_op jit(solution)/shard_map/all_gather | solution.py:1587
  9.4 103.7 %all-gather.15.cloned.1.call-start = ((), (), s32[]{:S(2)}) async-start(), calls=%async_computation.4 | async-start | bytes 2359296 | tf_op jit(solution)/shard_map/all_gather | solution.py:1587
  10.0 103.1 %all-gather.13.cloned.1.call-start = ((), (), s32[]{:S(2)}) async-start(), calls=%async_computation.3 | async-start | bytes 4718592 | tf_op jit(solution)/shard_map/all_gather | solution.py:1587
  10.6 37.2 %collective-permute-start.6 = (bf16[384,2304]{1,0:T(8,128)(2,1)S(1)}, bf16[384,2304]{1,0:T(8,128)(2,1)S(1)}, u32[]{:S(2)}, u32[]{:S(2)}) collective-permute-start(bf16[384,2304]{1,0:T(8,128)(2,1)S(1)} %copy-done), channel_id=1, source_target_pairs={{0,1},{1,0},{2,3},{3,2},{4,5},{5,4},{6,7},{7,6},{8,9},{9,8},{10,11... | collective-permute-start | bytes 5308424 | tf_op jit(solution)/shard_map/ppermute | solution.py:1582
  11.9 448.3 %all-gather.17.cloned.1.call-start = ((), (), s32[]{:S(2)}) async-start(), calls=%async_computation.5 | async-start | bytes 10027008 | tf_op jit(solution)/shard_map/all_gather | solution.py:1698
  43.3 25.3 %collective-permute-start.9 = (bf16[2,128,1024]{2,1,0:T(8,128)(2,1)}, bf16[2,128,1024]{2,1,0:T(8,128)(2,1)}, u32[]{:S(2)}, u32[]{:S(2)}) collective-permute-start(bf16[2,128,1024]{2,1,0:T(8,128)(2,1)} %get-tuple-element.425), channel_id=1, source_target_pairs={{0,2},{2,4},{4,6},{6,8},{8,10},{10,12},{12,14},{14,16},{16,18},{18... | collective-permute-start | bytes 1572872 | tf_op jit(solution)/shard_map/ppermute | solution.py:1615
  46.5 24.5 %collective-permute-start.10 = (bf16[2,128,1024]{2,1,0:T(8,128)(2,1)}, bf16[2,128,1024]{2,1,0:T(8,128)(2,1)}, u32[]{:S(2)}, u32[]{:S(2)}) collective-permute-start(bf16[2,128,1024]{2,1,0:T(8,128)(2,1)} %get-tuple-element.424), channel_id=1, source_target_pairs={{2,0},{4,2},{6,4},{8,6},{10,8},{12,10},{14,12},{16,14},{18,16},{20... | collective-permute-start | bytes 1572872 | tf_op jit(solution)/shard_map/ppermute | solution.py:1616
  74.0 23.0 %collective-permute-start.11 = (bf16[512,896]{1,0:T(8,128)(2,1)S(1)}, bf16[512,896]{1,0:T(8,128)(2,1)S(1)}, u32[]{:S(2)}, u32[]{:S(2)}) collective-permute-start(bf16[512,896]{1,0:T(8,128)(2,1)S(1)} %pad_maximum_fusion.2.kin.kin_a.refs_6_), channel_id=1, source_target_pairs={{0,2},{2,0},{4,6},{6,4},{8,10},{10,8},{12,14},{14,12},{16,18},{18,... | collective-permute-start | bytes 2752520 | tf_op jit(solution)/shard_map/ppermute | solution.py:1221
  78.6 34.6 %collective-permute-start.13 = (bf16[256,768]{1,0:T(8,128)(2,1)}, bf16[256,768]{1,0:T(8,128)(2,1)}, u32[]{:S(2)}, u32[]{:S(2)}) collective-permute-start(bf16[256,768]{1,0:T(8,128)(2,1)} %lout.3), channel_id=1, source_target_pairs={{0,1},{1,0},{2,3},{3,2},{4,5},{5,4},{6,7},{7,6},{8,9},{9,8},{10,11... | collective-permute-start | bytes 1179656 | tf_op jit(solution)/shard_map/ppermute | solution.py:1582
  158.7 28.4 %collective-permute-start.19 = (bf16[2,6,192,256]{3,2,1,0:T(8,128)(2,1)S(1)}, bf16[2,6,192,256]{3,2,1,0:T(8,128)(2,1)S(1)}, u32[]{:S(2)}, u32[]{:S(2)}) collective-permute-start(bf16[2,6,192,256]{3,2,1,0:T(8,128)(2,1)S(1)} %get-tuple-element.251), channel_id=1, source_target_pairs={{0,8},{2,10},{4,12},{6,14},{8,0},{10,2},{12,4},{14,6},{16,24},{18,... | collective-permute-start | bytes 3538952 | tf_op jit(solution)/shard_map/ppermute | solution.py:1221
  187.3 28.7 %collective-permute-start.20 = (bf16[1,6,192,256]{3,2,1,0:T(8,128)(2,1)S(1)}, bf16[1,6,192,256]{3,2,1,0:T(8,128)(2,1)S(1)}, u32[]{:S(2)}, u32[]{:S(2)}) collective-permute-start(bf16[1,6,192,256]{3,2,1,0:T(8,128)(2,1)S(1)} %add_convert_fusion.4), channel_id=1, source_target_pairs={{0,16},{2,18},{4,20},{6,22},{8,24},{10,26},{12,28},{14,30},{16,0},... | collective-permute-start | bytes 1769480 | tf_op jit(solution)/shard_map/ppermute | solution.py:1221
  217.9 27.6 %collective-permute-start.21 = (bf16[2,128,1024]{2,1,0:T(8,128)(2,1)}, bf16[2,128,1024]{2,1,0:T(8,128)(2,1)S(1)}, u32[]{:S(2)}, u32[]{:S(2)}) collective-permute-start(bf16[2,128,1024]{2,1,0:T(8,128)(2,1)} %copy-done.64), channel_id=1, source_target_pairs={{0,2},{2,4},{4,6},{6,8},{8,10},{10,12},{12,14},{14,16},{16,18},{18... | collective-permute-start | bytes 1572872 | tf_op jit(solution)/shard_map/ppermute | solution.py:1700
  220.4 28.0 %collective-permute-start.22 = (bf16[2,128,1024]{2,1,0:T(8,128)(2,1)}, bf16[2,128,1024]{2,1,0:T(8,128)(2,1)S(1)}, u32[]{:S(2)}, u32[]{:S(2)}) collective-permute-start(bf16[2,128,1024]{2,1,0:T(8,128)(2,1)} %copy-done.63), channel_id=1, source_target_pairs={{2,0},{4,2},{6,4},{8,6},{10,8},{12,10},{14,12},{16,14},{18,16},{20... | collective-permute-start | bytes 1572872 | tf_op jit(solution)/shard_map/ppermute | solution.py:1701
  248.4 28.2 %collective-permute-start.23 = (bf16[8,64,768]{2,1,0:T(8,128)(2,1)S(1)}, bf16[8,64,768]{2,1,0:T(8,128)(2,1)}, u32[]{:S(2)}, u32[]{:S(2)}) collective-permute-start(bf16[8,64,768]{2,1,0:T(8,128)(2,1)S(1)} %bitcast.70), channel_id=1, source_target_pairs={{0,2},{2,0},{4,6},{6,4},{8,10},{10,8},{12,14},{14,12},{16,18},{18,... | collective-permute-start | bytes 2359304 | tf_op jit(solution)/shard_map/ppermute | solution.py:1221
  250.1 26.5 %collective-permute-start.24 = (bf16[8,64,768]{2,1,0:T(8,128)(2,1)S(1)}, bf16[8,64,768]{2,1,0:T(8,128)(2,1)S(1)}, u32[]{:S(2)}, u32[]{:S(2)}) collective-permute-start(bf16[8,64,768]{2,1,0:T(8,128)(2,1)S(1)} %bitcast.71), channel_id=1, source_target_pairs={{0,4},{2,6},{4,0},{6,2},{8,12},{10,14},{12,8},{14,10},{16,20},{18,... | collective-permute-start | bytes 2359304 | tf_op jit(solution)/shard_map/ppermute | solution.py:1221
  304.7 21.6 %collective-permute-start.28 = (bf16[2,64,768]{2,1,0:T(8,128)(2,1)S(1)}, bf16[2,64,768]{2,1,0:T(8,128)(2,1)S(1)}, u32[]{:S(2)}, u32[]{:S(2)}) collective-permute-start(bf16[2,64,768]{2,1,0:T(8,128)(2,1)S(1)} %get-tuple-element.445), channel_id=1, source_target_pairs={{0,8},{2,10},{4,12},{6,14},{8,0},{10,2},{12,4},{14,6},{16,24},{18,... | collective-permute-start | bytes 589832 | tf_op jit(solution)/shard_map/ppermute | solution.py:1221
  327.7 43.6 %collective-permute-start.35 = (bf16[8,6,48,256]{3,2,1,0:T(8,128)(2,1)}, bf16[8,6,48,256]{3,2,1,0:T(8,128)(2,1)}, u32[]{:S(2)}, u32[]{:S(2)}) collective-permute-start(bf16[8,6,48,256]{3,2,1,0:T(8,128)(2,1)} %get-tuple-element.336), channel_id=1, source_target_pairs={{0,2},{2,0},{4,6},{6,4},{8,10},{10,8},{12,14},{14,12},{16,18},{18,... | collective-permute-start | bytes 3538952 | tf_op jit(solution)/shard_map/ppermute | solution.py:1221
  328.1 36.5 %collective-permute-start.36 = (bf16[8,5,48,256]{3,2,1,0:T(8,128)(2,1)}, bf16[8,5,48,256]{3,2,1,0:T(8,128)(2,1)}, u32[]{:S(2)}, u32[]{:S(2)}) collective-permute-start(bf16[8,5,48,256]{3,2,1,0:T(8,128)(2,1)} %get-tuple-element.337), channel_id=1, source_target_pairs={{0,4},{2,6},{4,0},{6,2},{8,12},{10,14},{12,8},{14,10},{16,20},{18,... | collective-permute-start | bytes 2949128 | tf_op jit(solution)/shard_map/ppermute | solution.py:1221
  330.7 46.1 %collective-permute-start.33 = (bf16[1,64,768]{2,1,0:T(8,128)(2,1)S(1)}, bf16[1,64,768]{2,1,0:T(8,128)(2,1)S(1)}, u32[]{:S(2)}, u32[]{:S(2)}) collective-permute-start(bf16[1,64,768]{2,1,0:T(8,128)(2,1)S(1)} %get-tuple-element.448), channel_id=1, source_target_pairs={{0,16},{2,18},{4,20},{6,22},{8,24},{10,26},{12,28},{14,30},{16,0},... | collective-permute-start | bytes 294920 | tf_op jit(solution)/shard_map/ppermute | solution.py:1221
  333.8 43.0 %collective-permute-start.34 = (bf16[1,64,768]{2,1,0:T(8,128)(2,1)S(1)}, bf16[1,64,768]{2,1,0:T(8,128)(2,1)S(1)}, u32[]{:S(2)}, u32[]{:S(2)}) collective-permute-start(bf16[1,64,768]{2,1,0:T(8,128)(2,1)S(1)} %get-tuple-element.446), channel_id=1, source_target_pairs={{0,16},{2,18},{4,20},{6,22},{8,24},{10,26},{12,28},{14,30},{16,0},... | collective-permute-start | bytes 294920 | tf_op jit(solution)/shard_map/ppermute | solution.py:1221
  334.8 54.3 %collective-permute-start.39 = (bf16[8,5,48,256]{3,2,1,0:T(8,128)(2,1)}, bf16[8,5,48,256]{3,2,1,0:T(8,128)(2,1)S(1)}, u32[]{:S(2)}, u32[]{:S(2)}) collective-permute-start(bf16[8,5,48,256]{3,2,1,0:T(8,128)(2,1)} %copy-done.60), channel_id=1, source_target_pairs={{0,8},{2,10},{4,12},{6,14},{8,0},{10,2},{12,4},{14,6},{16,24},{18,... | collective-permute-start | bytes 2949128 | tf_op jit(solution)/shard_map/ppermute | solution.py:1221
  470.4 25.1 %collective-permute-start.61 = (bf16[8,6,48,256]{3,2,1,0:T(8,128)(2,1)S(1)}, bf16[8,6,48,256]{3,2,1,0:T(8,128)(2,1)S(1)}, u32[]{:S(2)}, u32[]{:S(2)}) collective-permute-start(bf16[8,6,48,256]{3,2,1,0:T(8,128)(2,1)S(1)} %constant_dynamic-update-slice_fusion.refs_0_), channel_id=1, source_target_pairs={{0,2},{2,0},{4,6},{6,4},{8,10},{10,8},{12,14},{14,12},{16,18},{18,... | collective-permute-start | bytes 3538952 | tf_op jit(solution)/shard_map/ppermute | solution.py:1221
  (148 other events, 1240.7 us)
Sparse Core Ops, SparseCore 0:
  9.6 11.9 all-gather.6
  23.1 17.9 all-gather.10
  42.6 26.0 all-gather.8
  70.1 11.4 all-gather.14
  82.9 12.8 all-gather.12
  218.0 170.5 all-gather.16
